TPU v7x, 32 devices: a whole 2x2x4 slice. The times are simulated.
32 devices in a mesh: dp: 8 (over z, x), section: 4 (over y, core).
Axes of the slice: x: 2, y: 2, z: 4, core: 2. Of those that a mesh axis runs over, the one named last changes fastest.
Arguments:
- stream: bfloat16 [24, 512, 768], P('dp'), may hold values from -6 to 6
- cotangent: bfloat16 [24, 512, 768], P('dp'), may hold values from -6 to 6
- segments: int32 [24, 512], P('dp'), may hold values from 0 to 3, never falling along the last dimension, each value on 1 to 256 neighbouring positions
- word_boxes: int32 [4, 24, 512], P(None, 'dp'), may hold values from 0 to 1023
- valid_mask: int32 [24, 512], P('dp'), may hold values 0 or 1
- w_qkv: bfloat16 [2, 768, 2304], replicated, may hold values from -0.21875 to 0.21875
- qv_bias: bfloat16 [2, 2, 768], replicated, may hold values from -3 to 3
- w_out: bfloat16 [2, 768, 768], replicated, may hold values from -1.75 to 1.75
- out_bias: bfloat16 [2, 768], replicated, may hold values from -2 to 2
- rel_proj: bfloat16 [2, 12, 64, 128], replicated, may hold values from -0.75 to 0.75
- ln_scale: bfloat16 [2, 2, 768], replicated, may hold values from 0.5 to 1.5
- ln_shift: bfloat16 [2, 2, 768], replicated, may hold values from -2 to 2
- ffn_in: bfloat16 [2, 768, 3072], replicated, may hold values from -0.21875 to 0.21875
- ffn_in_bias: bfloat16 [2, 3072], replicated, may hold values from -2 to 2
- ffn_out: bfloat16 [2, 3072, 768], replicated, may hold values from -0.109375 to 0.109375
- ffn_out_bias: bfloat16 [2, 768], replicated, may hold values from -2 to 2
Outputs:
- section_outputs: bfloat16 [4, 24, 512, 768], P('section', 'dp')
- section_input_grads: float32 [4, 24, 512, 768], P('section', 'dp')
- grad_w_qkv: float32 [2, 768, 2304], P(None, 'dp')
- grad_qv_bias: float32 [2, 2, 768], P(None, None, 'dp')
- grad_w_out: float32 [2, 768, 768], P(None, 'dp')
- grad_out_bias: float32 [2, 768], P(None, 'dp')
- grad_rel_proj: float32 [2, 12, 64, 128], P(None, None, None, 'dp')
- grad_ln_scale: float32 [2, 2, 768], P(None, None, 'dp')
- grad_ln_shift: float32 [2, 2, 768], P(None, None, 'dp')
- grad_ffn_in: float32 [2, 768, 3072], P(None, 'dp')
- grad_ffn_in_bias: float32 [2, 3072], P(None, 'dp')
- grad_ffn_out: float32 [2, 3072, 768], P(None, 'dp')
- grad_ffn_out_bias: float32 [2, 768], P(None, 'dp')
- root_mean_squares: float32 [4, 24, 2], P('section', 'dp')
All inputs are finite; a program needn't handle non-finite values. No bound on the sum of `valid_mask` on one device may be relied on, other than what follows from the above.
Results may differ from a plain program's by a relative error of at most 0.035.
Values may be sent and summed in bfloat16 or wider, within the bound.
No kernel may reach another device: no remote copies, remote signals or barrier semaphores. Data moves between devices by JAX's collectives and lax.ppermute only.
A program may use at most 768 MiB of HBM per device.

v0:
```python
import jax
import jax.numpy as jnp
from jax import lax
from jax.sharding import PartitionSpec as P

MB = 3


ln_eps = 1e-05
masked_score = -1e30
text_pairs = 32
box_pairs = 8


def shifted(shard, axis, by):
    size = lax.axis_size(axis)
    pairs = [(i, i + by) for i in range(size) if 0 <= i + by < size]
    return lax.ppermute(shard, axis, pairs)


def angle_tables(word_boxes, length):
    row_count = word_boxes.shape[1]
    positions = jnp.arange(length, dtype=jnp.float32)
    text_rate = jnp.exp(-jnp.log(10000.0) * jnp.arange(text_pairs, dtype=jnp.float32) / text_pairs)
    text_angle = jnp.broadcast_to(
        positions[:, None] * text_rate[None, :], (row_count, length, text_pairs)
    )
    box_rate = jnp.exp2(-jnp.arange(box_pairs, dtype=jnp.float32))
    coords = jnp.moveaxis(word_boxes.astype(jnp.float32), 0, -1)
    box_angle = (coords[..., None] * box_rate).reshape(row_count, length, 4 * box_pairs)
    angles = jnp.concatenate([text_angle, box_angle], -1)
    return (jnp.cos(angles), jnp.sin(angles))


def allowed_mask(segments, valid_mask):
    length = segments.shape[-1]
    same_page = segments[:, :, None] == segments[:, None, :]
    diagonal = jnp.arange(length)[:, None] == jnp.arange(length)[None, :]
    return same_page & (valid_mask[:, None, :] > 0) | diagonal[None]


def rotate(coefficients, cosines, sines):
    half = coefficients.shape[-1] // 2
    first = coefficients[..., :half]
    second = coefficients[..., half:]
    return jnp.concatenate([first * cosines + second * sines, first * sines - second * cosines], -1)


def norm_parts(residual):
    average = jnp.mean(residual, -1, keepdims=True)
    centered = residual - average
    inverse = lax.rsqrt(jnp.mean(centered * centered, -1, keepdims=True) + ln_eps)
    return (centered * inverse, inverse)


def norm_back(gradient, scale, normed, inverse):
    dnormed = gradient * scale
    return inverse * (
        dnormed
        - jnp.mean(dnormed, -1, keepdims=True)
        - normed * jnp.mean(dnormed * normed, -1, keepdims=True)
    )


def gelu_slope(preact):
    return (
        0.5 * (1.0 + lax.erf(preact * 0.7071067811865476))
        + preact * jnp.exp(-0.5 * preact * preact) * 0.3989422804014327
    )


def joined_sides(query_part, key_part, turned, key_feat):
    head_count, head_size = (query_part.shape[-2], query_part.shape[-1])
    score_scale = jnp.asarray(head_size ** (-0.5), jnp.bfloat16)
    query_side = jnp.concatenate([query_part, turned], -1) * score_scale
    feat_heads = jnp.broadcast_to(
        key_feat[..., None, :], key_feat.shape[:-1] + (head_count, key_feat.shape[-1])
    )
    key_side = jnp.concatenate([key_part, feat_heads], -1)
    return (query_side, key_side)


def row_scores(query_side, key_side, allowed):
    plain_scores = jnp.einsum(
        "ihc,jhc->hij", query_side, key_side, preferred_element_type=jnp.float32
    )
    return jnp.where(allowed[None], plain_scores, masked_score)


def row_forward(pieces):
    query_side, key_side, value_part, allowed = pieces
    scores = row_scores(query_side, key_side, allowed)
    row_max = jnp.max(scores, -1, keepdims=True)
    exponent = jnp.exp(scores - row_max)
    total = jnp.sum(exponent, -1, keepdims=True)
    shares = (exponent / total).astype(jnp.bfloat16)
    context = jnp.einsum("hij,jhd->ihd", shares, value_part, preferred_element_type=jnp.float32)
    return (context.astype(jnp.bfloat16), row_max + jnp.log(total))


def row_backward(pieces):
    query_side, key_side, query_part, value_part, allowed, log_total, grad_context = pieces
    head_size = query_part.shape[-1]
    score_scale = head_size ** (-0.5)
    shares = jnp.exp(row_scores(query_side, key_side, allowed) - log_total)
    grad_value = jnp.einsum(
        "hij,ihd->jhd",
        shares.astype(jnp.bfloat16),
        grad_context,
        preferred_element_type=jnp.float32,
    )
    grad_shares = jnp.einsum(
        "ihd,jhd->hij", grad_context, value_part, preferred_element_type=jnp.float32
    )
    grad_scores = (
        shares * (grad_shares - jnp.sum(shares * grad_shares, -1, keepdims=True))
    ).astype(jnp.bfloat16)
    grad_side = score_scale * jnp.einsum(
        "hij,jhc->ihc", grad_scores, key_side, preferred_element_type=jnp.float32
    )
    grad_key = score_scale * jnp.einsum(
        "hij,ihd->jhd", grad_scores, query_part, preferred_element_type=jnp.float32
    )
    return (grad_side[..., :head_size], grad_key, grad_value, grad_side[..., head_size:])


def attention_forward(stream, params, gain, shift, tables):
    w_qkv, qv_bias, w_out, out_bias, rel_proj = params
    cosines, sines, key_feat, allowed = tables
    row_count, length, model_width = stream.shape
    head_count, head_size = (rel_proj.shape[0], rel_proj.shape[1])
    tokens = row_count * length
    flattened = stream.reshape(tokens, model_width)
    joint_proj = jnp.dot(flattened, w_qkv, preferred_element_type=jnp.float32)
    query_part = (
        (joint_proj[:, :model_width] + qv_bias[0])
        .astype(jnp.bfloat16)
        .reshape(row_count, length, head_count, head_size)
    )
    key_part = (
        joint_proj[:, model_width : 2 * model_width]
        .astype(jnp.bfloat16)
        .reshape(row_count, length, head_count, head_size)
    )
    value_part = (
        (joint_proj[:, 2 * model_width :] + qv_bias[1])
        .astype(jnp.bfloat16)
        .reshape(row_count, length, head_count, head_size)
    )
    coefficients = jnp.einsum(
        "rthd,hdf->rthf", query_part, rel_proj, preferred_element_type=jnp.float32
    )
    turned = rotate(coefficients, cosines[:, :, None], sines[:, :, None]).astype(jnp.bfloat16)
    query_side, key_side = joined_sides(query_part, key_part, turned, key_feat)
    context, log_total = lax.map(row_forward, (query_side, key_side, value_part, allowed))
    context_flat = context.reshape(tokens, model_width)
    attention_out = jnp.dot(context_flat, w_out, preferred_element_type=jnp.float32) + out_bias
    residual_one = flattened.astype(jnp.float32) + attention_out
    normed_one, inverse_one = norm_parts(residual_one)
    mixed_rows = (normed_one * gain + shift).astype(jnp.bfloat16)
    stored = (query_part, key_part, value_part, turned, log_total, context_flat, residual_one)
    return (mixed_rows.reshape(stream.shape), attention_out, stored)


def feed_forward(mixed, params, gain, shift):
    ffn_in, ffn_in_bias, ffn_out, ffn_out_bias = params
    row_count, length, model_width = mixed.shape
    mixed_rows = mixed.reshape(row_count * length, model_width)
    preact = jnp.dot(mixed_rows, ffn_in, preferred_element_type=jnp.float32) + ffn_in_bias
    activated = jax.nn.gelu(preact, approximate=False).astype(jnp.bfloat16)
    feed_out = jnp.dot(activated, ffn_out, preferred_element_type=jnp.float32) + ffn_out_bias
    residual_two = mixed_rows.astype(jnp.float32) + feed_out
    normed_two, inverse_two = norm_parts(residual_two)
    output = normed_two * gain + shift
    return (output.astype(jnp.bfloat16).reshape(mixed.shape), feed_out, (preact, residual_two))


def attention_backward(grad_mixed, stream, stored, params, gain, tables):
    w_qkv, qv_bias, w_out, out_bias, rel_proj = params
    cosines, sines, key_feat, allowed = tables
    query_part, key_part, value_part, turned, log_total, context_flat, residual_one = stored
    row_count, length, model_width = stream.shape
    head_count, head_size = (rel_proj.shape[0], rel_proj.shape[1])
    tokens = row_count * length
    flattened = stream.reshape(tokens, model_width)
    normed_one, inverse_one = norm_parts(residual_one)
    scale_one = jnp.sum(grad_mixed * normed_one, 0)
    shift_one = jnp.sum(grad_mixed, 0)
    grad_res_one = norm_back(grad_mixed, gain, normed_one, inverse_one)
    grad_attention = grad_res_one.astype(jnp.bfloat16)
    grad_context = jnp.einsum(
        "ne,de->nd", grad_attention, w_out, preferred_element_type=jnp.float32
    ).astype(jnp.bfloat16)
    grad_context = grad_context.reshape(row_count, length, head_count, head_size)
    query_side, key_side = joined_sides(query_part, key_part, turned, key_feat)
    grad_query, grad_key, grad_value, grad_turned = lax.map(
        row_backward,
        (query_side, key_side, query_part, value_part, allowed, log_total, grad_context),
    )
    grad_coef = rotate(grad_turned, cosines[:, :, None], sines[:, :, None]).astype(jnp.bfloat16)
    grad_query = grad_query + jnp.einsum(
        "rthf,hdf->rthd", grad_coef, rel_proj, preferred_element_type=jnp.float32
    )
    grad_query = grad_query.astype(jnp.bfloat16).reshape(tokens, model_width)
    grad_key = grad_key.astype(jnp.bfloat16).reshape(tokens, model_width)
    grad_value = grad_value.astype(jnp.bfloat16).reshape(tokens, model_width)
    grad_joint = jnp.concatenate([grad_query, grad_key, grad_value], 1)
    grad_stream = (
        jnp.einsum("ne,de->nd", grad_joint, w_qkv, preferred_element_type=jnp.float32)
        + grad_res_one
    )
    grad_stream = grad_stream.astype(jnp.bfloat16).astype(jnp.float32)
    minor_grads = (
        jnp.stack(
            [jnp.sum(grad_query.astype(jnp.float32), 0), jnp.sum(grad_value.astype(jnp.float32), 0)]
        ),
        jnp.sum(grad_attention.astype(jnp.float32), 0),
        scale_one,
        shift_one,
    )
    operands = (flattened, grad_joint, query_part, grad_coef, context_flat, grad_attention)
    return (grad_stream.reshape(stream.shape), minor_grads, operands)


def feed_backward(grad_top, mixed, stored, params, gain):
    ffn_in, ffn_in_bias, ffn_out, ffn_out_bias = params
    preact, residual_two = stored
    row_count, length, model_width = mixed.shape
    mixed_rows = mixed.reshape(row_count * length, model_width)
    normed_two, inverse_two = norm_parts(residual_two)
    scale_two = jnp.sum(grad_top * normed_two, 0)
    shift_two = jnp.sum(grad_top, 0)
    grad_res_two = norm_back(grad_top, gain, normed_two, inverse_two)
    grad_feed = grad_res_two.astype(jnp.bfloat16)
    activated = jax.nn.gelu(preact, approximate=False).astype(jnp.bfloat16)
    grad_pre = (
        jnp.einsum("nd,fd->nf", grad_feed, ffn_out, preferred_element_type=jnp.float32)
        * gelu_slope(preact)
    ).astype(jnp.bfloat16)
    grad_mixed = (
        jnp.einsum("nf,df->nd", grad_pre, ffn_in, preferred_element_type=jnp.float32) + grad_res_two
    )
    minor_grads = (
        scale_two,
        shift_two,
        jnp.sum(grad_pre.astype(jnp.float32), 0),
        jnp.sum(grad_feed.astype(jnp.float32), 0),
    )
    operands = (mixed_rows, grad_pre, activated, grad_feed)
    return (grad_mixed.reshape(mixed.shape), minor_grads, operands)


def attention_products(operands):
    flattened, grad_joint, query_part, grad_coef, context_flat, grad_attention = operands
    return (
        jnp.einsum("nd,ne->de", flattened, grad_joint, preferred_element_type=jnp.float32),
        jnp.einsum("rthd,rthf->hdf", query_part, grad_coef, preferred_element_type=jnp.float32),
        jnp.einsum("nd,ne->de", context_flat, grad_attention, preferred_element_type=jnp.float32),
    )


def feed_products(operands):
    mixed_rows, grad_pre, activated, grad_feed = operands
    return (
        jnp.einsum("nd,nf->df", mixed_rows, grad_pre, preferred_element_type=jnp.float32),
        jnp.einsum("nf,nd->fd", activated, grad_feed, preferred_element_type=jnp.float32),
    )


def store_at(buffer, batch_index, active, update):
    current = lax.dynamic_index_in_dim(buffer, batch_index, 0, keepdims=False)
    return lax.dynamic_update_index_in_dim(
        buffer, jnp.where(active, update, current), batch_index, 0
    )


def pick_at(buffer, batch_index):
    return lax.dynamic_index_in_dim(buffer, batch_index, 0, keepdims=False)


def when_active(active, action, operands):

    def skipped(*pieces):
        return jax.tree.map(jnp.zeros_like, action(*pieces))

    return lax.cond(active, action, skipped, *operands)


def body(
    stream,
    cotangent,
    segments,
    word_boxes,
    valid_mask,
    w_qkv,
    qv_bias,
    w_out,
    out_bias,
    rel_proj,
    ln_scale,
    ln_shift,
    ffn_in,
    ffn_in_bias,
    ffn_out,
    ffn_out_bias,
):
    sections = lax.axis_size("section")
    section_index = lax.axis_index("section")
    layer_index = section_index // 2
    is_attention = section_index % 2 == 0

    def pick_layer(weight):
        return lax.dynamic_index_in_dim(weight, layer_index, 0, keepdims=False)

    attention_params = tuple((pick_layer(w) for w in (w_qkv, qv_bias, w_out, out_bias, rel_proj)))
    ffn_params = tuple((pick_layer(w) for w in (ffn_in, ffn_in_bias, ffn_out, ffn_out_bias)))
    scale_pair = pick_layer(ln_scale)
    shift_pair = pick_layer(ln_shift)
    norm_gain = jnp.where(is_attention, scale_pair[0], scale_pair[1])
    norm_bias = jnp.where(is_attention, shift_pair[0], shift_pair[1])
    local_rows, length, model_width = stream.shape
    head_count, head_size, rel_width = (rel_proj.shape[1], rel_proj.shape[2], rel_proj.shape[3])
    ff_width = ffn_in.shape[2]
    per_batch = local_rows // MB
    tokens = per_batch * length
    ticks = MB + sections - 1
    bf16 = jnp.bfloat16
    f32 = jnp.float32

    def blank_attention_store():
        heads_shape = (per_batch, length, head_count, head_size)
        return (
            jnp.zeros(heads_shape, bf16),
            jnp.zeros(heads_shape, bf16),
            jnp.zeros(heads_shape, bf16),
            jnp.zeros((per_batch, length, head_count, rel_width), bf16),
            jnp.zeros((per_batch, head_count, length, 1), f32),
            jnp.zeros((tokens, model_width), bf16),
            jnp.zeros((tokens, model_width), f32),
        )

    def blank_feed_store():
        return (jnp.zeros((tokens, ff_width), f32), jnp.zeros((tokens, model_width), f32))

    def blank_attention_operands():
        return (
            jnp.zeros((tokens, model_width), bf16),
            jnp.zeros((tokens, 3 * model_width), bf16),
            jnp.zeros((per_batch, length, head_count, head_size), bf16),
            jnp.zeros((per_batch, length, head_count, rel_width), bf16),
            jnp.zeros((tokens, model_width), bf16),
            jnp.zeros((tokens, model_width), bf16),
        )

    def blank_feed_operands():
        return (
            jnp.zeros((tokens, model_width), bf16),
            jnp.zeros((tokens, ff_width), bf16),
            jnp.zeros((tokens, ff_width), bf16),
            jnp.zeros((tokens, model_width), bf16),
        )

    def batch_slice(source, batch_index, dimension):
        return lax.dynamic_slice_in_dim(source, batch_index * per_batch, per_batch, dimension)

    def tables_for(batch_index):
        cosines, sines = angle_tables(batch_slice(word_boxes, batch_index, 1), length)
        key_feat = jnp.concatenate([cosines, sines], -1).astype(bf16)
        allowed = allowed_mask(
            batch_slice(segments, batch_index, 0), batch_slice(valid_mask, batch_index, 0)
        )
        return (cosines, sines, key_feat, allowed)

    def run_forward(inputs, batch_index):

        def attention_branch(source):
            output, branch, stored = attention_forward(
                source, attention_params, norm_gain, norm_bias, tables_for(batch_index)
            )
            return (output, branch, (stored, blank_feed_store()))

        def feed_branch(source):
            output, branch, stored = feed_forward(source, ffn_params, norm_gain, norm_bias)
            return (output, branch, (blank_attention_store(), stored))

        output, branch, stored = lax.cond(is_attention, attention_branch, feed_branch, inputs)
        weight = batch_slice(valid_mask, batch_index, 0).reshape(-1, 1).astype(f32)

        def row_sums(values):
            return jnp.sum((values * values * weight).reshape(per_batch, -1), 1)

        square_sums = jnp.stack(
            [row_sums(branch), row_sums(output.astype(f32).reshape(tokens, model_width))], -1
        )
        return (output, square_sums, stored)

    def run_backward(grad_out, inputs, stored, batch_index):
        attention_stored, feed_stored = stored
        grad_flat = grad_out.reshape(tokens, model_width)

        def attention_branch(pieces):
            gradient, source = pieces
            grad_in, minor_grads, operands = attention_backward(
                gradient,
                source,
                attention_stored,
                attention_params,
                norm_gain,
                tables_for(batch_index),
            )
            qv_grad, bias_grad, gain_grad, shift_grad = minor_grads
            return (
                grad_in,
                (
                    qv_grad,
                    bias_grad,
                    gain_grad,
                    shift_grad,
                    jnp.zeros((ff_width,), f32),
                    jnp.zeros((model_width,), f32),
                ),
                (operands, blank_feed_operands()),
            )

        def feed_branch(pieces):
            gradient, source = pieces
            grad_in, minor_grads, operands = feed_backward(
                gradient, source, feed_stored, ffn_params, norm_gain
            )
            gain_grad, shift_grad, in_bias_grad, out_bias_grad = minor_grads
            return (
                grad_in,
                (
                    jnp.zeros((2, model_width), f32),
                    jnp.zeros((model_width,), f32),
                    gain_grad,
                    shift_grad,
                    in_bias_grad,
                    out_bias_grad,
                ),
                (blank_attention_operands(), operands),
            )

        return lax.cond(is_attention, attention_branch, feed_branch, (grad_flat, inputs))

    def major_products(operands):

        def attention_branch(pieces):
            return attention_products(pieces[0]) + (
                jnp.zeros((model_width, ff_width), f32),
                jnp.zeros((ff_width, model_width), f32),
            )

        def feed_branch(pieces):
            return (
                jnp.zeros((model_width, 3 * model_width), f32),
                jnp.zeros((head_count, head_size, rel_width), f32),
                jnp.zeros((model_width, model_width), f32),
            ) + feed_products(pieces[1])

        return lax.cond(is_attention, attention_branch, feed_branch, operands)

    def run_backward_full(grad_out, inputs, stored, batch_index):
        grad_in, minor_grads, operands = run_backward(grad_out, inputs, stored, batch_index)
        return (grad_in, minor_grads, major_products(operands))

    arriving = jnp.zeros((per_batch, length, model_width), bf16)
    for ticker in range(ticks):
        batch_index = ticker - section_index
        active = (batch_index >= 0) & (batch_index < MB)
        batch_index = jnp.clip(batch_index, 0, MB - 1)
        inputs = jnp.where(section_index == 0, batch_slice(stream, batch_index, 0), arriving)
        output, square_sums, stored = when_active(active, run_forward, (inputs, batch_index))
        if ticker == 0:
            section_outs = jnp.zeros((MB,) + output.shape, output.dtype)
            square_rows = jnp.zeros((MB,) + square_sums.shape, square_sums.dtype)
            saved_inputs = jnp.zeros((MB,) + inputs.shape, inputs.dtype)
            saved = jax.tree.map(lambda piece: jnp.zeros((MB,) + piece.shape, piece.dtype), stored)
        section_outs = store_at(section_outs, batch_index, active, output)
        square_rows = store_at(square_rows, batch_index, active, square_sums)
        saved_inputs = store_at(saved_inputs, batch_index, active, inputs)
        saved = jax.tree.map(
            lambda buffer, piece: store_at(buffer, batch_index, active, piece), saved, stored
        )
        arriving = shifted(output, "section", 1)
    returning = jnp.zeros((per_batch, length, model_width), f32)
    for ticker in range(ticks):
        batch_index = ticker - (sections - 1 - section_index)
        active = (batch_index >= 0) & (batch_index < MB)
        batch_index = jnp.clip(batch_index, 0, MB - 1)
        grad_out = jnp.where(
            section_index == sections - 1,
            batch_slice(cotangent, batch_index, 0).astype(f32),
            returning,
        )
        inputs = pick_at(saved_inputs, batch_index)
        stored = jax.tree.map(lambda buffer: pick_at(buffer, batch_index), saved)
        grad_in, minor_grads, major_now = when_active(
            active, run_backward_full, (grad_out, inputs, stored, batch_index)
        )
        if ticker == 0:
            major = major_now
        else:
            major = jax.tree.map(jnp.add, major, major_now)
        if ticker == 0:
            minor = minor_grads
            in_grads = jnp.zeros((MB,) + grad_in.shape, grad_in.dtype)
        else:
            minor = jax.tree.map(jnp.add, minor, minor_grads)
        in_grads = store_at(in_grads, batch_index, active, grad_in)
        returning = shifted(grad_in.astype(jnp.bfloat16), "section", -1).astype(grad_in.dtype)
    qv_grad, bias_grad, gain_grad, shift_grad, in_bias_grad, out_ffn_bias_grad = minor
    qkv_grad, relative_grad, attn_out_grad, ffn_in_grad, ffn_out_grad = major
    members = (
        qkv_grad[None],
        qv_grad[None],
        attn_out_grad[None],
        bias_grad[None],
        relative_grad[None],
        gain_grad[None],
        shift_grad[None],
        ffn_in_grad[None],
        in_bias_grad[None],
        ffn_out_grad[None],
        out_ffn_bias_grad[None],
    )
    summed = (
        lax.psum_scatter(members[0], "dp", scatter_dimension=1, tiled=True),
        lax.psum_scatter(members[1], "dp", scatter_dimension=2, tiled=True),
        lax.psum_scatter(members[2], "dp", scatter_dimension=1, tiled=True),
        lax.psum_scatter(members[3], "dp", scatter_dimension=1, tiled=True),
        lax.psum_scatter(members[4], "dp", scatter_dimension=3, tiled=True),
        lax.psum_scatter(members[5], "dp", scatter_dimension=1, tiled=True),
        lax.psum_scatter(members[6], "dp", scatter_dimension=1, tiled=True),
        lax.psum_scatter(members[7], "dp", scatter_dimension=1, tiled=True),
        lax.psum_scatter(members[8], "dp", scatter_dimension=1, tiled=True),
        lax.psum_scatter(members[9], "dp", scatter_dimension=1, tiled=True),
        lax.psum_scatter(members[10], "dp", scatter_dimension=1, tiled=True),
    )
    gathered = (
        lax.all_gather(summed[0].astype(jnp.bfloat16), "section", axis=0, tiled=True).astype(
            jnp.float32
        ),
        lax.all_gather(summed[1].astype(jnp.bfloat16), "section", axis=0, tiled=True).astype(
            jnp.float32
        ),
        lax.all_gather(summed[2].astype(jnp.bfloat16), "section", axis=0, tiled=True).astype(
            jnp.float32
        ),
        lax.all_gather(summed[3].astype(jnp.bfloat16), "section", axis=0, tiled=True).astype(
            jnp.float32
        ),
        lax.all_gather(summed[4].astype(jnp.bfloat16), "section", axis=0, tiled=True).astype(
            jnp.float32
        ),
        lax.all_gather(summed[5].astype(jnp.bfloat16), "section", axis=0, tiled=True).astype(
            jnp.float32
        ),
        lax.all_gather(summed[6].astype(jnp.bfloat16), "section", axis=0, tiled=True).astype(
            jnp.float32
        ),
        lax.all_gather(summed[7].astype(jnp.bfloat16), "section", axis=0, tiled=True).astype(
            jnp.float32
        ),
        lax.all_gather(summed[8].astype(jnp.bfloat16), "section", axis=0, tiled=True).astype(
            jnp.float32
        ),
        lax.all_gather(summed[9].astype(jnp.bfloat16), "section", axis=0, tiled=True).astype(
            jnp.float32
        ),
        lax.all_gather(summed[10].astype(jnp.bfloat16), "section", axis=0, tiled=True).astype(
            jnp.float32
        ),
    )
    layer_count = sections // 2
    grad_w_qkv = gathered[0][0::2]
    grad_qv_bias = gathered[1][0::2]
    grad_w_out = gathered[2][0::2]
    grad_out_bias = gathered[3][0::2]
    grad_rel_proj = gathered[4][0::2]
    grad_ln_scale = gathered[5].reshape((layer_count, 2) + gathered[5].shape[1:])
    grad_ln_shift = gathered[6].reshape((layer_count, 2) + gathered[6].shape[1:])
    grad_ffn_in = gathered[7][1::2]
    grad_ffn_in_bias = gathered[8][1::2]
    grad_ffn_out = gathered[9][1::2]
    grad_ffn_out_bias = gathered[10][1::2]
    row_counts = jnp.sum(valid_mask.astype(f32), 1)
    square_flat = square_rows.reshape(local_rows, 2)
    root_mean_squares = jnp.sqrt(
        square_flat / (model_width * jnp.maximum(row_counts, 1.0))[:, None]
    )[None]
    return (
        section_outs.reshape((1, local_rows, length, model_width)),
        in_grads.reshape((1, local_rows, length, model_width)),
        grad_w_qkv,
        grad_qv_bias,
        grad_w_out,
        grad_out_bias,
        grad_rel_proj,
        grad_ln_scale,
        grad_ln_shift,
        grad_ffn_in,
        grad_ffn_in_bias,
        grad_ffn_out,
        grad_ffn_out_bias,
        root_mean_squares,
    )


def solution(mesh):
    return jax.shard_map(
        body,
        mesh=mesh,
        in_specs=(
            P("dp", None, None),
            P("dp", None, None),
            P("dp", None),
            P(None, "dp", None),
            P("dp", None),
            P(),
            P(),
            P(),
            P(),
            P(),
            P(),
            P(),
            P(),
            P(),
            P(),
            P(),
        ),
        out_specs=(
            P("section", "dp", None, None),
            P("section", "dp", None, None),
            P(None, "dp", None),
            P(None, None, "dp"),
            P(None, "dp", None),
            P(None, "dp"),
            P(None, None, None, "dp"),
            P(None, None, "dp"),
            P(None, None, "dp"),
            P(None, "dp", None),
            P(None, "dp"),
            P(None, "dp", None),
            P(None, "dp"),
            P("section", "dp", None),
        ),
        check_vma=False,
    )
```

profile of v0, /device:TPU:0, one launch (start us, length us, event | category | flops | bytes accessed | tf_op | source)
XLA Modules:
  0.0 2604.9 jit_solution(12548811162811824100)
XLA Ops:
  28.1 104.5 %conditional.30 = (bf16[1,512,768]{2,1,0:T(8,128)(2,1)}, f32[1,2]{1,0:T(1,128)}, bf16[512,768]{1,0:T(8,128)(2,1)}, f32[512,768]{1,0:T(8,128)}, f32[512,3072]{1,0...) conditional(s32[]{:T(128)} %convert_element_type.1577, ...), branch_computations={%region_0.1_spmd, %region_1.12_spmd} | conditional | flops 4943124992 | bytes 133785528 | solution.py:286
  29.5 79.7 %conditional = (bf16[1,512,768]{2,1,0:T(8,128)(2,1)}, f32[512,768]{1,0:T(8,128)S(1)}, bf16[1,512,12,64]{3,2,1,0:T(8,128)(2,1)}, bf16[1,512,12,64]{3,2,1,0:T(8,12...) conditional(s32[]{:T(128)} %convert_element_type.1287, ...), branch_computations={%region_2.4_spmd, %region_5.9_spmd} | conditional | flops 4941158400 | bytes 122717840 | solution.py:386
  170.4 8.8 broadcast_in_dim.1034
  199.8 104.3 %conditional.31 = (bf16[1,512,768]{2,1,0:T(8,128)(2,1)}, f32[1,2]{1,0:T(1,128)}, bf16[512,768]{1,0:T(8,128)(2,1)}, f32[512,768]{1,0:T(8,128)}, f32[512,3072]{1,0...) conditional(s32[]{:T(128)} %convert_element_type.1578, ...), branch_computations={%region_12.13_spmd, %region_13.24_spmd} | conditional | flops 4943124992 | bytes 133785528 | solution.py:286
  201.1 79.5 %conditional.1 = (bf16[1,512,768]{2,1,0:T(8,128)(2,1)}, f32[512,768]{1,0:T(8,128)S(1)}, bf16[1,512,12,64]{3,2,1,0:T(8,128)(2,1)}, bf16[1,512,12,64]{3,2,1,0:T(8,...) conditional(s32[]{:T(128)} %convert_element_type.1310, ...), branch_computations={%region_14.16_spmd, %region_17.21_spmd} | conditional | flops 4941158400 | bytes 122717840 | solution.py:386
  353.6 104.4 %conditional.32 = (bf16[1,512,768]{2,1,0:T(8,128)(2,1)}, f32[1,2]{1,0:T(1,128)}, bf16[512,768]{1,0:T(8,128)(2,1)}, f32[512,768]{1,0:T(8,128)}, f32[512,3072]{1,0...) conditional(s32[]{:T(128)} %convert_element_type.1579, ...), branch_computations={%region_24.25_spmd, %region_25.36_spmd} | conditional | flops 4943124992 | bytes 133785528 | solution.py:286
  354.9 79.6 %conditional.2 = (bf16[1,512,768]{2,1,0:T(8,128)(2,1)}, f32[512,768]{1,0:T(8,128)S(1)}, bf16[1,512,12,64]{3,2,1,0:T(8,128)(2,1)}, bf16[1,512,12,64]{3,2,1,0:T(8,...) conditional(s32[]{:T(128)} %convert_element_type.1333, ...), branch_computations={%region_26.28_spmd, %region_29.33_spmd} | conditional | flops 4941158400 | bytes 122717840 | solution.py:386
  507.4 18.3 conditional.33
  534.7 24.6 collective-permute-start.3
  588.4 18.1 conditional.34
  615.4 9.3 collective-permute-start.4
  652.2 18.2 conditional.35
  687.5 27.2 %conditional.36 = (f32[1,512,768]{2,1,0:T(8,128)}, f32[2,768]{1,0:T(2,128)}, f32[768]{0:T(1024)}, f32[768]{0:T(1024)}, f32[768]{0:T(1024)}, /*index=5*/f32[3072]...) conditional(s32[]{:T(128)} %convert_element_type.1583, ...), branch_computations={%region_72.73_spmd, %region_73.96_spmd} | conditional | flops 11060244480 | bytes 406505248 | solution.py:286
  718.3 71.5 %collective-permute-done.5 = bf16[1,512,768]{2,1,0:T(8,128)(2,1)} collective-permute-done((bf16[1,512,768]{2,1,0:T(8,128)(2,1)}, bf16[1,512,768]{2,1,0:T(8,128)(2,1)}, u32[]{:S(2)}, u32[]{:S(2)}) %collective-permute-start.5) | collective-permute-done | bytes 786464 | tf_op jit(solution)/shard_map/ppermute | solution.py:18
  792.2 27.3 %conditional.37 = (f32[1,512,768]{2,1,0:T(8,128)}, f32[2,768]{1,0:T(2,128)}, f32[768]{0:T(1024)}, f32[768]{0:T(1024)}, f32[768]{0:T(1024)}, /*index=5*/f32[3072]...) conditional(s32[]{:T(128)} %convert_element_type.1585, ...), branch_computations={%region_96.97_spmd, %region_97.120_spmd} | conditional | flops 11060244480 | bytes 406505248 | solution.py:286
  823.2 18.1 collective-permute-done.6
  843.6 27.2 %conditional.38 = (f32[1,512,768]{2,1,0:T(8,128)}, f32[2,768]{1,0:T(2,128)}, f32[768]{0:T(1024)}, f32[768]{0:T(1024)}, f32[768]{0:T(1024)}, /*index=5*/f32[3072]...) conditional(s32[]{:T(128)} %convert_element_type.1589, ...), branch_computations={%region_120.121_spmd, %region_121.144_spmd} | conditional | flops 11060244480 | bytes 406505248 | solution.py:286
  874.5 200.7 %collective-permute-done.7 = bf16[1,512,768]{2,1,0:T(8,128)(2,1)} collective-permute-done((bf16[1,512,768]{2,1,0:T(8,128)(2,1)}, bf16[1,512,768]{2,1,0:T(8,128)(2,1)}, u32[]{:S(2)}, u32[]{:S(2)}) %collective-permute-start.7) | collective-permute-done | bytes 786464 | tf_op jit(solution)/shard_map/ppermute | solution.py:18
  1077.6 114.2 %conditional.39 = (f32[1,512,768]{2,1,0:T(8,128)}, f32[2,768]{1,0:T(2,128)}, f32[768]{0:T(1024)}, f32[768]{0:T(1024)}, f32[768]{0:T(1024)}, /*index=5*/f32[3072]...) conditional(s32[]{:T(128)} %convert_element_type.1593, ...), branch_computations={%region_144.145_spmd, %region_145.168_spmd} | conditional | flops 11060244480 | bytes 406505248 | solution.py:286
  1083.2 86.4 %conditional.12 = (f32[1,512,768]{2,1,0:T(8,128)}, f32[2,768]{1,0:T(2,128)}, f32[768]{0:T(1024)}, f32[768]{0:T(1024)}, f32[768]{0:T(1024)}, /*index=5*/f32[3072]...) conditional(s32[]{:T(128)} %convert_element_type.1492, ...), branch_computations={%region_146.154_spmd, %region_155.165_spmd} | conditional | flops 6228012544 | bytes 344376640 | solution.py:444
  1125.3 11.3 multiply_reduce_fusion.63
  1169.6 22.1 conditional.13
  1195.5 10.3 collective-permute-done.8
  1208.2 114.2 %conditional.40 = (f32[1,512,768]{2,1,0:T(8,128)}, f32[2,768]{1,0:T(2,128)}, f32[768]{0:T(1024)}, f32[768]{0:T(1024)}, f32[768]{0:T(1024)}, /*index=5*/f32[3072]...) conditional(s32[]{:T(128)} %convert_element_type.1597, ...), branch_computations={%region_168.169_spmd, %region_169.192_spmd} | conditional | flops 11060244480 | bytes 406505248 | solution.py:286
  1213.8 86.4 %conditional.14 = (f32[1,512,768]{2,1,0:T(8,128)}, f32[2,768]{1,0:T(2,128)}, f32[768]{0:T(1024)}, f32[768]{0:T(1024)}, f32[768]{0:T(1024)}, /*index=5*/f32[3072]...) conditional(s32[]{:T(128)} %convert_element_type.1514, ...), branch_computations={%region_170.178_spmd, %region_179.189_spmd} | conditional | flops 6228012544 | bytes 344376640 | solution.py:444
  1255.9 11.3 multiply_reduce_fusion.68
  1300.2 22.0 conditional.15
  1326.0 10.6 collective-permute-done.9
  1339.1 110.2 %conditional.41 = (f32[1,512,768]{2,1,0:T(8,128)}, f32[2,768]{1,0:T(2,128)}, f32[768]{0:T(1024)}, f32[768]{0:T(1024)}, f32[768]{0:T(1024)}, /*index=5*/f32[3072]...) conditional(s32[]{:T(128)} %convert_element_type.1601, ...), branch_computations={%region_192.193_spmd, %region_193.216_spmd} | conditional | flops 11060244480 | bytes 413321376 | solution.py:286
  1344.7 83.2 %conditional.16 = (f32[1,512,768]{2,1,0:T(8,128)}, f32[2,768]{1,0:T(2,128)}, f32[768]{0:T(1024)}, f32[768]{0:T(1024)}, f32[768]{0:T(1024)}, /*index=5*/f32[3072]...) conditional(s32[]{:T(128)} %convert_element_type.1536, ...), branch_computations={%region_194.202_spmd, %region_203.213_spmd} | conditional | flops 6228012544 | bytes 351192800 | solution.py:444
  1386.8 11.3 multiply_reduce_fusion.73
  1427.9 21.2 conditional.17
  1449.3 17.5 add_bitcast_fusion.14
  1466.9 24.0 add_bitcast_fusion.13
  1491.0 23.5 add_bitcast_fusion.12
  1539.0 58.7 %reduce-scatter.23.cloned.1.call-done = f32[1,96,2304]{2,1,0:T(8,128)} async-done(((f32[1,768,2304]{2,1,0:T(8,128)}), f32[1,96,2304]{2,1,0:T(8,128)}) %reduce-scatter.23.cloned.1.call-update) | async-done | bytes 884752 | tf_op jit(solution)/shard_map/reduce_scatter | solution.py:528
  1607.9 156.3 %reduce-scatter.27.cloned.1.call-done = f32[1,96,3072]{2,1,0:T(8,128)} async-done(((f32[1,768,3072]{2,1,0:T(8,128)}), f32[1,96,3072]{2,1,0:T(8,128)}) %reduce-scatter.27.cloned.1.call-update) | async-done | bytes 1179664 | tf_op jit(solution)/shard_map/reduce_scatter | solution.py:535
  1790.3 299.1 %all-reduce.2 = bf16[1,12,64,128]{2,0,1,3:T(2,128)(2,1)S(1)} all-reduce(f32[1,12,64,128]{2,0,1,3:T(1,128)S(1)} %copy.1084), channel_id=6, replica_groups=mesh['dp'=8,'section'=4] {'dp'}, use_global_device_ids=true, to_apply=%region_220.221.clone | all-reduce | flops 98304 | bytes 589824
  2101.2 24.7 reduce-scatter.33.cloned.1.call-done
  2132.5 57.3 %reduce-scatter.35.cloned.1.call-done = f32[96,1]{1,0:T(8,128)} async-done(((f32[768,1]{1,0:T(8,128)}), f32[96,1]{1,0:T(8,128)}) %reduce-scatter.35.cloned.1.call-update) | async-done | bytes 400
  2196.3 57.3 %reduce-scatter.37.cloned.1.call-done = f32[96,1]{1,0:T(8,128)} async-done(((f32[768,1]{1,0:T(8,128)}), f32[96,1]{1,0:T(8,128)}) %reduce-scatter.37.cloned.1.call-update) | async-done | bytes 400
  2260.1 57.5 %reduce-scatter.41.cloned.1.call-done = f32[96,1]{1,0:T(8,128)} async-done(((f32[768,1]{1,0:T(8,128)}), f32[96,1]{1,0:T(8,128)}) %reduce-scatter.41.cloned.1.call-update) | async-done | bytes 400
  2324.1 58.0 %reduce-scatter.31.cloned.1.call-done = f32[96,2]{1,0:T(8,128)} async-done(((f32[768,2]{1,0:T(8,128)}), f32[96,2]{1,0:T(8,128)}) %reduce-scatter.31.cloned.1.call-update) | async-done | bytes 784
  2388.6 61.7 %reduce-scatter.39.cloned.1.call-done = f32[384,1]{1,0:T(8,128)} async-done(((f32[3072,1]{1,0:T(8,128)}), f32[384,1]{1,0:T(8,128)}) %reduce-scatter.39.cloned.1.call-update) | async-done | bytes 1552
  2457.1 65.0 %reduce-scatter.25.cloned.1.call-done = f32[1,96,768]{2,1,0:T(8,128)} async-done(((f32[1,768,768]{2,1,0:T(8,128)}), f32[1,96,768]{2,1,0:T(8,128)}) %reduce-scatter.25.cloned.1.call-update) | async-done | bytes 294928 | tf_op jit(solution)/shard_map/reduce_scatter | solution.py:530
  2531.5 12.1 all-gather.9.cloned.1.call-done
  2546.2 23.5 all-gather.11.cloned.1.call-done
  2572.6 22.7 all-gather.13.cloned.1.call-done
  (1098 shorter events, 1138.0 us)
Async XLA Ops:
  7.2 1590.5 %reduce-scatter.23.cloned.1.call-start = ((), (), s32[]{:S(2)}) async-start(), calls=%async_computation.10 | async-start | bytes 7962624 | tf_op jit(solution)/shard_map/reduce_scatter | solution.py:528
  28.1 106.8 %copy-start.18 = (bf16[3,1,512,768]{3,2,0,1:T(8,128)(2,1)}, bf16[3,1,512,768]{3,2,0,1:T(8,128)(2,1)S(1)}, u32[]{:S(2)}) copy-start(bf16[3,1,512,768]{3,2,0,1:T(8,128)(2,1)S(1)} %get-tuple-element.7147) | copy-start | bytes 7077892
  132.7 63.0 %collective-permute-start = (bf16[1,512,768]{2,1,0:T(8,128)(2,1)}, bf16[1,512,768]{2,1,0:T(8,128)(2,1)}, u32[]{:S(2)}, u32[]{:S(2)}) collective-permute-start(bf16[1,512,768]{2,1,0:T(8,128)(2,1)} %get-tuple-element.4286), channel_id=1, source_target_pairs={{0,1},{1,2},{2,3},{4,5},{5,6},{6,7},{8,9},{9,10},{10,11},{12,13},{... | collective-permute-start | bytes 2359304 | tf_op jit(solution)/shard_map/ppermute | solution.py:18
  170.4 15.2 copy-start.213
  304.2 18.6 slice-start.26
  315.7 33.8 %collective-permute-start.1 = (bf16[1,512,768]{2,1,0:T(8,128)(2,1)}, bf16[1,512,768]{2,1,0:T(8,128)(2,1)S(1)}, u32[]{:S(2)}, u32[]{:S(2)}) collective-permute-start(bf16[1,512,768]{2,1,0:T(8,128)(2,1)} %get-tuple-element.4287), channel_id=1, source_target_pairs={{0,1},{1,2},{2,3},{4,5},{5,6},{6,7},{8,9},{9,10},{10,11},{12,13},{... | collective-permute-start | bytes 2359304 | tf_op jit(solution)/shard_map/ppermute | solution.py:18
  458.1 18.6 slice-start.28
  469.7 33.6 %collective-permute-start.2 = (bf16[1,512,768]{2,1,0:T(8,128)(2,1)}, bf16[1,512,768]{2,1,0:T(8,128)(2,1)S(1)}, u32[]{:S(2)}, u32[]{:S(2)}) collective-permute-start(bf16[1,512,768]{2,1,0:T(8,128)(2,1)} %get-tuple-element.4288), channel_id=1, source_target_pairs={{0,1},{1,2},{2,3},{4,5},{5,6},{6,7},{8,9},{9,10},{10,11},{12,13},{... | collective-permute-start | bytes 2359304 | tf_op jit(solution)/shard_map/ppermute | solution.py:18
  525.8 38.4 %slice-start.30 = ((s8[4718592]{0:T(1024)(128)(4,1)}), s8[4194304]{0:T(1024)(128)(4,1)S(1)}, s32[]{:S(2)}) async-start(s8[4718592]{0:T(1024)(128)(4,1)} %bitcast.1959), calls=%async_computation.53 | async-start | bytes 8388608
  530.2 29.1 %copy-start.97 = (f32[1,512,768]{2,1,0:T(8,128)S(1)}, f32[1,512,768]{2,1,0:T(8,128)}, u32[]{:S(2)}) copy-start(f32[1,512,768]{2,1,0:T(8,128)} %constant_dynamic-slice_fusion.71) | copy-start | bytes 4718596
  533.5 30.7 %slice-start.31 = ((s8[4718592]{0:T(1024)(128)(4,1)}), s8[524288]{0:T(1024)(128)(4,1)S(1)}, s32[]{:S(2)}) async-start(s8[4718592]{0:T(1024)(128)(4,1)} %bitcast.1959), calls=%async_computation.54 | async-start | bytes 1048576
  534.7 49.6 %collective-permute-start.3 = (bf16[1,512,768]{2,1,0:T(8,128)(2,1)}, bf16[1,512,768]{2,1,0:T(8,128)(2,1)S(1)}, u32[]{:S(2)}, u32[]{:S(2)}) collective-permute-start(bf16[1,512,768]{2,1,0:T(8,128)(2,1)} %get-tuple-element.4289), channel_id=1, source_target_pairs={{0,1},{1,2},{2,3},{4,5},{5,6},{6,7},{8,9},{9,10},{10,11},{12,13},{... | collective-permute-start | bytes 2359304 | tf_op jit(solution)/shard_map/ppermute | solution.py:18
  606.5 23.2 slice-start.32
  611.0 13.7 copy-start.100
  614.2 15.4 slice-start.33
  615.4 34.2 %collective-permute-start.4 = (bf16[1,512,768]{2,1,0:T(8,128)(2,1)}, bf16[1,512,768]{2,1,0:T(8,128)(2,1)S(1)}, u32[]{:S(2)}, u32[]{:S(2)}) collective-permute-start(bf16[1,512,768]{2,1,0:T(8,128)(2,1)} %get-tuple-element.4290), channel_id=1, source_target_pairs={{0,1},{1,2},{2,3},{4,5},{5,6},{6,7},{8,9},{9,10},{10,11},{12,13},{... | collective-permute-start | bytes 2359304 | tf_op jit(solution)/shard_map/ppermute | solution.py:18
  717.1 72.8 %collective-permute-start.5 = (bf16[1,512,768]{2,1,0:T(8,128)(2,1)}, bf16[1,512,768]{2,1,0:T(8,128)(2,1)}, u32[]{:S(2)}, u32[]{:S(2)}) collective-permute-start(bf16[1,512,768]{2,1,0:T(8,128)(2,1)} %convert_element_type.1587), channel_id=1, source_target_pairs={{1,0},{2,1},{3,2},{5,4},{6,5},{7,6},{9,8},{10,9},{11,10},{13,12},{... | collective-permute-start | bytes 2359304 | tf_op jit(solution)/shard_map/ppermute | solution.py:18
  821.9 19.4 collective-permute-start.6
  873.2 202.0 %collective-permute-start.7 = (bf16[1,512,768]{2,1,0:T(8,128)(2,1)}, bf16[1,512,768]{2,1,0:T(8,128)(2,1)}, u32[]{:S(2)}, u32[]{:S(2)}) collective-permute-start(bf16[1,512,768]{2,1,0:T(8,128)(2,1)} %convert_element_type.1595), channel_id=1, source_target_pairs={{1,0},{2,1},{3,2},{5,4},{6,5},{7,6},{9,8},{10,9},{11,10},{13,12},{... | collective-permute-start | bytes 2359304 | tf_op jit(solution)/shard_map/ppermute | solution.py:18
  1125.2 11.4 slice-start.17
  1125.2 11.4 slice-start.18
  1125.2 12.9 slice-start.19
  1125.2 12.9 copy-start.208
  1125.3 12.9 copy-start.260
  1194.2 11.6 collective-permute-start.8
  1255.9 11.4 slice-start.20
  1255.9 11.4 slice-start.21
  1255.9 12.9 slice-start.22
  1255.9 12.9 copy-start.210
  1255.9 12.9 copy-start.262
  1324.8 11.9 collective-permute-start.9
  1386.7 11.3 slice-start.23
  1386.7 11.3 slice-start.24
  1386.7 12.9 slice-start.25
  1386.7 12.9 copy-start.264
  1466.8 297.4 %reduce-scatter.27.cloned.1.call-start = ((), (), s32[]{:S(2)}) async-start(), calls=%async_computation.13 | async-start | bytes 10616832 | tf_op jit(solution)/shard_map/reduce_scatter | solution.py:535
  1490.9 607.4 %reduce-scatter.29.cloned.1.call-start = ((), (), s32[]{:S(2)}) async-start(), calls=%async_computation.15 | async-start | bytes 10616832 | tf_op jit(solution)/shard_map/reduce_scatter | solution.py:537
  1514.4 611.5 %reduce-scatter.33.cloned.1.call-start = ((), (), s32[]{:S(2)}) async-start(), calls=%async_computation.18 | async-start | bytes 442368
  1516.1 673.6 %reduce-scatter.35.cloned.1.call-start = ((), (), s32[]{:S(2)}) async-start(), calls=%async_computation.19 | async-start | bytes 442368
  1517.9 735.7 %reduce-scatter.37.cloned.1.call-start = ((), (), s32[]{:S(2)}) async-start(), calls=%async_computation.20 | async-start | bytes 442368
  1519.6 797.9 %reduce-scatter.41.cloned.1.call-start = ((), (), s32[]{:S(2)}) async-start(), calls=%async_computation.22 | async-start | bytes 442368
  1521.4 860.7 %reduce-scatter.31.cloned.1.call-start = ((), (), s32[]{:S(2)}) async-start(), calls=%async_computation.17 | async-start | bytes 442368
  1523.2 927.1 %reduce-scatter.39.cloned.1.call-start = ((), (), s32[]{:S(2)}) async-start(), calls=%async_computation.21 | async-start | bytes 1769472
  1525.8 996.4 %reduce-scatter.25.cloned.1.call-start = ((), (), s32[]{:S(2)}) async-start(), calls=%async_computation.12 | async-start | bytes 2654208 | tf_op jit(solution)/shard_map/reduce_scatter | solution.py:530
  1533.4 1010.2 %all-gather.9.cloned.1.call-start = ((), (), s32[]{:S(2)}) async-start(), calls=%async_computation.11 | async-start | bytes 2211840 | tf_op jit(solution)/shard_map/all_gather | solution.py:541
  1599.7 969.9 %all-gather.11.cloned.1.call-start = ((), (), s32[]{:S(2)}) async-start(), calls=%async_computation.14 | async-start | bytes 2949120 | tf_op jit(solution)/shard_map/all_gather | solution.py:562
  1766.4 828.9 %all-gather.13.cloned.1.call-start = ((), (), s32[]{:S(2)}) async-start(), calls=%async_computation.16 | async-start | bytes 2949120 | tf_op jit(solution)/shard_map/all_gather | solution.py:568
  2543.6 54.6 %copy-start.1 = (bf16[2,768,768]{2,1,0:T(8,128)(2,1)S(1)}, bf16[2,768,768]{2,1,0:T(8,128)(2,1)}, u32[]{:S(2)}) copy-start(bf16[2,768,768]{2,1,0:T(8,128)(2,1)} %param.83) | copy-start | bytes 7077892
  (186 other events, 832.9 us)
Sparse Core Ops, SparseCore 0:
  1466.9 130.7 reduce-scatter.22
  1601.7 162.4 reduce-scatter.26
  1768.3 290.0 reduce-scatter.28
  2061.8 64.0 reduce-scatter.32
  2129.4 60.3 reduce-scatter.34
  2193.2 60.3 reduce-scatter.36
  2257.2 60.3 reduce-scatter.40
  2321.7 60.3 reduce-scatter.30
  2386.5 63.7 reduce-scatter.38
  2454.2 67.8 reduce-scatter.24
  2523.7 19.7 all-gather.8
  2545.6 24.0 all-gather.10
  2571.2 24.0 all-gather.12
where the time goes:
time: 2640 us; the launch traced here: 2600 us
  waiting for transfers between devices  966 us (37%)
  local copies, waits for them, and re-layouts  548 us (21%)
  other arithmetic  450 us (17%)
  blocking collectives  343 us (13%)
  matrix products  192 us (7%)
  starting transfers between devices  45.8 us (2%)
  loops' own time  43.8 us (2%)
    unnamed x19, waiting for transfers between devices  317 us
    ppermute x10, waiting for transfers between devices, shifted(): return lax.ppermute(shard, axis, pairs)  311 us
    unnamed x1, blocking collectives  299 us
    another operation x126, local copies, waits for them, and re-layouts  219 us
    reduce_scatter x1, waiting for transfers between devices, body(): lax.psum_scatter(members[7], 'dp', scatter_dimension=1, tiled=True)  156 us
    dynamic_update_slice x77, other arithmetic, store_at(): lax.dynamic_update_index_in_dim(buffer, jnp.where(active, update, current...  137 us
    dynamic_slice x53, local copies, waits for them, and re-layouts, store_at(): current = lax.dynamic_index_in_dim(buffer, batch_index, 0, keepdims=False)  102 us
    reduce_scatter x1, waiting for transfers between devices, body(): lax.psum_scatter(members[2], 'dp', scatter_dimension=1, tiled=True)  65 us
  transfers between devices with their start and end apart: 23, of which 17 were waited for; matrix products, arithmetic and copies ran while one was open for 11% of the time, Pallas kernels for 0%

commit v1 on v0

v1 whole, which is shorter than its diff:
```python
import jax
import jax.numpy as jnp
from jax import lax
from jax.experimental import pallas as pl
from jax.experimental.pallas import tpu as pltpu
from jax.sharding import PartitionSpec as P

ln_eps = 1e-05
masked_score = -1e30
text_pairs = 32
box_pairs = 8
bf16 = jnp.bfloat16
f32 = jnp.float32
MB = 1 << 20


def dot(a, b):
    return lax.dot_general(a, b, (((1,), (0,)), ((), ())), preferred_element_type=f32)


def dot_nt(a, b):
    return lax.dot_general(a, b, (((1,), (1,)), ((), ())), preferred_element_type=f32)


def dot_tn(a, b):
    return lax.dot_general(a, b, (((0,), (0,)), ((), ())), preferred_element_type=f32)


def angle_tables(boxes, positions):
    count = boxes.shape[1]
    text_rate = jnp.exp(-jnp.log(10000.0) * jnp.arange(text_pairs, dtype=f32) / text_pairs)
    text_angle = positions[None, :] * text_rate[:, None]
    box_rate = jnp.exp2(-jnp.arange(box_pairs, dtype=f32))
    box_angle = boxes.astype(f32)[:, None, :] * box_rate[None, :, None]
    angles = jnp.concatenate([text_angle, box_angle.reshape(4 * box_pairs, count)], 0)
    return (jnp.cos(angles), jnp.sin(angles))


def norm_parts(residual):
    average = jnp.mean(residual, -1, keepdims=True)
    centered = residual - average
    inverse = lax.rsqrt(jnp.mean(centered * centered, -1, keepdims=True) + ln_eps)
    return (centered * inverse, inverse)


def norm_back(gradient, scale, normed, inverse):
    dnormed = gradient * scale
    return inverse * (
        dnormed
        - jnp.mean(dnormed, -1, keepdims=True)
        - normed * jnp.mean(dnormed * normed, -1, keepdims=True)
    )


def lane_half(shape, half):
    lane = lax.broadcasted_iota(jnp.int32, shape, 1)
    return (lane < 64) if half == 0 else (lane >= 64)


def fill_bias(code_ref, segq_ref, bias_ref):
    shape = bias_ref.shape
    same = code_ref[...] == segq_ref[...]
    key_at = lax.broadcasted_iota(jnp.int32, shape, 0)
    query_at = lax.broadcasted_iota(jnp.int32, shape, 1)
    bias_ref[...] = jnp.where(same | (key_at == query_at), 0.0, masked_score)


def attention_fwd_kernel(
    code_ref, segq_ref, q_ref, k_ref, v_ref, rel_ref, ctab_ref, stab_ref, kf_ref,
    ctx_ref, lse_ref, turned_ref, bias_ref,
):
    @pl.when(pl.program_id(0) == 0)
    def _():
        fill_bias(code_ref, segq_ref, bias_ref)

    q_pair = q_ref[...]
    kside = jnp.concatenate([kf_ref[...], k_ref[...]], 1)
    v_t = v_ref[...].T
    rel = rel_ref[0]
    ctab, stab = ctab_ref[...], stab_ref[...]
    parts = []
    for half in range(2):
        q_mine = jnp.where(lane_half(q_pair.shape, half), q_pair, 0)
        coef = dot(q_mine, rel)
        turned = (coef * ctab + pltpu.roll(coef, 64, 1) * stab).astype(bf16)
        turned_ref[:, 128 * half : 128 * half + 128] = turned
        qside = jnp.concatenate([turned, q_mine], 1) * jnp.asarray(0.125, bf16)
        scores = dot_nt(kside, qside) + bias_ref[...]
        top = jnp.max(scores, 0, keepdims=True)
        expo = jnp.exp(scores - top)
        total = jnp.sum(expo, 0, keepdims=True)
        ctx = dot(v_t[64 * half : 64 * half + 64], expo.astype(bf16))
        parts.append(ctx * (1.0 / total))
        lse_ref[0, half : half + 1, :] = top + jnp.log(total)
    ctx_ref[...] = jnp.concatenate(parts, 0).T.astype(bf16)


def attention_fwd(q, k, v, rel, ctab, stab, kf, segq, code):
    nq, width = q.shape
    nk = k.shape[0]
    pairs = width // 128
    rel_pairs = rel.reshape(pairs, 128, 128)
    whole = lambda shape: pl.BlockSpec(shape, lambda p: (0, 0))
    cols = lambda rows, lanes: pl.BlockSpec((rows, lanes), lambda p: (0, p))
    return pl.pallas_call(
        attention_fwd_kernel,
        grid=(pairs,),
        in_specs=[
            whole((nk, 1)), whole((1, nq)), cols(nq, 128), cols(nk, 128), cols(nk, 128),
            pl.BlockSpec((1, 128, 128), lambda p: (p, 0, 0)),
            whole((nq, 128)), whole((nq, 128)), whole((nk, 128)),
        ],
        out_specs=[
            cols(nq, 128), pl.BlockSpec((1, 2, nq), lambda p: (p, 0, 0)), cols(nq, 256),
        ],
        out_shape=[
            jax.ShapeDtypeStruct((nq, width), bf16),
            jax.ShapeDtypeStruct((pairs, 2, nq), f32),
            jax.ShapeDtypeStruct((nq, 2 * width), bf16),
        ],
        scratch_shapes=[pltpu.VMEM((nk, nq), f32)],
        compiler_params=pltpu.CompilerParams(vmem_limit_bytes=40 * MB),
        name="attention_forward",
    )(code, segq, q, k, v, rel_pairs, ctab, stab, kf)


def attention_bwd_kernel(
    code_ref, segq_ref, q_ref, k_ref, v_ref, turned_ref, gc_ref, lse_ref, rel_ref, cos_ref, sin_ref,
    kf_ref, dq_ref, dk_ref, dv_ref, drel_ref, bias_ref, kft_ref,
):
    @pl.when(pl.program_id(0) == 0)
    def _():
        fill_bias(code_ref, segq_ref, bias_ref)
        kft_ref[...] = kf_ref[...].T

    q_pair, gc_pair = q_ref[...], gc_ref[...]
    kside = jnp.concatenate([kf_ref[...], k_ref[...]], 1)
    k_t = k_ref[...].T
    v_pair = v_ref[...]
    cosines, sines = cos_ref[...], sin_ref[...]
    scale = jnp.asarray(0.125, bf16)
    dk, dv, drel, dqs = 0.0, 0.0, 0.0, []
    for half in range(2):
        mine = lane_half(q_pair.shape, half)
        q_mine = jnp.where(mine, q_pair, 0)
        gc_mine = jnp.where(mine, gc_pair, 0)
        q_scaled = q_mine * scale
        qside = jnp.concatenate([turned_ref[:, 128 * half : 128 * half + 128] * scale, q_scaled], 1)
        scores = dot_nt(kside, qside) + bias_ref[...]
        shares = jnp.exp(scores - lse_ref[0, half : half + 1, :])
        gp = dot_nt(v_pair, gc_mine)
        dv = dv + dot(shares.astype(bf16), gc_mine)
        weighted = shares * gp
        delta = jnp.sum(weighted, 0, keepdims=True)
        gs = (weighted - shares * delta).astype(bf16)
        dk = dk + dot(gs, q_scaled)
        side_t = jnp.concatenate([kft_ref[...], k_t[64 * half : 64 * half + 64]], 0)
        dside = dot(side_t, gs) * 0.125
        g_cos, g_sin = dside[0:64], dside[64:128]
        gcoef = jnp.concatenate(
            [g_cos * cosines + g_sin * sines, g_cos * sines - g_sin * cosines], 0
        ).astype(bf16)
        dqs.append(dside[128:192] + dot(rel_ref[0, 64 * half : 64 * half + 64], gcoef))
        drel = drel + dot(gcoef, q_mine)
    dq_ref[...] = jnp.concatenate(dqs, 0).T.astype(bf16)
    dk_ref[...] = dk.astype(dk_ref.dtype)
    dv_ref[...] = dv.astype(dv_ref.dtype)
    drel_ref[...] = drel


def attention_bwd(q, k, v, turned, gc, lse, rel, cosines, sines, kf, segq, code, out_type):
    nq, width = q.shape
    nk = k.shape[0]
    pairs = width // 128
    rel_pairs = rel.reshape(pairs, 128, 128)
    whole = lambda shape: pl.BlockSpec(shape, lambda p: (0, 0))
    cols = lambda rows, lanes: pl.BlockSpec((rows, lanes), lambda p: (0, p))
    return pl.pallas_call(
        attention_bwd_kernel,
        grid=(pairs,),
        in_specs=[
            whole((nk, 1)), whole((1, nq)), cols(nq, 128), cols(nk, 128), cols(nk, 128),
            cols(nq, 256), cols(nq, 128), pl.BlockSpec((1, 2, nq), lambda p: (p, 0, 0)),
            pl.BlockSpec((1, 128, 128), lambda p: (p, 0, 0)),
            whole((64, nq)), whole((64, nq)), whole((nk, 128)),
        ],
        out_specs=[cols(nq, 128), cols(nk, 128), cols(nk, 128), cols(128, 128)],
        out_shape=[
            jax.ShapeDtypeStruct((nq, width), bf16),
            jax.ShapeDtypeStruct((nk, width), out_type),
            jax.ShapeDtypeStruct((nk, width), out_type),
            jax.ShapeDtypeStruct((128, width), f32),
        ],
        scratch_shapes=[pltpu.VMEM((nk, nq), f32), pltpu.VMEM((128, nk), bf16)],
        compiler_params=pltpu.CompilerParams(vmem_limit_bytes=40 * MB),
        name="attention_backward",
    )(code, segq, q, k, v, turned, gc, lse, rel_pairs, cosines, sines, kf)


def body(
    stream, cotangent, segments, word_boxes, valid_mask, w_qkv, qv_bias, w_out, out_bias, rel_proj,
    ln_scale, ln_shift, ffn_in, ffn_in_bias, ffn_out, ffn_out_bias,
):
    sections = lax.axis_size("section")
    dp = lax.axis_size("dp")
    section = lax.axis_index("section")
    dp_index = lax.axis_index("dp")
    core, layer_side = section % 2, section // 2
    rows, length, width = stream.shape
    layers = w_qkv.shape[0]
    ff_width = ffn_in.shape[2]
    assert rows == 3 and sections == 2 * layers and layers == 2
    half = length // 2
    tokens = length + half
    bits = dp.bit_length() - 1

    def flip(x, bit):
        return lax.ppermute(x, "section", [(i, i ^ bit) for i in range(sections)])

    def mine(x):
        own = lax.dynamic_index_in_dim(x, core, 0, keepdims=False)
        part = lax.dynamic_slice_in_dim(x[2], core * half, half, 0)
        return jnp.concatenate([own, part], 0)

    def whole_rows(own, other):
        first = jnp.where(core == 0, own, other)
        second = jnp.where(core == 0, other, own)
        return jnp.stack(
            [first[:length], second[:length], jnp.concatenate([first[length:], second[length:]], 0)]
        )

    def own_first(x):
        low = lax.dynamic_slice_in_dim(x, core * half, half, 0)
        high = lax.dynamic_slice_in_dim(x, (1 - core) * half, half, 0)
        return jnp.concatenate([low, high], 0)

    def both(x):
        own = lax.dynamic_index_in_dim(x, core, 0, keepdims=False)
        return jnp.concatenate([own, own_first(x[2])], 0)

    positions = jnp.arange(length, dtype=f32)
    positions = jnp.concatenate([positions, own_first(positions)])
    boxes = jnp.stack([both(word_boxes[i]) for i in range(4)])
    cos_t, sin_t = angle_tables(boxes, positions)
    kf = jnp.concatenate([cos_t, sin_t], 0).T.astype(bf16)
    ctab = jnp.concatenate([cos_t, -cos_t], 0)[:, :tokens].T
    stab = jnp.concatenate([sin_t, sin_t], 0)[:, :tokens].T
    seg_all, valid_all = both(segments), both(valid_mask)
    code_all = jnp.where(valid_all > 0, seg_all, -1)
    jobs = []
    for start, queries in ((0, length), (length, half)):
        q_at = slice(start, start + queries)
        k_at = slice(start, start + length)
        jobs.append(
            (q_at, ctab[q_at], stab[q_at], cos_t[:, q_at], sin_t[:, q_at], kf[k_at],
             seg_all[q_at][None, :], code_all[k_at][:, None])
        )

    h = mine(stream)
    valid = mine(valid_mask).astype(f32)[:, None]
    kept, square_parts = [], []

    def squares(values):
        per_token = jnp.sum(values * values, 1, keepdims=True) * valid
        return [jnp.sum(per_token[:length]), jnp.sum(per_token[length:])]

    for l in range(layers):
        gain, shift = ln_scale[l].astype(f32), ln_shift[l].astype(f32)
        joint = dot(h, w_qkv[l])
        q = (joint[:, :width] + qv_bias[l, 0]).astype(bf16)
        k = joint[:, width : 2 * width].astype(bf16)
        v = (joint[:, 2 * width :] + qv_bias[l, 1]).astype(bf16)
        other_k, other_v = flip(k[length:], 1), flip(v[length:], 1)
        keys = (k[:length], jnp.concatenate([k[length:], other_k], 0))
        values = (v[:length], jnp.concatenate([v[length:], other_v], 0))
        results = []
        for i, (q_at, ct, st, c_t, s_t, kfi, segq, code) in enumerate(jobs):
            results.append(
                attention_fwd(q[q_at], keys[i], values[i], rel_proj[l], ct, st, kfi, segq, code)
            )
        ctx = jnp.concatenate([results[0][0], results[1][0]], 0)
        attention_out = dot(ctx, w_out[l]) + out_bias[l]
        res_one = h.astype(f32) + attention_out
        normed_one, inverse_one = norm_parts(res_one)
        mixed = (normed_one * gain[0] + shift[0]).astype(bf16)
        preact = dot(mixed, ffn_in[l]) + ffn_in_bias[l]
        phi = 0.5 * (1.0 + lax.erf(preact * 0.7071067811865476))
        act = (preact * phi).astype(bf16)
        slope = (phi + preact * jnp.exp(-0.5 * preact * preact) * 0.3989422804014327).astype(bf16)
        feed_out = dot(act, ffn_out[l]) + ffn_out_bias[l]
        res_two = mixed.astype(f32) + feed_out
        normed_two, inverse_two = norm_parts(res_two)
        out = normed_two * gain[1] + shift[1]
        square_parts.append(
            [squares(attention_out), squares(mixed.astype(f32)), squares(feed_out), squares(out)]
        )
        out = out.astype(bf16)
        kept.append(
            (h, q, keys, values, results, ctx, res_one, mixed, act, slope, res_two, out)
        )
        h = out

    def flip_dp(x, bit):
        return lax.ppermute(x, "dp", [(i, i ^ bit) for i in range(dp)])

    def reduce_pieces(pieces):
        def halve(x, bit_value, axis, send):
            keep = lax.dynamic_index_in_dim(x, bit_value, axis, keepdims=False)
            away = lax.dynamic_index_in_dim(x, 1 - bit_value, axis, keepdims=False)
            return keep + send(away)

        reduced = []
        for x in pieces:
            slabs, double, cols = x.shape
            x = x.reshape(slabs, 2, double // 2, cols)
            x = halve(x, core, 1, lambda v: flip(v, 1))
            for bit in range(bits):
                x = x.reshape((x.shape[0] // 2, 2) + x.shape[1:])
                value = (dp_index >> bit) & 1
                x = halve(x, value, 1, lambda v: flip_dp(v, 1 << bit))
            reduced.append(x.reshape(x.shape[-2:]))
        return reduced

    def spread(x):
        far = flip(x, 2)
        x = jnp.where(layer_side == 0, jnp.concatenate([x, far], 1), jnp.concatenate([far, x], 1))
        near = flip(x, 1)
        return jnp.where(core == 0, jnp.concatenate([x, near], 0), jnp.concatenate([near, x], 0))

    def side(x):
        cols = x.shape[1] // 2
        return lax.dynamic_slice_in_dim(x, layer_side * cols, cols, 1)

    def product(left, right):
        result = dot_tn(left, side(right)).astype(bf16)
        return result.reshape(dp, result.shape[0] // dp, result.shape[1])

    grad = mine(cotangent).astype(f32)
    big, small, mixed_grads, input_grads = {}, {}, [None] * layers, [None] * layers
    for l in reversed(range(layers)):
        gain = ln_scale[l].astype(f32)
        h, q, keys, values, results, ctx, res_one, mixed, act, slope, res_two, out = kept[l]
        normed, inverse = norm_parts(res_two)
        scale_two, shift_two = jnp.sum(grad * normed, 0), jnp.sum(grad, 0)
        g_res_two = norm_back(grad, gain[1], normed, inverse)
        g_feed = g_res_two.astype(bf16)
        d_ffn_out = product(act, g_feed)
        g_pre = (dot_nt(g_feed, ffn_out[l]) * slope.astype(f32)).astype(bf16)
        d_ffn_in = product(mixed, g_pre)
        big[l, "ffn"] = reduce_pieces([d_ffn_out, d_ffn_in])
        g_mixed = dot_nt(g_pre, ffn_in[l]) + g_res_two
        mixed_grads[l] = g_mixed
        normed, inverse = norm_parts(res_one)
        scale_one, shift_one = jnp.sum(g_mixed * normed, 0), jnp.sum(g_mixed, 0)
        g_res_one = norm_back(g_mixed, gain[0], normed, inverse)
        g_attn = g_res_one.astype(bf16)
        d_out = product(ctx, g_attn)
        g_ctx = dot_nt(g_attn, w_out[l]).astype(bf16)
        grads = []
        for i, (q_at, ct, st, c_t, s_t, kfi, segq, code) in reversed(list(enumerate(jobs))):
            grads.append(
                attention_bwd(
                    q[q_at], keys[i], values[i], results[i][2], g_ctx[q_at], results[i][1],
                    rel_proj[l], c_t, s_t, kfi, segq, code, bf16 if i == 0 else f32,
                )
            )
        shared_grads, own_grads = grads
        dq = jnp.concatenate([own_grads[0], shared_grads[0]], 0)

        def joined(own, shared):
            arrived = flip(shared[half:].astype(bf16), 1)
            return jnp.concatenate([own, (shared[:half] + arrived).astype(bf16)], 0)

        dk, dv = joined(own_grads[1], shared_grads[1]), joined(own_grads[2], shared_grads[2])
        g_joint = jnp.concatenate([dq, dk, dv], 1)
        d_qkv = product(h, g_joint)
        g_h = (dot_nt(g_joint, w_qkv[l]) + g_res_one).astype(bf16)
        input_grads[l] = g_h
        grad = g_h.astype(f32)
        total = lambda x: jnp.sum(x.astype(f32), 0)
        vectors = [total(dq), total(dv), total(g_attn), scale_one, scale_two, shift_one, shift_two,
                   total(g_feed)]
        small_rows = jnp.concatenate(
            [x.reshape(dp, width // dp) for x in vectors]
            + [total(g_pre).reshape(dp, ff_width // dp)], 1,
        )
        d_rel = side(own_grads[3] + shared_grads[3])
        rel_rows = d_rel.shape[0] // dp
        d_rel = d_rel.reshape(dp, rel_rows, width // 2).astype(bf16)
        room = rel_rows * (width // 2)
        small_rows = jnp.pad(small_rows, ((0, 0), (0, room - small_rows.shape[1])))
        small_rows = small_rows.astype(bf16).reshape(dp, rel_rows, width // 2)
        misc = jnp.concatenate([d_rel, small_rows], 1)
        big[l, "attn"] = reduce_pieces([d_qkv, d_out, misc])

    def pick(pair):
        return jnp.where(layer_side == 0, pair[0], pair[1])

    mixed_side, out_side = pick([kept[0][7], kept[1][7]]), pick([kept[0][11], kept[1][11]])
    own_piece = jnp.where(core == 0, mixed_side, out_side)
    away_piece = jnp.where(core == 0, out_side, mixed_side)
    section_outs = whole_rows(own_piece, flip(away_piece, 1))[None]
    h_side, m_side = pick(input_grads), pick(mixed_grads)
    own_piece = jnp.where(core == 0, h_side.astype(f32), m_side)
    away_piece = jnp.where(core == 0, m_side.astype(bf16), h_side)
    in_grads = whole_rows(own_piece, flip(away_piece, 1).astype(f32))[None]

    squares_all = jnp.stack([jnp.stack([jnp.stack(pair) for pair in four]) for four in square_parts])
    squares_mine = pick(squares_all).reshape(2, 2, 2)
    squares_far = flip(squares_mine, 1)
    sub = lambda x: lax.dynamic_index_in_dim(x, core, 0, keepdims=False)
    near, far = sub(squares_mine), sub(squares_far)
    first = jnp.where(core == 0, near[:, 0], far[:, 0])
    second = jnp.where(core == 0, far[:, 0], near[:, 0])
    square_rows = jnp.stack([first, second, near[:, 1] + far[:, 1]])
    row_counts = jnp.sum(valid_mask.astype(f32), 1)
    root_mean_squares = jnp.sqrt(square_rows / (width * jnp.maximum(row_counts, 1.0))[:, None])[None]

    out = {}
    for l in range(layers):
        out[l, "ffn_out"], out[l, "ffn_in"] = [spread(x) for x in big[l, "ffn"]]
        qkv, w_o, misc = big[l, "attn"]
        out[l, "qkv"], out[l, "out"] = spread(qkv), spread(w_o)
        misc_rows = misc.shape[0]
        near = flip(misc, 1)
        rel_part = jnp.where(core == 0, misc, near)
        small_part = jnp.where(core == 0, near, misc)
        rel_far = flip(rel_part, 2)
        rel_all = jnp.where(
            layer_side == 0,
            jnp.concatenate([rel_part, rel_far], 1), jnp.concatenate([rel_far, rel_part], 1),
        )
        out[l, "rel"] = rel_all.astype(f32).T.reshape(width // 64, 64, misc_rows)
        flat = small_part.astype(f32).reshape(-1)
        n = width // dp
        pieces = [flat[i * n : (i + 1) * n] for i in range(8)] + [flat[8 * n : 8 * n + ff_width // dp]]
        out[l, "small"] = pieces

    both_layers = lambda name: jnp.stack([out[0, name].astype(f32), out[1, name].astype(f32)])
    small_at = lambda i: jnp.stack([out[l, "small"][i] for l in range(layers)])
    return (
        section_outs,
        in_grads,
        both_layers("qkv"),
        jnp.stack([small_at(0), small_at(1)], 1),
        both_layers("out"),
        small_at(2),
        both_layers("rel"),
        jnp.stack([small_at(3), small_at(4)], 1),
        jnp.stack([small_at(5), small_at(6)], 1),
        both_layers("ffn_in"),
        small_at(8),
        both_layers("ffn_out"),
        small_at(7),
        root_mean_squares,
    )


def solution(mesh):
    return jax.shard_map(
        body,
        mesh=mesh,
        in_specs=(
            P("dp", None, None),
            P("dp", None, None),
            P("dp", None),
            P(None, "dp", None),
            P("dp", None),
        )
        + (P(),) * 11,
        out_specs=(
            P("section", "dp", None, None),
            P("section", "dp", None, None),
            P(None, "dp", None),
            P(None, None, "dp"),
            P(None, "dp", None),
            P(None, "dp"),
            P(None, None, None, "dp"),
            P(None, None, "dp"),
            P(None, None, "dp"),
            P(None, "dp", None),
            P(None, "dp"),
            P(None, "dp", None),
            P(None, "dp"),
            P("section", "dp", None),
        ),
        check_vma=False,
    )
```

time: 2640 us -> 693 us (0.26); the launches traced: 2600 us -> 686 us
  waiting for transfers between devices: 966 us -> 90.3 us
  local copies, waits for them, and re-layouts: 548 us -> 130 us
  blocking collectives: 343 us -> 0 us
  other arithmetic: 450 us -> 153 us
  Pallas kernels: 0 us -> 95.3 us
  matrix products: 192 us -> 143 us
  loops' own time: 43.8 us -> 0 us
    unnamed x19 -> x0, waiting for transfers between devices: 317 us -> none
    unnamed x1 -> x0, blocking collectives: 299 us -> none
    reduce_scatter x4 -> x0, waiting for transfers between devices: 280 us -> none  [the longest x1 156 us: body(): lax.psum_scatter(members[7], 'dp', scatter_dimension=1, tiled=True)]
    another operation x132 -> x8, local copies, waits for them, and re-layouts: 224 us -> 2.14 us  [the longest x2 0.86 us: body(): jnp.stack([out[0, name].astype(f32), out[1, name].astype(f32)])]
    ppermute x10 -> x71, waiting for transfers between devices: 311 us -> 90.3 us  [the longest x30 75.4 us: flip_dp(): return lax.ppermute(x, 'dp', [(i, i ^ bit) for i in range(dp)])]
    dynamic_update_slice x77 -> x0, other arithmetic: 137 us -> none  [store_at(): lax.dynamic_update_index_in_dim(buffer, jnp.where(active, update, current...]
    dynamic_slice x61 -> x23, local copies, waits for them, and re-layouts: 108 us -> 7.02 us  [the longest x2 2.59 us: mine(): own = lax.dynamic_index_in_dim(x, core, 0, keepdims=False)]
    pallas_call x0 -> x8, Pallas kernels: none -> 95.3 us  [the longest x4 53.2 us: attention_bwd(): pl.pallas_call(attention_bwd_kernel, grid=(pairs,), in_specs=[whole((nk,...]
  transfers between devices with their start and end apart: 23 -> 71, of which waited for: 17 -> 32; matrix products, arithmetic and copies ran while one was open for 11% -> 43% of each run, Pallas kernels for 0% -> 11%
where the time goes in v1:
time: 693 us; the launch traced here: 686 us
  other arithmetic  153 us (22%)
  matrix products  143 us (21%)
  local copies, waits for them, and re-layouts  130 us (19%)
  Pallas kernels  95.3 us (14%)
  waiting for transfers between devices  90.3 us (13%)
  starting transfers between devices  69.3 us (10%)
    dot_general x8, matrix products, dot_nt(): lax.dot_general(a, b, (((1,), (1,)), ((), ())), preferred_element_type=f32)  75.9 us
    ppermute x30, waiting for transfers between devices, flip_dp(): return lax.ppermute(x, 'dp', [(i, i ^ bit) for i in range(dp)])  75.4 us
    pallas_call x4, Pallas kernels, attention_bwd(): pl.pallas_call(attention_bwd_kernel, grid=(pairs,), in_specs=[whole((nk,...  53.2 us
    unnamed x501, local copies, waits for them, and re-layouts  48.4 us
    ppermute x30, starting transfers between devices, flip_dp(): return lax.ppermute(x, 'dp', [(i, i ^ bit) for i in range(dp)])  48.3 us
    dot_general x8, matrix products, dot(): lax.dot_general(a, b, (((1,), (0,)), ((), ())), preferred_element_type=f32)  47.2 us
    pallas_call x4, Pallas kernels, attention_fwd(): pl.pallas_call(attention_fwd_kernel, grid=(pairs,), in_specs=[whole((nk,...  42.1 us
    concatenate x2, other arithmetic, body(): g_joint = jnp.concatenate([dq, dk, dv], 1)  38.7 us
  transfers between devices with their start and end apart: 71, of which 32 were waited for; matrix products, arithmetic and copies ran while one was open for 43% of the time, Pallas kernels for 11%

profile of v1, /device:TPU:0, one launch (start us, length us, event | category | flops | bytes accessed | tf_op | source)
XLA Modules:
  0.0 685.6 jit_solution(575844962142382445)
XLA Ops:
  0.7 3.9 constant_dynamic-slice_fusion.39
  5.0 5.3 fusion.157
  26.8 11.2 %attention_forward.4 = (bf16[512,768]{1,0:T(8,128)(2,1)S(1)}, f32[6,2,512]{2,1,0:T(2,128)S(1)}, bf16[512,1536]{1,0:T(8,128)(2,1)S(1)}) custom-call(s32[512,1]{1,0:T(8,128)S(1)} %copy.138.code_ref, s32[1,512]{1,0:T(1,128)S(1)} %get-tuple-element.255.segq_ref, bf16[512,768]{1,0:T(8,128)(2,1)S(1)} %slice.590.q_ref, bf16[512,768]{1,0:T(8,128)(2,1)S(1)} %slice.591.k_ref, ...), custom_call_target="tpu_custom_call" | custom-call | tf_op jit(solution)/shard_map/attention_forward/pallas_call | solution.py:105
  51.4 9.8 %attention_forward.5 = (bf16[256,768]{1,0:T(8,128)(2,1)S(1)}, f32[6,2,256]{2,1,0:T(2,128)S(1)}, bf16[256,1536]{1,0:T(8,128)(2,1)S(1)}) custom-call(s32[512,1]{1,0:T(8,128)S(1)} %copy-done.2, s32[1,256]{1,0:T(1,128)S(1)} %get-tuple-element.281.segq_ref, bf16[256,768]{1,0:T(8,128)(2,1)S(1)} %copy-done.10, bf16[512,768]{1,0:T(8,128)(2,1)S(1)} %pad_maximum_fusion.2.k_ref, ...), custom_call_target="tpu_custom_call" | custom-call | tf_op jit(solution)/shard_map/attention_forward/pallas_call | solution.py:105
  65.2 10.3 %multiply_convert_fusion.3 = (bf16[768,3072]{1,0:T(8,128)(2,1)S(1)}, f32[768,3072]{1,0:T(8,128)}) fusion(f32[3072]{0:T(1024)S(1)} %bitcast.570, bf16[768,768]{0,1:T(8,128)(2,1)S(1)} %get-tuple-element.164, bf16[2,768,3072]{2,1,0:T(8,128)(2,1)} %param.28), kind=kOutput, calls=%fused_computation.16 | convolution fusion | flops 3638034432 | bytes 20066304 | tf_op jit(solution)/shard_map/dot_general | solution.py:18
  75.5 5.1 fusion.146
  82.2 5.4 fusion.158
  117.1 11.2 %attention_forward.6 = (bf16[512,768]{1,0:T(8,128)(2,1)S(1)}, f32[6,2,512]{2,1,0:T(2,128)S(1)}, bf16[512,1536]{1,0:T(8,128)(2,1)S(1)}) custom-call(s32[512,1]{1,0:T(8,128)S(1)} %copy.138.code_ref, s32[1,512]{1,0:T(1,128)S(1)} %get-tuple-element.255.segq_ref, bf16[512,768]{1,0:T(8,128)(2,1)S(1)} %slice.608.q_ref, bf16[512,768]{1,0:T(8,128)(2,1)S(1)} %slice.609.k_ref, ...), custom_call_target="tpu_custom_call" | custom-call | tf_op jit(solution)/shard_map/attention_forward/pallas_call | solution.py:105
  131.1 10.0 %attention_forward.7 = (bf16[256,768]{1,0:T(8,128)(2,1)S(1)}, f32[6,2,256]{2,1,0:T(2,128)S(1)}, bf16[256,1536]{1,0:T(8,128)(2,1)S(1)}) custom-call(s32[512,1]{1,0:T(8,128)S(1)} %copy-done.3, s32[1,256]{1,0:T(1,128)S(1)} %get-tuple-element.281.segq_ref, bf16[256,768]{1,0:T(8,128)(2,1)S(1)} %slice.612.q_ref, bf16[512,768]{1,0:T(8,128)(2,1)S(1)} %pad_maximum_fusion.4.k_ref, ...), custom_call_target="tpu_custom_call" | custom-call | tf_op jit(solution)/shard_map/attention_forward/pallas_call | solution.py:105
  144.4 9.8 %multiply_convert_fusion.2 = (bf16[768,3072]{1,0:T(8,128)(2,1)}, f32[768,3072]{1,0:T(8,128)}) fusion(f32[3072]{0:T(1024)S(1)} %bitcast.572, bf16[768,768]{0,1:T(8,128)(2,1)S(1)} %get-tuple-element.162, bf16[2,768,3072]{2,1,0:T(8,128)(2,1)} %param.28), kind=kOutput, calls=%fused_computation.14 | convolution fusion | flops 3638034432 | bytes 20066304 | tf_op jit(solution)/shard_map/dot_general | solution.py:18
  154.2 7.9 %fusion.144 = (f32[768]{0:T(1024)S(1)}, f32[768,768]{0,1:T(8,128)S(1)}, f32[768]{0:T(1024)}) fusion(f32[768]{0:T(1024)S(1)} %copy-done.204, bf16[768,768]{0,1:T(8,128)(2,1)S(1)} %get-tuple-element.162, bf16[768,3072]{1,0:T(8,128)(2,1)} %get-tuple-element.289, bf16[2,3072,768]{2,1,0:T(8,128)(2,1)} %param.30), kind=kOutput, calls=%fused_computation.487 | convolution fusion | flops 3627416064 | bytes 12985344 | tf_op jit(solution)/shard_map/dot_general | solution.py:18
  165.5 3.9 fusion.136
  170.5 10.4 %fusion.159 = (bf16[3072]{0:T(1024)(128)(2,1)}, bf16[768,3072]{1,0:T(8,128)(2,1)}) fusion(f32[768,3072]{1,0:T(8,128)S(1)} %copy-done.234, f32[3072]{0:T(1024)S(1)} %bitcast.573, bf16[768,768]{0,1:T(8,128)(2,1)S(1)} %get-tuple-element.172, bf16[2,3072,768]{2,1,0:T(8,128)(2,1)} %param.30), kind=kOutput, calls=%fused_computation.500 | convolution fusion | flops 3656905728 | bytes 20072448 | tf_op jit(solution)/shard_map/dot_general | solution.py:22
  180.9 9.0 %multiply_reduce_fusion.6 = (bf16[768]{0:T(1024)(128)(2,1)}, f32[768]{0:T(1024)S(1)}, f32[768]{0:T(1024)S(1)}, bf16[768]{0:T(1024)(128)(2,1)}, f32[768,768]{0,1:T(8,128)S(1)}) fusion(f32[768,768]{0,1:T(8,128)S(1)} %get-tuple-element.189, f32[768]{0:T(1024)S(1)} %add_rsqrt_fusion.1, f32[768]{0:T(1024)S(1)} %broadcast_multiply_fusion.11, ...), kind=kOutput, calls=%fused_computation.104 | convolution fusion | flops 3636261888 | bytes 17728512 | tf_op jit(solution)/shard_map/dot_general | solution.py:22
  194.9 2.9 convolution_convert_fusion
  204.7 10.8 %attention_backward.5 = (bf16[256,768]{1,0:T(8,128)(2,1)S(1)}, f32[512,768]{1,0:T(8,128)S(1)}, f32[512,768]{1,0:T(8,128)S(1)}, f32[128,768]{1,0:T(8,128)S(1)}) custom-call(s32[512,1]{1,0:T(8,128)S(1)} %copy-done.3, s32[1,256]{1,0:T(1,128)S(1)} %get-tuple-element.281.segq_ref, bf16[256,768]{1,0:T(8,128)(2,1)S(1)} %slice.612.q_ref, ...), custom_call_target="tpu_custom_call" | custom-call | tf_op jit(solution)/shard_map/attention_backward/pallas_call | solution.py:178
  218.9 3.7 convolution_convert_fusion.2
  224.1 16.0 %attention_backward.4 = (bf16[512,768]{1,0:T(8,128)(2,1)S(1)}, bf16[512,768]{1,0:T(8,128)(2,1)S(1)}, bf16[512,768]{1,0:T(8,128)(2,1)S(1)}, f32[128,768]{1,0:T(8,128)S(1)}) custom-call(s32[512,1]{1,0:T(8,128)S(1)} %copy.138.code_ref, s32[1,512]{1,0:T(1,128)S(1)} %get-tuple-element.255.segq_ref, bf16[512,768]{1,0:T(8,128)(2,1)S(1)} %slice.608.q_ref, ...), custom_call_target="tpu_custom_call" | custom-call | tf_op jit(solution)/shard_map/attention_backward/pallas_call | solution.py:178
  272.6 2.9 collective-permute-start.39
  278.9 8.9 %fusion.59 = (bf16[768]{0:T(1024)(128)(2,1)}, f32[768]{0:T(1024)S(1)}, f32[768]{0:T(1024)S(1)}, f32[768]{0:T(1024)S(1)}, bf16[768,768]{0,1:T(8,128)(2,1)S(1)}) fusion(f32[768,768]{0,1:T(8,128)} %copy-done.65, f32[768]{0:T(1024)} %copy-done.136, f32[768]{0:T(1024)S(1)} %broadcast_multiply_fusion.12, f32[768]{0:T(1024)S(1)} %get-tuple-element.150, ...), kind=kOutput, calls=%fused_computation.86 | convolution fusion | flops 2752115712 | bytes 15380992 | tf_op jit(solution)/shard_map/dot_general | solution.py:22
  289.5 12.1 %fusion.160 = (bf16[3072]{0:T(1024)(128)(2,1)}, bf16[768,3072]{1,0:T(8,128)(2,1)}) fusion(f32[768,3072]{1,0:T(8,128)} %get-tuple-element.286, f32[3072]{0:T(1024)S(1)} %bitcast.571, bf16[768,768]{0,1:T(8,128)(2,1)S(1)} %get-tuple-element.166, bf16[2,3072,768]{2,1,0:T(8,128)(2,1)} %param.30), kind=kOutput, calls=%fused_computation.501 | convolution fusion | flops 3656905728 | bytes 20072448 | tf_op jit(solution)/shard_map/dot_general | solution.py:22
  301.6 9.2 %multiply_reduce_fusion.7 = (bf16[768]{0:T(1024)(128)(2,1)}, f32[768]{0:T(1024)S(1)}, f32[768]{0:T(1024)S(1)}, bf16[768]{0:T(1024)(128)(2,1)}, f32[768,768]{0,1:T(8,128)S(1)}) fusion(f32[768,768]{0,1:T(8,128)S(1)} %copy-done.69, f32[768]{0:T(1024)S(1)} %copy-done.156, f32[768]{0:T(1024)S(1)} %copy-done.140, f32[768]{0:T(1024)S(1)} %copy-done.152, ...), kind=kOutput, calls=%fused_computation.105 | convolution fusion | flops 3634492416 | bytes 17728512 | tf_op jit(solution)/shard_map/dot_general | solution.py:22
  316.2 19.8 %maximum_maximum_fusion = bf16[768,2304]{1,0:T(8,128)(2,1)} fusion(bf16[256,768]{1,0:T(8,128)(2,1)S(1)} %get-tuple-element.180, bf16[512,768]{1,0:T(8,128)(2,1)S(1)} %copy-done.23, bf16[256,768]{1,0:T(8,128)(2,1)S(1)} %add_convert_fusion.7, bf16[512,768]{1,0:T(8,128)(2,1)S(1)} %copy-done.52, bf16[256,768]{1,0:T(8,128)(2,1)S(1)} %copy-done.31, ...), kind=kLoop, calls=%fused_computation.43 | loop fusion | flops 21233664 | bytes 7077888 | tf_op jit(solution)/shard_map/concatenate | solution.py:375
  337.7 3.4 convolution_convert_fusion.3
  341.2 4.4 convolution_convert_fusion.1
  365.0 10.4 %attention_backward.7 = (bf16[256,768]{1,0:T(8,128)(2,1)S(1)}, f32[512,768]{1,0:T(8,128)S(1)}, f32[512,768]{1,0:T(8,128)S(1)}, f32[128,768]{1,0:T(8,128)S(1)}) custom-call(s32[512,1]{1,0:T(8,128)S(1)} %copy-done.4, s32[1,256]{1,0:T(1,128)S(1)} %get-tuple-element.281.segq_ref, bf16[256,768]{1,0:T(8,128)(2,1)S(1)} %copy-done.11, ...), custom_call_target="tpu_custom_call" | custom-call | tf_op jit(solution)/shard_map/attention_backward/pallas_call | solution.py:178
  386.1 16.0 %attention_backward.6 = (bf16[512,768]{1,0:T(8,128)(2,1)S(1)}, bf16[512,768]{1,0:T(8,128)(2,1)S(1)}, bf16[512,768]{1,0:T(8,128)(2,1)S(1)}, f32[128,768]{1,0:T(8,128)S(1)}) custom-call(s32[512,1]{1,0:T(8,128)S(1)} %copy.138.code_ref, s32[1,512]{1,0:T(1,128)S(1)} %get-tuple-element.255.segq_ref, bf16[512,768]{1,0:T(8,128)(2,1)S(1)} %slice.590.q_ref, ...), custom_call_target="tpu_custom_call" | custom-call | tf_op jit(solution)/shard_map/attention_backward/pallas_call | solution.py:178
  426.0 3.0 collective-permute-done.40
  429.4 3.7 collective-permute-done.28
  437.0 2.7 collective-permute-start.41
  442.0 2.8 collective-permute-start.30
  462.9 24.1 %convert_select_fusion.3 = (bf16[768,768]{0,1:T(8,128)(2,1)}, f32[768,768]{0,1:T(8,128)}, bf16[768,768]{0,1:T(8,128)(2,1)}) fusion(pred[]{:T(512)S(6)} %eq.6, f32[768,768]{0,1:T(8,128)} %copy-done.93, f32[768,768]{0,1:T(8,128)} %copy-done.92, pred[]{:T(512)S(6)} %eq.7, bf16[768,768]{0,1:T(8,128)(2,1)} %copy-done.115, ...), kind=kOutput, calls=%fused_computation.162 | convolution fusion | flops 2746810368 | bytes 20070402 | tf_op jit(solution)/shard_map/dot_general | solution.py:22
  487.0 18.9 %maximum_maximum_fusion.1 = bf16[768,2304]{1,0:T(8,128)(2,1)S(1)} fusion(bf16[256,768]{1,0:T(8,128)(2,1)S(1)} %get-tuple-element.170, bf16[512,768]{1,0:T(8,128)(2,1)S(1)} %copy-done.19, bf16[256,768]{1,0:T(8,128)(2,1)S(1)} %add_convert_fusion.5, bf16[512,768]{1,0:T(8,128)(2,1)S(1)} %copy-done.50, bf16[256,768]{1,0:T(8,128)(2,1)S(1)} %copy-done.29, ...), kind=kLoop, calls=%fused_computation.44 | loop fusion | flops 21233664 | bytes 7077888 | tf_op jit(solution)/shard_map/concatenate | solution.py:375
  524.1 3.1 collective-permute-start.25
  528.9 2.9 collective-permute-start.35
  555.0 4.3 copy.168
  572.7 25.1 %collective-permute-done.17 = bf16[4,48,1152]{2,1,0:T(8,128)(2,1)S(1)} collective-permute-done((bf16[4,48,1152]{2,1,0:T(8,128)(2,1)S(1)}, bf16[4,48,1152]{2,1,0:T(8,128)(2,1)S(1)}, u32[]{:S(2)}, u32[]{:S(2)}) %collective-permute-start.17) | collective-permute-done | bytes 442400 | tf_op jit(solution)/shard_map/ppermute | solution.py:304
  608.0 2.9 collective-permute-start.19
  613.4 2.7 maximum_bitcast_fusion
  616.1 6.3 copy.169
  626.3 3.3 collective-permute-done.66
  632.0 2.8 collective-permute-start.67
  645.0 2.6 collective-permute-done.12
  650.0 2.8 collective-permute-done.68
  653.5 3.8 collective-permute-done.13
  658.9 3.4 collective-permute-start.49
  663.2 9.0 %collective-permute-done.49 = bf16[1,48,1536]{2,1,0:T(8,128)(2,1)S(1)} collective-permute-done((bf16[1,48,1536]{2,1,0:T(8,128)(2,1)S(1)}, bf16[1,48,1536]{2,1,0:T(8,128)(2,1)S(1)}, u32[]{:S(2)}, u32[]{:S(2)}) %collective-permute-start.49) | collective-permute-done | bytes 147488 | tf_op jit(solution)/shard_map/ppermute | solution.py:304
  675.1 3.4 collective-permute-done.50
  (976 shorter events, 313.4 us)
Async XLA Ops:
  11.3 35.4 %collective-permute-start = (bf16[256,768]{1,0:T(8,128)(2,1)}, bf16[256,768]{1,0:T(8,128)(2,1)}, u32[]{:S(2)}, u32[]{:S(2)}) collective-permute-start(bf16[256,768]{1,0:T(8,128)(2,1)} %slice.598), channel_id=1, source_target_pairs={{0,1},{1,0},{2,3},{3,2},{4,5},{5,4},{6,7},{7,6},{8,9},{9,8},{10,11... | collective-permute-start | bytes 1179656 | tf_op jit(solution)/shard_map/ppermute | solution.py:218
  14.6 33.4 %collective-permute-start.1 = (bf16[256,768]{1,0:T(8,128)(2,1)}, bf16[256,768]{1,0:T(8,128)(2,1)}, u32[]{:S(2)}, u32[]{:S(2)}) collective-permute-start(bf16[256,768]{1,0:T(8,128)(2,1)} %slice.599), channel_id=1, source_target_pairs={{0,1},{1,0},{2,3},{3,2},{4,5},{5,4},{6,7},{7,6},{8,9},{9,8},{10,11... | collective-permute-start | bytes 1179656 | tf_op jit(solution)/shard_map/ppermute | solution.py:218
  88.5 40.0 %collective-permute-start.2 = (bf16[256,768]{1,0:T(8,128)(2,1)}, bf16[256,768]{1,0:T(8,128)(2,1)}, u32[]{:S(2)}, u32[]{:S(2)}) collective-permute-start(bf16[256,768]{1,0:T(8,128)(2,1)} %slice.613), channel_id=1, source_target_pairs={{0,1},{1,0},{2,3},{3,2},{4,5},{5,4},{6,7},{7,6},{8,9},{9,8},{10,11... | collective-permute-start | bytes 1179656 | tf_op jit(solution)/shard_map/ppermute | solution.py:218
  91.9 37.9 %collective-permute-start.3 = (bf16[256,768]{1,0:T(8,128)(2,1)}, bf16[256,768]{1,0:T(8,128)(2,1)}, u32[]{:S(2)}, u32[]{:S(2)}) collective-permute-start(bf16[256,768]{1,0:T(8,128)(2,1)} %slice.614), channel_id=1, source_target_pairs={{0,1},{1,0},{2,3},{3,2},{4,5},{5,4},{6,7},{7,6},{8,9},{9,8},{10,11... | collective-permute-start | bytes 1179656 | tf_op jit(solution)/shard_map/ppermute | solution.py:218
  204.6 341.9 %collective-permute-start.4 = (bf16[768,768]{0,1:T(8,128)(2,1)}, bf16[768,768]{0,1:T(8,128)(2,1)}, u32[]{:S(2)}, u32[]{:S(2)}) collective-permute-start(bf16[768,768]{0,1:T(8,128)(2,1)} %get-tuple-element.206), channel_id=1, source_target_pairs={{0,1},{1,0},{2,3},{3,2},{4,5},{5,4},{6,7},{7,6},{8,9},{9,8},{10,11... | collective-permute-start | bytes 3538952 | tf_op jit(solution)/shard_map/ppermute | solution.py:218
  216.4 56.2 %collective-permute-start.6 = (bf16[256,768]{1,0:T(8,128)(2,1)}, bf16[256,768]{1,0:T(8,128)(2,1)}, u32[]{:S(2)}, u32[]{:S(2)}) collective-permute-start(bf16[256,768]{1,0:T(8,128)(2,1)} %slice.833), channel_id=1, source_target_pairs={{0,1},{1,0},{2,3},{3,2},{4,5},{5,4},{6,7},{7,6},{8,9},{9,8},{10,11... | collective-permute-start | bytes 1179656 | tf_op jit(solution)/shard_map/ppermute | solution.py:218
  217.6 59.8 %collective-permute-start.5 = (bf16[256,768]{1,0:T(8,128)(2,1)}, bf16[256,768]{1,0:T(8,128)(2,1)}, u32[]{:S(2)}, u32[]{:S(2)}) collective-permute-start(bf16[256,768]{1,0:T(8,128)(2,1)} %slice.834), channel_id=1, source_target_pairs={{0,1},{1,0},{2,3},{3,2},{4,5},{5,4},{6,7},{7,6},{8,9},{9,8},{10,11... | collective-permute-start | bytes 1179656 | tf_op jit(solution)/shard_map/ppermute | solution.py:218
  218.7 51.7 %collective-permute-start.38 = (bf16[8,48,384]{2,1,0:T(8,128)(2,1)}, bf16[8,48,384]{2,1,0:T(8,128)(2,1)}, u32[]{:S(2)}, u32[]{:S(2)}) collective-permute-start(bf16[8,48,384]{2,1,0:T(8,128)(2,1)} %dynamic-slice_bitcast_fusion.16), channel_id=1, source_target_pairs={{0,1},{1,0},{2,3},{3,2},{4,5},{5,4},{6,7},{7,6},{8,9},{9,8},{10,11... | collective-permute-start | bytes 884744 | tf_op jit(solution)/shard_map/ppermute | solution.py:218
  223.7 324.5 %collective-permute-start.52 = (bf16[8,48,1536]{2,1,0:T(8,128)(2,1)}, bf16[8,48,1536]{2,1,0:T(8,128)(2,1)}, u32[]{:S(2)}, u32[]{:S(2)}) collective-permute-start(bf16[8,48,1536]{2,1,0:T(8,128)(2,1)} %dynamic-slice_bitcast_fusion.2), channel_id=1, source_target_pairs={{0,1},{1,0},{2,3},{3,2},{4,5},{5,4},{6,7},{7,6},{8,9},{9,8},{10,11... | collective-permute-start | bytes 3538952 | tf_op jit(solution)/shard_map/ppermute | solution.py:218
  270.4 280.7 %collective-permute-start.64 = (bf16[8,192,384]{2,1,0:T(8,128)(2,1)}, bf16[8,192,384]{2,1,0:T(8,128)(2,1)}, u32[]{:S(2)}, u32[]{:S(2)}) collective-permute-start(bf16[8,192,384]{2,1,0:T(8,128)(2,1)} %dynamic-slice_bitcast_fusion), channel_id=1, source_target_pairs={{0,1},{1,0},{2,3},{3,2},{4,5},{5,4},{6,7},{7,6},{8,9},{9,8},{10,11... | collective-permute-start | bytes 3538952 | tf_op jit(solution)/shard_map/ppermute | solution.py:218
  272.6 150.6 %collective-permute-start.39 = (bf16[4,48,384]{2,1,0:T(8,128)(2,1)}, bf16[4,48,384]{2,1,0:T(8,128)(2,1)}, u32[]{:S(2)}, u32[]{:S(2)}) collective-permute-start(bf16[4,48,384]{2,1,0:T(8,128)(2,1)} %dynamic-slice_bitcast_fusion.20), channel_id=1, source_target_pairs={{0,4},{4,0},{8,12},{12,8},{16,20},{20,16},{24,28},{28,24},{1,5},{5... | collective-permute-start | bytes 442376 | tf_op jit(solution)/shard_map/ppermute | solution.py:304
  354.3 66.7 %collective-permute-start.70 = (f32[2,2,2]{1,0,2:T(2,128)}, f32[2,2,2]{1,0,2:T(2,128)}, u32[]{:S(2)}, u32[]{:S(2)}) collective-permute-start(f32[2,2,2]{1,0,2:T(2,128)} %copy.180), channel_id=1, source_target_pairs={{0,1},{1,0},{2,3},{3,2},{4,5},{5,4},{6,7},{7,6},{8,9},{9,8},{10,11... | collective-permute-start | bytes 104 | tf_op jit(solution)/shard_map/ppermute | solution.py:218
  423.3 34.3 %collective-permute-start.32 = (bf16[8,48,384]{2,1,0:T(8,128)(2,1)}, bf16[8,48,384]{2,1,0:T(8,128)(2,1)}, u32[]{:S(2)}, u32[]{:S(2)}) collective-permute-start(bf16[8,48,384]{2,1,0:T(8,128)(2,1)} %dynamic-slice_bitcast_fusion.17), channel_id=1, source_target_pairs={{0,1},{1,0},{2,3},{3,2},{4,5},{5,4},{6,7},{7,6},{8,9},{9,8},{10,11... | collective-permute-start | bytes 884744 | tf_op jit(solution)/shard_map/ppermute | solution.py:218
  437.0 5.0 collective-permute-start.41
  459.8 99.7 %collective-permute-start.16 = (bf16[8,48,1152]{2,1,0:T(8,128)(2,1)}, bf16[8,48,1152]{2,1,0:T(8,128)(2,1)}, u32[]{:S(2)}, u32[]{:S(2)}) collective-permute-start(bf16[8,48,1152]{2,1,0:T(8,128)(2,1)} %dynamic-slice_bitcast_fusion.4), channel_id=1, source_target_pairs={{0,1},{1,0},{2,3},{3,2},{4,5},{5,4},{6,7},{7,6},{8,9},{9,8},{10,11... | collective-permute-start | bytes 2654216 | tf_op jit(solution)/shard_map/ppermute | solution.py:218
  461.2 49.1 %collective-permute-start.33 = (bf16[4,48,384]{2,1,0:T(8,128)(2,1)}, bf16[4,48,384]{2,1,0:T(8,128)(2,1)}, u32[]{:S(2)}, u32[]{:S(2)}) collective-permute-start(bf16[4,48,384]{2,1,0:T(8,128)(2,1)} %dynamic-slice_bitcast_fusion.21), channel_id=1, source_target_pairs={{0,4},{4,0},{8,12},{12,8},{16,20},{20,16},{24,28},{28,24},{1,5},{5... | collective-permute-start | bytes 442376 | tf_op jit(solution)/shard_map/ppermute | solution.py:304
  545.1 21.0 %collective-permute-start.46 = (bf16[8,48,1536]{2,1,0:T(8,128)(2,1)}, bf16[8,48,1536]{2,1,0:T(8,128)(2,1)}, u32[]{:S(2)}, u32[]{:S(2)}) collective-permute-start(bf16[8,48,1536]{2,1,0:T(8,128)(2,1)} %dynamic-slice_bitcast_fusion.3), channel_id=1, source_target_pairs={{0,1},{1,0},{2,3},{3,2},{4,5},{5,4},{6,7},{7,6},{8,9},{9,8},{10,11... | collective-permute-start | bytes 3538952 | tf_op jit(solution)/shard_map/ppermute | solution.py:218
  546.5 15.9 %collective-permute-start.58 = (bf16[8,192,384]{2,1,0:T(8,128)(2,1)}, bf16[8,192,384]{2,1,0:T(8,128)(2,1)}, u32[]{:S(2)}, u32[]{:S(2)}) collective-permute-start(bf16[8,192,384]{2,1,0:T(8,128)(2,1)} %dynamic-slice_bitcast_fusion.1), channel_id=1, source_target_pairs={{0,1},{1,0},{2,3},{3,2},{4,5},{5,4},{6,7},{7,6},{8,9},{9,8},{10,11... | collective-permute-start | bytes 3538952 | tf_op jit(solution)/shard_map/ppermute | solution.py:218
  548.2 59.8 %collective-permute-start.9 = (bf16[768,768]{0,1:T(8,128)(2,1)}, bf16[768,768]{0,1:T(8,128)(2,1)}, u32[]{:S(2)}, u32[]{:S(2)}) collective-permute-start(bf16[768,768]{0,1:T(8,128)(2,1)} %get-tuple-element.181), channel_id=1, source_target_pairs={{0,1},{1,0},{2,3},{3,2},{4,5},{5,4},{6,7},{7,6},{8,9},{9,8},{10,11... | collective-permute-start | bytes 3538952 | tf_op jit(solution)/shard_map/ppermute | solution.py:218
  551.2 18.1 %collective-permute-start.10 = (bf16[8,48,1152]{2,1,0:T(8,128)(2,1)}, bf16[8,48,1152]{2,1,0:T(8,128)(2,1)}, u32[]{:S(2)}, u32[]{:S(2)}) collective-permute-start(bf16[8,48,1152]{2,1,0:T(8,128)(2,1)} %dynamic-slice_bitcast_fusion.5), channel_id=1, source_target_pairs={{0,1},{1,0},{2,3},{3,2},{4,5},{5,4},{6,7},{7,6},{8,9},{9,8},{10,11... | collective-permute-start | bytes 2654216 | tf_op jit(solution)/shard_map/ppermute | solution.py:218
  559.4 39.9 %collective-permute-start.53 = (bf16[4,48,1536]{2,1,0:T(8,128)(2,1)S(1)}, bf16[4,48,1536]{2,1,0:T(8,128)(2,1)S(1)}, u32[]{:S(2)}, u32[]{:S(2)}) collective-permute-start(bf16[4,48,1536]{2,1,0:T(8,128)(2,1)S(1)} %dynamic-slice_bitcast_fusion.8), channel_id=1, source_target_pairs={{0,4},{4,0},{8,12},{12,8},{16,20},{20,16},{24,28},{28,24},{1,5},{5... | collective-permute-start | bytes 1769480 | tf_op jit(solution)/shard_map/ppermute | solution.py:304
  562.4 37.7 %collective-permute-start.65 = (bf16[4,192,384]{2,1,0:T(8,128)(2,1)S(1)}, bf16[4,192,384]{2,1,0:T(8,128)(2,1)S(1)}, u32[]{:S(2)}, u32[]{:S(2)}) collective-permute-start(bf16[4,192,384]{2,1,0:T(8,128)(2,1)S(1)} %dynamic-slice_bitcast_fusion.6), channel_id=1, source_target_pairs={{0,4},{4,0},{8,12},{12,8},{16,20},{20,16},{24,28},{28,24},{1,5},{5... | collective-permute-start | bytes 1769480 | tf_op jit(solution)/shard_map/ppermute | solution.py:304
  566.1 31.7 %collective-permute-start.17 = (bf16[4,48,1152]{2,1,0:T(8,128)(2,1)S(1)}, bf16[4,48,1152]{2,1,0:T(8,128)(2,1)S(1)}, u32[]{:S(2)}, u32[]{:S(2)}) collective-permute-start(bf16[4,48,1152]{2,1,0:T(8,128)(2,1)S(1)} %dynamic-slice_bitcast_fusion.10), channel_id=1, source_target_pairs={{0,4},{4,0},{8,12},{12,8},{16,20},{20,16},{24,28},{28,24},{1,5},{5... | collective-permute-start | bytes 1327112 | tf_op jit(solution)/shard_map/ppermute | solution.py:304
  569.3 68.6 %collective-permute-start.47 = (bf16[4,48,1536]{2,1,0:T(8,128)(2,1)}, bf16[4,48,1536]{2,1,0:T(8,128)(2,1)}, u32[]{:S(2)}, u32[]{:S(2)}) collective-permute-start(bf16[4,48,1536]{2,1,0:T(8,128)(2,1)} %dynamic-slice_bitcast_fusion.9), channel_id=1, source_target_pairs={{0,4},{4,0},{8,12},{12,8},{16,20},{20,16},{24,28},{28,24},{1,5},{5... | collective-permute-start | bytes 1769480 | tf_op jit(solution)/shard_map/ppermute | solution.py:304
  597.8 41.4 %collective-permute-start.59 = (bf16[4,192,384]{2,1,0:T(8,128)(2,1)}, bf16[4,192,384]{2,1,0:T(8,128)(2,1)}, u32[]{:S(2)}, u32[]{:S(2)}) collective-permute-start(bf16[4,192,384]{2,1,0:T(8,128)(2,1)} %dynamic-slice_bitcast_fusion.7), channel_id=1, source_target_pairs={{0,4},{4,0},{8,12},{12,8},{16,20},{20,16},{24,28},{28,24},{1,5},{5... | collective-permute-start | bytes 1769480 | tf_op jit(solution)/shard_map/ppermute | solution.py:304
  599.4 32.6 %collective-permute-start.11 = (bf16[4,48,1152]{2,1,0:T(8,128)(2,1)}, bf16[4,48,1152]{2,1,0:T(8,128)(2,1)}, u32[]{:S(2)}, u32[]{:S(2)}) collective-permute-start(bf16[4,48,1152]{2,1,0:T(8,128)(2,1)} %dynamic-slice_bitcast_fusion.11), channel_id=1, source_target_pairs={{0,4},{4,0},{8,12},{12,8},{16,20},{20,16},{24,28},{28,24},{1,5},{5... | collective-permute-start | bytes 1327112 | tf_op jit(solution)/shard_map/ppermute | solution.py:304
  600.1 6.0 collective-permute-start.18
  606.1 17.6 %collective-permute-start.54 = (bf16[2,48,1536]{2,1,0:T(8,128)(2,1)}, bf16[2,48,1536]{2,1,0:T(8,128)(2,1)}, u32[]{:S(2)}, u32[]{:S(2)}) collective-permute-start(bf16[2,48,1536]{2,1,0:T(8,128)(2,1)} %dynamic-slice_bitcast_fusion.14), channel_id=1, source_target_pairs={{0,8},{4,12},{8,0},{12,4},{16,24},{20,28},{24,16},{28,20},{1,9},{5... | collective-permute-start | bytes 884744 | tf_op jit(solution)/shard_map/ppermute | solution.py:304
  608.0 14.5 %collective-permute-start.19 = (bf16[1,48,1152]{2,1,0:T(8,128)(2,1)S(1)}, bf16[1,48,1152]{2,1,0:T(8,128)(2,1)}, u32[]{:S(2)}, u32[]{:S(2)}) collective-permute-start(bf16[1,48,1152]{2,1,0:T(8,128)(2,1)S(1)} %constant_dynamic-slice_fusion.16), channel_id=1, source_target_pairs={{0,16},{4,20},{8,24},{12,28},{16,0},{20,4},{24,8},{28,12},{1,17},{... | collective-permute-start | bytes 331784 | tf_op jit(solution)/shard_map/ppermute | solution.py:304
  622.5 7.0 %collective-permute-start.66 = (bf16[2,192,384]{2,1,0:T(8,128)(2,1)}, bf16[2,192,384]{2,1,0:T(8,128)(2,1)S(1)}, u32[]{:S(2)}, u32[]{:S(2)}) collective-permute-start(bf16[2,192,384]{2,1,0:T(8,128)(2,1)} %dynamic-slice_bitcast_fusion.12), channel_id=1, source_target_pairs={{0,8},{4,12},{8,0},{12,4},{16,24},{20,28},{24,16},{28,20},{1,9},{5... | collective-permute-start | bytes 884744 | tf_op jit(solution)/shard_map/ppermute | solution.py:304
  623.7 12.2 %collective-permute-start.20 = (bf16[48,1152]{1,0:T(8,128)(2,1)S(1)}, bf16[48,1152]{1,0:T(8,128)(2,1)S(1)}, u32[]{:S(2)}, u32[]{:S(2)}) collective-permute-start(bf16[48,1152]{1,0:T(8,128)(2,1)S(1)} %add_bitcast_fusion.4), channel_id=1, source_target_pairs={{0,2},{1,3},{2,0},{3,1},{4,6},{5,7},{6,4},{7,5},{8,10},{9,11},{10,... | collective-permute-start | bytes 331784 | tf_op jit(solution)/shard_map/ppermute | solution.py:218
  629.6 11.8 %collective-permute-start.55 = (bf16[1,48,1536]{2,1,0:T(8,128)(2,1)S(1)}, bf16[1,48,1536]{2,1,0:T(8,128)(2,1)S(1)}, u32[]{:S(2)}, u32[]{:S(2)}) collective-permute-start(bf16[1,48,1536]{2,1,0:T(8,128)(2,1)S(1)} %constant_dynamic-slice_fusion.4), channel_id=1, source_target_pairs={{0,16},{4,20},{8,24},{12,28},{16,0},{20,4},{24,8},{28,12},{1,17},{... | collective-permute-start | bytes 442376 | tf_op jit(solution)/shard_map/ppermute | solution.py:304
  632.0 11.6 %collective-permute-start.67 = (bf16[1,192,384]{2,1,0:T(8,128)(2,1)S(1)}, bf16[1,192,384]{2,1,0:T(8,128)(2,1)S(1)}, u32[]{:S(2)}, u32[]{:S(2)}) collective-permute-start(bf16[1,192,384]{2,1,0:T(8,128)(2,1)S(1)} %constant_dynamic-slice_fusion.2), channel_id=1, source_target_pairs={{0,16},{4,20},{8,24},{12,28},{16,0},{20,4},{24,8},{28,12},{1,17},{... | collective-permute-start | bytes 442376 | tf_op jit(solution)/shard_map/ppermute | solution.py:304
  635.9 11.7 %collective-permute-start.12 = (bf16[2,48,1152]{2,1,0:T(8,128)(2,1)S(1)}, bf16[2,48,1152]{2,1,0:T(8,128)(2,1)S(1)}, u32[]{:S(2)}, u32[]{:S(2)}) collective-permute-start(bf16[2,48,1152]{2,1,0:T(8,128)(2,1)S(1)} %dynamic-slice_bitcast_fusion.19), channel_id=1, source_target_pairs={{0,8},{4,12},{8,0},{12,4},{16,24},{20,28},{24,16},{28,20},{1,9},{5... | collective-permute-start | bytes 663560 | tf_op jit(solution)/shard_map/ppermute | solution.py:304
  637.9 14.9 %collective-permute-start.21 = (bf16[48,2304]{1,0:T(8,128)(2,1)S(1)}, bf16[48,2304]{1,0:T(8,128)(2,1)S(1)}, u32[]{:S(2)}, u32[]{:S(2)}) collective-permute-start(bf16[48,2304]{1,0:T(8,128)(2,1)S(1)} %maximum_select_fusion.11), channel_id=1, source_target_pairs={{0,1},{1,0},{2,3},{3,2},{4,5},{5,4},{6,7},{7,6},{8,9},{9,8},{10,11... | collective-permute-start | bytes 663560 | tf_op jit(solution)/shard_map/ppermute | solution.py:218
  639.2 19.6 %collective-permute-start.48 = (bf16[2,48,1536]{2,1,0:T(8,128)(2,1)S(1)}, bf16[2,48,1536]{2,1,0:T(8,128)(2,1)S(1)}, u32[]{:S(2)}, u32[]{:S(2)}) collective-permute-start(bf16[2,48,1536]{2,1,0:T(8,128)(2,1)S(1)} %dynamic-slice_bitcast_fusion.15), channel_id=1, source_target_pairs={{0,8},{4,12},{8,0},{12,4},{16,24},{20,28},{24,16},{28,20},{1,9},{5... | collective-permute-start | bytes 884744 | tf_op jit(solution)/shard_map/ppermute | solution.py:304
  641.3 21.6 %collective-permute-start.60 = (bf16[2,192,384]{2,1,0:T(8,128)(2,1)S(1)}, bf16[2,192,384]{2,1,0:T(8,128)(2,1)S(1)}, u32[]{:S(2)}, u32[]{:S(2)}) collective-permute-start(bf16[2,192,384]{2,1,0:T(8,128)(2,1)S(1)} %dynamic-slice_bitcast_fusion.13), channel_id=1, source_target_pairs={{0,8},{4,12},{8,0},{12,4},{16,24},{20,28},{24,16},{28,20},{1,9},{5... | collective-permute-start | bytes 884744 | tf_op jit(solution)/shard_map/ppermute | solution.py:304
  643.6 5.7 collective-permute-start.56
  647.6 5.1 collective-permute-start.68
  649.3 8.0 %collective-permute-start.13 = (bf16[1,48,1152]{2,1,0:T(8,128)(2,1)S(1)}, bf16[1,48,1152]{2,1,0:T(8,128)(2,1)S(1)}, u32[]{:S(2)}, u32[]{:S(2)}) collective-permute-start(bf16[1,48,1152]{2,1,0:T(8,128)(2,1)S(1)} %constant_dynamic-slice_fusion.17), channel_id=1, source_target_pairs={{0,16},{4,20},{8,24},{12,28},{16,0},{20,4},{24,8},{28,12},{1,17},{... | collective-permute-start | bytes 331784 | tf_op jit(solution)/shard_map/ppermute | solution.py:304
  652.8 22.0 %collective-permute-start.57 = (bf16[48,3072]{1,0:T(8,128)(2,1)S(1)}, bf16[48,3072]{1,0:T(8,128)(2,1)S(1)}, u32[]{:S(2)}, u32[]{:S(2)}) collective-permute-start(bf16[48,3072]{1,0:T(8,128)(2,1)S(1)} %maximum_select_fusion.7), channel_id=1, source_target_pairs={{0,1},{1,0},{2,3},{3,2},{4,5},{5,4},{6,7},{7,6},{8,9},{9,8},{10,11... | collective-permute-start | bytes 884744 | tf_op jit(solution)/shard_map/ppermute | solution.py:218
  652.9 22.0 %collective-permute-start.69 = (bf16[192,768]{1,0:T(8,128)(2,1)S(1)}, bf16[192,768]{1,0:T(8,128)(2,1)S(1)}, u32[]{:S(2)}, u32[]{:S(2)}) collective-permute-start(bf16[192,768]{1,0:T(8,128)(2,1)S(1)} %maximum_select_fusion.9), channel_id=1, source_target_pairs={{0,1},{1,0},{2,3},{3,2},{4,5},{5,4},{6,7},{7,6},{8,9},{9,8},{10,11... | collective-permute-start | bytes 884744 | tf_op jit(solution)/shard_map/ppermute | solution.py:218
  657.4 5.7 collective-permute-start.14
  658.9 13.4 %collective-permute-start.49 = (bf16[1,48,1536]{2,1,0:T(8,128)(2,1)S(1)}, bf16[1,48,1536]{2,1,0:T(8,128)(2,1)S(1)}, u32[]{:S(2)}, u32[]{:S(2)}) collective-permute-start(bf16[1,48,1536]{2,1,0:T(8,128)(2,1)S(1)} %constant_dynamic-slice_fusion.5), channel_id=1, source_target_pairs={{0,16},{4,20},{8,24},{12,28},{16,0},{20,4},{24,8},{28,12},{1,17},{... | collective-permute-start | bytes 442376 | tf_op jit(solution)/shard_map/ppermute | solution.py:304
  663.0 11.0 %collective-permute-start.61 = (bf16[1,192,384]{2,1,0:T(8,128)(2,1)S(1)}, bf16[1,192,384]{2,1,0:T(8,128)(2,1)S(1)}, u32[]{:S(2)}, u32[]{:S(2)}) collective-permute-start(bf16[1,192,384]{2,1,0:T(8,128)(2,1)S(1)} %constant_dynamic-slice_fusion.3), channel_id=1, source_target_pairs={{0,16},{4,20},{8,24},{12,28},{16,0},{20,4},{24,8},{28,12},{1,17},{... | collective-permute-start | bytes 442376 | tf_op jit(solution)/shard_map/ppermute | solution.py:304
  663.2 17.1 %collective-permute-start.15 = (bf16[48,2304]{1,0:T(8,128)(2,1)S(1)}, bf16[48,2304]{1,0:T(8,128)(2,1)S(1)}, u32[]{:S(2)}, u32[]{:S(2)}) collective-permute-start(bf16[48,2304]{1,0:T(8,128)(2,1)S(1)} %maximum_select_fusion.10), channel_id=1, source_target_pairs={{0,1},{1,0},{2,3},{3,2},{4,5},{5,4},{6,7},{7,6},{8,9},{9,8},{10,11... | collective-permute-start | bytes 663560 | tf_op jit(solution)/shard_map/ppermute | solution.py:218
  672.3 6.2 collective-permute-start.50
  674.0 6.1 collective-permute-start.62
  (268 other events, 2288.2 us)

commit v2 on v1

v2 whole, which is shorter than its diff:
```python
import functools

import jax
import jax.numpy as jnp
from jax import lax
from jax.experimental import pallas as pl
from jax.experimental.pallas import tpu as pltpu
from jax.sharding import PartitionSpec as P

ln_eps = 1e-05
masked_score = -1e30
bf16 = jnp.bfloat16
f32 = jnp.float32
MB = 1 << 20
SUPER = 8
LANES = 384

ERF_COEFS = (
    0.7978849414899046, 0.0363330844086688, -3.259474462099993e-05, -5.5306316685416947e-05,
    3.964773125473232e-06, -1.322662757755248e-07, 1.7562773256476674e-09,
)


def dot(a, b):
    return lax.dot_general(a, b, (((1,), (0,)), ((), ())), preferred_element_type=f32)


def dot_nt(a, b):
    return lax.dot_general(a, b, (((1,), (1,)), ((), ())), preferred_element_type=f32)


def gelu_and_slope(x):
    square = x * x
    g = ERF_COEFS[-1]
    for c in ERF_COEFS[-2::-1]:
        g = g * square + c
    phi = 0.5 * jnp.tanh(x * g) + 0.5
    density = jnp.exp2(square * (-0.5 * 1.4426950408889634)) * 0.3989422804014327
    return x * phi, phi + x * density


def norm_parts(residual):
    average = jnp.mean(residual, -1, keepdims=True)
    centered = residual - average
    inverse = lax.rsqrt(jnp.mean(centered * centered, -1, keepdims=True) + ln_eps)
    return centered * inverse, inverse


def norm_back(gradient, gain, normed, inverse):
    dnormed = gradient * gain
    return inverse * (
        dnormed
        - jnp.mean(dnormed, -1, keepdims=True)
        - normed * jnp.mean(dnormed * normed, -1, keepdims=True)
    )


def col_sum(x):
    return jnp.sum(x, 0, keepdims=True)


def call(kernel, name, grid, ids, in_specs, inputs, out_specs, out_shape, scratch=()):
    return pl.pallas_call(
        kernel,
        grid_spec=pltpu.PrefetchScalarGridSpec(
            num_scalar_prefetch=1,
            grid=grid,
            in_specs=in_specs,
            out_specs=out_specs,
            scratch_shapes=list(scratch),
        ),
        out_shape=out_shape,
        compiler_params=pltpu.CompilerParams(vmem_limit_bytes=62 * MB),
        name=name,
    )(ids, *inputs)


def spec(shape, *index):
    def index_map(i, ids):
        return tuple(x(i, ids) if callable(x) else x for x in index)

    return pl.BlockSpec(shape, index_map)


def shape_of(shape, dtype):
    return jax.ShapeDtypeStruct(shape, dtype)


step = lambda i, ids: i


def row_tiles(half, width, gathered):
    if not gathered:
        return [spec((1, half, width), t, 0, 0) for t in range(3)]
    core = lambda ids: ids[0]
    return [
        spec((1, half, width), lambda i, ids: 2 * core(ids), 0, 0),
        spec((1, half, width), lambda i, ids: 2 * core(ids) + 1, 0, 0),
        spec((1, half, width), lambda i, ids: 4 + core(ids), 0, 0),
    ]


def tables_kernel(
    ids, boxes_ref, seg_ref, valid_ref,
    cos_ref, sin_ref, kf_ref, ctab_ref, stab_ref, code_ref, segrow_ref, valid_col_ref,
):
    core = ids[0]
    length = seg_ref.shape[1]
    half = length // 2

    def ordered(read):
        near = pl.multiple_of(core * half, half)
        far = pl.multiple_of((1 - core) * half, half)
        return jnp.concatenate(
            [read(pl.ds(core, 1), slice(None)), read(2, pl.ds(near, half)), read(2, pl.ds(far, half))], 1
        )

    def row_of(ref):
        def read(r, c):
            r = pl.ds(2, 1) if isinstance(r, int) else r
            return ref[r, c]
        return ordered(read)

    count = length * 2
    at = lax.broadcasted_iota(jnp.int32, (1, count), 1)
    shared = jnp.where(
        at < length + half, at - length + core * half, at - length - half + (1 - core) * half
    )
    position = jnp.where(at < length, at, shared).astype(f32)
    rate_at = lax.broadcasted_iota(jnp.int32, (32, 1), 0).astype(f32)
    text = position * jnp.exp(rate_at * (-9.210340371976184 / 32))
    box_rate = jnp.exp2(-lax.broadcasted_iota(jnp.int32, (8, 1), 0).astype(f32))
    angles = [text]
    for c in range(4):
        coords = row_of(boxes_ref.at[c]).astype(f32)
        angles.append(coords * box_rate)
    angles = jnp.concatenate(angles, 0)
    cosines, sines = jnp.cos(angles), jnp.sin(angles)
    cos_ref[...], sin_ref[...] = cosines, sines
    kf_ref[...] = jnp.concatenate([cosines, sines], 0).T.astype(bf16)
    ctab_ref[...] = jnp.concatenate([cosines, -cosines], 0).T
    stab_ref[...] = jnp.concatenate([sines, sines], 0).T
    seg = row_of(seg_ref).astype(f32)
    valid = row_of(valid_ref).astype(f32)
    segrow_ref[...] = jnp.broadcast_to(seg, segrow_ref.shape)
    code_ref[...] = jnp.broadcast_to(jnp.where(valid > 0, seg, -1.0), (128, count)).T
    valid_col_ref[...] = jnp.broadcast_to(valid, (128, count)).T


def make_tables(ids, word_boxes, segments, valid_mask):
    length = segments.shape[1]
    count = 2 * length
    full = lambda *shape: spec(shape, *([0] * len(shape)))
    outs = [
        ((64, count), f32), ((64, count), f32), ((count, 128), bf16), ((count, 128), f32),
        ((count, 128), f32), ((count, 128), f32), ((8, count), f32), ((count, 128), f32),
    ]
    return call(
        tables_kernel, "tables", (1,), ids,
        [full(*word_boxes.shape), full(*segments.shape), full(*valid_mask.shape)],
        [word_boxes, segments, valid_mask],
        [full(*s) for s, _ in outs], [shape_of(s, d) for s, d in outs],
    )


def qkv_kernel(
    ids, x0, x1, x2, w_ref, bias_ref, rel_ref, ctab_ref, stab_ref, joint_ref, turned_ref, kv_ref, x_ref,
    *, layer,
):
    j = pl.program_id(0)
    half = x0.shape[1]

    @pl.when(j == 0)
    def _():
        x_ref[0:half], x_ref[half : 2 * half], x_ref[2 * half :] = x0[0], x1[0], x2[0]

    flags = [(j == 0).astype(f32), (j == 2).astype(f32)]
    bias = bias_ref[layer, 0:1, :].astype(f32) * flags[0] + bias_ref[layer, 1:2, :].astype(f32) * flags[1]
    joint = (dot(x_ref[...], w_ref[0]) + bias).astype(bf16)
    joint_ref[...] = joint
    kv_ref[...] = joint[2 * half :]

    @pl.when(j == 0)
    def _():
        ctab, stab = ctab_ref[...], stab_ref[...]
        row = lax.broadcasted_iota(jnp.int32, (128, 128), 0)
        for p in range(rel_ref.shape[1]):
            rel = rel_ref[0, p]
            zero = jnp.zeros_like(rel)
            block = jnp.concatenate([jnp.where(row < 64, rel, zero), jnp.where(row < 64, zero, rel)], 1)
            coef = dot(joint[:, 128 * p : 128 * p + 128], block)
            for e in range(2):
                c = coef[:, 128 * e : 128 * e + 128]
                at = 256 * p + 128 * e
                turned_ref[:, at : at + 128] = (c * ctab + pltpu.roll(c, 64, 1) * stab).astype(bf16)


def project(ids, x, gathered, w_qkv, qv_bias, rel_pairs, ctab, stab, layer):
    half, width = x.shape[1], x.shape[2]
    tokens = 3 * half
    pairs = rel_pairs.shape[1]
    return call(
        functools.partial(qkv_kernel, layer=layer), "projections", (3,), ids,
        row_tiles(half, width, gathered)
        + [
            spec((1, width, width), layer, 0, step), spec(qv_bias.shape, 0, 0, 0),
            spec((1, pairs, 128, 128), layer, 0, 0, 0), spec((tokens, 128), 0, 0),
            spec((tokens, 128), 0, 0),
        ],
        [x, x, x, w_qkv, qv_bias, rel_pairs, ctab, stab],
        [
            spec((tokens, width), 0, step), spec((tokens, 2 * width), 0, 0),
            spec((half, width), 0, lambda i, ids: jnp.maximum(i - 1, 0)),
        ],
        [
            shape_of((tokens, 3 * width), bf16), shape_of((tokens, 2 * width), bf16),
            shape_of((half, 2 * width), bf16),
        ],
        [pltpu.VMEM((tokens, width), bf16)],
    )


def lane_half(shape, half):
    lane = lax.broadcasted_iota(jnp.int32, shape, 1)
    return (lane < 64) if half == 0 else (lane >= 64)


def only_half(x, half):
    return jnp.where(lane_half(x.shape, half), x, jnp.zeros_like(x))


def fill_bias(code_ref, seg_ref, bias_ref):
    shape = bias_ref.shape
    code = jnp.concatenate([code_ref[...]] * (shape[1] // 128), 1)
    same = code == seg_ref[0:1, :]
    key_at = lax.broadcasted_iota(jnp.int32, shape, 0)
    query_at = lax.broadcasted_iota(jnp.int32, shape, 1)
    bias_ref[...] = jnp.where(same | (key_at == query_at), 0.0, masked_score)


def attention_fwd_kernel(
    ids, code_ref, seg_ref, kf_ref, q_ref, turned_ref, k_ref, v_ref, *rest, per_step, shared,
):
    if shared:
        k_far, v_far, ctx_ref, lse_ref, bias_ref, k_all, v_all = rest
        half = k_ref.shape[0]
        k_all[0:half], k_all[half:] = k_ref[...], k_far[...]
        v_all[0:half], v_all[half:] = v_ref[...], v_far[...]
        k_ref, v_ref = k_all, v_all
    else:
        ctx_ref, lse_ref, bias_ref = rest

    @pl.when(pl.program_id(0) == 0)
    def _():
        fill_bias(code_ref, seg_ref, bias_ref)

    scale = jnp.asarray(0.125, bf16)
    units = [(pair, e) for pair in range(per_step) for e in range(2)]
    values_t = {}

    def scores_of(unit):
        pair, e = unit
        at = slice(128 * pair, 128 * pair + 128)
        turned = turned_ref[:, 256 * pair + 128 * e : 256 * pair + 128 * e + 128]
        qside = jnp.concatenate([turned, only_half(q_ref[:, at], e)], 1) * scale
        kside = jnp.concatenate([kf_ref[...], k_ref[:, at]], 1)
        return dot_nt(kside, qside) + bias_ref[...]

    def finish(unit, scores):
        pair, e = unit
        top = jnp.max(scores, 0, keepdims=True)
        expo = jnp.exp(scores - top)
        total = jnp.sum(expo, 0, keepdims=True)
        if pair not in values_t:
            values_t[pair] = v_ref[:, 128 * pair : 128 * pair + 128].T
        ctx = dot(values_t[pair][64 * e : 64 * e + 64], expo.astype(bf16))
        at = 128 * pair + 64 * e
        ctx_ref[at : at + 64, :] = (ctx * (1.0 / total)).astype(bf16)
        lse_ref[0, 2 * pair + e : 2 * pair + e + 1, :] = top + jnp.log(total)

    scores = scores_of(units[0])
    for i, unit in enumerate(units):
        upcoming = scores_of(units[i + 1]) if i + 1 < len(units) else None
        finish(unit, scores)
        scores = upcoming


def attention_fwd(ids, shared, tables, joint, turned, kv_far, per_step=2):
    cos_t, sin_t, kf, ctab, stab, code, seg, valid = tables
    tokens, width = joint.shape[0], joint.shape[1] // 3
    half = tokens // 3
    nk = 2 * half
    nq = half if shared else nk
    key_rows = half if shared else nk
    lanes = 128 * per_step
    steps = width // lanes
    q_row = 2 if shared else 0
    at = lambda off: (lambda i, ids: i + off)
    in_specs = [
        spec((nk, 128), int(shared), 0), spec((8, nq), 0, q_row), spec((nk, 128), int(shared), 0),
        spec((nq, lanes), q_row, step), spec((nq, 2 * lanes), q_row, step),
        spec((key_rows, lanes), q_row, at(steps)), spec((key_rows, lanes), q_row, at(2 * steps)),
    ]
    inputs = [code, seg, kf, joint, turned, joint, joint]
    scratch = [pltpu.VMEM((nk, nq), f32)]
    if shared:
        in_specs += [spec((half, lanes), 0, step), spec((half, lanes), 0, at(steps))]
        inputs += [kv_far, kv_far]
        scratch += [pltpu.VMEM((nk, lanes), bf16)] * 2
    return call(
        functools.partial(attention_fwd_kernel, per_step=per_step, shared=shared),
        "attention_forward", (steps,), ids, in_specs, inputs,
        [spec((lanes, nq), step, 0), spec((1, 2 * per_step, nq), step, 0, 0)],
        [shape_of((width, nq), bf16), shape_of((steps, 2 * per_step, nq), f32)],
        scratch,
    )


def attention_bwd_kernel(
    ids, code_ref, seg_ref, kf_ref, cos_ref, sin_ref, rel_ref, lse_ref, gc_ref, q_ref, turned_ref,
    k_ref, v_ref, *rest, per_step, shared,
):
    if shared:
        k_far, v_far, keep_ref, send_ref, drel_ref, bias_ref, kft_ref, k_all, v_all = rest
        half = k_ref.shape[0]
        k_all[0:half], k_all[half:] = k_ref[...], k_far[...]
        v_all[0:half], v_all[half:] = v_ref[...], v_far[...]
        k_ref, v_ref = k_all, v_all
    else:
        keep_ref, drel_ref, bias_ref, kft_ref = rest

    @pl.when(pl.program_id(0) == 0)
    def _():
        fill_bias(code_ref, seg_ref, bias_ref)
        kft_ref[...] = kf_ref[...].T

    scale = jnp.asarray(0.125, bf16)
    cosines, sines = cos_ref[...], sin_ref[...]
    units = [(pair, e) for pair in range(per_step) for e in range(2)]
    store = {}

    def scores_of(unit):
        pair, e = unit
        at = slice(128 * pair, 128 * pair + 128)
        q_mine = only_half(q_ref[:, at], e)
        gc_mine = only_half(gc_ref[:, at], e)
        q_scaled = q_mine * scale
        turned = turned_ref[:, 256 * pair + 128 * e : 256 * pair + 128 * e + 128]
        qside = jnp.concatenate([turned * scale, q_scaled], 1)
        kside = jnp.concatenate([kf_ref[...], k_ref[:, at]], 1)
        scores = dot_nt(kside, qside) + bias_ref[...]
        gp = dot_nt(v_ref[:, at], gc_mine)
        return scores, gp, q_mine, gc_mine, q_scaled

    def finish(unit, parts):
        pair, e = unit
        scores, gp, q_mine, gc_mine, q_scaled = parts
        at = slice(128 * pair, 128 * pair + 128)
        shares = jnp.exp(scores - lse_ref[0, 2 * pair + e : 2 * pair + e + 1, :])
        dv = dot(shares.astype(bf16), gc_mine)
        weighted = shares * gp
        delta = jnp.sum(weighted, 0, keepdims=True)
        gs = (weighted - shares * delta).astype(bf16)
        dk = dot(gs, q_scaled)
        if pair not in store:
            store[pair] = k_ref[:, at].T
        side_t = jnp.concatenate([kft_ref[...], store[pair][64 * e : 64 * e + 64]], 0)
        dside = dot(side_t, gs) * 0.125
        g_cos, g_sin = dside[0:64], dside[64:128]
        gcoef = jnp.concatenate(
            [g_cos * cosines + g_sin * sines, g_cos * sines - g_sin * cosines], 0
        ).astype(bf16)
        dq = dside[128:192] + dot(rel_ref[0, pair, 64 * e : 64 * e + 64], gcoef)
        drel = dot(gcoef, q_mine)
        if e == 0:
            store["even"] = (dq, dk, dv, drel)
            return
        dq0, dk0, dv0, drel0 = store["even"]
        dq = jnp.concatenate([dq0, dq], 0).T.astype(bf16)
        dk, dv = (dk0 + dk).astype(bf16), (dv0 + dv).astype(bf16)
        drel_ref[:, at] = drel0 + drel
        n = keep_ref.shape[1]
        keep_ref[0, :, at] = dq
        keep_ref[1, :, at], keep_ref[2, :, at] = dk[0:n], dv[0:n]
        if shared:
            send_ref[0, :, at], send_ref[1, :, at] = dk[n:], dv[n:]

    parts = scores_of(units[0])
    for i, unit in enumerate(units):
        upcoming = scores_of(units[i + 1]) if i + 1 < len(units) else None
        finish(unit, parts)
        parts = upcoming


def attention_bwd(ids, shared, tables, joint, turned, kv_far, lse, g_ctx, rel_pairs, layer, per_step=2):
    cos_t, sin_t, kf, ctab, stab, code, seg, valid = tables
    tokens, width = joint.shape[0], joint.shape[1] // 3
    half = tokens // 3
    nk = 2 * half
    nq = half if shared else nk
    key_rows = half if shared else nk
    lanes = 128 * per_step
    steps = width // lanes
    q_row = 2 if shared else 0
    at = lambda off: (lambda i, ids: i + off)
    in_specs = [
        spec((nk, 128), int(shared), 0), spec((8, nq), 0, q_row), spec((nk, 128), int(shared), 0),
        spec((64, nq), 0, q_row), spec((64, nq), 0, q_row),
        spec((1, per_step, 128, 128), layer, step, 0, 0),
        spec((1, 2 * per_step, nq), step, 0, 0), spec((nq, lanes), q_row, step),
        spec((nq, lanes), q_row, step), spec((nq, 2 * lanes), q_row, step),
        spec((key_rows, lanes), q_row, at(steps)), spec((key_rows, lanes), q_row, at(2 * steps)),
    ]
    inputs = [code, seg, kf, cos_t, sin_t, rel_pairs, lse, g_ctx, joint, turned, joint, joint]
    scratch = [pltpu.VMEM((nk, nq), f32), pltpu.VMEM((128, nk), bf16)]
    out_specs = [spec((3, key_rows, lanes), 0, 0, step)]
    out_shape = [shape_of((3, key_rows, width), bf16)]
    if shared:
        in_specs += [spec((half, lanes), 0, step), spec((half, lanes), 0, at(steps))]
        inputs += [kv_far, kv_far]
        scratch += [pltpu.VMEM((nk, lanes), bf16)] * 2
        out_specs.append(spec((2, half, lanes), 0, 0, step))
        out_shape.append(shape_of((2, half, width), bf16))
    out_specs.append(spec((128, lanes), 0, step))
    out_shape.append(shape_of((128, width), f32))
    return call(
        functools.partial(attention_bwd_kernel, per_step=per_step, shared=shared),
        "attention_backward", (steps,), ids, in_specs, inputs, out_specs, out_shape, scratch,
    )


def feed_fwd_kernel(
    ids, x0, x1, x2, own_ref, shared_ref, valid_ref, w_out_ref, out_bias_ref, scale_ref, shift_ref,
    in_ref, in_bias_ref, out_ref, ffn_bias_ref,
    n1_ref, r1_ref, n2_ref, r2_ref, mixed_ref, act_ref, slope_ref, h_ref, squares_ref,
    feed_ref,
    *, layer, parts,
):
    j = pl.program_id(0)
    half = x0.shape[1]
    long = 2 * half
    row = lambda ref, *at: ref[at[:-1] + (slice(at[-1], at[-1] + 1),)].astype(f32)

    def add_squares(values, k):
        weighted = values * values * valid_ref[:, 0:1]
        squares_ref[k : k + 1, :] = col_sum(weighted[0:long])
        squares_ref[k + 1 : k + 2, :] = col_sum(weighted[long:])

    @pl.when(j == 0)
    def _():
        ctx = jnp.concatenate([own_ref[...].T, shared_ref[...].T], 0)
        attention = dot(ctx, w_out_ref[0]) + row(out_bias_ref, layer)
        add_squares(attention, 0)
        x = jnp.concatenate([x0[0], x1[0], x2[0]], 0).astype(f32)
        normed, inverse = norm_parts(x + attention)
        mixed = (normed * row(scale_ref, layer, 0) + row(shift_ref, layer, 0)).astype(bf16)
        n1_ref[...] = normed.astype(bf16)
        r1_ref[...] = jnp.broadcast_to(inverse, r1_ref.shape)
        mixed_ref[...] = mixed
        add_squares(mixed.astype(f32), 2)

    cols = in_ref.shape[2] // parts
    at = lambda k: slice(cols * k, cols * k + cols)
    bias = in_bias_ref[layer : layer + 1, :].astype(f32)
    pre = dot(mixed_ref[...], in_ref[0, :, at(0)]) + bias[:, at(0)]
    feed = None
    for k in range(parts):
        coming = None
        if k + 1 < parts:
            coming = dot(mixed_ref[...], in_ref[0, :, at(k + 1)]) + bias[:, at(k + 1)]
        act, slope = gelu_and_slope(pre)
        act = act.astype(bf16)
        act_ref[:, at(k)] = act
        slope_ref[:, at(k)] = slope.astype(bf16)
        part = dot(act, out_ref[0, at(k)])
        feed = part if feed is None else feed + part
        pre = coming

    @pl.when(j == 0)
    def _():
        feed_ref[...] = feed

    @pl.when(j > 0)
    def _():
        feed_ref[...] += feed

    @pl.when(j == pl.num_programs(0) - 1)
    def _():
        total = feed_ref[...] + row(ffn_bias_ref, layer)
        add_squares(total, 4)
        normed, inverse = norm_parts(mixed_ref[...].astype(f32) + total)
        out = normed * row(scale_ref, layer, 1) + row(shift_ref, layer, 1)
        add_squares(out, 6)
        n2_ref[...] = normed.astype(bf16)
        r2_ref[...] = jnp.broadcast_to(inverse, r2_ref.shape)
        h_ref[...] = out.astype(bf16)


def feed_fwd(ids, x, gathered, ctx_own, ctx_shared, valid, weights, layer, chunk=768, parts=3):
    w_out, out_bias, ln_scale, ln_shift, ffn_in, ffn_in_bias, ffn_out, ffn_out_bias = weights
    half, width = x.shape[1], x.shape[2]
    tokens, ff = 3 * half, ffn_in.shape[2]
    full = lambda *shape: spec(shape, *([0] * len(shape)))
    dense = ((tokens, width), bf16)
    column = ((tokens, 128), f32)
    outs = [dense, column, dense, column, dense, ((tokens, ff), bf16), ((tokens, ff), bf16), dense,
            ((8, width), f32)]
    out_specs = [full(*s) for s, _ in outs]
    out_specs[5] = out_specs[6] = spec((tokens, chunk), 0, step)
    return call(
        functools.partial(feed_fwd_kernel, layer=layer, parts=parts), "feed_forward", (ff // chunk,), ids,
        row_tiles(half, width, gathered)
        + [
            full(*ctx_own.shape), full(*ctx_shared.shape), spec((tokens, 128), 0, 0),
            spec((1, width, width), layer, 0, 0), full(*out_bias.shape), full(*ln_scale.shape),
            full(*ln_shift.shape), spec((1, width, chunk), layer, 0, step),
            spec((ffn_in_bias.shape[0], chunk), 0, step), spec((1, chunk, width), layer, step, 0),
            full(*ffn_out_bias.shape),
        ],
        [x, x, x, ctx_own, ctx_shared, valid, w_out, out_bias, ln_scale, ln_shift, ffn_in, ffn_in_bias,
         ffn_out, ffn_out_bias],
        out_specs, [shape_of(s, d) for s, d in outs], [pltpu.VMEM((tokens, width), f32)],
    )


def feed_bwd_kernel(
    ids, g0, g1, g2, n2_ref, r2_ref, n1_ref, r1_ref, scale_ref, out_ref, slope_ref, in_ref, w_out_ref,
    feed_ref, pre_ref, mixed_ref, attn_ref, ctx_ref, sums_ref, pre_sum_ref,
    res_ref, acc_ref,
    *, layer, parts,
):
    j = pl.program_id(0)
    row = lambda k: scale_ref[layer, k : k + 1, :].astype(f32)

    @pl.when(j == 0)
    def _():
        grad = jnp.concatenate([g0[0], g1[0], g2[0]], 0).astype(f32)
        normed = n2_ref[...].astype(f32)
        sums_ref[1:2, :] = col_sum(grad * normed)
        sums_ref[3:4, :] = col_sum(grad)
        back = norm_back(grad, row(1), normed, r2_ref[:, 0:1])
        res_ref[...] = back
        feed = back.astype(bf16)
        feed_ref[...] = feed
        sums_ref[5:6, :] = col_sum(feed.astype(f32))
        sums_ref[6:8, :] = jnp.zeros((2, sums_ref.shape[1]), f32)

    cols = slope_ref.shape[1] // parts
    at = lambda k: slice(cols * k, cols * k + cols)
    g_act = dot_nt(feed_ref[...], out_ref[0, at(0)])
    total = None
    for k in range(parts):
        coming = dot_nt(feed_ref[...], out_ref[0, at(k + 1)]) if k + 1 < parts else None
        g_pre = (g_act * slope_ref[:, at(k)].astype(f32)).astype(bf16)
        pre_ref[:, at(k)] = g_pre
        pre_sum_ref[:, at(k)] = jnp.broadcast_to(col_sum(g_pre.astype(f32)), (8, cols))
        part = dot_nt(g_pre, in_ref[0, :, at(k)])
        total = part if total is None else total + part
        g_act = coming

    @pl.when(j == 0)
    def _():
        acc_ref[...] = total

    @pl.when(j > 0)
    def _():
        acc_ref[...] += total

    @pl.when(j == pl.num_programs(0) - 1)
    def _():
        g_mixed = acc_ref[...] + res_ref[...]
        mixed_ref[...] = g_mixed.astype(bf16)
        normed = n1_ref[...].astype(f32)
        sums_ref[0:1, :] = col_sum(g_mixed * normed)
        sums_ref[2:3, :] = col_sum(g_mixed)
        attn = norm_back(g_mixed, row(0), normed, r1_ref[:, 0:1]).astype(bf16)
        attn_ref[...] = attn
        sums_ref[4:5, :] = col_sum(attn.astype(f32))
        ctx_ref[...] = dot_nt(attn, w_out_ref[0]).astype(bf16)


def feed_bwd(ids, grad, gathered, kept, slope, weights, layer, chunk=768, parts=3):
    w_out, out_bias, ln_scale, ln_shift, ffn_in, ffn_in_bias, ffn_out, ffn_out_bias = weights
    n1, r1, n2, r2 = kept
    half, width = grad.shape[1], grad.shape[2]
    tokens, ff = 3 * half, ffn_in.shape[2]
    full = lambda *shape: spec(shape, *([0] * len(shape)))
    dense = ((tokens, width), bf16)
    outs = [dense, ((tokens, ff), bf16), dense, dense, dense, ((8, width), f32), ((8, ff), f32)]
    out_specs = [full(*s) for s, _ in outs]
    out_specs[1] = spec((tokens, chunk), 0, step)
    out_specs[6] = spec((8, chunk), 0, step)
    return call(
        functools.partial(feed_bwd_kernel, layer=layer, parts=parts), "feed_backward", (ff // chunk,), ids,
        row_tiles(half, width, gathered)
        + [
            full(tokens, width), full(tokens, 128), full(tokens, width), full(tokens, 128),
            full(*ln_scale.shape), spec((1, chunk, width), layer, step, 0), spec((tokens, chunk), 0, step),
            spec((1, width, chunk), layer, 0, step), spec((1, width, width), layer, 0, 0),
        ],
        [grad, grad, grad, n2, r2, n1, r1, ln_scale, ffn_out, slope, ffn_in, w_out],
        out_specs, [shape_of(s, d) for s, d in outs],
        [pltpu.VMEM((tokens, width), f32), pltpu.VMEM((tokens, width), f32)],
    )


def joint_bwd_kernel(
    ids, own_ref, shared_ref, arrived_ref, w_ref, attn_ref, joint_ref, h_ref, sums_ref, acc_ref,
):
    j = pl.program_id(0)
    far = arrived_ref[0].astype(f32) * (j > 0).astype(f32)
    near = (shared_ref[0].astype(f32) + far).astype(bf16)
    joint = jnp.concatenate([own_ref[0], near], 0)
    joint_ref[...] = joint
    part = dot_nt(joint, w_ref[0])
    sums_ref[...] = jnp.broadcast_to(col_sum(joint.astype(f32)), sums_ref.shape)

    @pl.when(j == 0)
    def _():
        acc_ref[...] = part + attn_ref[...].astype(f32)

    @pl.when(j > 0)
    def _():
        acc_ref[...] += part

    @pl.when(j == pl.num_programs(0) - 1)
    def _():
        h_ref[...] = acc_ref[...].astype(bf16)


def joint_bwd(ids, own, shared, arrived, w_qkv, g_attn, layer):
    _, length, width = own.shape
    half = shared.shape[1]
    tokens = length + half
    full = lambda *shape: spec(shape, *([0] * len(shape)))
    return call(
        joint_bwd_kernel, "projections_backward", (3,), ids,
        [
            spec((1, length, width), step, 0, 0), spec((1, half, width), step, 0, 0),
            spec((1, half, width), lambda i, ids: jnp.maximum(i - 1, 0), 0, 0),
            spec((1, width, width), layer, 0, step), full(tokens, width),
        ],
        [own, shared, arrived, w_qkv, g_attn],
        [spec((tokens, width), 0, step), full(tokens, width), spec((8, width), 0, step)],
        [
            shape_of((tokens, 3 * width), bf16), shape_of((tokens, width), bf16),
            shape_of((8, 3 * width), f32),
        ],
        [pltpu.VMEM((tokens, width), f32)],
    )


def slab_place(ids, slab):
    relative = jnp.bitwise_xor(ids[2], slab)
    return (
        jnp.bitwise_or(
            jnp.left_shift(jnp.bitwise_and(relative, 1), 2),
            jnp.bitwise_or(jnp.bitwise_and(relative, 2), jnp.right_shift(relative, 2)),
        )
    )


def store_piece(ids, keep_ref, send_ref, slab, core_rows, row, value):
    place = slab_place(ids, slab)
    core = ids[0]
    low, high = value[0:core_rows], value[core_rows:]
    at = slice(row, row + core_rows)

    @pl.when(core == 0)
    def _():
        keep_ref[place, at, :], send_ref[place, at, :] = low, high

    @pl.when(core != 0)
    def _():
        keep_ref[place, at, :], send_ref[place, at, :] = high, low


def feed_weights_kernel(ids, act_ref, feed_ref, mixed_ref, pre_ref, keep_ref, send_ref, feed_t, mixed_t):
    i = pl.program_id(0)

    @pl.when(i == 0)
    def _():
        feed_t[...] = feed_ref[...].T
        mixed_t[...] = mixed_ref[...].T

    slabs = act_ref.shape[1] // LANES
    out_steps = SUPER // slabs

    for s in range(out_steps):
        @pl.when(i == s)
        def _():
            result = dot(feed_t[...], act_ref[...]).astype(bf16)
            for k in range(slabs):
                store_piece(ids, keep_ref, send_ref, s * slabs + k, LANES // 2, 0,
                            result[:, LANES * k : LANES * k + LANES])

    groups = pre_ref.shape[1] // LANES
    rows = mixed_t.shape[0] // SUPER
    for s in range(4 // groups):
        @pl.when(i == out_steps + s)
        def _():
            result = dot(mixed_t[...], pre_ref[...]).astype(bf16)
            for slab in range(SUPER):
                for k in range(groups):
                    store_piece(
                        ids, keep_ref, send_ref, slab, rows // 2,
                        LANES // 2 + (s * groups + k) * (rows // 2),
                        result[rows * slab : rows * slab + rows, LANES * k : LANES * k + LANES],
                    )


def feed_weights(ids, act, g_feed, mixed, g_pre):
    tokens, width = mixed.shape
    block = 2 * LANES
    piece = (SUPER, LANES, LANES)
    full = lambda *shape: spec(shape, *([0] * len(shape)))
    return call(
        feed_weights_kernel, "feed_weights", (6,), ids,
        [
            spec((tokens, block), 0, lambda i, ids: jnp.minimum(i, 3)),
            spec((tokens, LANES), 0, lambda i, ids: ids[1]),
            full(tokens, width),
            spec((tokens, block), 0, lambda i, ids: 2 * ids[1] + jnp.maximum(i - 4, 0)),
        ],
        [act, g_feed, mixed, g_pre],
        [full(*piece), full(*piece)], [shape_of(piece, bf16), shape_of(piece, bf16)],
        [pltpu.VMEM((LANES, tokens), bf16), pltpu.VMEM((width, tokens), bf16)],
    )


def attention_weights_kernel(
    ids, x0, x1, x2, joint_ref, own_ref, shared_ref, attn_ref, rel0_ref, rel1_ref, small_ref,
    keep_ref, send_ref,
):
    x_t = jnp.concatenate([x0[0].T, x1[0].T, x2[0].T], 1)
    width = x_t.shape[0]
    rows = width // SUPER
    half = rows // 2
    groups = joint_ref.shape[1] // LANES
    for g in range(groups):
        result = dot(x_t, joint_ref[:, LANES * g : LANES * g + LANES]).astype(bf16)
        for slab in range(SUPER):
            store_piece(ids, keep_ref, send_ref, slab, half, g * half,
                        result[rows * slab : rows * slab + rows])
    long = own_ref.shape[1]
    result = dot(own_ref[...], attn_ref[0:long]) + dot(shared_ref[...], attn_ref[long:])
    result = result.astype(bf16)
    for slab in range(SUPER):
        store_piece(ids, keep_ref, send_ref, slab, half, groups * half,
                    result[rows * slab : rows * slab + rows])
    rel = (rel0_ref[...] + rel1_ref[...]).astype(bf16)
    count = rel.shape[0] // SUPER
    for slab in range(SUPER):
        both = jnp.concatenate([rel[count * slab : count * slab + count], small_ref[slab]], 0)
        store_piece(ids, keep_ref, send_ref, slab, count, (groups + 1) * half, both)


def attention_weights(ids, x, gathered, g_joint, ctx_own, ctx_shared, g_attn, rel0, rel1, small):
    half, width = x.shape[1], x.shape[2]
    tokens = 3 * half
    rows = (width // SUPER // 2) * 4 + rel0.shape[0] // SUPER
    piece = (SUPER, rows, LANES)
    side = lambda i, ids: ids[1]
    full = lambda *shape: spec(shape, *([0] * len(shape)))
    return call(
        attention_weights_kernel, "attention_weights", (1,), ids,
        row_tiles(half, width, gathered)
        + [
            spec((tokens, 3 * LANES), 0, side), full(*ctx_own.shape), full(*ctx_shared.shape),
            spec((tokens, LANES), 0, side), spec((rel0.shape[0], LANES), 0, side),
            spec((rel0.shape[0], LANES), 0, side), full(*small.shape),
        ],
        [x, x, x, g_joint, ctx_own, ctx_shared, g_attn, rel0, rel1, small],
        [full(*piece), full(*piece)], [shape_of(piece, bf16), shape_of(piece, bf16)],
    )


def place_rows_kernel(ids, own_ref, other_ref, out_ref):
    i = pl.program_id(0)
    core = ids[0]
    row = i // 2
    mine = jnp.where(row == 2, (i - 4) == core, row == core)

    @pl.when(mine)
    def _():
        out_ref[0] = own_ref[0].astype(out_ref.dtype)

    @pl.when(jnp.logical_not(mine))
    def _():
        out_ref[0] = other_ref[0].astype(out_ref.dtype)


def place_rows(ids, own, other, dtype):
    tokens, width = own.shape
    half = tokens // 3
    tile = lambda i, ids: jnp.where(i < 4, i % 2, 2)
    tiles = lambda x: x.reshape(3, half, width)
    return call(
        place_rows_kernel, "place_rows", (6,), ids,
        [spec((1, half, width), tile, 0, 0)] * 2, [tiles(own), tiles(other)],
        spec((1, half, width), step, 0, 0), shape_of((6, half, width), dtype),
    )


def body(
    stream, cotangent, segments, word_boxes, valid_mask, w_qkv, qv_bias, w_out, out_bias, rel_proj,
    ln_scale, ln_shift, ffn_in, ffn_in_bias, ffn_out, ffn_out_bias,
):
    sections = lax.axis_size("section")
    dp = lax.axis_size("dp")
    section = lax.axis_index("section")
    dp_index = lax.axis_index("dp")
    core, side = section % 2, section // 2
    rows, length, width = stream.shape
    layers = w_qkv.shape[0]
    ff = ffn_in.shape[2]
    half = length // 2
    assert rows == 3 and sections == 4 and layers == 2 and dp % SUPER == 0 and width == 2 * LANES
    fine = dp // SUPER
    ids = jnp.stack([core, side, dp_index // fine]).astype(jnp.int32)
    weights = (w_out, out_bias, ln_scale, ln_shift, ffn_in, ffn_in_bias, ffn_out, ffn_out_bias)
    rel_pairs = rel_proj.reshape(layers, width // 128, 128, 128)

    def flip(x, bit):
        return lax.ppermute(x, "section", [(i, i ^ bit) for i in range(sections)])

    def flip_dp(x, bit):
        return lax.ppermute(x, "dp", [(i, i ^ bit) for i in range(dp)])

    tables = make_tables(ids, word_boxes, segments, valid_mask)
    ctab, stab, valid_col = tables[3], tables[4], tables[7]

    halves = lambda x: x.reshape(-1, half, width)
    x, gathered = halves(stream), True
    kept = []
    for l in range(layers):
        joint, turned, kv = project(ids, x, gathered, w_qkv, qv_bias, rel_pairs, ctab, stab, l)
        kv_far = flip(kv, 1)
        ctx_own, lse_own = attention_fwd(ids, False, tables, joint, turned, None)
        ctx_shared, lse_shared = attention_fwd(ids, True, tables, joint, turned, kv_far)
        n1, r1, n2, r2, mixed, act, slope, out, squares = feed_fwd(
            ids, x, gathered, ctx_own, ctx_shared, valid_col, weights, l
        )
        kept.append(
            dict(x=x, gathered=gathered, joint=joint, turned=turned, kv_far=kv_far, ctx_own=ctx_own,
                 ctx_shared=ctx_shared, lse_own=lse_own, lse_shared=lse_shared, norms=(n1, r1, n2, r2),
                 mixed=mixed, act=act, slope=slope, out=out, squares=squares)
        )
        x, gathered = halves(out), False

    def reduce_start(keep, send):
        return keep + flip(send, 1)

    def reduce_rest(x):
        for bit in range(3):
            n = x.shape[0] // 2
            x = x[:n] + flip_dp(x[n:], fine << bit)
        x = x[0]
        bit = 1
        while bit < fine:
            x = x + flip_dp(x, bit)
            bit *= 2
        return x

    grad, gathered = halves(cotangent), True
    sums = {}
    for l in reversed(range(layers)):
        k = kept[l]
        g_feed, g_pre, g_mixed, g_attn, g_ctx, vec, pre_sum = feed_bwd(
            ids, grad, gathered, k["norms"], k["slope"], weights, l
        )
        keep, send = feed_weights(ids, k["act"], g_feed, k["mixed"], g_pre)
        sums[l, "feed"] = reduce_rest(reduce_start(keep, send))
        shared_keep, shared_send, rel_shared = attention_bwd(
            ids, True, tables, k["joint"], k["turned"], k["kv_far"], k["lse_shared"], g_ctx, rel_pairs, l
        )
        arrived = flip(shared_send, 1)
        own_grads, rel_own = attention_bwd(
            ids, False, tables, k["joint"], k["turned"], None, k["lse_own"], g_ctx, rel_pairs, l
        )
        g_joint, g_h, joint_sum = joint_bwd(ids, own_grads, shared_keep, arrived, w_qkv, g_attn, l)
        vectors = jnp.concatenate([vec, joint_sum[0:1, :width], joint_sum[0:1, 2 * width :]], 0)
        order = [8, 9, 4, 0, 1, 2, 3, 5]
        lines = jnp.stack([vectors[i] for i in order]).reshape(8, SUPER, width // SUPER)
        lines = jnp.pad(jnp.transpose(lines, (1, 0, 2)), ((0, 0), (0, 0), (0, LANES - width // SUPER)))
        lines = jnp.concatenate([lines, pre_sum[0].reshape(SUPER, 1, ff // SUPER)], 1)
        small = jnp.pad(lines, ((0, 0), (0, 16 - 9), (0, 0))).astype(bf16)
        keep, send = attention_weights(
            ids, k["x"], k["gathered"], g_joint, k["ctx_own"], k["ctx_shared"], g_attn, rel_own,
            rel_shared, small,
        )
        sums[l, "attention"] = reduce_rest(reduce_start(keep, send))
        k["g_mixed"], k["g_h"] = g_mixed, g_h
        grad, gathered = halves(g_h), False

    def of_layer(name):
        return jnp.where(side == 0, kept[0][name], kept[1][name])

    def to_section(first, second, dtype):
        a, b = of_layer(first), of_layer(second)
        own, away = jnp.where(core == 0, a, b), jnp.where(core == 0, b, a)
        return place_rows(ids, own, flip(away, 1), dtype).reshape(1, rows, length, width)

    section_outs = to_section("mixed", "out", bf16)
    in_grads = to_section("g_h", "g_mixed", f32)

    squares_mine = jnp.sum(of_layer("squares"), 1).reshape(2, 2, 2)
    squares_far = flip(squares_mine, 1)
    sub = lambda v: lax.dynamic_index_in_dim(v, core, 0, keepdims=False)
    near, far = sub(squares_mine), sub(squares_far)
    first = jnp.where(core == 0, near[:, 0], far[:, 0])
    second = jnp.where(core == 0, far[:, 0], near[:, 0])
    square_rows = jnp.stack([first, second, near[:, 1] + far[:, 1]])
    row_counts = jnp.sum(valid_mask.astype(f32), 1)
    root_mean_squares = jnp.sqrt(square_rows / (width * jnp.maximum(row_counts, 1.0))[:, None])[None]

    fine_at = dp_index % fine
    core_rows = width // SUPER // 2
    found = {}
    for l in range(layers):
        piece = jnp.concatenate([sums[l, "feed"], sums[l, "attention"]], 0)
        far = flip(piece, 2)
        sides = [jnp.where(side == 0, piece, far), jnp.where(side == 0, far, piece)]
        both = jnp.stack(sides)
        other = flip(both, 1)
        found[l] = jnp.where(core == 0, jnp.stack([both, other]), jnp.stack([other, both])).astype(f32)

    def fine_part(x, axis):
        n = x.shape[axis] // fine
        return x if fine == 1 else lax.dynamic_slice_in_dim(x, fine_at * n, n, axis)

    def gather(l):
        x = found[l]
        ffn_out_t = x[:, :, : LANES // 2]
        d_ffn_out = jnp.transpose(ffn_out_t, (3, 1, 0, 2)).reshape(LANES, width)
        at = LANES // 2

        def columns(at, groups):
            part = x[:, :, at : at + groups * core_rows].reshape(2, 2, groups, core_rows, LANES)
            part = jnp.transpose(part, (0, 3, 1, 2, 4))
            return part.reshape(2 * core_rows, 2 * groups * LANES)

        d_ffn_in = columns(at, 4)
        at += 4 * core_rows
        d_qkv = columns(at, 3)
        at += 3 * core_rows
        d_out = columns(at, 1)
        at += core_rows
        rel = jnp.concatenate([x[0, 0, at:], x[0, 1, at:]], 1)
        small = x[1, 0, at:]
        return (
            fine_part(d_qkv, 0), small, fine_part(d_out, 0),
            fine_part(rel.T, 1).reshape(width // 64, 64, -1), fine_part(d_ffn_in, 0),
            fine_part(d_ffn_out, 0),
        )

    parts = [gather(l) for l in range(layers)]
    stacked = [jnp.stack(pair) for pair in zip(*parts)]
    d_qkv, small, d_out, d_rel, d_ffn_in, d_ffn_out = stacked
    vector = lambda i: fine_part(small[:, i, : width // SUPER], 1)
    return (
        section_outs,
        in_grads,
        d_qkv,
        jnp.stack([vector(0), vector(1)], 1),
        d_out,
        vector(2),
        d_rel,
        jnp.stack([vector(3), vector(4)], 1),
        jnp.stack([vector(5), vector(6)], 1),
        d_ffn_in,
        fine_part(small[:, 8], 1),
        d_ffn_out,
        vector(7),
        root_mean_squares,
    )


def solution(mesh):
    return jax.shard_map(
        body,
        mesh=mesh,
        in_specs=(
            P("dp", None, None),
            P("dp", None, None),
            P("dp", None),
            P(None, "dp", None),
            P("dp", None),
        )
        + (P(),) * 11,
        out_specs=(
            P("section", "dp", None, None),
            P("section", "dp", None, None),
            P(None, "dp", None),
            P(None, None, "dp"),
            P(None, "dp", None),
            P(None, "dp"),
            P(None, None, None, "dp"),
            P(None, None, "dp"),
            P(None, None, "dp"),
            P(None, "dp", None),
            P(None, "dp"),
            P(None, "dp", None),
            P(None, "dp"),
            P("section", "dp", None),
        ),
        check_vma=False,
    )
```

time: 693 us -> 478 us (0.69)
  Pallas kernels: 95.3 us -> 287 us
  matrix products: 143 us -> 0 us
  other arithmetic: 153 us -> 27.5 us
  local copies, waits for them, and re-layouts: 130 us -> 31.8 us
  starting transfers between devices: 69.3 us -> 25 us
  waiting for transfers between devices: 90.3 us -> 98.2 us
    pallas_call x8 -> x23, Pallas kernels: 95.3 us -> 287 us  [call(): pl.pallas_call(kernel, grid_spec=pltpu.PrefetchScalarGridSpec(num_scalar_...]
    dot_general x24 -> x0, matrix products: 143 us -> none  [the longest x8 75.9 us: dot_nt(): lax.dot_general(a, b, (((1,), (1,)), ((), ())), preferred_element_type=f32)]
    concatenate x19 -> x4, other arithmetic: 44.9 us -> 0.13 us  [the longest x2 0.1 us: body(): piece = jnp.concatenate([sums[l, 'feed'], sums[l, 'attention']], 0)]
    reduce_sum x41 -> x1, other arithmetic: 40.5 us -> 0.12 us  [body(): squares_mine = jnp.sum(of_layer('squares'), 1).reshape(2, 2, 2)]
    unnamed x501 -> x61, local copies, waits for them, and re-layouts: 48.4 us -> 11.2 us
    slice x46 -> x23, local copies, waits for them, and re-layouts: 34.3 us -> 4.5 us  [the longest x2 1.99 us: columns(): x[:, :, at:at + groups * core_rows].reshape(2, 2, groups, core_rows, LANES)]
    ppermute x30 -> x12, starting transfers between devices: 48.3 us -> 18.8 us  [flip_dp(): return lax.ppermute(x, 'dp', [(i, i ^ bit) for i in range(dp)])]
    squeeze x40 -> x4, local copies, waits for them, and re-layouts: 18.5 us -> 1.25 us  [the longest x2 1.24 us: gather(): rel = jnp.concatenate([x[0, 0, at:], x[0, 1, at:]], 1)]
  transfers between devices with their start and end apart: 71 -> 27, of which waited for: 32 -> 8; matrix products, arithmetic and copies ran while one was open for 43% -> 5% of each run, Pallas kernels for 11% -> 34%
where the time goes in v2:
time: 478 us; the launch traced here: 471 us
  Pallas kernels  287 us (60%)
  waiting for transfers between devices  98.2 us (21%)
  local copies, waits for them, and re-layouts  31.8 us (7%)
  other arithmetic  27.5 us (6%)
  starting transfers between devices  25 us (5%)
    pallas_call x23, Pallas kernels, call(): pl.pallas_call(kernel, grid_spec=pltpu.PrefetchScalarGridSpec(num_scalar_...  287 us
    ppermute x12, waiting for transfers between devices, flip_dp(): return lax.ppermute(x, 'dp', [(i, i ^ bit) for i in range(dp)])  90.1 us
    ppermute x12, starting transfers between devices, flip_dp(): return lax.ppermute(x, 'dp', [(i, i ^ bit) for i in range(dp)])  18.8 us
    unnamed x61, local copies, waits for them, and re-layouts  11.2 us
  transfers between devices with their start and end apart: 27, of which 8 were waited for; matrix products, arithmetic and copies ran while one was open for 5% of the time, Pallas kernels for 34%

profile of v2, /device:TPU:0, one launch (start us, length us, event | category | flops | bytes accessed | tf_op | source)
XLA Modules:
  0.0 471.3 jit_solution(4733950969067860544)
XLA Ops:
  2.6 4.2 tables.1
  6.8 9.9 %projections.2 = (bf16[768,2304]{1,0:T(8,128)(2,1)}, bf16[768,1536]{1,0:T(8,128)(2,1)}, bf16[256,1536]{1,0:T(8,128)(2,1)}) custom-call(s32[3]{0:T(128)} %pad_add_fusion.ids, bf16[6,256,768]{2,1,0:T(8,128)(2,1)} %bitcast.108, bf16[6,256,768]{2,1,0:T(8,128)(2,1)} %bitcast.109, bf16[6,256,768]{2,1,0:T(8,128)(2,1)} %bitcast.110, bf16[2,768,2304]{2,1,0:T(8,128)(2,1)} %w_ref.7, ...), custom_call_target="tpu_custom_call" | custom-call | tf_op jit(solution)/shard_map/projections/pallas_call | solution.py:63
  17.3 8.6 %attention_forward.4 = (bf16[768,512]{1,0:T(8,128)(2,1)}, f32[3,4,512]{2,1,0:T(4,128)}) custom-call(s32[3]{0:T(128)} %pad_add_fusion.ids, f32[1024,128]{1,0:T(8,128)} %get-tuple-element.92.code_ref, f32[8,1024]{1,0:T(8,128)} %get-tuple-element.93.seg_ref, bf16[1024,128]{1,0:T(8,128)(2,1)} %get-tuple-element.94.kf_ref, ...), custom_call_target="tpu_custom_call" | custom-call | tf_op jit(solution)/shard_map/attention_forward/pallas_call | solution.py:63
  26.8 6.3 %attention_forward.5 = (bf16[768,256]{1,0:T(8,128)(2,1)}, f32[3,4,256]{2,1,0:T(4,128)}) custom-call(s32[3]{0:T(128)} %pad_add_fusion.ids, f32[1024,128]{1,0:T(8,128)} %get-tuple-element.92.code_ref, f32[8,1024]{1,0:T(8,128)} %get-tuple-element.93.seg_ref, bf16[1024,128]{1,0:T(8,128)(2,1)} %get-tuple-element.94.kf_ref, ...), custom_call_target="tpu_custom_call" | custom-call | tf_op jit(solution)/shard_map/attention_forward/pallas_call | solution.py:63
  33.1 28.1 %feed_forward.2 = (bf16[768,768]{1,0:T(8,128)(2,1)}, f32[768,128]{1,0:T(8,128)}, bf16[768,768]{1,0:T(8,128)(2,1)}, f32[768,128]{1,0:T(8,128)}, bf16[768,768]{1,0...) custom-call(s32[3]{0:T(128)} %pad_add_fusion.ids, ...), custom_call_target="tpu_custom_call" | custom-call | tf_op jit(solution)/shard_map/feed_forward/pallas_call | solution.py:63
  61.2 9.9 %projections.3 = (bf16[768,2304]{1,0:T(8,128)(2,1)}, bf16[768,1536]{1,0:T(8,128)(2,1)}, bf16[256,1536]{1,0:T(8,128)(2,1)}) custom-call(s32[3]{0:T(128)} %pad_add_fusion.ids, bf16[3,256,768]{2,1,0:T(8,128)(2,1)} %bitcast.117, bf16[3,256,768]{2,1,0:T(8,128)(2,1)} %bitcast.118, bf16[3,256,768]{2,1,0:T(8,128)(2,1)} %bitcast.119, bf16[2,768,2304]{2,1,0:T(8,128)(2,1)} %w_ref.7, ...), custom_call_target="tpu_custom_call" | custom-call | tf_op jit(solution)/shard_map/projections/pallas_call | solution.py:63
  71.1 8.7 %attention_forward.6 = (bf16[768,512]{1,0:T(8,128)(2,1)}, f32[3,4,512]{2,1,0:T(4,128)}) custom-call(s32[3]{0:T(128)} %pad_add_fusion.ids, f32[1024,128]{1,0:T(8,128)} %get-tuple-element.92.code_ref, f32[8,1024]{1,0:T(8,128)} %get-tuple-element.93.seg_ref, bf16[1024,128]{1,0:T(8,128)(2,1)} %get-tuple-element.94.kf_ref, ...), custom_call_target="tpu_custom_call" | custom-call | tf_op jit(solution)/shard_map/attention_forward/pallas_call | solution.py:63
  80.7 6.3 %attention_forward.7 = (bf16[768,256]{1,0:T(8,128)(2,1)}, f32[3,4,256]{2,1,0:T(4,128)}) custom-call(s32[3]{0:T(128)} %pad_add_fusion.ids, f32[1024,128]{1,0:T(8,128)} %get-tuple-element.92.code_ref, f32[8,1024]{1,0:T(8,128)} %get-tuple-element.93.seg_ref, bf16[1024,128]{1,0:T(8,128)(2,1)} %get-tuple-element.94.kf_ref, ...), custom_call_target="tpu_custom_call" | custom-call | tf_op jit(solution)/shard_map/attention_forward/pallas_call | solution.py:63
  87.0 27.5 %feed_forward.3 = (bf16[768,768]{1,0:T(8,128)(2,1)}, f32[768,128]{1,0:T(8,128)}, bf16[768,768]{1,0:T(8,128)(2,1)}, f32[768,128]{1,0:T(8,128)}, bf16[768,768]{1,0...) custom-call(s32[3]{0:T(128)} %pad_add_fusion.ids, ...), custom_call_target="tpu_custom_call" | custom-call | tf_op jit(solution)/shard_map/feed_forward/pallas_call | solution.py:63
  114.6 25.1 %feed_backward.2 = (bf16[768,768]{1,0:T(8,128)(2,1)}, bf16[768,3072]{1,0:T(8,128)(2,1)}, bf16[768,768]{1,0:T(8,128)(2,1)}, bf16[768,768]{1,0:T(8,128)(2,1)}, bf1...) custom-call(s32[3]{0:T(128)} %pad_add_fusion.ids, bf16[6,256,768]{2,1,0:T(8,128)(2,1)} %bitcast.126, ...), custom_call_target="tpu_custom_call" | custom-call | tf_op jit(solution)/shard_map/feed_backward/pallas_call | solution.py:63
  139.6 11.1 %attention_backward.5 = (bf16[3,256,768]{2,1,0:T(8,128)(2,1)}, bf16[2,256,768]{2,1,0:T(8,128)(2,1)}, f32[128,768]{1,0:T(8,128)}) custom-call(s32[3]{0:T(128)} %pad_add_fusion.ids, f32[1024,128]{1,0:T(8,128)} %get-tuple-element.92.code_ref, f32[8,1024]{1,0:T(8,128)} %get-tuple-element.93.seg_ref, bf16[1024,128]{1,0:T(8,128)(2,1)} %get-tuple-element.94.kf_ref, ...), custom_call_target="tpu_custom_call" | custom-call | tf_op jit(solution)/shard_map/attention_backward/pallas_call | solution.py:63
  151.4 12.0 %feed_weights.3 = (bf16[8,384,384]{2,1,0:T(8,128)(2,1)}, bf16[8,384,384]{2,1,0:T(8,128)(2,1)}) custom-call(s32[3]{0:T(128)} %pad_add_fusion.ids, bf16[768,3072]{1,0:T(8,128)(2,1)} %get-tuple-element.155.act_ref, bf16[768,768]{1,0:T(8,128)(2,1)} %get-tuple-element.156.feed_ref, bf16[768,768]{1,0:T(8,128)(2,1)} %get-tuple-element.110.mixed_ref, ...), custom_call_target="tpu_custom_call" | custom-call | tf_op jit(solution)/shard_map/feed_weights/pallas_call | solution.py:63
  163.5 16.3 %attention_backward.4 = (bf16[3,512,768]{2,1,0:T(8,128)(2,1)}, f32[128,768]{1,0:T(8,128)}) custom-call(s32[3]{0:T(128)} %pad_add_fusion.ids, f32[1024,128]{1,0:T(8,128)} %get-tuple-element.92.code_ref, f32[8,1024]{1,0:T(8,128)} %get-tuple-element.93.seg_ref, bf16[1024,128]{1,0:T(8,128)(2,1)} %get-tuple-element.94.kf_ref, ...), custom_call_target="tpu_custom_call" | custom-call | tf_op jit(solution)/shard_map/attention_backward/pallas_call | solution.py:63
  181.6 9.7 %projections_backward.2 = (bf16[768,2304]{1,0:T(8,128)(2,1)}, bf16[768,768]{1,0:T(8,128)(2,1)}, f32[8,2304]{1,0:T(8,128)}) custom-call(s32[3]{0:T(128)} %pad_add_fusion.ids, bf16[3,512,768]{2,1,0:T(8,128)(2,1)} %get-tuple-element.122.own_ref, bf16[3,256,768]{2,1,0:T(8,128)(2,1)} %get-tuple-element.124.shared_ref, bf16[2,256,768]{2,1,0:T(8,128)(2,1)} %copy-done.21, ...), custom_call_target="tpu_custom_call" | custom-call | tf_op jit(solution)/shard_map/projections_backward/pallas_call | solution.py:63
  192.2 25.0 %feed_backward.3 = (bf16[768,768]{1,0:T(8,128)(2,1)}, bf16[768,3072]{1,0:T(8,128)(2,1)}, bf16[768,768]{1,0:T(8,128)(2,1)}, bf16[768,768]{1,0:T(8,128)(2,1)}, bf1...) custom-call(s32[3]{0:T(128)} %pad_add_fusion.ids, bf16[3,256,768]{2,1,0:T(8,128)(2,1)} %bitcast.129, ...), custom_call_target="tpu_custom_call" | custom-call | tf_op jit(solution)/shard_map/feed_backward/pallas_call | solution.py:63
  217.2 11.6 %feed_weights.2 = (bf16[8,384,384]{2,1,0:T(8,128)(2,1)}, bf16[8,384,384]{2,1,0:T(8,128)(2,1)}) custom-call(s32[3]{0:T(128)} %pad_add_fusion.ids, bf16[768,3072]{1,0:T(8,128)(2,1)} %get-tuple-element.142.act_ref, bf16[768,768]{1,0:T(8,128)(2,1)} %get-tuple-element.143.feed_ref, bf16[768,768]{1,0:T(8,128)(2,1)} %get-tuple-element.103.mixed_ref, ...), custom_call_target="tpu_custom_call" | custom-call | tf_op jit(solution)/shard_map/feed_weights/pallas_call | solution.py:63
  229.3 11.4 %attention_backward.7 = (bf16[3,256,768]{2,1,0:T(8,128)(2,1)}, bf16[2,256,768]{2,1,0:T(8,128)(2,1)}, f32[128,768]{1,0:T(8,128)}) custom-call(s32[3]{0:T(128)} %pad_add_fusion.ids, f32[1024,128]{1,0:T(8,128)} %get-tuple-element.92.code_ref, f32[8,1024]{1,0:T(8,128)} %get-tuple-element.93.seg_ref, bf16[1024,128]{1,0:T(8,128)(2,1)} %get-tuple-element.94.kf_ref, ...), custom_call_target="tpu_custom_call" | custom-call | tf_op jit(solution)/shard_map/attention_backward/pallas_call | solution.py:63
  241.6 8.4 %attention_weights.3 = (bf16[8,208,384]{2,1,0:T(8,128)(2,1)}, bf16[8,208,384]{2,1,0:T(8,128)(2,1)}) custom-call(s32[3]{0:T(128)} %pad_add_fusion.ids, bf16[3,256,768]{2,1,0:T(8,128)(2,1)} %bitcast.123, bf16[3,256,768]{2,1,0:T(8,128)(2,1)} %bitcast.124, bf16[3,256,768]{2,1,0:T(8,128)(2,1)} %bitcast.125, bf16[768,2304]{1,0:T(8,128)(2,1)} %get-tuple-element.160.joint_ref, ...), custom_call_target="tpu_custom_call" | custom-call | tf_op jit(solution)/shard_map/attention_weights/pallas_call | solution.py:63
  250.4 16.4 %attention_backward.6 = (bf16[3,512,768]{2,1,0:T(8,128)(2,1)}, f32[128,768]{1,0:T(8,128)}) custom-call(s32[3]{0:T(128)} %pad_add_fusion.ids, f32[1024,128]{1,0:T(8,128)} %get-tuple-element.92.code_ref, f32[8,1024]{1,0:T(8,128)} %get-tuple-element.93.seg_ref, bf16[1024,128]{1,0:T(8,128)(2,1)} %get-tuple-element.94.kf_ref, ...), custom_call_target="tpu_custom_call" | custom-call | tf_op jit(solution)/shard_map/attention_backward/pallas_call | solution.py:63
  268.7 9.6 %projections_backward.3 = (bf16[768,2304]{1,0:T(8,128)(2,1)}, bf16[768,768]{1,0:T(8,128)(2,1)}, f32[8,2304]{1,0:T(8,128)}) custom-call(s32[3]{0:T(128)} %pad_add_fusion.ids, bf16[3,512,768]{2,1,0:T(8,128)(2,1)} %get-tuple-element.134.own_ref, bf16[3,256,768]{2,1,0:T(8,128)(2,1)} %get-tuple-element.136.shared_ref, bf16[2,256,768]{2,1,0:T(8,128)(2,1)} %copy-done.20, ...), custom_call_target="tpu_custom_call" | custom-call | tf_op jit(solution)/shard_map/projections_backward/pallas_call | solution.py:63
  280.0 8.9 %attention_weights.2 = (bf16[8,208,384]{2,1,0:T(8,128)(2,1)}, bf16[8,208,384]{2,1,0:T(8,128)(2,1)}) custom-call(s32[3]{0:T(128)} %pad_add_fusion.ids, bf16[6,256,768]{2,1,0:T(8,128)(2,1)} %bitcast.114, bf16[6,256,768]{2,1,0:T(8,128)(2,1)} %bitcast.115, bf16[6,256,768]{2,1,0:T(8,128)(2,1)} %bitcast.116, bf16[768,2304]{1,0:T(8,128)(2,1)} %get-tuple-element.147.joint_ref, ...), custom_call_target="tpu_custom_call" | custom-call | tf_op jit(solution)/shard_map/attention_weights/pallas_call | solution.py:63
  288.9 1.6 add.97
  290.6 2.9 collective-permute-start.21
  293.5 3.0 add.93
  296.7 12.0 %collective-permute-done.21 = bf16[4,208,384]{2,1,0:T(8,128)(2,1)S(1)} collective-permute-done((bf16[4,208,384]{2,1,0:T(8,128)(2,1)S(1)}, bf16[4,208,384]{2,1,0:T(8,128)(2,1)S(1)}, u32[]{:S(2)}, u32[]{:S(2)}) %collective-permute-start.21) | collective-permute-done | bytes 639008 | tf_op jit(solution)/shard_map/ppermute | solution.py:828
  308.8 2.2 collective-permute-start.22
  311.0 1.8 add.89
  314.5 2.4 add.85
  319.8 2.6 collective-permute-start.23
  322.5 25.2 %collective-permute-done.11 = bf16[4,208,384]{2,1,0:T(8,128)(2,1)S(1)} collective-permute-done((bf16[4,208,384]{2,1,0:T(8,128)(2,1)S(1)}, bf16[4,208,384]{2,1,0:T(8,128)(2,1)S(1)}, u32[]{:S(2)}, u32[]{:S(2)}) %collective-permute-start.11) | collective-permute-done | bytes 639008 | tf_op jit(solution)/shard_map/ppermute | solution.py:828
  347.8 2.2 collective-permute-start.12
  350.3 22.1 %collective-permute-done.7 = bf16[4,384,384]{2,1,0:T(8,128)(2,1)S(1)} collective-permute-done((bf16[4,384,384]{2,1,0:T(8,128)(2,1)S(1)}, bf16[4,384,384]{2,1,0:T(8,128)(2,1)S(1)}, u32[]{:S(2)}, u32[]{:S(2)}) %collective-permute-start.7) | collective-permute-done | bytes 1179680 | tf_op jit(solution)/shard_map/ppermute | solution.py:828
  372.6 1.9 collective-permute-start.8
  374.5 2.7 collective-permute-start.13
  377.7 14.0 %collective-permute-done.13 = bf16[1,208,384]{2,1,0:T(8,128)(2,1)S(1)} collective-permute-done((bf16[1,208,384]{2,1,0:T(8,128)(2,1)S(1)}, bf16[1,208,384]{2,1,0:T(8,128)(2,1)S(1)}, u32[]{:S(2)}, u32[]{:S(2)}) %collective-permute-start.13) | collective-permute-done | bytes 159776 | tf_op jit(solution)/shard_map/ppermute | solution.py:828
  391.7 5.5 %collective-permute-done.8 = bf16[2,384,384]{2,1,0:T(8,128)(2,1)S(1)} collective-permute-done((bf16[2,384,384]{2,1,0:T(8,128)(2,1)S(1)}, bf16[2,384,384]{2,1,0:T(8,128)(2,1)S(1)}, u32[]{:S(2)}, u32[]{:S(2)}) %collective-permute-start.8) | collective-permute-done | bytes 589856 | tf_op jit(solution)/shard_map/ppermute | solution.py:828
  397.3 1.7 collective-permute-start.9
  399.1 1.6 collective-permute-start.24
  400.7 11.4 %collective-permute-done.9 = bf16[1,384,384]{2,1,0:T(8,128)(2,1)S(1)} collective-permute-done((bf16[1,384,384]{2,1,0:T(8,128)(2,1)S(1)}, bf16[1,384,384]{2,1,0:T(8,128)(2,1)S(1)}, u32[]{:S(2)}, u32[]{:S(2)}) %collective-permute-start.9) | collective-permute-done | bytes 294944 | tf_op jit(solution)/shard_map/ppermute | solution.py:828
  413.4 1.8 broadcast_select_fusion.4
  417.0 6.5 %collective-permute-done.14 = bf16[592,384]{1,0:T(8,128)(2,1)S(1)} collective-permute-done((bf16[592,384]{1,0:T(8,128)(2,1)S(1)}, bf16[592,384]{1,0:T(8,128)(2,1)S(1)}, u32[]{:S(2)}, u32[]{:S(2)}) %collective-permute-start.14) | collective-permute-done | bytes 454688 | tf_op jit(solution)/shard_map/ppermute | solution.py:825
  425.7 1.6 collective-permute-done.26
  428.2 5.7 %place_rows.2 = bf16[6,256,768]{2,1,0:T(8,128)(2,1)} custom-call(s32[3]{0:T(128)} %pad_add_fusion.ids, bf16[3,256,768]{2,1,0:T(8,128)(2,1)} %bitcast.145, bf16[3,256,768]{2,1,0:T(8,128)(2,1)} %bitcast.7.other_ref), custom_call_target="tpu_custom_call" | custom-call | tf_op jit(solution)/shard_map/place_rows/pallas_call | solution.py:63
  434.0 6.6 %place_rows.3 = f32[6,256,768]{2,1,0:T(8,128)} custom-call(s32[3]{0:T(128)} %pad_add_fusion.ids, bf16[3,256,768]{2,1,0:T(8,128)(2,1)} %bitcast.146, bf16[3,256,768]{2,1,0:T(8,128)(2,1)} %bitcast.12.other_ref), custom_call_target="tpu_custom_call" | custom-call | tf_op jit(solution)/shard_map/place_rows/pallas_call | solution.py:63
  440.6 2.7 fusion
  450.8 2.0 copy.50
  460.7 1.6 copy.59
  463.8 1.6 copy.58
  (193 shorter events, 48.2 us)
Async XLA Ops:
  16.7 9.1 %collective-permute-start = (bf16[256,1536]{1,0:T(8,128)(2,1)}, bf16[256,1536]{1,0:T(8,128)(2,1)S(1)}, u32[]{:S(2)}, u32[]{:S(2)}) collective-permute-start(bf16[256,1536]{1,0:T(8,128)(2,1)} %get-tuple-element.100), channel_id=1, source_target_pairs={{0,1},{1,0},{2,3},{3,2},{4,5},{5,4},{6,7},{7,6},{8,9},{9,8},{10,11... | collective-permute-start | bytes 2359304 | tf_op jit(solution)/shard_map/ppermute | solution.py:825
  71.1 8.8 %collective-permute-start.1 = (bf16[256,1536]{1,0:T(8,128)(2,1)}, bf16[256,1536]{1,0:T(8,128)(2,1)S(1)}, u32[]{:S(2)}, u32[]{:S(2)}) collective-permute-start(bf16[256,1536]{1,0:T(8,128)(2,1)} %get-tuple-element.108), channel_id=1, source_target_pairs={{0,1},{1,0},{2,3},{3,2},{4,5},{5,4},{6,7},{7,6},{8,9},{9,8},{10,11... | collective-permute-start | bytes 2359304 | tf_op jit(solution)/shard_map/ppermute | solution.py:825
  150.8 29.9 %collective-permute-start.3 = (bf16[2,256,768]{2,1,0:T(8,128)(2,1)}, bf16[2,256,768]{2,1,0:T(8,128)(2,1)S(1)}, u32[]{:S(2)}, u32[]{:S(2)}) collective-permute-start(bf16[2,256,768]{2,1,0:T(8,128)(2,1)} %get-tuple-element.125), channel_id=1, source_target_pairs={{0,1},{1,0},{2,3},{3,2},{4,5},{5,4},{6,7},{7,6},{8,9},{9,8},{10,11... | collective-permute-start | bytes 2359304 | tf_op jit(solution)/shard_map/ppermute | solution.py:825
  151.4 12.1 %copy-start.27 = (f32[8,768]{1,0:T(8,128)S(1)}, f32[8,768]{1,0:T(8,128)}, u32[]{:S(2)}) copy-start(f32[8,768]{1,0:T(8,128)} %get-tuple-element.164) | copy-start | bytes 73732
  163.4 130.1 %collective-permute-start.16 = (bf16[8,384,384]{2,1,0:T(8,128)(2,1)}, bf16[8,384,384]{2,1,0:T(8,128)(2,1)}, u32[]{:S(2)}, u32[]{:S(2)}) collective-permute-start(bf16[8,384,384]{2,1,0:T(8,128)(2,1)} %get-tuple-element.159), channel_id=1, source_target_pairs={{0,1},{1,0},{2,3},{3,2},{4,5},{5,4},{6,7},{7,6},{8,9},{9,8},{10,11... | collective-permute-start | bytes 7077896 | tf_op jit(solution)/shard_map/ppermute | solution.py:825
  163.5 16.3 %copy-start.22 = (bf16[8,768]{1,0:T(8,128)(2,1)}, bf16[8,768]{1,0:T(8,128)(2,1)S(1)}, u32[]{:S(2)}) copy-start(bf16[8,768]{1,0:T(8,128)(2,1)S(1)} %convert.56) | copy-start | bytes 36868
  228.8 85.7 %collective-permute-start.6 = (bf16[8,384,384]{2,1,0:T(8,128)(2,1)}, bf16[8,384,384]{2,1,0:T(8,128)(2,1)}, u32[]{:S(2)}, u32[]{:S(2)}) collective-permute-start(bf16[8,384,384]{2,1,0:T(8,128)(2,1)} %get-tuple-element.146), channel_id=1, source_target_pairs={{0,1},{1,0},{2,3},{3,2},{4,5},{5,4},{6,7},{7,6},{8,9},{9,8},{10,11... | collective-permute-start | bytes 7077896 | tf_op jit(solution)/shard_map/ppermute | solution.py:825
  229.3 11.5 %slice-start = ((bf16[8,768]{1,0:T(8,128)(2,1)}), bf16[4,768]{1,0:T(4,128)(2,1)S(1)}, s32[]{:S(2)}) async-start(bf16[8,768]{1,0:T(8,128)(2,1)} %copy-done.22), calls=%async_computation | async-start | bytes 12288 | tf_op jit(solution)/shard_map/slice | solution.py:884
  240.7 27.1 %collective-permute-start.4 = (bf16[2,256,768]{2,1,0:T(8,128)(2,1)}, bf16[2,256,768]{2,1,0:T(8,128)(2,1)S(1)}, u32[]{:S(2)}, u32[]{:S(2)}) collective-permute-start(bf16[2,256,768]{2,1,0:T(8,128)(2,1)} %get-tuple-element.137), channel_id=1, source_target_pairs={{0,1},{1,0},{2,3},{3,2},{4,5},{5,4},{6,7},{7,6},{8,9},{9,8},{10,11... | collective-permute-start | bytes 2359304 | tf_op jit(solution)/shard_map/ppermute | solution.py:825
  250.0 39.0 %collective-permute-start.20 = (bf16[8,208,384]{2,1,0:T(8,128)(2,1)}, bf16[8,208,384]{2,1,0:T(8,128)(2,1)}, u32[]{:S(2)}, u32[]{:S(2)}) collective-permute-start(bf16[8,208,384]{2,1,0:T(8,128)(2,1)} %get-tuple-element.167), channel_id=1, source_target_pairs={{0,1},{1,0},{2,3},{3,2},{4,5},{5,4},{6,7},{7,6},{8,9},{9,8},{10,11... | collective-permute-start | bytes 3833864 | tf_op jit(solution)/shard_map/ppermute | solution.py:825
  250.4 16.4 %copy-start.26 = (f32[8,768]{1,0:T(8,128)S(1)}, f32[8,768]{1,0:T(8,128)}, u32[]{:S(2)}) copy-start(f32[8,768]{1,0:T(8,128)} %get-tuple-element.151) | copy-start | bytes 73732
  280.0 8.9 %copy-start.10 = (bf16[8,208,384]{2,1,0:T(8,128)(2,1)S(1)}, bf16[8,208,384]{2,1,0:T(8,128)(2,1)}, u32[]{:S(2)}) copy-start(bf16[8,208,384]{2,1,0:T(8,128)(2,1)} %get-tuple-element.166) | copy-start | bytes 3833860
  288.9 22.1 %collective-permute-start.10 = (bf16[8,208,384]{2,1,0:T(8,128)(2,1)}, bf16[8,208,384]{2,1,0:T(8,128)(2,1)}, u32[]{:S(2)}, u32[]{:S(2)}) collective-permute-start(bf16[8,208,384]{2,1,0:T(8,128)(2,1)} %get-tuple-element.154), channel_id=1, source_target_pairs={{0,1},{1,0},{2,3},{3,2},{4,5},{5,4},{6,7},{7,6},{8,9},{9,8},{10,11... | collective-permute-start | bytes 3833864 | tf_op jit(solution)/shard_map/ppermute | solution.py:825
  290.6 18.1 %collective-permute-start.21 = (bf16[4,208,384]{2,1,0:T(8,128)(2,1)S(1)}, bf16[4,208,384]{2,1,0:T(8,128)(2,1)S(1)}, u32[]{:S(2)}, u32[]{:S(2)}) collective-permute-start(bf16[4,208,384]{2,1,0:T(8,128)(2,1)S(1)} %slice.291), channel_id=1, source_target_pairs={{0,4},{4,0},{8,12},{12,8},{16,20},{20,16},{24,28},{28,24},{1,5},{5... | collective-permute-start | bytes 1916936 | tf_op jit(solution)/shard_map/ppermute | solution.py:828
  296.6 14.4 %copy-start.11 = (bf16[8,208,384]{2,1,0:T(8,128)(2,1)S(1)}, bf16[8,208,384]{2,1,0:T(8,128)(2,1)}, u32[]{:S(2)}) copy-start(bf16[8,208,384]{2,1,0:T(8,128)(2,1)} %get-tuple-element.153) | copy-start | bytes 3833860
  296.6 53.4 %collective-permute-start.17 = (bf16[4,384,384]{2,1,0:T(8,128)(2,1)S(1)}, bf16[4,384,384]{2,1,0:T(8,128)(2,1)S(1)}, u32[]{:S(2)}, u32[]{:S(2)}) collective-permute-start(bf16[4,384,384]{2,1,0:T(8,128)(2,1)S(1)} %slice.279), channel_id=1, source_target_pairs={{0,4},{4,0},{8,12},{12,8},{16,20},{20,16},{24,28},{28,24},{1,5},{5... | collective-permute-start | bytes 3538952 | tf_op jit(solution)/shard_map/ppermute | solution.py:828
  308.8 10.9 %collective-permute-start.22 = (bf16[2,208,384]{2,1,0:T(8,128)(2,1)S(1)}, bf16[2,208,384]{2,1,0:T(8,128)(2,1)S(1)}, u32[]{:S(2)}, u32[]{:S(2)}) collective-permute-start(bf16[2,208,384]{2,1,0:T(8,128)(2,1)S(1)} %slice.293), channel_id=1, source_target_pairs={{0,8},{4,12},{8,0},{12,4},{16,24},{20,28},{24,16},{28,20},{1,9},{5... | collective-permute-start | bytes 958472 | tf_op jit(solution)/shard_map/ppermute | solution.py:828
  311.0 3.4 copy-start.9
  312.9 34.8 %collective-permute-start.11 = (bf16[4,208,384]{2,1,0:T(8,128)(2,1)S(1)}, bf16[4,208,384]{2,1,0:T(8,128)(2,1)S(1)}, u32[]{:S(2)}, u32[]{:S(2)}) collective-permute-start(bf16[4,208,384]{2,1,0:T(8,128)(2,1)S(1)} %slice.272), channel_id=1, source_target_pairs={{0,4},{4,0},{8,12},{12,8},{16,20},{20,16},{24,28},{28,24},{1,5},{5... | collective-permute-start | bytes 1916936 | tf_op jit(solution)/shard_map/ppermute | solution.py:828
  314.5 3.1 copy-start.5
  314.5 3.1 copy-start.18
  316.9 1.6 copy-start.4
  317.0 55.4 %collective-permute-start.7 = (bf16[4,384,384]{2,1,0:T(8,128)(2,1)S(1)}, bf16[4,384,384]{2,1,0:T(8,128)(2,1)S(1)}, u32[]{:S(2)}, u32[]{:S(2)}) collective-permute-start(bf16[4,384,384]{2,1,0:T(8,128)(2,1)S(1)} %slice.260), channel_id=1, source_target_pairs={{0,4},{4,0},{8,12},{12,8},{16,20},{20,16},{24,28},{28,24},{1,5},{5... | collective-permute-start | bytes 3538952 | tf_op jit(solution)/shard_map/ppermute | solution.py:828
  319.8 108.5 %collective-permute-start.2 = (bf16[768,768]{1,0:T(8,128)(2,1)S(1)}, bf16[768,768]{1,0:T(8,128)(2,1)}, u32[]{:S(2)}, u32[]{:S(2)}) collective-permute-start(bf16[768,768]{1,0:T(8,128)(2,1)S(1)} %get-tuple-element.203), channel_id=1, source_target_pairs={{0,1},{1,0},{2,3},{3,2},{4,5},{5,4},{6,7},{7,6},{8,9},{9,8},{10,11... | collective-permute-start | bytes 3538952 | tf_op jit(solution)/shard_map/ppermute | solution.py:825
  319.8 30.4 %collective-permute-start.23 = (bf16[1,208,384]{2,1,0:T(8,128)(2,1)S(1)}, bf16[1,208,384]{2,1,0:T(8,128)(2,1)S(1)}, u32[]{:S(2)}, u32[]{:S(2)}) collective-permute-start(bf16[1,208,384]{2,1,0:T(8,128)(2,1)S(1)} %slice.295), channel_id=1, source_target_pairs={{0,16},{4,20},{8,24},{12,28},{16,0},{20,4},{24,8},{28,12},{1,17},{... | collective-permute-start | bytes 479240 | tf_op jit(solution)/shard_map/ppermute | solution.py:828
  347.8 26.6 %collective-permute-start.12 = (bf16[2,208,384]{2,1,0:T(8,128)(2,1)S(1)}, bf16[2,208,384]{2,1,0:T(8,128)(2,1)S(1)}, u32[]{:S(2)}, u32[]{:S(2)}) collective-permute-start(bf16[2,208,384]{2,1,0:T(8,128)(2,1)S(1)} %slice.274), channel_id=1, source_target_pairs={{0,8},{4,12},{8,0},{12,4},{16,24},{20,28},{24,16},{28,20},{1,9},{5... | collective-permute-start | bytes 958472 | tf_op jit(solution)/shard_map/ppermute | solution.py:828
  350.2 27.0 %collective-permute-start.18 = (bf16[2,384,384]{2,1,0:T(8,128)(2,1)S(1)}, bf16[2,384,384]{2,1,0:T(8,128)(2,1)S(1)}, u32[]{:S(2)}, u32[]{:S(2)}) collective-permute-start(bf16[2,384,384]{2,1,0:T(8,128)(2,1)S(1)} %slice.281), channel_id=1, source_target_pairs={{0,8},{4,12},{8,0},{12,4},{16,24},{20,28},{24,16},{28,20},{1,9},{5... | collective-permute-start | bytes 1769480 | tf_op jit(solution)/shard_map/ppermute | solution.py:828
  372.6 24.6 %collective-permute-start.8 = (bf16[2,384,384]{2,1,0:T(8,128)(2,1)S(1)}, bf16[2,384,384]{2,1,0:T(8,128)(2,1)S(1)}, u32[]{:S(2)}, u32[]{:S(2)}) collective-permute-start(bf16[2,384,384]{2,1,0:T(8,128)(2,1)S(1)} %slice.262), channel_id=1, source_target_pairs={{0,8},{4,12},{8,0},{12,4},{16,24},{20,28},{24,16},{28,20},{1,9},{5... | collective-permute-start | bytes 1769480 | tf_op jit(solution)/shard_map/ppermute | solution.py:828
  374.5 17.1 %collective-permute-start.13 = (bf16[1,208,384]{2,1,0:T(8,128)(2,1)S(1)}, bf16[1,208,384]{2,1,0:T(8,128)(2,1)S(1)}, u32[]{:S(2)}, u32[]{:S(2)}) collective-permute-start(bf16[1,208,384]{2,1,0:T(8,128)(2,1)S(1)} %slice.276), channel_id=1, source_target_pairs={{0,16},{4,20},{8,24},{12,28},{16,0},{20,4},{24,8},{28,12},{1,17},{... | collective-permute-start | bytes 479240 | tf_op jit(solution)/shard_map/ppermute | solution.py:828
  377.3 21.6 %collective-permute-start.19 = (bf16[1,384,384]{2,1,0:T(8,128)(2,1)S(1)}, bf16[1,384,384]{2,1,0:T(8,128)(2,1)S(1)}, u32[]{:S(2)}, u32[]{:S(2)}) collective-permute-start(bf16[1,384,384]{2,1,0:T(8,128)(2,1)S(1)} %slice.283), channel_id=1, source_target_pairs={{0,16},{4,20},{8,24},{12,28},{16,0},{20,4},{24,8},{28,12},{1,17},{... | collective-permute-start | bytes 884744 | tf_op jit(solution)/shard_map/ppermute | solution.py:828
  397.2 16.3 %copy-start.19 = (bf16[768,768]{1,0:T(8,128)(2,1)S(1)}, bf16[768,768]{1,0:T(8,128)(2,1)}, u32[]{:S(2)}) copy-start(bf16[768,768]{1,0:T(8,128)(2,1)} %get-tuple-element.139) | copy-start | bytes 3538948
  397.3 14.8 %collective-permute-start.9 = (bf16[1,384,384]{2,1,0:T(8,128)(2,1)S(1)}, bf16[1,384,384]{2,1,0:T(8,128)(2,1)S(1)}, u32[]{:S(2)}, u32[]{:S(2)}) collective-permute-start(bf16[1,384,384]{2,1,0:T(8,128)(2,1)S(1)} %slice.264), channel_id=1, source_target_pairs={{0,16},{4,20},{8,24},{12,28},{16,0},{20,4},{24,8},{28,12},{1,17},{... | collective-permute-start | bytes 884744 | tf_op jit(solution)/shard_map/ppermute | solution.py:828
  398.9 14.5 %copy-start.17 = (bf16[768,768]{1,0:T(8,128)(2,1)S(1)}, bf16[768,768]{1,0:T(8,128)(2,1)}, u32[]{:S(2)}) copy-start(bf16[768,768]{1,0:T(8,128)(2,1)} %get-tuple-element.140) | copy-start | bytes 3538948
  399.0 14.5 %copy-start.1 = (bf16[768,768]{1,0:T(8,128)(2,1)S(1)}, bf16[768,768]{1,0:T(8,128)(2,1)}, u32[]{:S(2)}) copy-start(bf16[768,768]{1,0:T(8,128)(2,1)} %get-tuple-element.127) | copy-start | bytes 3538948
  399.0 14.5 %copy-start.16 = (bf16[768,768]{1,0:T(8,128)(2,1)S(1)}, bf16[768,768]{1,0:T(8,128)(2,1)}, u32[]{:S(2)}) copy-start(bf16[768,768]{1,0:T(8,128)(2,1)} %get-tuple-element.141) | copy-start | bytes 3538948
  399.1 16.2 %collective-permute-start.24 = (bf16[592,384]{1,0:T(8,128)(2,1)S(1)}, bf16[592,384]{1,0:T(8,128)(2,1)S(1)}, u32[]{:S(2)}, u32[]{:S(2)}) collective-permute-start(bf16[592,384]{1,0:T(8,128)(2,1)S(1)} %pad_maximum_fusion.7), channel_id=1, source_target_pairs={{0,2},{1,3},{2,0},{3,1},{4,6},{5,7},{6,4},{7,5},{8,10},{9,11},{10,... | collective-permute-start | bytes 1363976 | tf_op jit(solution)/shard_map/ppermute | solution.py:825
  412.2 11.4 %collective-permute-start.14 = (bf16[592,384]{1,0:T(8,128)(2,1)S(1)}, bf16[592,384]{1,0:T(8,128)(2,1)S(1)}, u32[]{:S(2)}, u32[]{:S(2)}) collective-permute-start(bf16[592,384]{1,0:T(8,128)(2,1)S(1)} %pad_maximum_fusion.6), channel_id=1, source_target_pairs={{0,2},{1,3},{2,0},{3,1},{4,6},{5,7},{6,4},{7,5},{8,10},{9,11},{10,... | collective-permute-start | bytes 1363976 | tf_op jit(solution)/shard_map/ppermute | solution.py:825
  415.3 18.7 %collective-permute-start.5 = (bf16[768,768]{1,0:T(8,128)(2,1)}, bf16[768,768]{1,0:T(8,128)(2,1)}, u32[]{:S(2)}, u32[]{:S(2)}) collective-permute-start(bf16[768,768]{1,0:T(8,128)(2,1)} %get-tuple-element.201), channel_id=1, source_target_pairs={{0,1},{1,0},{2,3},{3,2},{4,5},{5,4},{6,7},{7,6},{8,9},{9,8},{10,11... | collective-permute-start | bytes 3538952 | tf_op jit(solution)/shard_map/ppermute | solution.py:825
  416.5 24.0 %collective-permute-start.25 = (bf16[2,592,384]{2,1,0:T(8,128)(2,1)}, bf16[2,592,384]{2,1,0:T(8,128)(2,1)}, u32[]{:S(2)}, u32[]{:S(2)}) collective-permute-start(bf16[2,592,384]{2,1,0:T(8,128)(2,1)} %get-tuple-element.220), channel_id=1, source_target_pairs={{0,1},{1,0},{2,3},{3,2},{4,5},{5,4},{6,7},{7,6},{8,9},{9,8},{10,11... | collective-permute-start | bytes 2727944 | tf_op jit(solution)/shard_map/ppermute | solution.py:825
  424.9 15.7 %collective-permute-start.15 = (bf16[2,592,384]{2,1,0:T(8,128)(2,1)}, bf16[2,592,384]{2,1,0:T(8,128)(2,1)}, u32[]{:S(2)}, u32[]{:S(2)}) collective-permute-start(bf16[2,592,384]{2,1,0:T(8,128)(2,1)} %get-tuple-element.216), channel_id=1, source_target_pairs={{0,1},{1,0},{2,3},{3,2},{4,5},{5,4},{6,7},{7,6},{8,9},{9,8},{10,11... | collective-permute-start | bytes 2727944 | tf_op jit(solution)/shard_map/ppermute | solution.py:825
  425.2 2.1 collective-permute-start.26
  453.8 1.3 copy-start.6
  456.0 2.5 copy-start.13
  456.8 2.8 copy-start.12
  466.8 1.6 copy-start.14
  466.8 1.6 copy-start.15
  466.8 2.4 copy-start.8
  468.4 1.4 copy-start.7
  (8 other events, 8.5 us)

commit v3 on v2

--- a/solution.py
+++ b/solution.py
@@ -14,6 +14,7 @@
 MB = 1 << 20
 SUPER = 8
 LANES = 384
+NORM_ROWS = 64
 
 ERF_COEFS = (
     0.7978849414899046, 0.0363330844086688, -3.259474462099993e-05, -5.5306316685416947e-05,
@@ -55,11 +56,29 @@
     )
 
 
+def row_loop(count, chunk, sums):
+    for i in range(count):
+        sums = chunk(i, sums)
+    return sums
+
+
+def fold(x):
+    return jnp.sum(x.reshape(-1, 8, x.shape[1]), 0)
+
+
 def col_sum(x):
     return jnp.sum(x, 0, keepdims=True)
 
 
+COST_US = dict(
+    tables=4, projections=8, attention_forward=7, feed_forward=24, feed_backward=30, attention_backward=12,
+    projections_backward=12, place_rows=4,
+    unpack_feed=4, unpack_attention=3,
+)
+
+
 def call(kernel, name, grid, ids, in_specs, inputs, out_specs, out_shape, scratch=()):
+    cost = pl.CostEstimate(flops=COST_US[name] * 1100000000, bytes_accessed=COST_US[name] * 1000000, transcendentals=0)
     return pl.pallas_call(
         kernel,
         grid_spec=pltpu.PrefetchScalarGridSpec(
@@ -71,6 +90,7 @@
         ),
         out_shape=out_shape,
         compiler_params=pltpu.CompilerParams(vmem_limit_bytes=62 * MB),
+        cost_estimate=cost,
         name=name,
     )(ids, *inputs)
 
@@ -276,7 +296,7 @@
         ctx = dot(values_t[pair][64 * e : 64 * e + 64], expo.astype(bf16))
         at = 128 * pair + 64 * e
         ctx_ref[at : at + 64, :] = (ctx * (1.0 / total)).astype(bf16)
-        lse_ref[0, 2 * pair + e : 2 * pair + e + 1, :] = top + jnp.log(total)
+        lse_ref[pair, e : e + 1, :] = top + jnp.log(total)
 
     scores = scores_of(units[0])
     for i, unit in enumerate(units):
@@ -310,8 +330,8 @@
     return call(
         functools.partial(attention_fwd_kernel, per_step=per_step, shared=shared),
         "attention_forward", (steps,), ids, in_specs, inputs,
-        [spec((lanes, nq), step, 0), spec((1, 2 * per_step, nq), step, 0, 0)],
-        [shape_of((width, nq), bf16), shape_of((steps, 2 * per_step, nq), f32)],
+        [spec((lanes, nq), step, 0), spec((per_step, 2, nq), step, 0, 0)],
+        [shape_of((width, nq), bf16), shape_of((width // 128, 2, nq), f32)],
         scratch,
     )
 
@@ -356,7 +376,7 @@
         pair, e = unit
         scores, gp, q_mine, gc_mine, q_scaled = parts
         at = slice(128 * pair, 128 * pair + 128)
-        shares = jnp.exp(scores - lse_ref[0, 2 * pair + e : 2 * pair + e + 1, :])
+        shares = jnp.exp(scores - lse_ref[pair, e : e + 1, :])
         dv = dot(shares.astype(bf16), gc_mine)
         weighted = shares * gp
         delta = jnp.sum(weighted, 0, keepdims=True)
@@ -392,7 +412,8 @@
         parts = upcoming
 
 
-def attention_bwd(ids, shared, tables, joint, turned, kv_far, lse, g_ctx, rel_pairs, layer, per_step=2):
+def attention_bwd(ids, shared, tables, joint, turned, kv_far, lse, g_ctx, rel_pairs, layer, split, per_step=2):
+    per_step = 1 if split else per_step
     cos_t, sin_t, kf, ctab, stab, code, seg, valid = tables
     tokens, width = joint.shape[0], joint.shape[1] // 3
     half = tokens // 3
@@ -400,29 +421,33 @@
     nq = half if shared else nk
     key_rows = half if shared else nk
     lanes = 128 * per_step
-    steps = width // lanes
+    all_steps = width // lanes
+    steps = all_steps // 2 if split else all_steps
+    out_width = lanes * steps
+    first = lambda ids: ids[1] * steps if split else 0
     q_row = 2 if shared else 0
-    at = lambda off: (lambda i, ids: i + off)
+    at = lambda off: (lambda i, ids: first(ids) + i + off)
+    here = at(0)
     in_specs = [
         spec((nk, 128), int(shared), 0), spec((8, nq), 0, q_row), spec((nk, 128), int(shared), 0),
         spec((64, nq), 0, q_row), spec((64, nq), 0, q_row),
-        spec((1, per_step, 128, 128), layer, step, 0, 0),
-        spec((1, 2 * per_step, nq), step, 0, 0), spec((nq, lanes), q_row, step),
-        spec((nq, lanes), q_row, step), spec((nq, 2 * lanes), q_row, step),
-        spec((key_rows, lanes), q_row, at(steps)), spec((key_rows, lanes), q_row, at(2 * steps)),
+        spec((1, per_step, 128, 128), layer, here, 0, 0),
+        spec((per_step, 2, nq), here, 0, 0), spec((nq, lanes), q_row, here),
+        spec((nq, lanes), q_row, here), spec((nq, 2 * lanes), q_row, here),
+        spec((key_rows, lanes), q_row, at(all_steps)), spec((key_rows, lanes), q_row, at(2 * all_steps)),
     ]
     inputs = [code, seg, kf, cos_t, sin_t, rel_pairs, lse, g_ctx, joint, turned, joint, joint]
     scratch = [pltpu.VMEM((nk, nq), f32), pltpu.VMEM((128, nk), bf16)]
     out_specs = [spec((3, key_rows, lanes), 0, 0, step)]
-    out_shape = [shape_of((3, key_rows, width), bf16)]
+    out_shape = [shape_of((3, key_rows, out_width), bf16)]
     if shared:
-        in_specs += [spec((half, lanes), 0, step), spec((half, lanes), 0, at(steps))]
+        in_specs += [spec((half, lanes), 0, here), spec((half, lanes), 0, at(all_steps))]
         inputs += [kv_far, kv_far]
         scratch += [pltpu.VMEM((nk, lanes), bf16)] * 2
         out_specs.append(spec((2, half, lanes), 0, 0, step))
-        out_shape.append(shape_of((2, half, width), bf16))
+        out_shape.append(shape_of((2, half, out_width), bf16))
     out_specs.append(spec((128, lanes), 0, step))
-    out_shape.append(shape_of((128, width), f32))
+    out_shape.append(shape_of((128, out_width), f32))
     return call(
         functools.partial(attention_bwd_kernel, per_step=per_step, shared=shared),
         "attention_backward", (steps,), ids, in_specs, inputs, out_specs, out_shape, scratch,
@@ -438,26 +463,39 @@
 ):
     j = pl.program_id(0)
     half = x0.shape[1]
-    long = 2 * half
     row = lambda ref, *at: ref[at[:-1] + (slice(at[-1], at[-1] + 1),)].astype(f32)
 
-    def add_squares(values, k):
-        weighted = values * values * valid_ref[:, 0:1]
-        squares_ref[k : k + 1, :] = col_sum(weighted[0:long])
-        squares_ref[k + 1 : k + 2, :] = col_sum(weighted[long:])
+    rows = NORM_ROWS
+    zero = jnp.zeros((8, x0.shape[2]), f32)
+
+    def add_squares(sums, k, tile):
+        for i, x in enumerate(sums):
+            at = k + 2 * i + tile // 2
+            squares_ref[at : at + 1, :] += col_sum(x)
 
     @pl.when(j == 0)
     def _():
         ctx = jnp.concatenate([own_ref[...].T, shared_ref[...].T], 0)
-        attention = dot(ctx, w_out_ref[0]) + row(out_bias_ref, layer)
-        add_squares(attention, 0)
-        x = jnp.concatenate([x0[0], x1[0], x2[0]], 0).astype(f32)
-        normed, inverse = norm_parts(x + attention)
-        mixed = (normed * row(scale_ref, layer, 0) + row(shift_ref, layer, 0)).astype(bf16)
-        n1_ref[...] = normed.astype(bf16)
-        r1_ref[...] = jnp.broadcast_to(inverse, r1_ref.shape)
-        mixed_ref[...] = mixed
-        add_squares(mixed.astype(f32), 2)
+        feed_ref[...] = dot(ctx, w_out_ref[0])
+        bias, gain, shift = row(out_bias_ref, layer), row(scale_ref, layer, 0), row(shift_ref, layer, 0)
+        squares_ref[...] = jnp.zeros_like(squares_ref)
+        for t, x_ref in enumerate((x0, x1, x2)):
+
+            def chunk(i, sums):
+                at = i * rows
+                to = pl.ds(t * half + at, rows)
+                valid = valid_ref[to, 0:1]
+                attention = feed_ref[to, :] + bias
+                normed, inverse = norm_parts(x_ref[0, pl.ds(at, rows), :].astype(f32) + attention)
+                mixed = (normed * gain + shift).astype(bf16)
+                n1_ref[to, :] = normed.astype(bf16)
+                r1_ref[to, :] = jnp.broadcast_to(inverse, (rows, 128))
+                mixed_ref[to, :] = mixed
+                mixed = mixed.astype(f32)
+                return (sums[0] + fold(attention * attention * valid), sums[1] + fold(mixed * mixed * valid))
+
+            sums = row_loop(half // rows, chunk, (zero, zero))
+            add_squares(sums, 0, t)
 
     cols = in_ref.shape[2] // parts
     at = lambda k: slice(cols * k, cols * k + cols)
@@ -486,14 +524,22 @@
 
     @pl.when(j == pl.num_programs(0) - 1)
     def _():
-        total = feed_ref[...] + row(ffn_bias_ref, layer)
-        add_squares(total, 4)
-        normed, inverse = norm_parts(mixed_ref[...].astype(f32) + total)
-        out = normed * row(scale_ref, layer, 1) + row(shift_ref, layer, 1)
-        add_squares(out, 6)
-        n2_ref[...] = normed.astype(bf16)
-        r2_ref[...] = jnp.broadcast_to(inverse, r2_ref.shape)
-        h_ref[...] = out.astype(bf16)
+        bias, gain, shift = row(ffn_bias_ref, layer), row(scale_ref, layer, 1), row(shift_ref, layer, 1)
+        for t in range(3):
+
+            def chunk(i, sums):
+                to = pl.ds(t * half + i * rows, rows)
+                valid = valid_ref[to, 0:1]
+                branch = feed_ref[to, :] + bias
+                normed, inverse = norm_parts(mixed_ref[to, :].astype(f32) + branch)
+                out = normed * gain + shift
+                n2_ref[to, :] = normed.astype(bf16)
+                r2_ref[to, :] = jnp.broadcast_to(inverse, (rows, 128))
+                h_ref[to, :] = out.astype(bf16)
+                return (sums[0] + fold(branch * branch * valid), sums[1] + fold(out * out * valid))
+
+            sums = row_loop(half // rows, chunk, (zero, zero))
+            add_squares(sums, 4, t)
 
 
 def feed_fwd(ids, x, gathered, ctx_own, ctx_shared, valid, weights, layer, chunk=768, parts=3):
@@ -523,133 +569,6 @@
     )
 
 
-def feed_bwd_kernel(
-    ids, g0, g1, g2, n2_ref, r2_ref, n1_ref, r1_ref, scale_ref, out_ref, slope_ref, in_ref, w_out_ref,
-    feed_ref, pre_ref, mixed_ref, attn_ref, ctx_ref, sums_ref, pre_sum_ref,
-    res_ref, acc_ref,
-    *, layer, parts,
-):
-    j = pl.program_id(0)
-    row = lambda k: scale_ref[layer, k : k + 1, :].astype(f32)
-
-    @pl.when(j == 0)
-    def _():
-        grad = jnp.concatenate([g0[0], g1[0], g2[0]], 0).astype(f32)
-        normed = n2_ref[...].astype(f32)
-        sums_ref[1:2, :] = col_sum(grad * normed)
-        sums_ref[3:4, :] = col_sum(grad)
-        back = norm_back(grad, row(1), normed, r2_ref[:, 0:1])
-        res_ref[...] = back
-        feed = back.astype(bf16)
-        feed_ref[...] = feed
-        sums_ref[5:6, :] = col_sum(feed.astype(f32))
-        sums_ref[6:8, :] = jnp.zeros((2, sums_ref.shape[1]), f32)
-
-    cols = slope_ref.shape[1] // parts
-    at = lambda k: slice(cols * k, cols * k + cols)
-    g_act = dot_nt(feed_ref[...], out_ref[0, at(0)])
-    total = None
-    for k in range(parts):
-        coming = dot_nt(feed_ref[...], out_ref[0, at(k + 1)]) if k + 1 < parts else None
-        g_pre = (g_act * slope_ref[:, at(k)].astype(f32)).astype(bf16)
-        pre_ref[:, at(k)] = g_pre
-        pre_sum_ref[:, at(k)] = jnp.broadcast_to(col_sum(g_pre.astype(f32)), (8, cols))
-        part = dot_nt(g_pre, in_ref[0, :, at(k)])
-        total = part if total is None else total + part
-        g_act = coming
-
-    @pl.when(j == 0)
-    def _():
-        acc_ref[...] = total
-
-    @pl.when(j > 0)
-    def _():
-        acc_ref[...] += total
-
-    @pl.when(j == pl.num_programs(0) - 1)
-    def _():
-        g_mixed = acc_ref[...] + res_ref[...]
-        mixed_ref[...] = g_mixed.astype(bf16)
-        normed = n1_ref[...].astype(f32)
-        sums_ref[0:1, :] = col_sum(g_mixed * normed)
-        sums_ref[2:3, :] = col_sum(g_mixed)
-        attn = norm_back(g_mixed, row(0), normed, r1_ref[:, 0:1]).astype(bf16)
-        attn_ref[...] = attn
-        sums_ref[4:5, :] = col_sum(attn.astype(f32))
-        ctx_ref[...] = dot_nt(attn, w_out_ref[0]).astype(bf16)
-
-
-def feed_bwd(ids, grad, gathered, kept, slope, weights, layer, chunk=768, parts=3):
-    w_out, out_bias, ln_scale, ln_shift, ffn_in, ffn_in_bias, ffn_out, ffn_out_bias = weights
-    n1, r1, n2, r2 = kept
-    half, width = grad.shape[1], grad.shape[2]
-    tokens, ff = 3 * half, ffn_in.shape[2]
-    full = lambda *shape: spec(shape, *([0] * len(shape)))
-    dense = ((tokens, width), bf16)
-    outs = [dense, ((tokens, ff), bf16), dense, dense, dense, ((8, width), f32), ((8, ff), f32)]
-    out_specs = [full(*s) for s, _ in outs]
-    out_specs[1] = spec((tokens, chunk), 0, step)
-    out_specs[6] = spec((8, chunk), 0, step)
-    return call(
-        functools.partial(feed_bwd_kernel, layer=layer, parts=parts), "feed_backward", (ff // chunk,), ids,
-        row_tiles(half, width, gathered)
-        + [
-            full(tokens, width), full(tokens, 128), full(tokens, width), full(tokens, 128),
-            full(*ln_scale.shape), spec((1, chunk, width), layer, step, 0), spec((tokens, chunk), 0, step),
-            spec((1, width, chunk), layer, 0, step), spec((1, width, width), layer, 0, 0),
-        ],
-        [grad, grad, grad, n2, r2, n1, r1, ln_scale, ffn_out, slope, ffn_in, w_out],
-        out_specs, [shape_of(s, d) for s, d in outs],
-        [pltpu.VMEM((tokens, width), f32), pltpu.VMEM((tokens, width), f32)],
-    )
-
-
-def joint_bwd_kernel(
-    ids, own_ref, shared_ref, arrived_ref, w_ref, attn_ref, joint_ref, h_ref, sums_ref, acc_ref,
-):
-    j = pl.program_id(0)
-    far = arrived_ref[0].astype(f32) * (j > 0).astype(f32)
-    near = (shared_ref[0].astype(f32) + far).astype(bf16)
-    joint = jnp.concatenate([own_ref[0], near], 0)
-    joint_ref[...] = joint
-    part = dot_nt(joint, w_ref[0])
-    sums_ref[...] = jnp.broadcast_to(col_sum(joint.astype(f32)), sums_ref.shape)
-
-    @pl.when(j == 0)
-    def _():
-        acc_ref[...] = part + attn_ref[...].astype(f32)
-
-    @pl.when(j > 0)
-    def _():
-        acc_ref[...] += part
-
-    @pl.when(j == pl.num_programs(0) - 1)
-    def _():
-        h_ref[...] = acc_ref[...].astype(bf16)
-
-
-def joint_bwd(ids, own, shared, arrived, w_qkv, g_attn, layer):
-    _, length, width = own.shape
-    half = shared.shape[1]
-    tokens = length + half
-    full = lambda *shape: spec(shape, *([0] * len(shape)))
-    return call(
-        joint_bwd_kernel, "projections_backward", (3,), ids,
-        [
-            spec((1, length, width), step, 0, 0), spec((1, half, width), step, 0, 0),
-            spec((1, half, width), lambda i, ids: jnp.maximum(i - 1, 0), 0, 0),
-            spec((1, width, width), layer, 0, step), full(tokens, width),
-        ],
-        [own, shared, arrived, w_qkv, g_attn],
-        [spec((tokens, width), 0, step), full(tokens, width), spec((8, width), 0, step)],
-        [
-            shape_of((tokens, 3 * width), bf16), shape_of((tokens, width), bf16),
-            shape_of((8, 3 * width), f32),
-        ],
-        [pltpu.VMEM((tokens, width), f32)],
-    )
-
-
 def slab_place(ids, slab):
     relative = jnp.bitwise_xor(ids[2], slab)
     return (
@@ -675,103 +594,237 @@
         keep_ref[place, at, :], send_ref[place, at, :] = high, low
 
 
-def feed_weights_kernel(ids, act_ref, feed_ref, mixed_ref, pre_ref, keep_ref, send_ref, feed_t, mixed_t):
-    i = pl.program_id(0)
-
-    @pl.when(i == 0)
-    def _():
-        feed_t[...] = feed_ref[...].T
-        mixed_t[...] = mixed_ref[...].T
-
+def feed_bwd_kernel(
+    ids, g0, g1, g2, n2_ref, r2_ref, n1_ref, r1_ref, scale_ref, out_ref, slope_ref, in_ref, w_out_ref,
+    act_ref, mixed_in_ref, own_ref, shared_ref,
+    mixed_ref, attn_ref, ctx_ref, sums_ref, pre_sum_ref, keep_ref, send_ref,
+    res_ref, acc_ref, feed_ref, pre_ref, feed_t, mixed_t,
+    *, layer, parts,
+):
+    j = pl.program_id(0)
+    tokens = n2_ref.shape[0]
+    gain = lambda k: scale_ref[layer, k : k + 1, :].astype(f32)
+    rows = NORM_ROWS
+
+    @pl.when(j == 0)
+    def _():
+        sums_ref[...] = jnp.zeros_like(sums_ref)
+        for t, g_ref in enumerate((g0, g1, g2)):
+            count = g_ref.shape[1]
+
+            def chunk(i, sums):
+                at = i * rows
+                to = pl.ds(t * count + at, rows)
+                grad = g_ref[0, pl.ds(at, rows), :].astype(f32)
+                normed = n2_ref[to, :].astype(f32)
+                back = norm_back(grad, gain(1), normed, r2_ref[to, 0:1])
+                res_ref[to, :] = back
+                feed = back.astype(bf16)
+                feed_ref[to, :] = feed
+                return (sums[0] + fold(grad * normed), sums[1] + fold(grad), sums[2] + fold(feed.astype(f32)))
+
+            zero = jnp.zeros((8, n2_ref.shape[1]), f32)
+            sums = row_loop(count // rows, chunk, (zero, zero, zero))
+            for k, x in zip((1, 3, 5), sums):
+                sums_ref[k : k + 1, :] += col_sum(x)
+        for side in range(2):
+
+            @pl.when(ids[1] == side)
+            def _():
+                feed_t[...] = feed_ref[:, LANES * side : LANES * side + LANES].T
+
+        mixed_t[...] = mixed_in_ref[...].T
+
+    cols = slope_ref.shape[1] // parts
+    at = lambda k: slice(cols * k, cols * k + cols)
+    g_act = dot_nt(feed_ref[...], out_ref[0, at(0)])
+    for k in range(parts):
+        coming = dot_nt(feed_ref[...], out_ref[0, at(k + 1)]) if k + 1 < parts else None
+        g_pre = (g_act * slope_ref[:, at(k)].astype(f32)).astype(bf16)
+        pre_ref[:, at(k)] = g_pre
+        pre_sum_ref[:, at(k)] = jnp.broadcast_to(col_sum(g_pre.astype(f32)), (8, cols))
+        g_act = coming
+    total = dot_nt(pre_ref[...], in_ref[0])
+
+    @pl.when(j == 0)
+    def _():
+        acc_ref[...] = total
+
+    @pl.when(j > 0)
+    def _():
+        acc_ref[...] += total
+
+    high = LANES // 2
     slabs = act_ref.shape[1] // LANES
-    out_steps = SUPER // slabs
-
-    for s in range(out_steps):
-        @pl.when(i == s)
-        def _():
-            result = dot(feed_t[...], act_ref[...]).astype(bf16)
-            for k in range(slabs):
-                store_piece(ids, keep_ref, send_ref, s * slabs + k, LANES // 2, 0,
-                            result[:, LANES * k : LANES * k + LANES])
-
-    groups = pre_ref.shape[1] // LANES
-    rows = mixed_t.shape[0] // SUPER
-    for s in range(4 // groups):
-        @pl.when(i == out_steps + s)
+    result = dot(feed_t[...], act_ref[...]).astype(bf16)
+    for k in range(slabs):
+        store_piece(ids, keep_ref, send_ref, j * slabs + k, high, 0, result[:, LANES * k : LANES * k + LANES])
+    width = mixed_t.shape[0]
+    slab_rows = width // SUPER
+    half = slab_rows // 2
+    steps = 4 // slabs
+    for s in range(2 * steps):
+
+        @pl.when((j == s) & (ids[1] == s // steps))
         def _():
             result = dot(mixed_t[...], pre_ref[...]).astype(bf16)
             for slab in range(SUPER):
-                for k in range(groups):
+                for k in range(slabs):
                     store_piece(
-                        ids, keep_ref, send_ref, slab, rows // 2,
-                        LANES // 2 + (s * groups + k) * (rows // 2),
-                        result[rows * slab : rows * slab + rows, LANES * k : LANES * k + LANES],
+                        ids, keep_ref, send_ref, slab, half, high + ((s % steps) * slabs + k) * half,
+                        result[slab_rows * slab : slab_rows * slab + slab_rows, LANES * k : LANES * k + LANES],
                     )
 
-
-def feed_weights(ids, act, g_feed, mixed, g_pre):
-    tokens, width = mixed.shape
-    block = 2 * LANES
-    piece = (SUPER, LANES, LANES)
+    @pl.when(j == pl.num_programs(0) - 1)
+    def _():
+        def chunk(i, sums):
+            to = pl.ds(i * rows, rows)
+            g_mixed = acc_ref[to, :] + res_ref[to, :]
+            mixed_ref[to, :] = g_mixed.astype(bf16)
+            normed = n1_ref[to, :].astype(f32)
+            attn = norm_back(g_mixed, gain(0), normed, r1_ref[to, 0:1]).astype(bf16)
+            attn_ref[to, :] = attn
+            return (sums[0] + fold(g_mixed * normed), sums[1] + fold(g_mixed), sums[2] + fold(attn.astype(f32)))
+
+        zero = jnp.zeros((8, width), f32)
+        sums = row_loop(tokens // rows, chunk, (zero, zero, zero))
+        for k, x in zip((0, 2, 4), sums):
+            sums_ref[k : k + 1, :] = col_sum(x)
+        ctx_ref[...] = dot_nt(attn_ref[...], w_out_ref[0]).astype(bf16)
+        long = own_ref.shape[1]
+        for side in range(2):
+
+            @pl.when(ids[1] == side)
+            def _():
+                lanes = slice(LANES * side, LANES * side + LANES)
+                result = dot(own_ref[...], attn_ref[0:long, lanes]) + dot(shared_ref[...], attn_ref[long:, lanes])
+                result = result.astype(bf16)
+                for slab in range(SUPER):
+                    store_piece(ids, keep_ref, send_ref, slab, half, high + 4 * half,
+                                result[slab_rows * slab : slab_rows * slab + slab_rows])
+
+
+def feed_bwd(ids, grad, gathered, kept, slope, act, mixed, ctx_own, ctx_shared, weights, layer, chunk=768, parts=3):
+    w_out, out_bias, ln_scale, ln_shift, ffn_in, ffn_in_bias, ffn_out, ffn_out_bias = weights
+    n1, r1, n2, r2 = kept
+    half, width = grad.shape[1], grad.shape[2]
+    tokens, ff = 3 * half, ffn_in.shape[2]
+    once = lambda *shape: pl.BlockSpec(shape, lambda i, ids: (0,) * len(shape), pipeline_mode=pl.Buffered(1))
     full = lambda *shape: spec(shape, *([0] * len(shape)))
+    dense = ((tokens, width), bf16)
+    piece = ((SUPER, LANES + width // SUPER // 2, LANES), bf16)
+    outs = [dense, dense, dense, ((8, width), f32), ((8, ff), f32), piece, piece]
+    out_specs = [full(*s) for s, _ in outs]
+    out_specs[4] = spec((8, chunk), 0, step)
     return call(
-        feed_weights_kernel, "feed_weights", (6,), ids,
+        functools.partial(feed_bwd_kernel, layer=layer, parts=parts), "feed_backward", (ff // chunk,), ids,
+        row_tiles(half, width, gathered)
+        + [
+            once(tokens, width), once(tokens, 128), once(tokens, width), once(tokens, 128),
+            full(*ln_scale.shape), spec((1, chunk, width), layer, step, 0), spec((tokens, chunk), 0, step),
+            spec((1, width, chunk), layer, 0, step), spec((1, width, width), layer, 0, 0),
+            spec((tokens, chunk), 0, step), once(tokens, width), once(*ctx_own.shape), once(*ctx_shared.shape),
+        ],
+        [grad, grad, grad, n2, r2, n1, r1, ln_scale, ffn_out, slope, ffn_in, w_out, act, mixed, ctx_own,
+         ctx_shared],
+        out_specs, [shape_of(s, d) for s, d in outs],
         [
-            spec((tokens, block), 0, lambda i, ids: jnp.minimum(i, 3)),
-            spec((tokens, LANES), 0, lambda i, ids: ids[1]),
-            full(tokens, width),
-            spec((tokens, block), 0, lambda i, ids: 2 * ids[1] + jnp.maximum(i - 4, 0)),
+            pltpu.VMEM((tokens, width), f32), pltpu.VMEM((tokens, width), f32),
+            pltpu.VMEM((tokens, width), bf16), pltpu.VMEM((tokens, chunk), bf16),
+            pltpu.VMEM((LANES, tokens), bf16), pltpu.VMEM((width, tokens), bf16),
         ],
-        [act, g_feed, mixed, g_pre],
-        [full(*piece), full(*piece)], [shape_of(piece, bf16), shape_of(piece, bf16)],
-        [pltpu.VMEM((LANES, tokens), bf16), pltpu.VMEM((width, tokens), bf16)],
-    )
-
-
-def attention_weights_kernel(
-    ids, x0, x1, x2, joint_ref, own_ref, shared_ref, attn_ref, rel0_ref, rel1_ref, small_ref,
-    keep_ref, send_ref,
+    )
+
+
+def joint_bwd_kernel(
+    ids, x0, x1, x2, own_ref, shared_ref, arrived_ref, w_ref, attn_ref, rel0_ref, rel1_ref, vec_ref, pre_sum_ref,
+    h_ref, keep_ref, send_ref, acc_ref, x_t, sums_ref, mine_ref,
+    *, split,
 ):
-    x_t = jnp.concatenate([x0[0].T, x1[0].T, x2[0].T], 1)
+    j = pl.program_id(0)
     width = x_t.shape[0]
     rows = width // SUPER
     half = rows // 2
-    groups = joint_ref.shape[1] // LANES
-    for g in range(groups):
-        result = dot(x_t, joint_ref[:, LANES * g : LANES * g + LANES]).astype(bf16)
+
+    @pl.when(j == 0)
+    def _():
+        x_t[...] = jnp.concatenate([x0[0].T, x1[0].T, x2[0].T], 1)
+        sums_ref[...] = jnp.zeros_like(sums_ref)
+
+    far = arrived_ref[0].astype(f32) * (j > 0).astype(f32)
+    near = (shared_ref[0].astype(f32) + far).astype(bf16)
+    joint = jnp.concatenate([own_ref[0], near], 0)
+    part = dot_nt(joint, w_ref[0])
+    if split:
+        mine_ref[...] = joint
+
+    @pl.when(j == 0)
+    def _():
+        flag = (ids[1] == 0).astype(f32) if split else 1.0
+        acc_ref[...] = part + attn_ref[...].astype(f32) * flag
+
+    @pl.when(j > 0)
+    def _():
+        acc_ref[...] += part
+
+    for side in range(2):
+        lanes = slice(LANES * side, LANES * side + LANES)
+
+        @pl.when(ids[1] == side)
+        def _():
+            if not split:
+                mine_ref[...] = joint[:, lanes]
+            sums_ref[j, :, lanes] = jnp.broadcast_to(col_sum(mine_ref[...].astype(f32)), (8, LANES))
+
+    result = dot(x_t[...], mine_ref[...]).astype(bf16)
+    for group in range(3):
+
+        @pl.when(j == group)
+        def _():
+            for slab in range(SUPER):
+                store_piece(ids, keep_ref, send_ref, slab, half, group * half,
+                            result[rows * slab : rows * slab + rows])
+
+    @pl.when(j == pl.num_programs(0) - 1)
+    def _():
+        h_ref[...] = acc_ref[...].astype(bf16)
+        rel = (rel0_ref[...] + rel1_ref[...]).astype(bf16)
+        count = rel.shape[0] // SUPER
+        lines = jnp.concatenate([vec_ref[0:6, :], sums_ref[0, 0:1], sums_ref[2, 0:1]], 0)
+        blank = jnp.zeros((8, LANES - rows), f32)
         for slab in range(SUPER):
-            store_piece(ids, keep_ref, send_ref, slab, half, g * half,
-                        result[rows * slab : rows * slab + rows])
-    long = own_ref.shape[1]
-    result = dot(own_ref[...], attn_ref[0:long]) + dot(shared_ref[...], attn_ref[long:])
-    result = result.astype(bf16)
-    for slab in range(SUPER):
-        store_piece(ids, keep_ref, send_ref, slab, half, groups * half,
-                    result[rows * slab : rows * slab + rows])
-    rel = (rel0_ref[...] + rel1_ref[...]).astype(bf16)
-    count = rel.shape[0] // SUPER
-    for slab in range(SUPER):
-        both = jnp.concatenate([rel[count * slab : count * slab + count], small_ref[slab]], 0)
-        store_piece(ids, keep_ref, send_ref, slab, count, (groups + 1) * half, both)
-
-
-def attention_weights(ids, x, gathered, g_joint, ctx_own, ctx_shared, g_attn, rel0, rel1, small):
-    half, width = x.shape[1], x.shape[2]
-    tokens = 3 * half
-    rows = (width // SUPER // 2) * 4 + rel0.shape[0] // SUPER
-    piece = (SUPER, rows, LANES)
-    side = lambda i, ids: ids[1]
+            narrow = jnp.concatenate([lines[:, rows * slab : rows * slab + rows], blank], 1)
+            wide = pre_sum_ref[0:1, LANES * slab : LANES * slab + LANES]
+            small = jnp.concatenate([narrow, wide, jnp.zeros((count - 9, LANES), f32)], 0).astype(bf16)
+            both = jnp.concatenate([rel[count * slab : count * slab + count], small], 0)
+            store_piece(ids, keep_ref, send_ref, slab, count, 3 * half, both)
+
+
+def joint_bwd(ids, x, gathered, own, shared, arrived, w_qkv, g_attn, rel0, rel1, vec, pre_sum, layer, split):
+    _, length, cols = own.shape
+    width = g_attn.shape[1]
+    half = shared.shape[1]
+    tokens = length + half
     full = lambda *shape: spec(shape, *([0] * len(shape)))
+    side = lambda i, ids: 0 if split else ids[1]
+    piece = (SUPER, (width // SUPER // 2) * 3 + rel0.shape[0] // SUPER, LANES)
     return call(
-        attention_weights_kernel, "attention_weights", (1,), ids,
+        functools.partial(joint_bwd_kernel, split=split), "projections_backward", (3,), ids,
         row_tiles(half, width, gathered)
         + [
-            spec((tokens, 3 * LANES), 0, side), full(*ctx_own.shape), full(*ctx_shared.shape),
-            spec((tokens, LANES), 0, side), spec((rel0.shape[0], LANES), 0, side),
-            spec((rel0.shape[0], LANES), 0, side), full(*small.shape),
+            spec((1, length, cols), step, 0, 0), spec((1, half, cols), step, 0, 0),
+            spec((1, half, cols), lambda i, ids: jnp.maximum(i - 1, 0), 0, 0),
+            spec((1, width, cols), layer, 0, lambda i, ids: 2 * i + ids[1] if split else i),
+            full(tokens, width), spec((rel0.shape[0], LANES), 0, side), spec((rel0.shape[0], LANES), 0, side),
+            full(*vec.shape), full(*pre_sum.shape),
         ],
-        [x, x, x, g_joint, ctx_own, ctx_shared, g_attn, rel0, rel1, small],
-        [full(*piece), full(*piece)], [shape_of(piece, bf16), shape_of(piece, bf16)],
+        [x, x, x, own, shared, arrived, w_qkv, g_attn, rel0, rel1, vec, pre_sum],
+        [full(tokens, width), full(*piece), full(*piece)],
+        [shape_of((tokens, width), bf16), shape_of(piece, bf16), shape_of(piece, bf16)],
+        [
+            pltpu.VMEM((tokens, width), f32), pltpu.VMEM((width, tokens), bf16),
+            pltpu.VMEM((3, 8, width), f32), pltpu.VMEM((tokens, LANES), bf16),
+        ],
     )
 
 
@@ -799,6 +852,72 @@
         place_rows_kernel, "place_rows", (6,), ids,
         [spec((1, half, width), tile, 0, 0)] * 2, [tiles(own), tiles(other)],
         spec((1, half, width), step, 0, 0), shape_of((6, half, width), dtype),
+    )
+
+
+def collect(ids, refs, scratch):
+    for core in range(2):
+        for side in range(2):
+
+            @pl.when((ids[0] == core) & (ids[1] == side))
+            def _():
+                scratch[core, side] = refs[0][...]
+                scratch[core, 1 - side] = refs[1][...]
+                scratch[1 - core, side] = refs[2][...]
+                scratch[1 - core, 1 - side] = refs[3][...]
+
+
+def spread_columns(scratch, out_ref, layer, at, groups, rows, inner=False):
+    for core in range(2):
+        for side in range(2):
+            for g in range(groups):
+                piece = scratch[core, side, at + g * rows : at + g * rows + rows, :]
+                lane = ((g * 2 + side) if inner else (side * groups + g)) * LANES
+                out_ref[layer, core * rows : core * rows + rows, lane : lane + LANES] = piece.astype(f32)
+
+
+def unpack_feed_kernel(ids, *refs):
+    inputs, (in_ref, out_ref, w_out_ref, scratch) = refs[:8], refs[8:]
+    high = LANES // 2
+    for layer in range(2):
+        collect(ids, inputs[4 * layer : 4 * layer + 4], scratch)
+        columns = [scratch[core, side, 0:high, :] for side in range(2) for core in range(2)]
+        out_ref[layer] = jnp.concatenate(columns, 0).astype(f32).T
+        rows = in_ref.shape[1] // 2
+        spread_columns(scratch, in_ref, layer, high, 4, rows)
+        spread_columns(scratch, w_out_ref, layer, high + 4 * rows, 1, rows)
+
+
+def unpack_attention_kernel(ids, *refs):
+    inputs = refs[:8]
+    qkv_ref, rel_ref, qv_ref, out_bias_ref, scale_ref, shift_ref, in_bias_ref, ffn_bias_ref = refs[8:16]
+    scratch = refs[16]
+    rows = qkv_ref.shape[1] // 2
+    wide = 2 * rows
+    for layer in range(2):
+        collect(ids, inputs[4 * layer : 4 * layer + 4], scratch)
+        spread_columns(scratch, qkv_ref, layer, 0, 3, rows, True)
+        at = 3 * rows
+        count = rel_ref.shape[2]
+        rel = jnp.concatenate([scratch[0, side, at : at + count, :] for side in range(2)], 1).astype(f32)
+        rel = jnp.concatenate([rel, jnp.zeros((128 - count, rel.shape[1]), f32)], 0)
+        rel_ref[layer] = rel.T[:, 0:count]
+        small = scratch[1, 0, at : at + count, :].astype(f32)
+        scale_ref[layer] = small[0:2, 0:wide]
+        shift_ref[layer] = small[2:4, 0:wide]
+        out_bias_ref[layer : layer + 1] = small[4:5, 0:wide]
+        ffn_bias_ref[layer : layer + 1] = small[5:6, 0:wide]
+        other = scratch[1, 1, at : at + count, :].astype(f32)
+        qv_ref[layer] = small[6:8, 0:wide] + other[6:8, 0:wide]
+        in_bias_ref[layer : layer + 1] = small[8:9]
+
+
+def unpack(kernel, name, ids, pieces, shapes):
+    full = lambda *shape: spec(shape, *([0] * len(shape)))
+    return call(
+        kernel, name, (1,), ids, [full(*p.shape) for p in pieces], pieces,
+        [full(*s) for s in shapes], [shape_of(s, f32) for s in shapes],
+        [pltpu.VMEM((2, 2) + pieces[0].shape, bf16)],
     )
 
 
@@ -848,50 +967,85 @@
         )
         x, gathered = halves(out), False
 
-    def reduce_start(keep, send):
-        return keep + flip(send, 1)
-
-    def reduce_rest(x):
-        for bit in range(3):
-            n = x.shape[0] // 2
-            x = x[:n] + flip_dp(x[n:], fine << bit)
-        x = x[0]
+    clock = [ids]
+
+    def pin(state):
+        clock[0], state = lax.optimization_barrier((clock[0], state))
+        return state
+
+    def absorb(keep, arrived):
+        n = keep.shape[0] // 2
+        return pin((keep[:n] + arrived[:n], keep[n:] + arrived[n:]))
+
+    def last(keep, arrived):
+        x = (keep + arrived)[0]
         bit = 1
         while bit < fine:
             x = x + flip_dp(x, bit)
             bit *= 2
-        return x
-
-    grad, gathered = halves(cotangent), True
-    sums = {}
-    for l in reversed(range(layers)):
+        return pin(x)
+
+    def hop(state, bit):
+        return state[0], flip_dp(state[1], fine << bit)
+
+    def all_sides(x):
+        far = flip(x, 2)
+        return [x, far, flip(x, 1), flip(far, 1)]
+
+    def feed_back(l, grad, gathered):
         k = kept[l]
-        g_feed, g_pre, g_mixed, g_attn, g_ctx, vec, pre_sum = feed_bwd(
-            ids, grad, gathered, k["norms"], k["slope"], weights, l
+        g_mixed, g_attn, g_ctx, vec, pre_sum, keep, send = feed_bwd(
+            clock[0], grad, gathered, k["norms"], k["slope"], k["act"], k["mixed"], k["ctx_own"],
+            k["ctx_shared"], weights, l,
         )
-        keep, send = feed_weights(ids, k["act"], g_feed, k["mixed"], g_pre)
-        sums[l, "feed"] = reduce_rest(reduce_start(keep, send))
-        shared_keep, shared_send, rel_shared = attention_bwd(
-            ids, True, tables, k["joint"], k["turned"], k["kv_far"], k["lse_shared"], g_ctx, rel_pairs, l
+        k["g_mixed"] = g_mixed
+        return g_attn, g_ctx, vec, pre_sum, (keep, flip(send, 1))
+
+    def attention_back(l, shared, g_ctx):
+        k = kept[l]
+        return attention_bwd(
+            clock[0], shared, tables, k["joint"], k["turned"], k["kv_far"] if shared else None,
+            k["lse_shared" if shared else "lse_own"], g_ctx, rel_pairs, l, l == 0,
         )
-        arrived = flip(shared_send, 1)
-        own_grads, rel_own = attention_bwd(
-            ids, False, tables, k["joint"], k["turned"], None, k["lse_own"], g_ctx, rel_pairs, l
+
+    def joint_back(l, own_grads, shared_keep, arrived, g_attn, rel_own, rel_shared, vec, pre_sum):
+        k = kept[l]
+        g_h, keep, send = joint_bwd(
+            clock[0], k["x"], k["gathered"], own_grads, shared_keep, arrived, w_qkv, g_attn, rel_own,
+            rel_shared, vec, pre_sum, l, l == 0,
         )
-        g_joint, g_h, joint_sum = joint_bwd(ids, own_grads, shared_keep, arrived, w_qkv, g_attn, l)
-        vectors = jnp.concatenate([vec, joint_sum[0:1, :width], joint_sum[0:1, 2 * width :]], 0)
-        order = [8, 9, 4, 0, 1, 2, 3, 5]
-        lines = jnp.stack([vectors[i] for i in order]).reshape(8, SUPER, width // SUPER)
-        lines = jnp.pad(jnp.transpose(lines, (1, 0, 2)), ((0, 0), (0, 0), (0, LANES - width // SUPER)))
-        lines = jnp.concatenate([lines, pre_sum[0].reshape(SUPER, 1, ff // SUPER)], 1)
-        small = jnp.pad(lines, ((0, 0), (0, 16 - 9), (0, 0))).astype(bf16)
-        keep, send = attention_weights(
-            ids, k["x"], k["gathered"], g_joint, k["ctx_own"], k["ctx_shared"], g_attn, rel_own,
-            rel_shared, small,
-        )
-        sums[l, "attention"] = reduce_rest(reduce_start(keep, send))
-        k["g_mixed"], k["g_h"] = g_mixed, g_h
-        grad, gathered = halves(g_h), False
+        k["g_h"] = g_h
+        return g_h, (keep, flip(send, 1))
+
+    g_attn, g_ctx, vec, pre_sum, f1 = feed_back(1, halves(cotangent), True)
+    shared_keep, shared_send, rel_shared = attention_back(1, True, g_ctx)
+    arrived = flip(shared_send, 1)
+    f1 = hop(absorb(*f1), 0)
+    own_grads, rel_own = attention_back(1, False, g_ctx)
+    g_h, a1 = joint_back(1, own_grads, shared_keep, arrived, g_attn, rel_own, rel_shared, vec, pre_sum)
+
+    f1 = hop(absorb(*f1), 1)
+    g_attn, g_ctx, vec, pre_sum, f0 = feed_back(0, halves(g_h), False)
+    f1 = hop(absorb(*f1), 2)
+    a1 = hop(absorb(*a1), 0)
+    shared_keep, shared_send, rel_shared = attention_back(0, True, g_ctx)
+    arrived = flip(shared_send, 1)
+    f0 = hop(absorb(*f0), 0)
+    own_grads, rel_own = attention_back(0, False, g_ctx)
+    f1 = last(*f1)
+    a1 = hop(absorb(*a1), 1)
+    f1 = all_sides(f1)
+    g_h, a0 = joint_back(0, own_grads, shared_keep, arrived, g_attn, rel_own, rel_shared, vec, pre_sum)
+    a1 = hop(absorb(*a1), 2)
+    a0 = hop(absorb(*a0), 0)
+    f0 = hop(absorb(*f0), 1)
+    a1 = all_sides(last(*a1))
+    a0 = hop(absorb(*a0), 1)
+    f0 = hop(absorb(*f0), 2)
+    a0 = hop(absorb(*a0), 2)
+    f0 = all_sides(last(*f0))
+    a0 = all_sides(last(*a0))
+    kept[0]["g_h"] = g_h + flip(g_h, 2)
 
     def of_layer(name):
         return jnp.where(side == 0, kept[0][name], kept[1][name])
@@ -914,64 +1068,37 @@
     row_counts = jnp.sum(valid_mask.astype(f32), 1)
     root_mean_squares = jnp.sqrt(square_rows / (width * jnp.maximum(row_counts, 1.0))[:, None])[None]
 
-    fine_at = dp_index % fine
-    core_rows = width // SUPER // 2
-    found = {}
-    for l in range(layers):
-        piece = jnp.concatenate([sums[l, "feed"], sums[l, "attention"]], 0)
-        far = flip(piece, 2)
-        sides = [jnp.where(side == 0, piece, far), jnp.where(side == 0, far, piece)]
-        both = jnp.stack(sides)
-        other = flip(both, 1)
-        found[l] = jnp.where(core == 0, jnp.stack([both, other]), jnp.stack([other, both])).astype(f32)
-
-    def fine_part(x, axis):
+    slab = width // SUPER
+    d_ffn_in, d_ffn_out, d_out = unpack(
+        unpack_feed_kernel, "unpack_feed", ids, f0 + f1,
+        [(2, slab, ff), (2, ff // SUPER, width), (2, slab, width)],
+    )
+    rel_rows = 128 // SUPER
+    d_qkv, d_rel, d_qv, d_out_bias, d_scale, d_shift, d_in_bias, d_ffn_bias = unpack(
+        unpack_attention_kernel, "unpack_attention", ids, a0 + a1,
+        [(2, slab, 3 * width), (2, width, rel_rows), (2, 2, slab), (2, slab),
+         (2, 2, slab), (2, 2, slab), (2, LANES), (2, slab)],
+    )
+
+    def own_part(x, axis):
         n = x.shape[axis] // fine
-        return x if fine == 1 else lax.dynamic_slice_in_dim(x, fine_at * n, n, axis)
-
-    def gather(l):
-        x = found[l]
-        ffn_out_t = x[:, :, : LANES // 2]
-        d_ffn_out = jnp.transpose(ffn_out_t, (3, 1, 0, 2)).reshape(LANES, width)
-        at = LANES // 2
-
-        def columns(at, groups):
-            part = x[:, :, at : at + groups * core_rows].reshape(2, 2, groups, core_rows, LANES)
-            part = jnp.transpose(part, (0, 3, 1, 2, 4))
-            return part.reshape(2 * core_rows, 2 * groups * LANES)
-
-        d_ffn_in = columns(at, 4)
-        at += 4 * core_rows
-        d_qkv = columns(at, 3)
-        at += 3 * core_rows
-        d_out = columns(at, 1)
-        at += core_rows
-        rel = jnp.concatenate([x[0, 0, at:], x[0, 1, at:]], 1)
-        small = x[1, 0, at:]
-        return (
-            fine_part(d_qkv, 0), small, fine_part(d_out, 0),
-            fine_part(rel.T, 1).reshape(width // 64, 64, -1), fine_part(d_ffn_in, 0),
-            fine_part(d_ffn_out, 0),
-        )
-
-    parts = [gather(l) for l in range(layers)]
-    stacked = [jnp.stack(pair) for pair in zip(*parts)]
-    d_qkv, small, d_out, d_rel, d_ffn_in, d_ffn_out = stacked
-    vector = lambda i: fine_part(small[:, i, : width // SUPER], 1)
+        return x if fine == 1 else lax.dynamic_slice_in_dim(x, (dp_index % fine) * n, n, axis)
+
+    d_rel = d_rel.reshape((2,) + rel_proj.shape[1:3] + (rel_rows,))
     return (
         section_outs,
         in_grads,
-        d_qkv,
-        jnp.stack([vector(0), vector(1)], 1),
-        d_out,
-        vector(2),
-        d_rel,
-        jnp.stack([vector(3), vector(4)], 1),
-        jnp.stack([vector(5), vector(6)], 1),
-        d_ffn_in,
-        fine_part(small[:, 8], 1),
-        d_ffn_out,
-        vector(7),
+        own_part(d_qkv, 1),
+        own_part(d_qv, 2),
+        own_part(d_out, 1),
+        own_part(d_out_bias, 1),
+        own_part(d_rel, 3),
+        own_part(d_scale, 2),
+        own_part(d_shift, 2),
+        own_part(d_ffn_in, 1),
+        own_part(d_in_bias, 1),
+        own_part(d_ffn_out, 1),
+        own_part(d_ffn_bias, 1),
         root_mean_squares,
     )
 

time: 478 us -> 398 us (0.83)
  waiting for transfers between devices: 98.2 us -> 58.5 us
  local copies, waits for them, and re-layouts: 31.8 us -> 8.22 us
  Pallas kernels: 287 us -> 265 us
    ppermute x12, waiting for transfers between devices: 90.1 us -> 52.2 us  [flip_dp(): return lax.ppermute(x, 'dp', [(i, i ^ bit) for i in range(dp)])]
    pallas_call x23 -> x21, Pallas kernels: 287 us -> 265 us  [call(): pl.pallas_call(kernel, grid_spec=pltpu.PrefetchScalarGridSpec(num_scalar_...]
    add x12, other arithmetic: 9.41 us -> 19.1 us  [absorb(): return pin((keep[:n] + arrived[:n], keep[n:] + arrived[n:]))]
    another operation x15 -> x0, other arithmetic: 9.41 us -> none  [the longest x6 4.48 us: body(): stacked = [jnp.stack(pair) for pair in zip(*parts)]]
    another operation x10 -> x0, local copies, waits for them, and re-layouts: 5.9 us -> none  [the longest x8 5.83 us: body(): stacked = [jnp.stack(pair) for pair in zip(*parts)]]
    unnamed x61 -> x45, local copies, waits for them, and re-layouts: 11.2 us -> 8.14 us
  transfers between devices with their start and end apart: 27 -> 36, of which waited for: 8 -> 11; matrix products, arithmetic and copies ran while one was open for 5% -> 9% of each run, Pallas kernels for 34% -> 35%
where the time goes in v3:
time: 398 us; the launch traced here: 392 us
  Pallas kernels  265 us (67%)
  waiting for transfers between devices  58.5 us (15%)
  other arithmetic  32.2 us (8%)
  starting transfers between devices  26.3 us (7%)
  local copies, waits for them, and re-layouts  8.22 us (2%)
    pallas_call x21, Pallas kernels, call(): pl.pallas_call(kernel, grid_spec=pltpu.PrefetchScalarGridSpec(num_scalar_...  265 us
    ppermute x12, waiting for transfers between devices, flip_dp(): return lax.ppermute(x, 'dp', [(i, i ^ bit) for i in range(dp)])  52.2 us
    add x12, other arithmetic, absorb(): return pin((keep[:n] + arrived[:n], keep[n:] + arrived[n:]))  19.1 us
    ppermute x12, starting transfers between devices, flip_dp(): return lax.ppermute(x, 'dp', [(i, i ^ bit) for i in range(dp)])  19 us
    unnamed x45, local copies, waits for them, and re-layouts  8.14 us
  transfers between devices with their start and end apart: 36, of which 11 were waited for; matrix products, arithmetic and copies ran while one was open for 9% of the time, Pallas kernels for 35%

profile of v3, /device:TPU:0, one launch (start us, length us, event | category | flops | bytes accessed | tf_op | source)
XLA Modules:
  0.0 391.6 jit_solution(15410853146225029596)
XLA Ops:
  2.6 4.2 %tables.1 = (f32[64,1024]{1,0:T(8,128)}, f32[64,1024]{1,0:T(8,128)}, bf16[1024,128]{1,0:T(8,128)(2,1)}, f32[1024,128]{1,0:T(8,128)}, f32[1024,128]{1,0:T(8,128)}...) custom-call(s32[3]{0:T(128)} %pad_add_fusion.ids, s32[4,3,512]{2,1,0:T(4,128)} %copy.33.boxes_ref, ...), custom_call_target="tpu_custom_call" | custom-call | flops 4400000000 | bytes 4000000 | tf_op jit(solution)/shard_map/tables/pallas_call | solution.py:82
  6.8 9.9 %projections.2 = (bf16[768,2304]{1,0:T(8,128)(2,1)}, bf16[768,1536]{1,0:T(8,128)(2,1)}, bf16[256,1536]{1,0:T(8,128)(2,1)}) custom-call(s32[3]{0:T(128)} %pad_add_fusion.ids, bf16[6,256,768]{2,1,0:T(8,128)(2,1)} %bitcast.51, bf16[6,256,768]{2,1,0:T(8,128)(2,1)} %bitcast.52, bf16[6,256,768]{2,1,0:T(8,128)(2,1)} %bitcast.53, bf16[2,768,2304]{2,1,0:T(8,128)(2,1)} %w_ref.7, ...), custom_call_target="tpu_custom_call" | custom-call | flops 8800000000 | bytes 8000000 | tf_op jit(solution)/shard_map/projections/pallas_call | solution.py:82
  17.1 8.6 %attention_forward.4 = (bf16[768,512]{1,0:T(8,128)(2,1)}, f32[6,2,512]{2,1,0:T(2,128)}) custom-call(s32[3]{0:T(128)} %pad_add_fusion.ids, f32[1024,128]{1,0:T(8,128)} %get-tuple-element.127.code_ref, f32[8,1024]{1,0:T(8,128)} %get-tuple-element.128.seg_ref, bf16[1024,128]{1,0:T(8,128)(2,1)} %get-tuple-element.129.kf_ref, ...), custom_call_target="tpu_custom_call" | custom-call | flops 7699999744 | bytes 7000000 | tf_op jit(solution)/shard_map/attention_forward/pallas_call | solution.py:82
  26.7 6.3 %attention_forward.5 = (bf16[768,256]{1,0:T(8,128)(2,1)}, f32[6,2,256]{2,1,0:T(2,128)}) custom-call(s32[3]{0:T(128)} %pad_add_fusion.ids, f32[1024,128]{1,0:T(8,128)} %get-tuple-element.127.code_ref, f32[8,1024]{1,0:T(8,128)} %get-tuple-element.128.seg_ref, bf16[1024,128]{1,0:T(8,128)(2,1)} %get-tuple-element.129.kf_ref, ...), custom_call_target="tpu_custom_call" | custom-call | flops 7699999744 | bytes 7000000 | tf_op jit(solution)/shard_map/attention_forward/pallas_call | solution.py:82
  33.0 27.6 %feed_forward.2 = (bf16[768,768]{1,0:T(8,128)(2,1)}, f32[768,128]{1,0:T(8,128)}, bf16[768,768]{1,0:T(8,128)(2,1)}, f32[768,128]{1,0:T(8,128)}, bf16[768,768]{1,0...) custom-call(s32[3]{0:T(128)} %pad_add_fusion.ids, ...), custom_call_target="tpu_custom_call" | custom-call | flops 26400000000 | bytes 24000000 | tf_op jit(solution)/shard_map/feed_forward/pallas_call | solution.py:82
  60.5 9.9 %projections.3 = (bf16[768,2304]{1,0:T(8,128)(2,1)}, bf16[768,1536]{1,0:T(8,128)(2,1)}, bf16[256,1536]{1,0:T(8,128)(2,1)}) custom-call(s32[3]{0:T(128)} %pad_add_fusion.ids, bf16[3,256,768]{2,1,0:T(8,128)(2,1)} %bitcast.34, bf16[3,256,768]{2,1,0:T(8,128)(2,1)} %bitcast.35, bf16[3,256,768]{2,1,0:T(8,128)(2,1)} %bitcast.36, bf16[2,768,2304]{2,1,0:T(8,128)(2,1)} %w_ref.7, ...), custom_call_target="tpu_custom_call" | custom-call | flops 8800000000 | bytes 8000000 | tf_op jit(solution)/shard_map/projections/pallas_call | solution.py:82
  70.6 8.8 %attention_forward.6 = (bf16[768,512]{1,0:T(8,128)(2,1)}, f32[6,2,512]{2,1,0:T(2,128)}) custom-call(s32[3]{0:T(128)} %pad_add_fusion.ids, f32[1024,128]{1,0:T(8,128)} %get-tuple-element.127.code_ref, f32[8,1024]{1,0:T(8,128)} %get-tuple-element.128.seg_ref, bf16[1024,128]{1,0:T(8,128)(2,1)} %get-tuple-element.129.kf_ref, ...), custom_call_target="tpu_custom_call" | custom-call | flops 7699999744 | bytes 7000000 | tf_op jit(solution)/shard_map/attention_forward/pallas_call | solution.py:82
  80.3 6.3 %attention_forward.7 = (bf16[768,256]{1,0:T(8,128)(2,1)}, f32[6,2,256]{2,1,0:T(2,128)}) custom-call(s32[3]{0:T(128)} %pad_add_fusion.ids, f32[1024,128]{1,0:T(8,128)} %get-tuple-element.127.code_ref, f32[8,1024]{1,0:T(8,128)} %get-tuple-element.128.seg_ref, bf16[1024,128]{1,0:T(8,128)(2,1)} %get-tuple-element.129.kf_ref, ...), custom_call_target="tpu_custom_call" | custom-call | flops 7699999744 | bytes 7000000 | tf_op jit(solution)/shard_map/attention_forward/pallas_call | solution.py:82
  86.6 27.3 %feed_forward.3 = (bf16[768,768]{1,0:T(8,128)(2,1)}, f32[768,128]{1,0:T(8,128)}, bf16[768,768]{1,0:T(8,128)(2,1)}, f32[768,128]{1,0:T(8,128)}, bf16[768,768]{1,0...) custom-call(s32[3]{0:T(128)} %pad_add_fusion.ids, ...), custom_call_target="tpu_custom_call" | custom-call | flops 26400000000 | bytes 24000000 | tf_op jit(solution)/shard_map/feed_forward/pallas_call | solution.py:82
  114.0 32.0 %feed_backward.2 = (bf16[768,768]{1,0:T(8,128)(2,1)}, bf16[768,768]{1,0:T(8,128)(2,1)}, bf16[768,768]{1,0:T(8,128)(2,1)}, f32[8,768]{1,0:T(8,128)}, f32[8,3072]{...) custom-call(s32[3]{0:T(128)} %pad_add_fusion.ids, bf16[6,256,768]{2,1,0:T(8,128)(2,1)} %bitcast.48, ...), custom_call_target="tpu_custom_call" | custom-call | flops 32999999488 | bytes 30000000 | tf_op jit(solution)/shard_map/feed_backward/pallas_call | solution.py:82
  146.5 11.1 %attention_backward.5 = (bf16[3,256,768]{2,1,0:T(8,128)(2,1)}, bf16[2,256,768]{2,1,0:T(8,128)(2,1)}, f32[128,768]{1,0:T(8,128)}) custom-call(s32[3]{0:T(128)} %pad_add_fusion.ids, f32[1024,128]{1,0:T(8,128)} %get-tuple-element.127.code_ref, f32[8,1024]{1,0:T(8,128)} %get-tuple-element.128.seg_ref, bf16[1024,128]{1,0:T(8,128)(2,1)} %get-tuple-element.129.kf_ref, ...), custom_call_target="tpu_custom_call" | custom-call | flops 13200000000 | bytes 12000000 | tf_op jit(solution)/shard_map/attention_backward/pallas_call | solution.py:82
  157.8 3.9 slice_add_fusion.2
  161.7 2.9 collective-permute-start.4
  164.6 16.4 %attention_backward.4 = (bf16[3,512,768]{2,1,0:T(8,128)(2,1)}, f32[128,768]{1,0:T(8,128)}) custom-call(s32[3]{0:T(128)} %pad_add_fusion.ids, f32[1024,128]{1,0:T(8,128)} %get-tuple-element.127.code_ref, f32[8,1024]{1,0:T(8,128)} %get-tuple-element.128.seg_ref, bf16[1024,128]{1,0:T(8,128)(2,1)} %get-tuple-element.129.kf_ref, ...), custom_call_target="tpu_custom_call" | custom-call | flops 13200000000 | bytes 12000000 | tf_op jit(solution)/shard_map/attention_backward/pallas_call | solution.py:82
  181.0 13.6 %projections_backward.2 = (bf16[768,768]{1,0:T(8,128)(2,1)}, bf16[8,160,384]{2,1,0:T(8,128)(2,1)}, bf16[8,160,384]{2,1,0:T(8,128)(2,1)}) custom-call(s32[3]{0:T(128)} %pad_add_fusion.ids, bf16[3,256,768]{2,1,0:T(8,128)(2,1)} %bitcast.40, bf16[3,256,768]{2,1,0:T(8,128)(2,1)} %bitcast.41, bf16[3,256,768]{2,1,0:T(8,128)(2,1)} %bitcast.42, ...), custom_call_target="tpu_custom_call" | custom-call | flops 13200000000 | bytes 12000000 | tf_op jit(solution)/shard_map/projections_backward/pallas_call | solution.py:82
  194.6 2.4 slice_add_fusion.6
  197.0 32.1 %feed_backward.3 = (bf16[768,768]{1,0:T(8,128)(2,1)}, bf16[768,768]{1,0:T(8,128)(2,1)}, bf16[768,768]{1,0:T(8,128)(2,1)}, f32[8,768]{1,0:T(8,128)}, f32[8,3072]{...) custom-call(s32[3]{0:T(128)} %pad_add_fusion.ids, bf16[3,256,768]{2,1,0:T(8,128)(2,1)} %bitcast.30, ...), custom_call_target="tpu_custom_call" | custom-call | flops 32999999488 | bytes 30000000 | tf_op jit(solution)/shard_map/feed_backward/pallas_call | solution.py:82
  229.6 1.6 collective-permute-start.5
  231.6 2.4 slice_add_fusion.10
  233.9 12.6 %collective-permute-done.5 = bf16[2,432,384]{2,1,0:T(8,128)(2,1)S(1)} collective-permute-done((bf16[2,432,384]{2,1,0:T(8,128)(2,1)S(1)}, bf16[2,432,384]{2,1,0:T(8,128)(2,1)S(1)}, u32[]{:S(2)}, u32[]{:S(2)}) %collective-permute-start.5) | collective-permute-done | bytes 663584 | tf_op jit(solution)/shard_map/ppermute | solution.py:947
  246.6 2.7 collective-permute-start.9
  250.6 7.4 %attention_backward.7 = (bf16[3,256,384]{2,1,0:T(8,128)(2,1)}, bf16[2,256,384]{2,1,0:T(8,128)(2,1)}, f32[128,384]{1,0:T(8,128)}) custom-call(s32[3]{0:T(128)} %pad_add_fusion.ids, f32[1024,128]{1,0:T(8,128)} %get-tuple-element.127.code_ref, f32[8,1024]{1,0:T(8,128)} %get-tuple-element.128.seg_ref, bf16[1024,128]{1,0:T(8,128)(2,1)} %get-tuple-element.129.kf_ref, ...), custom_call_target="tpu_custom_call" | custom-call | flops 13200000000 | bytes 12000000 | tf_op jit(solution)/shard_map/attention_backward/pallas_call | solution.py:82
  258.1 5.6 %collective-permute-done.9 = bf16[1,432,384]{2,1,0:T(8,128)(2,1)} collective-permute-done((bf16[1,432,384]{2,1,0:T(8,128)(2,1)S(1)}, bf16[1,432,384]{2,1,0:T(8,128)(2,1)}, u32[]{:S(2)}, u32[]{:S(2)}) %collective-permute-start.9) | collective-permute-done | bytes 331808 | tf_op jit(solution)/shard_map/ppermute | solution.py:947
  265.6 3.9 slice_add_fusion
  269.5 1.7 collective-permute-start.26
  271.2 9.9 %attention_backward.6 = (bf16[3,512,384]{2,1,0:T(8,128)(2,1)}, f32[128,384]{1,0:T(8,128)}) custom-call(s32[3]{0:T(128)} %pad_add_fusion.ids, f32[1024,128]{1,0:T(8,128)} %get-tuple-element.127.code_ref, f32[8,1024]{1,0:T(8,128)} %get-tuple-element.128.seg_ref, bf16[1024,128]{1,0:T(8,128)(2,1)} %get-tuple-element.129.kf_ref, ...), custom_call_target="tpu_custom_call" | custom-call | flops 13200000000 | bytes 12000000 | tf_op jit(solution)/shard_map/attention_backward/pallas_call | solution.py:82
  281.1 12.2 %projections_backward.3 = (bf16[768,768]{1,0:T(8,128)(2,1)}, bf16[8,160,384]{2,1,0:T(8,128)(2,1)}, bf16[8,160,384]{2,1,0:T(8,128)(2,1)}) custom-call(s32[3]{0:T(128)} %pad_add_fusion.ids, bf16[6,256,768]{2,1,0:T(8,128)(2,1)} %bitcast.57, bf16[6,256,768]{2,1,0:T(8,128)(2,1)} %bitcast.58, bf16[6,256,768]{2,1,0:T(8,128)(2,1)} %bitcast.59, ...), custom_call_target="tpu_custom_call" | custom-call | flops 13200000000 | bytes 12000000 | tf_op jit(solution)/shard_map/projections_backward/pallas_call | solution.py:82
  293.3 3.4 broadcast_select_fusion.5
  300.3 5.0 %collective-permute-done.21 = bf16[2,160,384]{2,1,0:T(8,128)(2,1)} collective-permute-done((bf16[2,160,384]{2,1,0:T(8,128)(2,1)S(1)}, bf16[2,160,384]{2,1,0:T(8,128)(2,1)}, u32[]{:S(2)}, u32[]{:S(2)}) %collective-permute-start.21) | collective-permute-done | bytes 245792 | tf_op jit(solution)/shard_map/ppermute | solution.py:947
  306.2 2.4 collective-permute-start.22
  308.6 1.6 slice_add_fusion.8
  310.6 3.7 collective-permute-done.22
  316.5 1.6 slice_add_fusion.4
  318.8 3.8 collective-permute-done.15
  324.2 3.4 collective-permute-done.12
  327.6 1.8 broadcast_select_fusion.3
  329.4 9.6 %collective-permute-done.16 = bf16[2,160,384]{2,1,0:T(8,128)(2,1)S(1)} collective-permute-done((bf16[2,160,384]{2,1,0:T(8,128)(2,1)S(1)}, bf16[2,160,384]{2,1,0:T(8,128)(2,1)S(1)}, u32[]{:S(2)}, u32[]{:S(2)}) %collective-permute-start.16) | collective-permute-done | bytes 245792 | tf_op jit(solution)/shard_map/ppermute | solution.py:947
  339.7 3.2 collective-permute-start.17
  343.7 5.5 %place_rows.2 = bf16[6,256,768]{2,1,0:T(8,128)(2,1)} custom-call(s32[3]{0:T(128)} %pad_add_fusion.ids, bf16[3,256,768]{2,1,0:T(8,128)(2,1)} %bitcast.43, bf16[3,256,768]{2,1,0:T(8,128)(2,1)} %bitcast.7.other_ref), custom_call_target="tpu_custom_call" | custom-call | flops 4400000000 | bytes 4000000 | tf_op jit(solution)/shard_map/place_rows/pallas_call | solution.py:82
  349.7 6.8 %collective-permute-done.17 = bf16[1,160,384]{2,1,0:T(8,128)(2,1)} collective-permute-done((bf16[1,160,384]{2,1,0:T(8,128)(2,1)}, bf16[1,160,384]{2,1,0:T(8,128)(2,1)}, u32[]{:S(2)}, u32[]{:S(2)}) %collective-permute-start.17) | collective-permute-done | bytes 122912 | tf_op jit(solution)/shard_map/ppermute | solution.py:947
  357.5 5.2 %collective-permute-done.28 = bf16[1,432,384]{2,1,0:T(8,128)(2,1)} collective-permute-done((bf16[1,432,384]{2,1,0:T(8,128)(2,1)}, bf16[1,432,384]{2,1,0:T(8,128)(2,1)}, u32[]{:S(2)}, u32[]{:S(2)}) %collective-permute-start.28) | collective-permute-done | bytes 331808 | tf_op jit(solution)/shard_map/ppermute | solution.py:947
  363.1 1.7 add_bitcast_fusion.refs_0_
  364.8 2.7 collective-permute-done.18.refs_1_
  368.0 2.6 broadcast_select_fusion.4
  371.9 3.8 unpack_attention.1
  375.8 2.1 copy.34
  378.4 6.6 %place_rows.3 = f32[6,256,768]{2,1,0:T(8,128)} custom-call(s32[3]{0:T(128)} %pad_add_fusion.ids, bf16[3,256,768]{2,1,0:T(8,128)(2,1)} %bitcast.33, bf16[3,256,768]{2,1,0:T(8,128)(2,1)} %bitcast.13.other_ref), custom_call_target="tpu_custom_call" | custom-call | flops 4400000000 | bytes 4000000 | tf_op jit(solution)/shard_map/place_rows/pallas_call | solution.py:82
  385.9 5.5 %unpack_feed.1 = (f32[2,96,3072]{2,1,0:T(8,128)}, f32[2,384,768]{2,1,0:T(8,128)}, f32[2,96,768]{2,1,0:T(8,128)}) custom-call(s32[3]{0:T(128)} %pad_add_fusion.ids, bf16[432,384]{1,0:T(8,128)(2,1)} %add_bitcast_fusion.refs_0_, bf16[432,384]{1,0:T(8,128)(2,1)} %copy-done.14, bf16[432,384]{1,0:T(8,128)(2,1)} %copy-done.17, ...), custom_call_target="tpu_custom_call" | custom-call | flops 4400000000 | bytes 4000000 | tf_op jit(solution)/shard_map/unpack_feed/pallas_call | solution.py:82
  (118 shorter events, 25.3 us)
Async XLA Ops:
  16.7 9.1 %collective-permute-start = (bf16[256,1536]{1,0:T(8,128)(2,1)}, bf16[256,1536]{1,0:T(8,128)(2,1)S(1)}, u32[]{:S(2)}, u32[]{:S(2)}) collective-permute-start(bf16[256,1536]{1,0:T(8,128)(2,1)} %get-tuple-element.135), channel_id=1, source_target_pairs={{0,1},{1,0},{2,3},{3,2},{4,5},{5,4},{6,7},{7,6},{8,9},{9,8},{10,11... | collective-permute-start | bytes 2359304 | tf_op jit(solution)/shard_map/ppermute | solution.py:944
  70.5 8.9 %collective-permute-start.1 = (bf16[256,1536]{1,0:T(8,128)(2,1)}, bf16[256,1536]{1,0:T(8,128)(2,1)S(1)}, u32[]{:S(2)}, u32[]{:S(2)}) collective-permute-start(bf16[256,1536]{1,0:T(8,128)(2,1)} %get-tuple-element.143), channel_id=1, source_target_pairs={{0,1},{1,0},{2,3},{3,2},{4,5},{5,4},{6,7},{7,6},{8,9},{9,8},{10,11... | collective-permute-start | bytes 2359304 | tf_op jit(solution)/shard_map/ppermute | solution.py:944
  146.0 11.8 %collective-permute-start.3 = (bf16[8,432,384]{2,1,0:T(8,128)(2,1)}, bf16[8,432,384]{2,1,0:T(8,128)(2,1)}, u32[]{:S(2)}, u32[]{:S(2)}) collective-permute-start(bf16[8,432,384]{2,1,0:T(8,128)(2,1)} %get-tuple-element.154), channel_id=1, source_target_pairs={{0,1},{1,0},{2,3},{3,2},{4,5},{5,4},{6,7},{7,6},{8,9},{9,8},{10,11... | collective-permute-start | bytes 7962632 | tf_op jit(solution)/shard_map/ppermute | solution.py:944
  157.6 23.3 %collective-permute-start.6 = (bf16[2,256,768]{2,1,0:T(8,128)(2,1)}, bf16[2,256,768]{2,1,0:T(8,128)(2,1)}, u32[]{:S(2)}, u32[]{:S(2)}) collective-permute-start(bf16[2,256,768]{2,1,0:T(8,128)(2,1)} %get-tuple-element.169), channel_id=1, source_target_pairs={{0,1},{1,0},{2,3},{3,2},{4,5},{5,4},{6,7},{7,6},{8,9},{9,8},{10,11... | collective-permute-start | bytes 2359304 | tf_op jit(solution)/shard_map/ppermute | solution.py:944
  161.7 32.9 %collective-permute-start.4 = (bf16[4,432,384]{2,1,0:T(8,128)(2,1)}, bf16[4,432,384]{2,1,0:T(8,128)(2,1)}, u32[]{:S(2)}, u32[]{:S(2)}) collective-permute-start(bf16[4,432,384]{2,1,0:T(8,128)(2,1)} %get-tuple-element.157), channel_id=1, source_target_pairs={{0,4},{4,0},{8,12},{12,8},{16,20},{20,16},{24,28},{28,24},{1,5},{5... | collective-permute-start | bytes 3981320 | tf_op jit(solution)/shard_map/ppermute | solution.py:947
  194.6 37.0 %collective-permute-start.7 = (bf16[8,160,384]{2,1,0:T(8,128)(2,1)}, bf16[8,160,384]{2,1,0:T(8,128)(2,1)}, u32[]{:S(2)}, u32[]{:S(2)}) collective-permute-start(bf16[8,160,384]{2,1,0:T(8,128)(2,1)} %get-tuple-element.176), channel_id=1, source_target_pairs={{0,1},{1,0},{2,3},{3,2},{4,5},{5,4},{6,7},{7,6},{8,9},{9,8},{10,11... | collective-permute-start | bytes 2949128 | tf_op jit(solution)/shard_map/ppermute | solution.py:944
  196.9 32.7 %copy-start.5 = (bf16[2,432,384]{2,1,0:T(8,128)(2,1)S(1)}, bf16[2,432,384]{2,1,0:T(8,128)(2,1)}, u32[]{:S(2)}) copy-start(bf16[2,432,384]{2,1,0:T(8,128)(2,1)} %get-tuple-element.160) | copy-start | bytes 1990660
  197.0 34.2 %copy-start.11 = (s32[3,512]{1,0:T(4,128)S(1)}, s32[3,512]{1,0:T(4,128)}, u32[]{:S(2)}) copy-start(s32[3,512]{1,0:T(4,128)} %valid_ref.1) | copy-start | bytes 18436
  197.0 34.4 %copy-start.9 = (f32[8,768]{1,0:T(8,128)S(1)}, f32[8,768]{1,0:T(8,128)}, u32[]{:S(2)}) copy-start(f32[8,768]{1,0:T(8,128)} %get-tuple-element.238) | copy-start | bytes 73732
  197.0 34.4 %copy-start.10 = (f32[8,768]{1,0:T(8,128)S(1)}, f32[8,768]{1,0:T(8,128)}, u32[]{:S(2)}) copy-start(f32[8,768]{1,0:T(8,128)} %get-tuple-element.239) | copy-start | bytes 73732
  229.1 36.5 %collective-permute-start.8 = (bf16[8,432,384]{2,1,0:T(8,128)(2,1)}, bf16[8,432,384]{2,1,0:T(8,128)(2,1)}, u32[]{:S(2)}, u32[]{:S(2)}) collective-permute-start(bf16[8,432,384]{2,1,0:T(8,128)(2,1)} %get-tuple-element.186), channel_id=1, source_target_pairs={{0,1},{1,0},{2,3},{3,2},{4,5},{5,4},{6,7},{7,6},{8,9},{9,8},{10,11... | collective-permute-start | bytes 7962632 | tf_op jit(solution)/shard_map/ppermute | solution.py:944
  229.6 16.9 %collective-permute-start.5 = (bf16[2,432,384]{2,1,0:T(8,128)(2,1)S(1)}, bf16[2,432,384]{2,1,0:T(8,128)(2,1)S(1)}, u32[]{:S(2)}, u32[]{:S(2)}) collective-permute-start(bf16[2,432,384]{2,1,0:T(8,128)(2,1)S(1)} %copy-done.5), channel_id=1, source_target_pairs={{0,8},{4,12},{8,0},{12,4},{16,24},{20,28},{24,16},{28,20},{1,9},{5... | collective-permute-start | bytes 1990664 | tf_op jit(solution)/shard_map/ppermute | solution.py:947
  231.6 65.6 %collective-permute-start.35 = (f32[2,2,2]{2,1,0:T(2,128)S(1)}, f32[2,2,2]{2,1,0:T(2,128)S(1)}, u32[]{:S(2)}, u32[]{:S(2)}) collective-permute-start(f32[2,2,2]{2,1,0:T(2,128)S(1)} %reshape.224), channel_id=1, source_target_pairs={{0,1},{1,0},{2,3},{3,2},{4,5},{5,4},{6,7},{7,6},{8,9},{9,8},{10,11... | collective-permute-start | bytes 104 | tf_op jit(solution)/shard_map/ppermute | solution.py:944
  246.6 17.1 %collective-permute-start.9 = (bf16[1,432,384]{2,1,0:T(8,128)(2,1)S(1)}, bf16[1,432,384]{2,1,0:T(8,128)(2,1)}, u32[]{:S(2)}, u32[]{:S(2)}) collective-permute-start(bf16[1,432,384]{2,1,0:T(8,128)(2,1)S(1)} %get-tuple-element.189), channel_id=1, source_target_pairs={{0,16},{4,20},{8,24},{12,28},{16,0},{20,4},{24,8},{28,12},{1,17},{... | collective-permute-start | bytes 995336 | tf_op jit(solution)/shard_map/ppermute | solution.py:947
  249.3 15.5 %collective-permute-start.10 = (bf16[4,160,384]{2,1,0:T(8,128)(2,1)}, bf16[4,160,384]{2,1,0:T(8,128)(2,1)S(1)}, u32[]{:S(2)}, u32[]{:S(2)}) collective-permute-start(bf16[4,160,384]{2,1,0:T(8,128)(2,1)} %get-tuple-element.192), channel_id=1, source_target_pairs={{0,4},{4,0},{8,12},{12,8},{16,20},{20,16},{24,28},{28,24},{1,5},{5... | collective-permute-start | bytes 1474568 | tf_op jit(solution)/shard_map/ppermute | solution.py:947
  258.0 23.1 %collective-permute-start.11 = (bf16[2,256,384]{2,1,0:T(8,128)(2,1)}, bf16[2,256,384]{2,1,0:T(8,128)(2,1)}, u32[]{:S(2)}, u32[]{:S(2)}) collective-permute-start(bf16[2,256,384]{2,1,0:T(8,128)(2,1)} %get-tuple-element.199), channel_id=1, source_target_pairs={{0,1},{1,0},{2,3},{3,2},{4,5},{5,4},{6,7},{7,6},{8,9},{9,8},{10,11... | collective-permute-start | bytes 1179656 | tf_op jit(solution)/shard_map/ppermute | solution.py:944
  264.8 105.9 %copy-start.6 = (bf16[432,384]{1,0:T(8,128)(2,1)}, bf16[432,384]{1,0:T(8,128)(2,1)S(1)}, u32[]{:S(2)}) copy-start(bf16[432,384]{1,0:T(8,128)(2,1)S(1)} %add_bitcast_fusion.1.refs_4_) | copy-start | bytes 995332
  269.5 47.0 %collective-permute-start.26 = (bf16[4,432,384]{2,1,0:T(8,128)(2,1)}, bf16[4,432,384]{2,1,0:T(8,128)(2,1)}, u32[]{:S(2)}, u32[]{:S(2)}) collective-permute-start(bf16[4,432,384]{2,1,0:T(8,128)(2,1)} %get-tuple-element.223), channel_id=1, source_target_pairs={{0,4},{4,0},{8,12},{12,8},{16,20},{20,16},{24,28},{28,24},{1,5},{5... | collective-permute-start | bytes 3981320 | tf_op jit(solution)/shard_map/ppermute | solution.py:947
  293.3 15.4 %collective-permute-start.14 = (bf16[8,160,384]{2,1,0:T(8,128)(2,1)}, bf16[8,160,384]{2,1,0:T(8,128)(2,1)}, u32[]{:S(2)}, u32[]{:S(2)}) collective-permute-start(bf16[8,160,384]{2,1,0:T(8,128)(2,1)} %get-tuple-element.209), channel_id=1, source_target_pairs={{0,1},{1,0},{2,3},{3,2},{4,5},{5,4},{6,7},{7,6},{8,9},{9,8},{10,11... | collective-permute-start | bytes 2949128 | tf_op jit(solution)/shard_map/ppermute | solution.py:944
  293.3 5.5 %copy-start.4 = (bf16[768,768]{1,0:T(8,128)(2,1)S(1)}, bf16[768,768]{1,0:T(8,128)(2,1)}, u32[]{:S(2)}) copy-start(bf16[768,768]{1,0:T(8,128)(2,1)} %get-tuple-element.205) | copy-start | bytes 3538948
  296.7 47.0 %collective-permute-start.2 = (bf16[768,768]{1,0:T(8,128)(2,1)}, bf16[768,768]{1,0:T(8,128)(2,1)}, u32[]{:S(2)}, u32[]{:S(2)}) collective-permute-start(bf16[768,768]{1,0:T(8,128)(2,1)} %get-tuple-element.277), channel_id=1, source_target_pairs={{0,1},{1,0},{2,3},{3,2},{4,5},{5,4},{6,7},{7,6},{8,9},{9,8},{10,11... | collective-permute-start | bytes 3538952 | tf_op jit(solution)/shard_map/ppermute | solution.py:944
  297.2 8.1 %collective-permute-start.21 = (bf16[2,160,384]{2,1,0:T(8,128)(2,1)S(1)}, bf16[2,160,384]{2,1,0:T(8,128)(2,1)}, u32[]{:S(2)}, u32[]{:S(2)}) collective-permute-start(bf16[2,160,384]{2,1,0:T(8,128)(2,1)S(1)} %copy-done.7), channel_id=1, source_target_pairs={{0,8},{4,12},{8,0},{12,4},{16,24},{20,28},{24,16},{28,20},{1,9},{5... | collective-permute-start | bytes 737288 | tf_op jit(solution)/shard_map/ppermute | solution.py:947
  298.7 28.9 %collective-permute-start.12 = (bf16[768,768]{1,0:T(8,128)(2,1)S(1)}, bf16[768,768]{1,0:T(8,128)(2,1)S(1)}, u32[]{:S(2)}, u32[]{:S(2)}) collective-permute-start(bf16[768,768]{1,0:T(8,128)(2,1)S(1)} %copy-done.4), channel_id=1, source_target_pairs={{0,2},{1,3},{2,0},{3,1},{4,6},{5,7},{6,4},{7,5},{8,10},{9,11},{10,... | collective-permute-start | bytes 3538952 | tf_op jit(solution)/shard_map/ppermute | solution.py:944
  306.2 8.0 %collective-permute-start.22 = (bf16[1,160,384]{2,1,0:T(8,128)(2,1)S(1)}, bf16[1,160,384]{2,1,0:T(8,128)(2,1)S(1)}, u32[]{:S(2)}, u32[]{:S(2)}) collective-permute-start(bf16[1,160,384]{2,1,0:T(8,128)(2,1)S(1)} %get-tuple-element.219), channel_id=1, source_target_pairs={{0,16},{4,20},{8,24},{12,28},{16,0},{20,4},{24,8},{28,12},{1,17},{... | collective-permute-start | bytes 368648 | tf_op jit(solution)/shard_map/ppermute | solution.py:947
  310.2 12.4 %collective-permute-start.15 = (bf16[4,160,384]{2,1,0:T(8,128)(2,1)S(1)}, bf16[4,160,384]{2,1,0:T(8,128)(2,1)S(1)}, u32[]{:S(2)}, u32[]{:S(2)}) collective-permute-start(bf16[4,160,384]{2,1,0:T(8,128)(2,1)S(1)} %get-tuple-element.211), channel_id=1, source_target_pairs={{0,4},{4,0},{8,12},{12,8},{16,20},{20,16},{24,28},{28,24},{1,5},{5... | collective-permute-start | bytes 1474568 | tf_op jit(solution)/shard_map/ppermute | solution.py:947
  314.9 34.8 %collective-permute-start.23 = (bf16[160,384]{1,0:T(8,128)(2,1)}, bf16[160,384]{1,0:T(8,128)(2,1)}, u32[]{:S(2)}, u32[]{:S(2)}) collective-permute-start(bf16[160,384]{1,0:T(8,128)(2,1)} %add_bitcast_fusion.2.refs_4_), channel_id=1, source_target_pairs={{0,2},{1,3},{2,0},{3,1},{4,6},{5,7},{6,4},{7,5},{8,10},{9,11},{10,... | collective-permute-start | bytes 368648 | tf_op jit(solution)/shard_map/ppermute | solution.py:944
  316.5 11.1 %copy-start.1 = (bf16[768,768]{1,0:T(8,128)(2,1)S(1)}, bf16[768,768]{1,0:T(8,128)(2,1)}, u32[]{:S(2)}) copy-start(bf16[768,768]{1,0:T(8,128)(2,1)} %get-tuple-element.206) | copy-start | bytes 3538948
  316.5 11.1 %copy-start.3 = (bf16[768,768]{1,0:T(8,128)(2,1)S(1)}, bf16[768,768]{1,0:T(8,128)(2,1)}, u32[]{:S(2)}) copy-start(bf16[768,768]{1,0:T(8,128)(2,1)} %get-tuple-element.178) | copy-start | bytes 3538948
  318.1 9.5 %copy-start = (bf16[768,768]{1,0:T(8,128)(2,1)S(1)}, bf16[768,768]{1,0:T(8,128)(2,1)}, u32[]{:S(2)}) copy-start(bf16[768,768]{1,0:T(8,128)(2,1)} %get-tuple-element.207) | copy-start | bytes 3538948
  318.1 24.8 %collective-permute-start.27 = (bf16[2,432,384]{2,1,0:T(8,128)(2,1)S(1)}, bf16[2,432,384]{2,1,0:T(8,128)(2,1)S(1)}, u32[]{:S(2)}, u32[]{:S(2)}) collective-permute-start(bf16[2,432,384]{2,1,0:T(8,128)(2,1)S(1)} %get-tuple-element.225), channel_id=1, source_target_pairs={{0,8},{4,12},{8,0},{12,4},{16,24},{20,28},{24,16},{28,20},{1,9},{5... | collective-permute-start | bytes 1990664 | tf_op jit(solution)/shard_map/ppermute | solution.py:947
  322.7 16.4 %collective-permute-start.16 = (bf16[2,160,384]{2,1,0:T(8,128)(2,1)S(1)}, bf16[2,160,384]{2,1,0:T(8,128)(2,1)S(1)}, u32[]{:S(2)}, u32[]{:S(2)}) collective-permute-start(bf16[2,160,384]{2,1,0:T(8,128)(2,1)S(1)} %get-tuple-element.213), channel_id=1, source_target_pairs={{0,8},{4,12},{8,0},{12,4},{16,24},{20,28},{24,16},{28,20},{1,9},{5... | collective-permute-start | bytes 737288 | tf_op jit(solution)/shard_map/ppermute | solution.py:947
  329.4 49.0 %collective-permute-start.13 = (bf16[768,768]{1,0:T(8,128)(2,1)}, bf16[768,768]{1,0:T(8,128)(2,1)}, u32[]{:S(2)}, u32[]{:S(2)}) collective-permute-start(bf16[768,768]{1,0:T(8,128)(2,1)} %get-tuple-element.271), channel_id=1, source_target_pairs={{0,1},{1,0},{2,3},{3,2},{4,5},{5,4},{6,7},{7,6},{8,9},{9,8},{10,11... | collective-permute-start | bytes 3538952 | tf_op jit(solution)/shard_map/ppermute | solution.py:944
  339.7 16.8 %collective-permute-start.17 = (bf16[1,160,384]{2,1,0:T(8,128)(2,1)}, bf16[1,160,384]{2,1,0:T(8,128)(2,1)}, u32[]{:S(2)}, u32[]{:S(2)}) collective-permute-start(bf16[1,160,384]{2,1,0:T(8,128)(2,1)} %get-tuple-element.215), channel_id=1, source_target_pairs={{0,16},{4,20},{8,24},{12,28},{16,0},{20,4},{24,8},{28,12},{1,17},{... | collective-permute-start | bytes 368648 | tf_op jit(solution)/shard_map/ppermute | solution.py:947
  343.7 18.9 %collective-permute-start.28 = (bf16[1,432,384]{2,1,0:T(8,128)(2,1)}, bf16[1,432,384]{2,1,0:T(8,128)(2,1)}, u32[]{:S(2)}, u32[]{:S(2)}) collective-permute-start(bf16[1,432,384]{2,1,0:T(8,128)(2,1)} %get-tuple-element.227), channel_id=1, source_target_pairs={{0,16},{4,20},{8,24},{12,28},{16,0},{20,4},{24,8},{28,12},{1,17},{... | collective-permute-start | bytes 995336 | tf_op jit(solution)/shard_map/ppermute | solution.py:947
  349.3 18.8 %copy-start.2 = (bf16[768,768]{1,0:T(8,128)(2,1)S(1)}, bf16[768,768]{1,0:T(8,128)(2,1)}, u32[]{:S(2)}) copy-start(bf16[768,768]{1,0:T(8,128)(2,1)} %get-tuple-element.206) | copy-start | bytes 3538948
  349.3 15.5 %collective-permute-start.32 = (bf16[432,384]{1,0:T(8,128)(2,1)S(1)}, bf16[432,384]{1,0:T(8,128)(2,1)}, u32[]{:S(2)}, u32[]{:S(2)}) collective-permute-start(bf16[432,384]{1,0:T(8,128)(2,1)S(1)} %add_bitcast_fusion.1.refs_4_), channel_id=1, source_target_pairs={{0,2},{1,3},{2,0},{3,1},{4,6},{5,7},{6,4},{7,5},{8,10},{9,11},{10,... | collective-permute-start | bytes 995336 | tf_op jit(solution)/shard_map/ppermute | solution.py:944
  349.7 17.7 %collective-permute-start.24 = (bf16[160,384]{1,0:T(8,128)(2,1)}, bf16[160,384]{1,0:T(8,128)(2,1)}, u32[]{:S(2)}, u32[]{:S(2)}) collective-permute-start(bf16[160,384]{1,0:T(8,128)(2,1)} %add_bitcast_fusion.2.refs_4_), channel_id=1, source_target_pairs={{0,1},{1,0},{2,3},{3,2},{4,5},{5,4},{6,7},{7,6},{8,9},{9,8},{10,11... | collective-permute-start | bytes 368648 | tf_op jit(solution)/shard_map/ppermute | solution.py:944
  356.5 14.1 %collective-permute-start.25 = (bf16[160,384]{1,0:T(8,128)(2,1)}, bf16[160,384]{1,0:T(8,128)(2,1)S(1)}, u32[]{:S(2)}, u32[]{:S(2)}) collective-permute-start(bf16[160,384]{1,0:T(8,128)(2,1)} %collective-permute-done.23.refs_5_), channel_id=1, source_target_pairs={{0,1},{1,0},{2,3},{3,2},{4,5},{5,4},{6,7},{7,6},{8,9},{9,8},{10,11... | collective-permute-start | bytes 368648 | tf_op jit(solution)/shard_map/ppermute | solution.py:944
  357.4 13.2 %copy-start.8 = (bf16[160,384]{1,0:T(8,128)(2,1)}, bf16[160,384]{1,0:T(8,128)(2,1)S(1)}, u32[]{:S(2)}) copy-start(bf16[160,384]{1,0:T(8,128)(2,1)S(1)} %add_bitcast_fusion.3.refs_0_) | copy-start | bytes 368644
  362.6 4.9 %collective-permute-start.18 = (bf16[160,384]{1,0:T(8,128)(2,1)S(1)}, bf16[160,384]{1,0:T(8,128)(2,1)S(1)}, u32[]{:S(2)}, u32[]{:S(2)}) collective-permute-start(bf16[160,384]{1,0:T(8,128)(2,1)S(1)} %add_bitcast_fusion.3.refs_0_), channel_id=1, source_target_pairs={{0,2},{1,3},{2,0},{3,1},{4,6},{5,7},{6,4},{7,5},{8,10},{9,11},{10,... | collective-permute-start | bytes 368648 | tf_op jit(solution)/shard_map/ppermute | solution.py:944
  364.8 5.9 %collective-permute-start.19 = (bf16[160,384]{1,0:T(8,128)(2,1)S(1)}, bf16[160,384]{1,0:T(8,128)(2,1)S(1)}, u32[]{:S(2)}, u32[]{:S(2)}) collective-permute-start(bf16[160,384]{1,0:T(8,128)(2,1)S(1)} %add_bitcast_fusion.3.refs_0_), channel_id=1, source_target_pairs={{0,1},{1,0},{2,3},{3,2},{4,5},{5,4},{6,7},{7,6},{8,9},{9,8},{10,11... | collective-permute-start | bytes 368648 | tf_op jit(solution)/shard_map/ppermute | solution.py:944
  367.5 4.5 %collective-permute-start.20 = (bf16[160,384]{1,0:T(8,128)(2,1)S(1)}, bf16[160,384]{1,0:T(8,128)(2,1)}, u32[]{:S(2)}, u32[]{:S(2)}) collective-permute-start(bf16[160,384]{1,0:T(8,128)(2,1)S(1)} %collective-permute-done.18.refs_1_), channel_id=1, source_target_pairs={{0,1},{1,0},{2,3},{3,2},{4,5},{5,4},{6,7},{7,6},{8,9},{9,8},{10,11... | collective-permute-start | bytes 368648 | tf_op jit(solution)/shard_map/ppermute | solution.py:944
  367.5 10.4 %collective-permute-start.29 = (bf16[432,384]{1,0:T(8,128)(2,1)}, bf16[432,384]{1,0:T(8,128)(2,1)S(1)}, u32[]{:S(2)}, u32[]{:S(2)}) collective-permute-start(bf16[432,384]{1,0:T(8,128)(2,1)} %add_bitcast_fusion.refs_0_), channel_id=1, source_target_pairs={{0,2},{1,3},{2,0},{3,1},{4,6},{5,7},{6,4},{7,5},{8,10},{9,11},{10,... | collective-permute-start | bytes 995336 | tf_op jit(solution)/shard_map/ppermute | solution.py:944
  370.6 14.3 %collective-permute-start.33 = (bf16[432,384]{1,0:T(8,128)(2,1)S(1)}, bf16[432,384]{1,0:T(8,128)(2,1)S(1)}, u32[]{:S(2)}, u32[]{:S(2)}) collective-permute-start(bf16[432,384]{1,0:T(8,128)(2,1)S(1)} %add_bitcast_fusion.1.refs_4_), channel_id=1, source_target_pairs={{0,1},{1,0},{2,3},{3,2},{4,5},{5,4},{6,7},{7,6},{8,9},{9,8},{10,11... | collective-permute-start | bytes 995336 | tf_op jit(solution)/shard_map/ppermute | solution.py:944
  371.3 13.7 %collective-permute-start.34 = (bf16[432,384]{1,0:T(8,128)(2,1)}, bf16[432,384]{1,0:T(8,128)(2,1)S(1)}, u32[]{:S(2)}, u32[]{:S(2)}) collective-permute-start(bf16[432,384]{1,0:T(8,128)(2,1)} %collective-permute-done.32.refs_5_), channel_id=1, source_target_pairs={{0,1},{1,0},{2,3},{3,2},{4,5},{5,4},{6,7},{7,6},{8,9},{9,8},{10,11... | collective-permute-start | bytes 995336 | tf_op jit(solution)/shard_map/ppermute | solution.py:944
  377.8 7.2 %collective-permute-start.30 = (bf16[432,384]{1,0:T(8,128)(2,1)}, bf16[432,384]{1,0:T(8,128)(2,1)S(1)}, u32[]{:S(2)}, u32[]{:S(2)}) collective-permute-start(bf16[432,384]{1,0:T(8,128)(2,1)} %add_bitcast_fusion.refs_0_), channel_id=1, source_target_pairs={{0,1},{1,0},{2,3},{3,2},{4,5},{5,4},{6,7},{7,6},{8,9},{9,8},{10,11... | collective-permute-start | bytes 995336 | tf_op jit(solution)/shard_map/ppermute | solution.py:944
  377.9 7.0 %copy-start.14 = (bf16[432,384]{1,0:T(8,128)(2,1)}, bf16[432,384]{1,0:T(8,128)(2,1)S(1)}, u32[]{:S(2)}) copy-start(bf16[432,384]{1,0:T(8,128)(2,1)S(1)} %collective-permute-done.29.refs_1_) | copy-start | bytes 995332
  377.9 7.1 %collective-permute-start.31 = (bf16[432,384]{1,0:T(8,128)(2,1)S(1)}, bf16[432,384]{1,0:T(8,128)(2,1)}, u32[]{:S(2)}, u32[]{:S(2)}) collective-permute-start(bf16[432,384]{1,0:T(8,128)(2,1)S(1)} %collective-permute-done.29.refs_1_), channel_id=1, source_target_pairs={{0,1},{1,0},{2,3},{3,2},{4,5},{5,4},{6,7},{7,6},{8,9},{9,8},{10,11... | collective-permute-start | bytes 995336 | tf_op jit(solution)/shard_map/ppermute | solution.py:944
  (9 other events, 12.7 us)

commit v4 on v3

--- a/solution.py
+++ b/solution.py
@@ -72,13 +72,14 @@
 
 COST_US = dict(
     tables=4, projections=8, attention_forward=7, feed_forward=24, feed_backward=30, attention_backward=12,
-    projections_backward=12, place_rows=4,
+    projections_backward=3, place_rows=4,
     unpack_feed=4, unpack_attention=3,
 )
 
 
-def call(kernel, name, grid, ids, in_specs, inputs, out_specs, out_shape, scratch=()):
-    cost = pl.CostEstimate(flops=COST_US[name] * 1100000000, bytes_accessed=COST_US[name] * 1000000, transcendentals=0)
+def call(kernel, name, grid, ids, in_specs, inputs, out_specs, out_shape, scratch=(), micros=None):
+    micros = COST_US[name] if micros is None else micros
+    cost = pl.CostEstimate(flops=micros * 1100000000, bytes_accessed=micros * 1000000, transcendentals=0)
     return pl.pallas_call(
         kernel,
         grid_spec=pltpu.PrefetchScalarGridSpec(
@@ -451,6 +452,7 @@
     return call(
         functools.partial(attention_bwd_kernel, per_step=per_step, shared=shared),
         "attention_backward", (steps,), ids, in_specs, inputs, out_specs, out_shape, scratch,
+        40 if shared else 12,
     )
 
 
@@ -542,7 +544,7 @@
             add_squares(sums, 4, t)
 
 
-def feed_fwd(ids, x, gathered, ctx_own, ctx_shared, valid, weights, layer, chunk=768, parts=3):
+def feed_fwd(ids, x, gathered, ctx_own, ctx_shared, valid, weights, layer, chunk=768, parts=1):
     w_out, out_bias, ln_scale, ln_shift, ffn_in, ffn_in_bias, ffn_out, ffn_out_bias = weights
     half, width = x.shape[1], x.shape[2]
     tokens, ff = 3 * half, ffn_in.shape[2]
@@ -900,8 +902,9 @@
         at = 3 * rows
         count = rel_ref.shape[2]
         rel = jnp.concatenate([scratch[0, side, at : at + count, :] for side in range(2)], 1).astype(f32)
-        rel = jnp.concatenate([rel, jnp.zeros((128 - count, rel.shape[1]), f32)], 0)
-        rel_ref[layer] = rel.T[:, 0:count]
+        size = rel_ref.shape[3]
+        for head in range(rel_ref.shape[1]):
+            rel_ref[layer, head] = rel[:, size * head : size * head + size]
         small = scratch[1, 0, at : at + count, :].astype(f32)
         scale_ref[layer] = small[0:2, 0:wide]
         shift_ref[layer] = small[2:4, 0:wide]
@@ -974,10 +977,12 @@
         return state
 
     def absorb(keep, arrived):
+        keep, arrived = pin((keep, arrived))
         n = keep.shape[0] // 2
         return pin((keep[:n] + arrived[:n], keep[n:] + arrived[n:]))
 
     def last(keep, arrived):
+        keep, arrived = pin((keep, arrived))
         x = (keep + arrived)[0]
         bit = 1
         while bit < fine:
@@ -1025,27 +1030,22 @@
     g_h, a1 = joint_back(1, own_grads, shared_keep, arrived, g_attn, rel_own, rel_shared, vec, pre_sum)
 
     f1 = hop(absorb(*f1), 1)
+    a1 = hop(absorb(*a1), 0)
     g_attn, g_ctx, vec, pre_sum, f0 = feed_back(0, halves(g_h), False)
     f1 = hop(absorb(*f1), 2)
-    a1 = hop(absorb(*a1), 0)
+    a1 = hop(absorb(*a1), 1)
     shared_keep, shared_send, rel_shared = attention_back(0, True, g_ctx)
     arrived = flip(shared_send, 1)
     f0 = hop(absorb(*f0), 0)
     own_grads, rel_own = attention_back(0, False, g_ctx)
     f1 = last(*f1)
-    a1 = hop(absorb(*a1), 1)
+    a1 = hop(absorb(*a1), 2)
+    g_h, a0 = joint_back(0, own_grads, shared_keep, arrived, g_attn, rel_own, rel_shared, vec, pre_sum)
+    g_h_far = flip(g_h, 2)
     f1 = all_sides(f1)
-    g_h, a0 = joint_back(0, own_grads, shared_keep, arrived, g_attn, rel_own, rel_shared, vec, pre_sum)
-    a1 = hop(absorb(*a1), 2)
+    f0 = hop(absorb(*f0), 1)
     a0 = hop(absorb(*a0), 0)
-    f0 = hop(absorb(*f0), 1)
     a1 = all_sides(last(*a1))
-    a0 = hop(absorb(*a0), 1)
-    f0 = hop(absorb(*f0), 2)
-    a0 = hop(absorb(*a0), 2)
-    f0 = all_sides(last(*f0))
-    a0 = all_sides(last(*a0))
-    kept[0]["g_h"] = g_h + flip(g_h, 2)
 
     def of_layer(name):
         return jnp.where(side == 0, kept[0][name], kept[1][name])
@@ -1055,8 +1055,14 @@
         own, away = jnp.where(core == 0, a, b), jnp.where(core == 0, b, a)
         return place_rows(ids, own, flip(away, 1), dtype).reshape(1, rows, length, width)
 
-    section_outs = to_section("mixed", "out", bf16)
-    in_grads = to_section("g_h", "g_mixed", f32)
+    section_outs = pin(to_section("mixed", "out", bf16))
+    a0 = hop(absorb(*a0), 1)
+    f0 = hop(absorb(*f0), 2)
+    kept[0]["g_h"] = pin(g_h + g_h_far)
+    in_grads = pin(to_section("g_h", "g_mixed", f32))
+    a0 = hop(absorb(*a0), 2)
+    f0 = all_sides(last(*f0))
+    a0 = all_sides(last(*a0))
 
     squares_mine = jnp.sum(of_layer("squares"), 1).reshape(2, 2, 2)
     squares_far = flip(squares_mine, 1)
@@ -1070,13 +1076,14 @@
 
     slab = width // SUPER
     d_ffn_in, d_ffn_out, d_out = unpack(
-        unpack_feed_kernel, "unpack_feed", ids, f0 + f1,
+        unpack_feed_kernel, "unpack_feed", clock[0], f0 + f1,
         [(2, slab, ff), (2, ff // SUPER, width), (2, slab, width)],
     )
+    d_ffn_in, d_ffn_out, d_out = pin((d_ffn_in, d_ffn_out, d_out))
     rel_rows = 128 // SUPER
     d_qkv, d_rel, d_qv, d_out_bias, d_scale, d_shift, d_in_bias, d_ffn_bias = unpack(
-        unpack_attention_kernel, "unpack_attention", ids, a0 + a1,
-        [(2, slab, 3 * width), (2, width, rel_rows), (2, 2, slab), (2, slab),
+        unpack_attention_kernel, "unpack_attention", clock[0], a0 + a1,
+        [(2, slab, 3 * width), (2, rel_proj.shape[1], rel_rows, rel_proj.shape[2]), (2, 2, slab), (2, slab),
          (2, 2, slab), (2, 2, slab), (2, LANES), (2, slab)],
     )
 
@@ -1084,7 +1091,6 @@
         n = x.shape[axis] // fine
         return x if fine == 1 else lax.dynamic_slice_in_dim(x, (dp_index % fine) * n, n, axis)
 
-    d_rel = d_rel.reshape((2,) + rel_proj.shape[1:3] + (rel_rows,))
     return (
         section_outs,
         in_grads,
@@ -1092,7 +1098,7 @@
         own_part(d_qv, 2),
         own_part(d_out, 1),
         own_part(d_out_bias, 1),
-        own_part(d_rel, 3),
+        own_part(jnp.swapaxes(d_rel, 2, 3), 3),
         own_part(d_scale, 2),
         own_part(d_shift, 2),
         own_part(d_ffn_in, 1),

time: 398 us -> 369 us (0.927)
  waiting for transfers between devices: 58.5 us -> 37.7 us
  Pallas kernels: 265 us -> 261 us
    ppermute x12, waiting for transfers between devices: 52.2 us -> 26.9 us  [flip_dp(): return lax.ppermute(x, 'dp', [(i, i ^ bit) for i in range(dp)])]
    ppermute x12, starting transfers between devices: 19 us -> 13.5 us  [flip_dp(): return lax.ppermute(x, 'dp', [(i, i ^ bit) for i in range(dp)])]
    ppermute x24, waiting for transfers between devices: 6.24 us -> 10.8 us  [flip(): return lax.ppermute(x, 'section', [(i, i ^ bit) for i in range(sections)])]
    unnamed x45 -> x62, local copies, waits for them, and re-layouts: 8.14 us -> 7.22 us
  transfers between devices with their start and end apart: 36 -> 36, of which waited for: 11 -> 10; matrix products, arithmetic and copies ran while one was open for 9% -> 7% of each run, Pallas kernels for 35% -> 38%
where the time goes in v4:
time: 369 us; the launch traced here: 362 us
  Pallas kernels  261 us (71%)
  waiting for transfers between devices  37.7 us (10%)
  other arithmetic  30.3 us (8%)
  starting transfers between devices  24.1 us (7%)
  local copies, waits for them, and re-layouts  7.32 us (2%)
    pallas_call x21, Pallas kernels, call(): pl.pallas_call(kernel, grid_spec=pltpu.PrefetchScalarGridSpec(num_scalar_...  261 us
    ppermute x12, waiting for transfers between devices, flip_dp(): return lax.ppermute(x, 'dp', [(i, i ^ bit) for i in range(dp)])  26.9 us
    add x12, other arithmetic, absorb(): return pin((keep[:n] + arrived[:n], keep[n:] + arrived[n:]))  21.8 us
    ppermute x12, starting transfers between devices, flip_dp(): return lax.ppermute(x, 'dp', [(i, i ^ bit) for i in range(dp)])  13.5 us
    ppermute x24, waiting for transfers between devices, flip(): return lax.ppermute(x, 'section', [(i, i ^ bit) for i in range(sections)])  10.8 us
    ppermute x24, starting transfers between devices, flip(): return lax.ppermute(x, 'section', [(i, i ^ bit) for i in range(sections)])  10.6 us
  transfers between devices with their start and end apart: 36, of which 10 were waited for; matrix products, arithmetic and copies ran while one was open for 7% of the time, Pallas kernels for 38%

profile of v4, /device:TPU:0, one launch (start us, length us, event | category | flops | bytes accessed | tf_op | source)
XLA Modules:
  0.0 362.0 jit_solution(12752326290597827138)
XLA Ops:
  0.7 1.4 copy.32.boxes_ref
  2.7 4.2 %tables.1 = (f32[64,1024]{1,0:T(8,128)}, f32[64,1024]{1,0:T(8,128)}, bf16[1024,128]{1,0:T(8,128)(2,1)}, f32[1024,128]{1,0:T(8,128)}, f32[1024,128]{1,0:T(8,128)}...) custom-call(s32[3]{0:T(128)} %pad_add_fusion.ids, s32[4,3,512]{2,1,0:T(4,128)} %copy.32.boxes_ref, ...), custom_call_target="tpu_custom_call" | custom-call | flops 4400000000 | bytes 4000000 | tf_op jit(solution)/shard_map/tables/pallas_call | solution.py:83
  6.8 9.9 %projections.2 = (bf16[768,2304]{1,0:T(8,128)(2,1)}, bf16[768,1536]{1,0:T(8,128)(2,1)}, bf16[256,1536]{1,0:T(8,128)(2,1)}) custom-call(s32[3]{0:T(128)} %pad_add_fusion.ids, bf16[6,256,768]{2,1,0:T(8,128)(2,1)} %bitcast.30, bf16[6,256,768]{2,1,0:T(8,128)(2,1)} %bitcast.31, bf16[6,256,768]{2,1,0:T(8,128)(2,1)} %bitcast.32, bf16[2,768,2304]{2,1,0:T(8,128)(2,1)} %w_ref.7, ...), custom_call_target="tpu_custom_call" | custom-call | flops 8800000000 | bytes 8000000 | tf_op jit(solution)/shard_map/projections/pallas_call | solution.py:83
  17.2 8.6 %attention_forward.4 = (bf16[768,512]{1,0:T(8,128)(2,1)}, f32[6,2,512]{2,1,0:T(2,128)}) custom-call(s32[3]{0:T(128)} %pad_add_fusion.ids, f32[1024,128]{1,0:T(8,128)} %get-tuple-element.197.code_ref, f32[8,1024]{1,0:T(8,128)} %get-tuple-element.198.seg_ref, bf16[1024,128]{1,0:T(8,128)(2,1)} %get-tuple-element.199.kf_ref, ...), custom_call_target="tpu_custom_call" | custom-call | flops 7699999744 | bytes 7000000 | tf_op jit(solution)/shard_map/attention_forward/pallas_call | solution.py:83
  26.8 6.3 %attention_forward.5 = (bf16[768,256]{1,0:T(8,128)(2,1)}, f32[6,2,256]{2,1,0:T(2,128)}) custom-call(s32[3]{0:T(128)} %pad_add_fusion.ids, f32[1024,128]{1,0:T(8,128)} %get-tuple-element.197.code_ref, f32[8,1024]{1,0:T(8,128)} %get-tuple-element.198.seg_ref, bf16[1024,128]{1,0:T(8,128)(2,1)} %get-tuple-element.199.kf_ref, ...), custom_call_target="tpu_custom_call" | custom-call | flops 7699999744 | bytes 7000000 | tf_op jit(solution)/shard_map/attention_forward/pallas_call | solution.py:83
  33.1 25.8 %feed_forward.2 = (bf16[768,768]{1,0:T(8,128)(2,1)}, f32[768,128]{1,0:T(8,128)}, bf16[768,768]{1,0:T(8,128)(2,1)}, f32[768,128]{1,0:T(8,128)}, bf16[768,768]{1,0...) custom-call(s32[3]{0:T(128)} %pad_add_fusion.ids, ...), custom_call_target="tpu_custom_call" | custom-call | flops 26400000000 | bytes 24000000 | tf_op jit(solution)/shard_map/feed_forward/pallas_call | solution.py:83
  58.9 9.9 %projections.3 = (bf16[768,2304]{1,0:T(8,128)(2,1)}, bf16[768,1536]{1,0:T(8,128)(2,1)}, bf16[256,1536]{1,0:T(8,128)(2,1)}) custom-call(s32[3]{0:T(128)} %pad_add_fusion.ids, bf16[3,256,768]{2,1,0:T(8,128)(2,1)} %bitcast.39, bf16[3,256,768]{2,1,0:T(8,128)(2,1)} %bitcast.40, bf16[3,256,768]{2,1,0:T(8,128)(2,1)} %bitcast.41, bf16[2,768,2304]{2,1,0:T(8,128)(2,1)} %w_ref.7, ...), custom_call_target="tpu_custom_call" | custom-call | flops 8800000000 | bytes 8000000 | tf_op jit(solution)/shard_map/projections/pallas_call | solution.py:83
  68.8 8.6 %attention_forward.6 = (bf16[768,512]{1,0:T(8,128)(2,1)}, f32[6,2,512]{2,1,0:T(2,128)}) custom-call(s32[3]{0:T(128)} %pad_add_fusion.ids, f32[1024,128]{1,0:T(8,128)} %get-tuple-element.197.code_ref, f32[8,1024]{1,0:T(8,128)} %get-tuple-element.198.seg_ref, bf16[1024,128]{1,0:T(8,128)(2,1)} %get-tuple-element.199.kf_ref, ...), custom_call_target="tpu_custom_call" | custom-call | flops 7699999744 | bytes 7000000 | tf_op jit(solution)/shard_map/attention_forward/pallas_call | solution.py:83
  78.4 6.5 %attention_forward.7 = (bf16[768,256]{1,0:T(8,128)(2,1)}, f32[6,2,256]{2,1,0:T(2,128)}) custom-call(s32[3]{0:T(128)} %pad_add_fusion.ids, f32[1024,128]{1,0:T(8,128)} %get-tuple-element.197.code_ref, f32[8,1024]{1,0:T(8,128)} %get-tuple-element.198.seg_ref, bf16[1024,128]{1,0:T(8,128)(2,1)} %get-tuple-element.199.kf_ref, ...), custom_call_target="tpu_custom_call" | custom-call | flops 7699999744 | bytes 7000000 | tf_op jit(solution)/shard_map/attention_forward/pallas_call | solution.py:83
  84.9 25.5 %feed_forward.3 = (bf16[768,768]{1,0:T(8,128)(2,1)}, f32[768,128]{1,0:T(8,128)}, bf16[768,768]{1,0:T(8,128)(2,1)}, f32[768,128]{1,0:T(8,128)}, bf16[768,768]{1,0...) custom-call(s32[3]{0:T(128)} %pad_add_fusion.ids, ...), custom_call_target="tpu_custom_call" | custom-call | flops 26400000000 | bytes 24000000 | tf_op jit(solution)/shard_map/feed_forward/pallas_call | solution.py:83
  110.4 32.0 %feed_backward.2 = (bf16[768,768]{1,0:T(8,128)(2,1)}, bf16[768,768]{1,0:T(8,128)(2,1)}, bf16[768,768]{1,0:T(8,128)(2,1)}, f32[8,768]{1,0:T(8,128)}, f32[8,3072]{...) custom-call(s32[3]{0:T(128)} %pad_add_fusion.ids, bf16[6,256,768]{2,1,0:T(8,128)(2,1)} %bitcast.56, ...), custom_call_target="tpu_custom_call" | custom-call | flops 32999999488 | bytes 30000000 | tf_op jit(solution)/shard_map/feed_backward/pallas_call | solution.py:83
  142.9 11.1 %attention_backward.5 = (bf16[3,256,768]{2,1,0:T(8,128)(2,1)}, bf16[2,256,768]{2,1,0:T(8,128)(2,1)}, f32[128,768]{1,0:T(8,128)}) custom-call(s32[3]{0:T(128)} %pad_add_fusion.ids, f32[1024,128]{1,0:T(8,128)} %get-tuple-element.197.code_ref, f32[8,1024]{1,0:T(8,128)} %get-tuple-element.198.seg_ref, bf16[1024,128]{1,0:T(8,128)(2,1)} %get-tuple-element.199.kf_ref, ...), custom_call_target="tpu_custom_call" | custom-call | flops 44000002048 | bytes 40000000 | tf_op jit(solution)/shard_map/attention_backward/pallas_call | solution.py:83
  154.2 3.9 %slice_add_fusion.2 = (bf16[4,432,384]{2,1,0:T(8,128)(2,1)}, bf16[4,432,384]{2,1,0:T(8,128)(2,1)S(1)}) fusion(bf16[8,432,384]{2,1,0:T(8,128)(2,1)} %collective-permute-done.2, bf16[8,432,384]{2,1,0:T(8,128)(2,1)} %get-tuple-element.224), kind=kLoop, calls=%fused_computation.2 | loop fusion | flops 1327104 | bytes 7962624 | tf_op jit(solution)/shard_map/add | solution.py:982
  158.1 2.9 collective-permute-start.3
  161.0 16.4 %attention_backward.4 = (bf16[3,512,768]{2,1,0:T(8,128)(2,1)}, f32[128,768]{1,0:T(8,128)}) custom-call(s32[3]{0:T(128)} %pad_add_fusion.ids, f32[1024,128]{1,0:T(8,128)} %get-tuple-element.197.code_ref, f32[8,1024]{1,0:T(8,128)} %get-tuple-element.198.seg_ref, bf16[1024,128]{1,0:T(8,128)(2,1)} %get-tuple-element.199.kf_ref, ...), custom_call_target="tpu_custom_call" | custom-call | flops 13200000000 | bytes 12000000 | tf_op jit(solution)/shard_map/attention_backward/pallas_call | solution.py:83
  177.4 13.6 %projections_backward.2 = (bf16[768,768]{1,0:T(8,128)(2,1)}, bf16[8,160,384]{2,1,0:T(8,128)(2,1)}, bf16[8,160,384]{2,1,0:T(8,128)(2,1)}) custom-call(s32[3]{0:T(128)} %pad_add_fusion.ids, bf16[3,256,768]{2,1,0:T(8,128)(2,1)} %bitcast.45, bf16[3,256,768]{2,1,0:T(8,128)(2,1)} %bitcast.46, bf16[3,256,768]{2,1,0:T(8,128)(2,1)} %bitcast.47, ...), custom_call_target="tpu_custom_call" | custom-call | flops 3300000000 | bytes 3000000 | tf_op jit(solution)/shard_map/projections_backward/pallas_call | solution.py:83
  191.0 2.4 slice_add_fusion.6
  193.9 1.6 collective-permute-start.6
  196.6 32.0 %feed_backward.3 = (bf16[768,768]{1,0:T(8,128)(2,1)}, bf16[768,768]{1,0:T(8,128)(2,1)}, bf16[768,768]{1,0:T(8,128)(2,1)}, f32[8,768]{1,0:T(8,128)}, f32[8,3072]{...) custom-call(s32[3]{0:T(128)} %pad_add_fusion.ids, bf16[3,256,768]{2,1,0:T(8,128)(2,1)} %bitcast.48, ...), custom_call_target="tpu_custom_call" | custom-call | flops 32999999488 | bytes 30000000 | tf_op jit(solution)/shard_map/feed_backward/pallas_call | solution.py:83
  228.6 1.9 slice_add_fusion.14
  230.5 1.8 slice_add_fusion.18
  232.3 7.5 %attention_backward.7 = (bf16[3,256,384]{2,1,0:T(8,128)(2,1)}, bf16[2,256,384]{2,1,0:T(8,128)(2,1)}, f32[128,384]{1,0:T(8,128)}) custom-call(s32[3]{0:T(128)} %pad_add_fusion.ids, f32[1024,128]{1,0:T(8,128)} %get-tuple-element.197.code_ref, f32[8,1024]{1,0:T(8,128)} %get-tuple-element.198.seg_ref, bf16[1024,128]{1,0:T(8,128)(2,1)} %get-tuple-element.199.kf_ref, ...), custom_call_target="tpu_custom_call" | custom-call | flops 44000002048 | bytes 40000000 | tf_op jit(solution)/shard_map/attention_backward/pallas_call | solution.py:83
  240.4 2.6 collective-permute-start.9
  243.5 4.3 %slice_add_fusion = (bf16[4,432,384]{2,1,0:T(8,128)(2,1)}, bf16[4,432,384]{2,1,0:T(8,128)(2,1)}) fusion(bf16[8,432,384]{2,1,0:T(8,128)(2,1)} %collective-permute-done.8, bf16[8,432,384]{2,1,0:T(8,128)(2,1)} %get-tuple-element.275), kind=kLoop, calls=%fused_computation | loop fusion | flops 1327104 | bytes 7962624 | tf_op jit(solution)/shard_map/add | solution.py:982
  247.8 9.9 %attention_backward.6 = (bf16[3,512,384]{2,1,0:T(8,128)(2,1)}, f32[128,384]{1,0:T(8,128)}) custom-call(s32[3]{0:T(128)} %pad_add_fusion.ids, f32[1024,128]{1,0:T(8,128)} %get-tuple-element.197.code_ref, f32[8,1024]{1,0:T(8,128)} %get-tuple-element.198.seg_ref, bf16[1024,128]{1,0:T(8,128)(2,1)} %get-tuple-element.199.kf_ref, ...), custom_call_target="tpu_custom_call" | custom-call | flops 13200000000 | bytes 12000000 | tf_op jit(solution)/shard_map/attention_backward/pallas_call | solution.py:83
  258.9 1.7 slice_add_fusion.22
  262.4 12.3 %projections_backward.3 = (bf16[768,768]{1,0:T(8,128)(2,1)}, bf16[8,160,384]{2,1,0:T(8,128)(2,1)}, bf16[8,160,384]{2,1,0:T(8,128)(2,1)}) custom-call(s32[3]{0:T(128)} %pad_add_fusion.ids, bf16[6,256,768]{2,1,0:T(8,128)(2,1)} %bitcast.36, bf16[6,256,768]{2,1,0:T(8,128)(2,1)} %bitcast.37, bf16[6,256,768]{2,1,0:T(8,128)(2,1)} %bitcast.38, ...), custom_call_target="tpu_custom_call" | custom-call | flops 3300000000 | bytes 3000000 | tf_op jit(solution)/shard_map/projections_backward/pallas_call | solution.py:83
  274.7 2.7 broadcast_select_fusion.6
  277.8 2.0 collective-permute-start.18
  279.8 12.2 %collective-permute-done.11 = bf16[4,432,384]{2,1,0:T(8,128)(2,1)} collective-permute-done((bf16[4,432,384]{2,1,0:T(8,128)(2,1)}, bf16[4,432,384]{2,1,0:T(8,128)(2,1)}, u32[]{:S(2)}, u32[]{:S(2)}) %collective-permute-start.11) | collective-permute-done | bytes 1327136 | tf_op jit(solution)/shard_map/ppermute | solution.py:950
  292.0 2.3 slice_add_fusion.4
  297.2 5.5 %place_rows.2 = bf16[6,256,768]{2,1,0:T(8,128)(2,1)} custom-call(s32[3]{0:T(128)} %pad_add_fusion.ids, bf16[3,256,768]{2,1,0:T(8,128)(2,1)} %bitcast.51, bf16[3,256,768]{2,1,0:T(8,128)(2,1)} %bitcast.59), custom_call_target="tpu_custom_call" | custom-call | flops 4400000000 | bytes 4000000 | tf_op jit(solution)/shard_map/place_rows/pallas_call | solution.py:83
  302.8 3.5 collective-permute-done.18
  306.3 1.9 add.140
  310.1 1.4 collective-permute-done.17
  311.5 1.9 slice_add_fusion.12
  313.5 1.3 broadcast_select_fusion.4
  315.6 1.6 collective-permute-start.26
  317.5 1.7 collective-permute-start.21
  319.2 6.6 %place_rows.3 = f32[6,256,768]{2,1,0:T(8,128)} custom-call(s32[3]{0:T(128)} %pad_add_fusion.ids, bf16[3,256,768]{2,1,0:T(8,128)(2,1)} %bitcast.52, bf16[3,256,768]{2,1,0:T(8,128)(2,1)} %bitcast.14.other_ref), custom_call_target="tpu_custom_call" | custom-call | flops 4400000000 | bytes 4000000 | tf_op jit(solution)/shard_map/place_rows/pallas_call | solution.py:83
  325.8 3.0 collective-permute-done.20
  328.8 6.1 %collective-permute-done.21 = bf16[1,432,384]{2,1,0:T(8,128)(2,1)S(1)} collective-permute-done((bf16[1,432,384]{2,1,0:T(8,128)(2,1)}, bf16[1,432,384]{2,1,0:T(8,128)(2,1)S(1)}, u32[]{:S(2)}, u32[]{:S(2)}) %collective-permute-start.21) | collective-permute-done | bytes 331808 | tf_op jit(solution)/shard_map/ppermute | solution.py:950
  336.4 1.6 collective-permute-start.32
  338.0 3.8 %collective-permute-done.22 = bf16[1,160,384]{2,1,0:T(8,128)(2,1)S(1)} collective-permute-done((bf16[1,160,384]{2,1,0:T(8,128)(2,1)S(1)}, bf16[1,160,384]{2,1,0:T(8,128)(2,1)S(1)}, u32[]{:S(2)}, u32[]{:S(2)}) %collective-permute-start.22) | collective-permute-done | bytes 122912 | tf_op jit(solution)/shard_map/ppermute | solution.py:950
  341.8 2.9 collective-permute-done.23.refs_1_
  346.6 4.0 %collective-permute-done.29.refs_1_ = bf16[160,384]{1,0:T(8,128)(2,1)S(1)} collective-permute-done((bf16[160,384]{1,0:T(8,128)(2,1)S(1)}, bf16[160,384]{1,0:T(8,128)(2,1)S(1)}, u32[]{:S(2)}, u32[]{:S(2)}) %collective-permute-start.29) | collective-permute-done | bytes 122912 | tf_op jit(solution)/shard_map/ppermute | solution.py:947
  351.4 5.5 %unpack_feed.1 = (f32[2,96,3072]{2,1,0:T(8,128)}, f32[2,384,768]{2,1,0:T(8,128)}, f32[2,96,768]{2,1,0:T(8,128)}) custom-call(s32[3]{0:T(128)} %pad_add_fusion.ids, bf16[432,384]{1,0:T(8,128)(2,1)} %copy-done.10, bf16[432,384]{1,0:T(8,128)(2,1)} %copy-done.20, bf16[432,384]{1,0:T(8,128)(2,1)} %copy-done.23, bf16[432,384]{1,0:T(8,128)(2,1)} %collective-permute-done.25.refs_3_, ...), custom_call_target="tpu_custom_call" | custom-call | flops 4400000000 | bytes 4000000 | tf_op jit(solution)/shard_map/unpack_feed/pallas_call | solution.py:83
  358.4 3.5 unpack_attention.1
  (135 shorter events, 21.0 us)
Async XLA Ops:
  16.8 9.1 %collective-permute-start = (bf16[256,1536]{1,0:T(8,128)(2,1)}, bf16[256,1536]{1,0:T(8,128)(2,1)S(1)}, u32[]{:S(2)}, u32[]{:S(2)}) collective-permute-start(bf16[256,1536]{1,0:T(8,128)(2,1)} %get-tuple-element.205), channel_id=1, source_target_pairs={{0,1},{1,0},{2,3},{3,2},{4,5},{5,4},{6,7},{7,6},{8,9},{9,8},{10,11... | collective-permute-start | bytes 2359304 | tf_op jit(solution)/shard_map/ppermute | solution.py:947
  68.8 8.7 %collective-permute-start.1 = (bf16[256,1536]{1,0:T(8,128)(2,1)}, bf16[256,1536]{1,0:T(8,128)(2,1)S(1)}, u32[]{:S(2)}, u32[]{:S(2)}) collective-permute-start(bf16[256,1536]{1,0:T(8,128)(2,1)} %get-tuple-element.212), channel_id=1, source_target_pairs={{0,1},{1,0},{2,3},{3,2},{4,5},{5,4},{6,7},{7,6},{8,9},{9,8},{10,11... | collective-permute-start | bytes 2359304 | tf_op jit(solution)/shard_map/ppermute | solution.py:947
  142.4 11.8 %collective-permute-start.2 = (bf16[8,432,384]{2,1,0:T(8,128)(2,1)}, bf16[8,432,384]{2,1,0:T(8,128)(2,1)}, u32[]{:S(2)}, u32[]{:S(2)}) collective-permute-start(bf16[8,432,384]{2,1,0:T(8,128)(2,1)} %get-tuple-element.222), channel_id=1, source_target_pairs={{0,1},{1,0},{2,3},{3,2},{4,5},{5,4},{6,7},{7,6},{8,9},{9,8},{10,11... | collective-permute-start | bytes 7962632 | tf_op jit(solution)/shard_map/ppermute | solution.py:947
  154.1 23.3 %collective-permute-start.4 = (bf16[2,256,768]{2,1,0:T(8,128)(2,1)}, bf16[2,256,768]{2,1,0:T(8,128)(2,1)}, u32[]{:S(2)}, u32[]{:S(2)}) collective-permute-start(bf16[2,256,768]{2,1,0:T(8,128)(2,1)} %get-tuple-element.240), channel_id=1, source_target_pairs={{0,1},{1,0},{2,3},{3,2},{4,5},{5,4},{6,7},{7,6},{8,9},{9,8},{10,11... | collective-permute-start | bytes 2359304 | tf_op jit(solution)/shard_map/ppermute | solution.py:947
  158.1 32.9 %collective-permute-start.3 = (bf16[4,432,384]{2,1,0:T(8,128)(2,1)}, bf16[4,432,384]{2,1,0:T(8,128)(2,1)}, u32[]{:S(2)}, u32[]{:S(2)}) collective-permute-start(bf16[4,432,384]{2,1,0:T(8,128)(2,1)} %get-tuple-element.228), channel_id=1, source_target_pairs={{0,4},{4,0},{8,12},{12,8},{16,20},{20,16},{24,28},{28,24},{1,5},{5... | collective-permute-start | bytes 3981320 | tf_op jit(solution)/shard_map/ppermute | solution.py:950
  191.0 2.8 collective-permute-start.5
  193.9 34.7 %collective-permute-start.6 = (bf16[2,432,384]{2,1,0:T(8,128)(2,1)}, bf16[2,432,384]{2,1,0:T(8,128)(2,1)}, u32[]{:S(2)}, u32[]{:S(2)}) collective-permute-start(bf16[2,432,384]{2,1,0:T(8,128)(2,1)} %get-tuple-element.253), channel_id=1, source_target_pairs={{0,8},{4,12},{8,0},{12,4},{16,24},{20,28},{24,16},{28,20},{1,9},{5... | collective-permute-start | bytes 1990664 | tf_op jit(solution)/shard_map/ppermute | solution.py:950
  195.5 34.9 %collective-permute-start.7 = (bf16[4,160,384]{2,1,0:T(8,128)(2,1)S(1)}, bf16[4,160,384]{2,1,0:T(8,128)(2,1)}, u32[]{:S(2)}, u32[]{:S(2)}) collective-permute-start(bf16[4,160,384]{2,1,0:T(8,128)(2,1)S(1)} %get-tuple-element.259), channel_id=1, source_target_pairs={{0,4},{4,0},{8,12},{12,8},{16,20},{20,16},{24,28},{28,24},{1,5},{5... | collective-permute-start | bytes 1474568 | tf_op jit(solution)/shard_map/ppermute | solution.py:950
  228.5 15.0 %collective-permute-start.8 = (bf16[8,432,384]{2,1,0:T(8,128)(2,1)}, bf16[8,432,384]{2,1,0:T(8,128)(2,1)}, u32[]{:S(2)}, u32[]{:S(2)}) collective-permute-start(bf16[8,432,384]{2,1,0:T(8,128)(2,1)} %get-tuple-element.273), channel_id=1, source_target_pairs={{0,1},{1,0},{2,3},{3,2},{4,5},{5,4},{6,7},{7,6},{8,9},{9,8},{10,11... | collective-permute-start | bytes 7962632 | tf_op jit(solution)/shard_map/ppermute | solution.py:947
  232.3 8.1 %copy-start.11 = (bf16[1,432,384]{2,1,0:T(8,128)(2,1)S(1)}, bf16[1,432,384]{2,1,0:T(8,128)(2,1)}, u32[]{:S(2)}) copy-start(bf16[1,432,384]{2,1,0:T(8,128)(2,1)} %get-tuple-element.279) | copy-start | bytes 995332
  232.3 10.7 %copy-start.12 = (bf16[2,160,384]{2,1,0:T(8,128)(2,1)S(1)}, bf16[2,160,384]{2,1,0:T(8,128)(2,1)}, u32[]{:S(2)}) copy-start(bf16[2,160,384]{2,1,0:T(8,128)(2,1)} %get-tuple-element.285) | copy-start | bytes 737284
  239.8 21.8 %collective-permute-start.12 = (bf16[2,256,384]{2,1,0:T(8,128)(2,1)}, bf16[2,256,384]{2,1,0:T(8,128)(2,1)S(1)}, u32[]{:S(2)}, u32[]{:S(2)}) collective-permute-start(bf16[2,256,384]{2,1,0:T(8,128)(2,1)} %get-tuple-element.301), channel_id=1, source_target_pairs={{0,1},{1,0},{2,3},{3,2},{4,5},{5,4},{6,7},{7,6},{8,9},{9,8},{10,11... | collective-permute-start | bytes 1179656 | tf_op jit(solution)/shard_map/ppermute | solution.py:947
  240.4 17.7 %collective-permute-start.9 = (bf16[1,432,384]{2,1,0:T(8,128)(2,1)S(1)}, bf16[1,432,384]{2,1,0:T(8,128)(2,1)S(1)}, u32[]{:S(2)}, u32[]{:S(2)}) collective-permute-start(bf16[1,432,384]{2,1,0:T(8,128)(2,1)S(1)} %copy-done.11), channel_id=1, source_target_pairs={{0,16},{4,20},{8,24},{12,28},{16,0},{20,4},{24,8},{28,12},{1,17},{... | collective-permute-start | bytes 995336 | tf_op jit(solution)/shard_map/ppermute | solution.py:950
  243.0 15.9 %collective-permute-start.10 = (bf16[2,160,384]{2,1,0:T(8,128)(2,1)S(1)}, bf16[2,160,384]{2,1,0:T(8,128)(2,1)}, u32[]{:S(2)}, u32[]{:S(2)}) collective-permute-start(bf16[2,160,384]{2,1,0:T(8,128)(2,1)S(1)} %copy-done.12), channel_id=1, source_target_pairs={{0,8},{4,12},{8,0},{12,4},{16,24},{20,28},{24,16},{28,20},{1,9},{5... | collective-permute-start | bytes 737288 | tf_op jit(solution)/shard_map/ppermute | solution.py:950
  260.6 31.4 %collective-permute-start.11 = (bf16[4,432,384]{2,1,0:T(8,128)(2,1)}, bf16[4,432,384]{2,1,0:T(8,128)(2,1)}, u32[]{:S(2)}, u32[]{:S(2)}) collective-permute-start(bf16[4,432,384]{2,1,0:T(8,128)(2,1)} %get-tuple-element.291), channel_id=1, source_target_pairs={{0,4},{4,0},{8,12},{12,8},{16,20},{20,16},{24,28},{28,24},{1,5},{5... | collective-permute-start | bytes 3981320 | tf_op jit(solution)/shard_map/ppermute | solution.py:950
  262.4 12.3 %copy-start = (bf16[768,768]{1,0:T(8,128)(2,1)S(1)}, bf16[768,768]{1,0:T(8,128)(2,1)}, u32[]{:S(2)}) copy-start(bf16[768,768]{1,0:T(8,128)(2,1)} %get-tuple-element.208) | copy-start | bytes 3538948
  274.7 19.6 %collective-permute-start.13 = (bf16[8,160,384]{2,1,0:T(8,128)(2,1)}, bf16[8,160,384]{2,1,0:T(8,128)(2,1)S(1)}, u32[]{:S(2)}, u32[]{:S(2)}) collective-permute-start(bf16[8,160,384]{2,1,0:T(8,128)(2,1)} %get-tuple-element.308), channel_id=1, source_target_pairs={{0,1},{1,0},{2,3},{3,2},{4,5},{5,4},{6,7},{7,6},{8,9},{9,8},{10,11... | collective-permute-start | bytes 2949128 | tf_op jit(solution)/shard_map/ppermute | solution.py:947
  274.7 17.3 %copy-start.1 = (bf16[4,432,384]{2,1,0:T(8,128)(2,1)S(1)}, bf16[4,432,384]{2,1,0:T(8,128)(2,1)}, u32[]{:S(2)}) copy-start(bf16[4,432,384]{2,1,0:T(8,128)(2,1)} %get-tuple-element.293) | copy-start | bytes 3981316
  277.3 18.9 %collective-permute-start.15 = (bf16[768,768]{1,0:T(8,128)(2,1)S(1)}, bf16[768,768]{1,0:T(8,128)(2,1)S(1)}, u32[]{:S(2)}, u32[]{:S(2)}) collective-permute-start(bf16[768,768]{1,0:T(8,128)(2,1)S(1)} %get-tuple-element.417), channel_id=1, source_target_pairs={{0,1},{1,0},{2,3},{3,2},{4,5},{5,4},{6,7},{7,6},{8,9},{9,8},{10,11... | collective-permute-start | bytes 3538952 | tf_op jit(solution)/shard_map/ppermute | solution.py:947
  277.8 16.4 %copy-start.5 = (bf16[8,160,384]{2,1,0:T(8,128)(2,1)S(1)}, bf16[8,160,384]{2,1,0:T(8,128)(2,1)}, u32[]{:S(2)}) copy-start(bf16[8,160,384]{2,1,0:T(8,128)(2,1)} %get-tuple-element.310) | copy-start | bytes 2949124
  277.8 28.4 %collective-permute-start.18 = (bf16[768,768]{1,0:T(8,128)(2,1)}, bf16[768,768]{1,0:T(8,128)(2,1)}, u32[]{:S(2)}, u32[]{:S(2)}) collective-permute-start(bf16[768,768]{1,0:T(8,128)(2,1)} %get-tuple-element.334), channel_id=1, source_target_pairs={{0,2},{1,3},{2,0},{3,1},{4,6},{5,7},{6,4},{7,5},{8,10},{9,11},{10,... | collective-permute-start | bytes 3538952 | tf_op jit(solution)/shard_map/ppermute | solution.py:947
  279.8 28.4 %collective-permute-start.14 = (bf16[1,160,384]{2,1,0:T(8,128)(2,1)}, bf16[1,160,384]{2,1,0:T(8,128)(2,1)S(1)}, u32[]{:S(2)}, u32[]{:S(2)}) collective-permute-start(bf16[1,160,384]{2,1,0:T(8,128)(2,1)} %get-tuple-element.314), channel_id=1, source_target_pairs={{0,16},{4,20},{8,24},{12,28},{16,0},{20,4},{24,8},{28,12},{1,17},{... | collective-permute-start | bytes 368648 | tf_op jit(solution)/shard_map/ppermute | solution.py:950
  294.4 14.5 %collective-permute-start.16 = (bf16[4,160,384]{2,1,0:T(8,128)(2,1)S(1)}, bf16[4,160,384]{2,1,0:T(8,128)(2,1)}, u32[]{:S(2)}, u32[]{:S(2)}) collective-permute-start(bf16[4,160,384]{2,1,0:T(8,128)(2,1)S(1)} %get-tuple-element.323), channel_id=1, source_target_pairs={{0,4},{4,0},{8,12},{12,8},{16,20},{20,16},{24,28},{28,24},{1,5},{5... | collective-permute-start | bytes 1474568 | tf_op jit(solution)/shard_map/ppermute | solution.py:950
  295.5 16.0 %collective-permute-start.17 = (bf16[2,432,384]{2,1,0:T(8,128)(2,1)}, bf16[2,432,384]{2,1,0:T(8,128)(2,1)}, u32[]{:S(2)}, u32[]{:S(2)}) collective-permute-start(bf16[2,432,384]{2,1,0:T(8,128)(2,1)} %get-tuple-element.329), channel_id=1, source_target_pairs={{0,8},{4,12},{8,0},{12,4},{16,24},{20,28},{24,16},{28,20},{1,9},{5... | collective-permute-start | bytes 1990664 | tf_op jit(solution)/shard_map/ppermute | solution.py:950
  302.8 5.4 %copy-start.7 = (bf16[1,160,384]{2,1,0:T(8,128)(2,1)S(1)}, bf16[1,160,384]{2,1,0:T(8,128)(2,1)}, u32[]{:S(2)}) copy-start(bf16[1,160,384]{2,1,0:T(8,128)(2,1)} %get-tuple-element.316) | copy-start | bytes 368644
  314.8 4.5 %collective-permute-start.19 = (bf16[768,768]{1,0:T(8,128)(2,1)S(1)}, bf16[768,768]{1,0:T(8,128)(2,1)}, u32[]{:S(2)}, u32[]{:S(2)}) collective-permute-start(bf16[768,768]{1,0:T(8,128)(2,1)S(1)} %get-tuple-element.415), channel_id=1, source_target_pairs={{0,1},{1,0},{2,3},{3,2},{4,5},{5,4},{6,7},{7,6},{8,9},{9,8},{10,11... | collective-permute-start | bytes 3538952 | tf_op jit(solution)/shard_map/ppermute | solution.py:947
  315.1 20.5 %collective-permute-start.35 = (f32[2,2,2]{2,1,0:T(2,128)S(1)}, f32[2,2,2]{2,1,0:T(2,128)S(1)}, u32[]{:S(2)}, u32[]{:S(2)}) collective-permute-start(f32[2,2,2]{2,1,0:T(2,128)S(1)} %reshape.220), channel_id=1, source_target_pairs={{0,1},{1,0},{2,3},{3,2},{4,5},{5,4},{6,7},{7,6},{8,9},{9,8},{10,11... | collective-permute-start | bytes 104 | tf_op jit(solution)/shard_map/ppermute | solution.py:947
  315.6 20.2 %collective-permute-start.26 = (bf16[432,384]{1,0:T(8,128)(2,1)S(1)}, bf16[432,384]{1,0:T(8,128)(2,1)}, u32[]{:S(2)}, u32[]{:S(2)}) collective-permute-start(bf16[432,384]{1,0:T(8,128)(2,1)S(1)} %copy-done.9), channel_id=1, source_target_pairs={{0,2},{1,3},{2,0},{3,1},{4,6},{5,7},{6,4},{7,5},{8,10},{9,11},{10,... | collective-permute-start | bytes 995336 | tf_op jit(solution)/shard_map/ppermute | solution.py:947
  317.2 11.6 %collective-permute-start.20 = (bf16[2,160,384]{2,1,0:T(8,128)(2,1)S(1)}, bf16[2,160,384]{2,1,0:T(8,128)(2,1)S(1)}, u32[]{:S(2)}, u32[]{:S(2)}) collective-permute-start(bf16[2,160,384]{2,1,0:T(8,128)(2,1)S(1)} %get-tuple-element.342), channel_id=1, source_target_pairs={{0,8},{4,12},{8,0},{12,4},{16,24},{20,28},{24,16},{28,20},{1,9},{5... | collective-permute-start | bytes 737288 | tf_op jit(solution)/shard_map/ppermute | solution.py:950
  317.5 17.5 %collective-permute-start.21 = (bf16[1,432,384]{2,1,0:T(8,128)(2,1)}, bf16[1,432,384]{2,1,0:T(8,128)(2,1)S(1)}, u32[]{:S(2)}, u32[]{:S(2)}) collective-permute-start(bf16[1,432,384]{2,1,0:T(8,128)(2,1)} %get-tuple-element.348), channel_id=1, source_target_pairs={{0,16},{4,20},{8,24},{12,28},{16,0},{20,4},{24,8},{28,12},{1,17},{... | collective-permute-start | bytes 995336 | tf_op jit(solution)/shard_map/ppermute | solution.py:950
  335.0 16.4 %copy-start.10 = (bf16[432,384]{1,0:T(8,128)(2,1)}, bf16[432,384]{1,0:T(8,128)(2,1)S(1)}, u32[]{:S(2)}) copy-start(bf16[432,384]{1,0:T(8,128)(2,1)S(1)} %add_bitcast_fusion.refs_0_) | copy-start | bytes 995332
  335.0 9.7 %collective-permute-start.23 = (bf16[432,384]{1,0:T(8,128)(2,1)S(1)}, bf16[432,384]{1,0:T(8,128)(2,1)S(1)}, u32[]{:S(2)}, u32[]{:S(2)}) collective-permute-start(bf16[432,384]{1,0:T(8,128)(2,1)S(1)} %add_bitcast_fusion.refs_0_), channel_id=1, source_target_pairs={{0,2},{1,3},{2,0},{3,1},{4,6},{5,7},{6,4},{7,5},{8,10},{9,11},{10,... | collective-permute-start | bytes 995336 | tf_op jit(solution)/shard_map/ppermute | solution.py:947
  335.6 6.3 %collective-permute-start.22 = (bf16[1,160,384]{2,1,0:T(8,128)(2,1)S(1)}, bf16[1,160,384]{2,1,0:T(8,128)(2,1)S(1)}, u32[]{:S(2)}, u32[]{:S(2)}) collective-permute-start(bf16[1,160,384]{2,1,0:T(8,128)(2,1)S(1)} %get-tuple-element.354), channel_id=1, source_target_pairs={{0,16},{4,20},{8,24},{12,28},{16,0},{20,4},{24,8},{28,12},{1,17},{... | collective-permute-start | bytes 368648 | tf_op jit(solution)/shard_map/ppermute | solution.py:950
  335.6 9.2 %collective-permute-start.27 = (bf16[432,384]{1,0:T(8,128)(2,1)S(1)}, bf16[432,384]{1,0:T(8,128)(2,1)S(1)}, u32[]{:S(2)}, u32[]{:S(2)}) collective-permute-start(bf16[432,384]{1,0:T(8,128)(2,1)S(1)} %copy-done.9), channel_id=1, source_target_pairs={{0,1},{1,0},{2,3},{3,2},{4,5},{5,4},{6,7},{7,6},{8,9},{9,8},{10,11... | collective-permute-start | bytes 995336 | tf_op jit(solution)/shard_map/ppermute | solution.py:947
  335.9 10.2 %collective-permute-start.28 = (bf16[432,384]{1,0:T(8,128)(2,1)}, bf16[432,384]{1,0:T(8,128)(2,1)S(1)}, u32[]{:S(2)}, u32[]{:S(2)}) collective-permute-start(bf16[432,384]{1,0:T(8,128)(2,1)} %collective-permute-done.26.refs_5_), channel_id=1, source_target_pairs={{0,1},{1,0},{2,3},{3,2},{4,5},{5,4},{6,7},{7,6},{8,9},{9,8},{10,11... | collective-permute-start | bytes 995336 | tf_op jit(solution)/shard_map/ppermute | solution.py:947
  336.4 9.9 %collective-permute-start.32 = (bf16[160,384]{1,0:T(8,128)(2,1)}, bf16[160,384]{1,0:T(8,128)(2,1)S(1)}, u32[]{:S(2)}, u32[]{:S(2)}) collective-permute-start(bf16[160,384]{1,0:T(8,128)(2,1)} %add_bitcast_fusion.3.refs_4_), channel_id=1, source_target_pairs={{0,2},{1,3},{2,0},{3,1},{4,6},{5,7},{6,4},{7,5},{8,10},{9,11},{10,... | collective-permute-start | bytes 368648 | tf_op jit(solution)/shard_map/ppermute | solution.py:947
  341.8 8.8 %collective-permute-start.24 = (bf16[432,384]{1,0:T(8,128)(2,1)S(1)}, bf16[432,384]{1,0:T(8,128)(2,1)S(1)}, u32[]{:S(2)}, u32[]{:S(2)}) collective-permute-start(bf16[432,384]{1,0:T(8,128)(2,1)S(1)} %add_bitcast_fusion.refs_0_), channel_id=1, source_target_pairs={{0,1},{1,0},{2,3},{3,2},{4,5},{5,4},{6,7},{7,6},{8,9},{9,8},{10,11... | collective-permute-start | bytes 995336 | tf_op jit(solution)/shard_map/ppermute | solution.py:947
  344.8 6.6 %copy-start.20 = (bf16[432,384]{1,0:T(8,128)(2,1)}, bf16[432,384]{1,0:T(8,128)(2,1)S(1)}, u32[]{:S(2)}) copy-start(bf16[432,384]{1,0:T(8,128)(2,1)S(1)} %collective-permute-done.23.refs_1_) | copy-start | bytes 995332
  344.8 6.6 %collective-permute-start.25 = (bf16[432,384]{1,0:T(8,128)(2,1)S(1)}, bf16[432,384]{1,0:T(8,128)(2,1)}, u32[]{:S(2)}, u32[]{:S(2)}) collective-permute-start(bf16[432,384]{1,0:T(8,128)(2,1)S(1)} %collective-permute-done.23.refs_1_), channel_id=1, source_target_pairs={{0,1},{1,0},{2,3},{3,2},{4,5},{5,4},{6,7},{7,6},{8,9},{9,8},{10,11... | collective-permute-start | bytes 995336 | tf_op jit(solution)/shard_map/ppermute | solution.py:947
  344.8 12.2 %copy-start.13 = (bf16[160,384]{1,0:T(8,128)(2,1)}, bf16[160,384]{1,0:T(8,128)(2,1)S(1)}, u32[]{:S(2)}) copy-start(bf16[160,384]{1,0:T(8,128)(2,1)S(1)} %add_bitcast_fusion.2.refs_0_) | copy-start | bytes 368644
  344.8 6.6 %copy-start.21 = (bf16[432,384]{1,0:T(8,128)(2,1)}, bf16[432,384]{1,0:T(8,128)(2,1)S(1)}, u32[]{:S(2)}) copy-start(bf16[432,384]{1,0:T(8,128)(2,1)S(1)} %collective-permute-done.27.refs_6_) | copy-start | bytes 995332
  344.8 5.8 %collective-permute-start.29 = (bf16[160,384]{1,0:T(8,128)(2,1)S(1)}, bf16[160,384]{1,0:T(8,128)(2,1)S(1)}, u32[]{:S(2)}, u32[]{:S(2)}) collective-permute-start(bf16[160,384]{1,0:T(8,128)(2,1)S(1)} %add_bitcast_fusion.2.refs_0_), channel_id=1, source_target_pairs={{0,2},{1,3},{2,0},{3,1},{4,6},{5,7},{6,4},{7,5},{8,10},{9,11},{10,... | collective-permute-start | bytes 368648 | tf_op jit(solution)/shard_map/ppermute | solution.py:947
  346.1 10.9 %collective-permute-start.33 = (bf16[160,384]{1,0:T(8,128)(2,1)}, bf16[160,384]{1,0:T(8,128)(2,1)S(1)}, u32[]{:S(2)}, u32[]{:S(2)}) collective-permute-start(bf16[160,384]{1,0:T(8,128)(2,1)} %add_bitcast_fusion.3.refs_4_), channel_id=1, source_target_pairs={{0,1},{1,0},{2,3},{3,2},{4,5},{5,4},{6,7},{7,6},{8,9},{9,8},{10,11... | collective-permute-start | bytes 368648 | tf_op jit(solution)/shard_map/ppermute | solution.py:947
  346.3 10.6 %copy-start.24 = (bf16[160,384]{1,0:T(8,128)(2,1)}, bf16[160,384]{1,0:T(8,128)(2,1)S(1)}, u32[]{:S(2)}) copy-start(bf16[160,384]{1,0:T(8,128)(2,1)S(1)} %collective-permute-done.32.refs_5_) | copy-start | bytes 368644
  346.3 10.7 %collective-permute-start.34 = (bf16[160,384]{1,0:T(8,128)(2,1)S(1)}, bf16[160,384]{1,0:T(8,128)(2,1)S(1)}, u32[]{:S(2)}, u32[]{:S(2)}) collective-permute-start(bf16[160,384]{1,0:T(8,128)(2,1)S(1)} %collective-permute-done.32.refs_5_), channel_id=1, source_target_pairs={{0,1},{1,0},{2,3},{3,2},{4,5},{5,4},{6,7},{7,6},{8,9},{9,8},{10,11... | collective-permute-start | bytes 368648 | tf_op jit(solution)/shard_map/ppermute | solution.py:947
  350.6 6.3 %copy-start.25 = (bf16[160,384]{1,0:T(8,128)(2,1)}, bf16[160,384]{1,0:T(8,128)(2,1)S(1)}, u32[]{:S(2)}) copy-start(bf16[160,384]{1,0:T(8,128)(2,1)S(1)} %collective-permute-done.29.refs_1_) | copy-start | bytes 368644
  350.6 6.4 %collective-permute-start.30 = (bf16[160,384]{1,0:T(8,128)(2,1)S(1)}, bf16[160,384]{1,0:T(8,128)(2,1)S(1)}, u32[]{:S(2)}, u32[]{:S(2)}) collective-permute-start(bf16[160,384]{1,0:T(8,128)(2,1)S(1)} %add_bitcast_fusion.2.refs_0_), channel_id=1, source_target_pairs={{0,1},{1,0},{2,3},{3,2},{4,5},{5,4},{6,7},{7,6},{8,9},{9,8},{10,11... | collective-permute-start | bytes 368648 | tf_op jit(solution)/shard_map/ppermute | solution.py:947
  350.7 6.4 %collective-permute-start.31 = (bf16[160,384]{1,0:T(8,128)(2,1)S(1)}, bf16[160,384]{1,0:T(8,128)(2,1)S(1)}, u32[]{:S(2)}, u32[]{:S(2)}) collective-permute-start(bf16[160,384]{1,0:T(8,128)(2,1)S(1)} %collective-permute-done.29.refs_1_), channel_id=1, source_target_pairs={{0,1},{1,0},{2,3},{3,2},{4,5},{5,4},{6,7},{7,6},{8,9},{9,8},{10,11... | collective-permute-start | bytes 368648 | tf_op jit(solution)/shard_map/ppermute | solution.py:947
  (18 other events, 33.8 us)

commit v5 on v4

--- a/solution.py
+++ b/solution.py
@@ -153,7 +153,7 @@
     box_rate = jnp.exp2(-lax.broadcasted_iota(jnp.int32, (8, 1), 0).astype(f32))
     angles = [text]
     for c in range(4):
-        coords = row_of(boxes_ref.at[c]).astype(f32)
+        coords = row_of(boxes_ref.at[:, c]).astype(f32)
         angles.append(coords * box_rate)
     angles = jnp.concatenate(angles, 0)
     cosines, sines = jnp.cos(angles), jnp.sin(angles)
@@ -413,8 +413,8 @@
         parts = upcoming
 
 
-def attention_bwd(ids, shared, tables, joint, turned, kv_far, lse, g_ctx, rel_pairs, layer, split, per_step=2):
-    per_step = 1 if split else per_step
+def attention_bwd(ids, shared, tables, joint, turned, kv_far, lse, g_ctx, rel_pairs, layer, split, per_step=3):
+    per_step = 3 if split else per_step
     cos_t, sin_t, kf, ctab, stab, code, seg, valid = tables
     tokens, width = joint.shape[0], joint.shape[1] // 3
     half = tokens // 3
@@ -600,10 +600,20 @@
     ids, g0, g1, g2, n2_ref, r2_ref, n1_ref, r1_ref, scale_ref, out_ref, slope_ref, in_ref, w_out_ref,
     act_ref, mixed_in_ref, own_ref, shared_ref,
     mixed_ref, attn_ref, ctx_ref, sums_ref, pre_sum_ref, keep_ref, send_ref,
-    res_ref, acc_ref, feed_ref, pre_ref, feed_t, mixed_t,
-    *, layer, parts,
+    res_ref, acc_ref, feed_ref, pre_ref, feed_t, mixed_t, *late,
+    layer, parts,
 ):
     j = pl.program_id(0)
+    buffers, sems = late[:-1], late[-1]
+    sources = (n1_ref, r1_ref, w_out_ref.at[layer], own_ref, shared_ref)
+    copies = [pltpu.make_async_copy(a, b, sems.at[k]) for k, (a, b) in enumerate(zip(sources, buffers))]
+    n1_ref, r1_ref, w_out_ref, own_ref, shared_ref = buffers
+
+    @pl.when(j == 0)
+    def _():
+        for copy in copies:
+            copy.start()
+
     tokens = n2_ref.shape[0]
     gain = lambda k: scale_ref[layer, k : k + 1, :].astype(f32)
     rows = NORM_ROWS
@@ -679,6 +689,9 @@
 
     @pl.when(j == pl.num_programs(0) - 1)
     def _():
+        for copy in copies:
+            copy.wait()
+
         def chunk(i, sums):
             to = pl.ds(i * rows, rows)
             g_mixed = acc_ref[to, :] + res_ref[to, :]
@@ -692,7 +705,7 @@
         sums = row_loop(tokens // rows, chunk, (zero, zero, zero))
         for k, x in zip((0, 2, 4), sums):
             sums_ref[k : k + 1, :] = col_sum(x)
-        ctx_ref[...] = dot_nt(attn_ref[...], w_out_ref[0]).astype(bf16)
+        ctx_ref[...] = dot_nt(attn_ref[...], w_out_ref[...]).astype(bf16)
         long = own_ref.shape[1]
         for side in range(2):
 
@@ -713,6 +726,7 @@
     tokens, ff = 3 * half, ffn_in.shape[2]
     once = lambda *shape: pl.BlockSpec(shape, lambda i, ids: (0,) * len(shape), pipeline_mode=pl.Buffered(1))
     full = lambda *shape: spec(shape, *([0] * len(shape)))
+    anywhere = pl.BlockSpec(memory_space=pl.ANY)
     dense = ((tokens, width), bf16)
     piece = ((SUPER, LANES + width // SUPER // 2, LANES), bf16)
     outs = [dense, dense, dense, ((8, width), f32), ((8, ff), f32), piece, piece]
@@ -722,10 +736,10 @@
         functools.partial(feed_bwd_kernel, layer=layer, parts=parts), "feed_backward", (ff // chunk,), ids,
         row_tiles(half, width, gathered)
         + [
-            once(tokens, width), once(tokens, 128), once(tokens, width), once(tokens, 128),
+            once(tokens, width), once(tokens, 128), anywhere, anywhere,
             full(*ln_scale.shape), spec((1, chunk, width), layer, step, 0), spec((tokens, chunk), 0, step),
-            spec((1, width, chunk), layer, 0, step), spec((1, width, width), layer, 0, 0),
-            spec((tokens, chunk), 0, step), once(tokens, width), once(*ctx_own.shape), once(*ctx_shared.shape),
+            spec((1, width, chunk), layer, 0, step), anywhere,
+            spec((tokens, chunk), 0, step), once(tokens, width), anywhere, anywhere,
         ],
         [grad, grad, grad, n2, r2, n1, r1, ln_scale, ffn_out, slope, ffn_in, w_out, act, mixed, ctx_own,
          ctx_shared],
@@ -734,6 +748,9 @@
             pltpu.VMEM((tokens, width), f32), pltpu.VMEM((tokens, width), f32),
             pltpu.VMEM((tokens, width), bf16), pltpu.VMEM((tokens, chunk), bf16),
             pltpu.VMEM((LANES, tokens), bf16), pltpu.VMEM((width, tokens), bf16),
+            pltpu.VMEM((tokens, width), bf16), pltpu.VMEM((tokens, 128), f32),
+            pltpu.VMEM((width, width), bf16), pltpu.VMEM(ctx_own.shape, bf16),
+            pltpu.VMEM(ctx_shared.shape, bf16), pltpu.SemaphoreType.DMA((5,)),
         ],
     )
 
@@ -949,7 +966,7 @@
     def flip_dp(x, bit):
         return lax.ppermute(x, "dp", [(i, i ^ bit) for i in range(dp)])
 
-    tables = make_tables(ids, word_boxes, segments, valid_mask)
+    tables = make_tables(ids, jnp.swapaxes(word_boxes, 0, 1), segments, valid_mask)
     ctab, stab, valid_col = tables[3], tables[4], tables[7]
 
     halves = lambda x: x.reshape(-1, half, width)

time: 369 us -> 365 us (0.989)
  transfers between devices with their start and end apart: 36 -> 36, of which waited for: 10 -> 10; matrix products, arithmetic and copies ran while one was open for 7% -> 8% of each run, Pallas kernels for 38% -> 38%
where the time goes in v5:
time: 365 us; the launch traced here: 358 us
  Pallas kernels  259 us (71%)
  waiting for transfers between devices  37 us (10%)
  other arithmetic  30.3 us (8%)
  starting transfers between devices  24.5 us (7%)
  local copies, waits for them, and re-layouts  5.95 us (2%)
    pallas_call x21, Pallas kernels, call(): pl.pallas_call(kernel, grid_spec=pltpu.PrefetchScalarGridSpec(num_scalar_...  259 us
    ppermute x12, waiting for transfers between devices, flip_dp(): return lax.ppermute(x, 'dp', [(i, i ^ bit) for i in range(dp)])  26.4 us
    add x12, other arithmetic, absorb(): return pin((keep[:n] + arrived[:n], keep[n:] + arrived[n:]))  21.8 us
    ppermute x12, starting transfers between devices, flip_dp(): return lax.ppermute(x, 'dp', [(i, i ^ bit) for i in range(dp)])  14 us
    ppermute x24, waiting for transfers between devices, flip(): return lax.ppermute(x, 'section', [(i, i ^ bit) for i in range(sections)])  10.6 us
    ppermute x24, starting transfers between devices, flip(): return lax.ppermute(x, 'section', [(i, i ^ bit) for i in range(sections)])  10.6 us
  transfers between devices with their start and end apart: 36, of which 10 were waited for; matrix products, arithmetic and copies ran while one was open for 8% of the time, Pallas kernels for 38%

profile of v5, /device:TPU:0, one launch (start us, length us, event | category | flops | bytes accessed | tf_op | source)
XLA Modules:
  0.0 358.1 jit_solution(7416800923225194000)
XLA Ops:
  1.3 4.1 %tables.1 = (f32[64,1024]{1,0:T(8,128)}, f32[64,1024]{1,0:T(8,128)}, bf16[1024,128]{1,0:T(8,128)(2,1)}, f32[1024,128]{1,0:T(8,128)}, f32[1024,128]{1,0:T(8,128)}...) custom-call(s32[3]{0:T(128)} %pad_add_fusion.ids, s32[3,4,512]{2,1,0:T(4,128)} %bitcast.67, ...), custom_call_target="tpu_custom_call" | custom-call | flops 4400000000 | bytes 4000000 | tf_op jit(solution)/shard_map/tables/pallas_call | solution.py:83
  5.5 9.9 %projections.2 = (bf16[768,2304]{1,0:T(8,128)(2,1)}, bf16[768,1536]{1,0:T(8,128)(2,1)}, bf16[256,1536]{1,0:T(8,128)(2,1)}) custom-call(s32[3]{0:T(128)} %pad_add_fusion.ids, bf16[6,256,768]{2,1,0:T(8,128)(2,1)} %bitcast.31, bf16[6,256,768]{2,1,0:T(8,128)(2,1)} %bitcast.32, bf16[6,256,768]{2,1,0:T(8,128)(2,1)} %bitcast.33, bf16[2,768,2304]{2,1,0:T(8,128)(2,1)} %w_ref.7, ...), custom_call_target="tpu_custom_call" | custom-call | flops 8800000000 | bytes 8000000 | tf_op jit(solution)/shard_map/projections/pallas_call | solution.py:83
  15.8 8.6 %attention_forward.4 = (bf16[768,512]{1,0:T(8,128)(2,1)}, f32[6,2,512]{2,1,0:T(2,128)}) custom-call(s32[3]{0:T(128)} %pad_add_fusion.ids, f32[1024,128]{1,0:T(8,128)} %get-tuple-element.197.code_ref, f32[8,1024]{1,0:T(8,128)} %get-tuple-element.198.seg_ref, bf16[1024,128]{1,0:T(8,128)(2,1)} %get-tuple-element.199.kf_ref, ...), custom_call_target="tpu_custom_call" | custom-call | flops 7699999744 | bytes 7000000 | tf_op jit(solution)/shard_map/attention_forward/pallas_call | solution.py:83
  25.4 6.3 %attention_forward.5 = (bf16[768,256]{1,0:T(8,128)(2,1)}, f32[6,2,256]{2,1,0:T(2,128)}) custom-call(s32[3]{0:T(128)} %pad_add_fusion.ids, f32[1024,128]{1,0:T(8,128)} %get-tuple-element.197.code_ref, f32[8,1024]{1,0:T(8,128)} %get-tuple-element.198.seg_ref, bf16[1024,128]{1,0:T(8,128)(2,1)} %get-tuple-element.199.kf_ref, ...), custom_call_target="tpu_custom_call" | custom-call | flops 7699999744 | bytes 7000000 | tf_op jit(solution)/shard_map/attention_forward/pallas_call | solution.py:83
  31.7 25.8 %feed_forward.2 = (bf16[768,768]{1,0:T(8,128)(2,1)}, f32[768,128]{1,0:T(8,128)}, bf16[768,768]{1,0:T(8,128)(2,1)}, f32[768,128]{1,0:T(8,128)}, bf16[768,768]{1,0...) custom-call(s32[3]{0:T(128)} %pad_add_fusion.ids, ...), custom_call_target="tpu_custom_call" | custom-call | flops 26400000000 | bytes 24000000 | tf_op jit(solution)/shard_map/feed_forward/pallas_call | solution.py:83
  57.5 9.9 %projections.3 = (bf16[768,2304]{1,0:T(8,128)(2,1)}, bf16[768,1536]{1,0:T(8,128)(2,1)}, bf16[256,1536]{1,0:T(8,128)(2,1)}) custom-call(s32[3]{0:T(128)} %pad_add_fusion.ids, bf16[3,256,768]{2,1,0:T(8,128)(2,1)} %bitcast.40, bf16[3,256,768]{2,1,0:T(8,128)(2,1)} %bitcast.41, bf16[3,256,768]{2,1,0:T(8,128)(2,1)} %bitcast.42, bf16[2,768,2304]{2,1,0:T(8,128)(2,1)} %w_ref.7, ...), custom_call_target="tpu_custom_call" | custom-call | flops 8800000000 | bytes 8000000 | tf_op jit(solution)/shard_map/projections/pallas_call | solution.py:83
  67.5 8.6 %attention_forward.6 = (bf16[768,512]{1,0:T(8,128)(2,1)}, f32[6,2,512]{2,1,0:T(2,128)}) custom-call(s32[3]{0:T(128)} %pad_add_fusion.ids, f32[1024,128]{1,0:T(8,128)} %get-tuple-element.197.code_ref, f32[8,1024]{1,0:T(8,128)} %get-tuple-element.198.seg_ref, bf16[1024,128]{1,0:T(8,128)(2,1)} %get-tuple-element.199.kf_ref, ...), custom_call_target="tpu_custom_call" | custom-call | flops 7699999744 | bytes 7000000 | tf_op jit(solution)/shard_map/attention_forward/pallas_call | solution.py:83
  77.0 6.7 %attention_forward.7 = (bf16[768,256]{1,0:T(8,128)(2,1)}, f32[6,2,256]{2,1,0:T(2,128)}) custom-call(s32[3]{0:T(128)} %pad_add_fusion.ids, f32[1024,128]{1,0:T(8,128)} %get-tuple-element.197.code_ref, f32[8,1024]{1,0:T(8,128)} %get-tuple-element.198.seg_ref, bf16[1024,128]{1,0:T(8,128)(2,1)} %get-tuple-element.199.kf_ref, ...), custom_call_target="tpu_custom_call" | custom-call | flops 7699999744 | bytes 7000000 | tf_op jit(solution)/shard_map/attention_forward/pallas_call | solution.py:83
  83.7 25.5 %feed_forward.3 = (bf16[768,768]{1,0:T(8,128)(2,1)}, f32[768,128]{1,0:T(8,128)}, bf16[768,768]{1,0:T(8,128)(2,1)}, f32[768,128]{1,0:T(8,128)}, bf16[768,768]{1,0...) custom-call(s32[3]{0:T(128)} %pad_add_fusion.ids, ...), custom_call_target="tpu_custom_call" | custom-call | flops 26400000000 | bytes 24000000 | tf_op jit(solution)/shard_map/feed_forward/pallas_call | solution.py:83
  109.2 31.0 %feed_backward.2 = (bf16[768,768]{1,0:T(8,128)(2,1)}, bf16[768,768]{1,0:T(8,128)(2,1)}, bf16[768,768]{1,0:T(8,128)(2,1)}, f32[8,768]{1,0:T(8,128)}, f32[8,3072]{...) custom-call(s32[3]{0:T(128)} %pad_add_fusion.ids, bf16[6,256,768]{2,1,0:T(8,128)(2,1)} %bitcast.57, ...), custom_call_target="tpu_custom_call" | custom-call | flops 32999999488 | bytes 30000000 | tf_op jit(solution)/shard_map/feed_backward/pallas_call | solution.py:83
  140.7 10.9 %attention_backward.5 = (bf16[3,256,768]{2,1,0:T(8,128)(2,1)}, bf16[2,256,768]{2,1,0:T(8,128)(2,1)}, f32[128,768]{1,0:T(8,128)}) custom-call(s32[3]{0:T(128)} %pad_add_fusion.ids, f32[1024,128]{1,0:T(8,128)} %get-tuple-element.197.code_ref, f32[8,1024]{1,0:T(8,128)} %get-tuple-element.198.seg_ref, bf16[1024,128]{1,0:T(8,128)(2,1)} %get-tuple-element.199.kf_ref, ...), custom_call_target="tpu_custom_call" | custom-call | flops 44000002048 | bytes 40000000 | tf_op jit(solution)/shard_map/attention_backward/pallas_call | solution.py:83
  151.8 3.9 %slice_add_fusion.2 = (bf16[4,432,384]{2,1,0:T(8,128)(2,1)}, bf16[4,432,384]{2,1,0:T(8,128)(2,1)S(1)}) fusion(bf16[8,432,384]{2,1,0:T(8,128)(2,1)} %collective-permute-done.2, bf16[8,432,384]{2,1,0:T(8,128)(2,1)} %get-tuple-element.224), kind=kLoop, calls=%fused_computation.2 | loop fusion | flops 1327104 | bytes 7962624 | tf_op jit(solution)/shard_map/add | solution.py:999
  155.6 2.9 collective-permute-start.3
  158.6 16.6 %attention_backward.4 = (bf16[3,512,768]{2,1,0:T(8,128)(2,1)}, f32[128,768]{1,0:T(8,128)}) custom-call(s32[3]{0:T(128)} %pad_add_fusion.ids, f32[1024,128]{1,0:T(8,128)} %get-tuple-element.197.code_ref, f32[8,1024]{1,0:T(8,128)} %get-tuple-element.198.seg_ref, bf16[1024,128]{1,0:T(8,128)(2,1)} %get-tuple-element.199.kf_ref, ...), custom_call_target="tpu_custom_call" | custom-call | flops 13200000000 | bytes 12000000 | tf_op jit(solution)/shard_map/attention_backward/pallas_call | solution.py:83
  175.1 13.6 %projections_backward.2 = (bf16[768,768]{1,0:T(8,128)(2,1)}, bf16[8,160,384]{2,1,0:T(8,128)(2,1)}, bf16[8,160,384]{2,1,0:T(8,128)(2,1)}) custom-call(s32[3]{0:T(128)} %pad_add_fusion.ids, bf16[3,256,768]{2,1,0:T(8,128)(2,1)} %bitcast.46, bf16[3,256,768]{2,1,0:T(8,128)(2,1)} %bitcast.47, bf16[3,256,768]{2,1,0:T(8,128)(2,1)} %bitcast.48, ...), custom_call_target="tpu_custom_call" | custom-call | flops 3300000000 | bytes 3000000 | tf_op jit(solution)/shard_map/projections_backward/pallas_call | solution.py:83
  188.7 2.4 slice_add_fusion.6
  191.6 1.7 collective-permute-start.6
  194.1 30.7 %feed_backward.3 = (bf16[768,768]{1,0:T(8,128)(2,1)}, bf16[768,768]{1,0:T(8,128)(2,1)}, bf16[768,768]{1,0:T(8,128)(2,1)}, f32[8,768]{1,0:T(8,128)}, f32[8,3072]{...) custom-call(s32[3]{0:T(128)} %pad_add_fusion.ids, bf16[3,256,768]{2,1,0:T(8,128)(2,1)} %bitcast.49, ...), custom_call_target="tpu_custom_call" | custom-call | flops 32999999488 | bytes 30000000 | tf_op jit(solution)/shard_map/feed_backward/pallas_call | solution.py:83
  224.9 1.9 slice_add_fusion.14
  226.8 1.8 slice_add_fusion.18
  228.6 6.9 %attention_backward.7 = (bf16[3,256,384]{2,1,0:T(8,128)(2,1)}, bf16[2,256,384]{2,1,0:T(8,128)(2,1)}, f32[128,384]{1,0:T(8,128)}) custom-call(s32[3]{0:T(128)} %pad_add_fusion.ids, f32[1024,128]{1,0:T(8,128)} %get-tuple-element.197.code_ref, f32[8,1024]{1,0:T(8,128)} %get-tuple-element.198.seg_ref, bf16[1024,128]{1,0:T(8,128)(2,1)} %get-tuple-element.199.kf_ref, ...), custom_call_target="tpu_custom_call" | custom-call | flops 44000002048 | bytes 40000000 | tf_op jit(solution)/shard_map/attention_backward/pallas_call | solution.py:83
  236.0 2.6 collective-permute-start.9
  239.0 4.3 %slice_add_fusion = (bf16[4,432,384]{2,1,0:T(8,128)(2,1)}, bf16[4,432,384]{2,1,0:T(8,128)(2,1)}) fusion(bf16[8,432,384]{2,1,0:T(8,128)(2,1)} %collective-permute-done.8, bf16[8,432,384]{2,1,0:T(8,128)(2,1)} %get-tuple-element.275), kind=kLoop, calls=%fused_computation | loop fusion | flops 1327104 | bytes 7962624 | tf_op jit(solution)/shard_map/add | solution.py:999
  243.3 9.9 %attention_backward.6 = (bf16[3,512,384]{2,1,0:T(8,128)(2,1)}, f32[128,384]{1,0:T(8,128)}) custom-call(s32[3]{0:T(128)} %pad_add_fusion.ids, f32[1024,128]{1,0:T(8,128)} %get-tuple-element.197.code_ref, f32[8,1024]{1,0:T(8,128)} %get-tuple-element.198.seg_ref, bf16[1024,128]{1,0:T(8,128)(2,1)} %get-tuple-element.199.kf_ref, ...), custom_call_target="tpu_custom_call" | custom-call | flops 13200000000 | bytes 12000000 | tf_op jit(solution)/shard_map/attention_backward/pallas_call | solution.py:83
  254.4 1.7 slice_add_fusion.22
  258.1 12.6 %projections_backward.3 = (bf16[768,768]{1,0:T(8,128)(2,1)}, bf16[8,160,384]{2,1,0:T(8,128)(2,1)}, bf16[8,160,384]{2,1,0:T(8,128)(2,1)}) custom-call(s32[3]{0:T(128)} %pad_add_fusion.ids, bf16[6,256,768]{2,1,0:T(8,128)(2,1)} %bitcast.37, bf16[6,256,768]{2,1,0:T(8,128)(2,1)} %bitcast.38, bf16[6,256,768]{2,1,0:T(8,128)(2,1)} %bitcast.39, ...), custom_call_target="tpu_custom_call" | custom-call | flops 3300000000 | bytes 3000000 | tf_op jit(solution)/shard_map/projections_backward/pallas_call | solution.py:83
  270.7 2.7 broadcast_select_fusion.6
  273.8 1.9 collective-permute-start.18
  275.8 11.7 %collective-permute-done.11 = bf16[4,432,384]{2,1,0:T(8,128)(2,1)} collective-permute-done((bf16[4,432,384]{2,1,0:T(8,128)(2,1)}, bf16[4,432,384]{2,1,0:T(8,128)(2,1)}, u32[]{:S(2)}, u32[]{:S(2)}) %collective-permute-start.11) | collective-permute-done | bytes 1327136 | tf_op jit(solution)/shard_map/ppermute | solution.py:967
  287.5 2.3 slice_add_fusion.4
  290.0 1.3 collective-permute-start.16
  293.0 5.5 %place_rows.2 = bf16[6,256,768]{2,1,0:T(8,128)(2,1)} custom-call(s32[3]{0:T(128)} %pad_add_fusion.ids, bf16[3,256,768]{2,1,0:T(8,128)(2,1)} %bitcast.52, bf16[3,256,768]{2,1,0:T(8,128)(2,1)} %bitcast.60), custom_call_target="tpu_custom_call" | custom-call | flops 4400000000 | bytes 4000000 | tf_op jit(solution)/shard_map/place_rows/pallas_call | solution.py:83
  298.5 3.7 %collective-permute-done.18 = bf16[768,768]{1,0:T(8,128)(2,1)} collective-permute-done((bf16[768,768]{1,0:T(8,128)(2,1)}, bf16[768,768]{1,0:T(8,128)(2,1)}, u32[]{:S(2)}, u32[]{:S(2)}) %collective-permute-start.18) | collective-permute-done | bytes 1179680 | tf_op jit(solution)/shard_map/ppermute | solution.py:964
  302.2 1.9 add.140
  304.8 1.2 slice_add_fusion.16
  307.3 1.9 slice_add_fusion.12
  309.2 1.3 broadcast_select_fusion.4
  311.4 1.6 collective-permute-start.26
  313.3 2.0 collective-permute-start.21
  315.3 6.6 %place_rows.3 = f32[6,256,768]{2,1,0:T(8,128)} custom-call(s32[3]{0:T(128)} %pad_add_fusion.ids, bf16[3,256,768]{2,1,0:T(8,128)(2,1)} %bitcast.53, bf16[3,256,768]{2,1,0:T(8,128)(2,1)} %bitcast.15.other_ref), custom_call_target="tpu_custom_call" | custom-call | flops 4400000000 | bytes 4000000 | tf_op jit(solution)/shard_map/place_rows/pallas_call | solution.py:83
  321.9 2.9 collective-permute-done.20
  324.8 6.0 %collective-permute-done.21 = bf16[1,432,384]{2,1,0:T(8,128)(2,1)S(1)} collective-permute-done((bf16[1,432,384]{2,1,0:T(8,128)(2,1)}, bf16[1,432,384]{2,1,0:T(8,128)(2,1)S(1)}, u32[]{:S(2)}, u32[]{:S(2)}) %collective-permute-start.21) | collective-permute-done | bytes 331808 | tf_op jit(solution)/shard_map/ppermute | solution.py:967
  332.3 1.5 collective-permute-start.32
  333.8 4.2 %collective-permute-done.22 = bf16[1,160,384]{2,1,0:T(8,128)(2,1)S(1)} collective-permute-done((bf16[1,160,384]{2,1,0:T(8,128)(2,1)S(1)}, bf16[1,160,384]{2,1,0:T(8,128)(2,1)S(1)}, u32[]{:S(2)}, u32[]{:S(2)}) %collective-permute-start.22) | collective-permute-done | bytes 122912 | tf_op jit(solution)/shard_map/ppermute | solution.py:967
  338.0 2.6 collective-permute-done.23.refs_1_
  342.5 4.0 %collective-permute-done.29.refs_1_ = bf16[160,384]{1,0:T(8,128)(2,1)S(1)} collective-permute-done((bf16[160,384]{1,0:T(8,128)(2,1)S(1)}, bf16[160,384]{1,0:T(8,128)(2,1)S(1)}, u32[]{:S(2)}, u32[]{:S(2)}) %collective-permute-start.29) | collective-permute-done | bytes 122912 | tf_op jit(solution)/shard_map/ppermute | solution.py:964
  347.2 5.5 %unpack_feed.1 = (f32[2,96,3072]{2,1,0:T(8,128)}, f32[2,384,768]{2,1,0:T(8,128)}, f32[2,96,768]{2,1,0:T(8,128)}) custom-call(s32[3]{0:T(128)} %pad_add_fusion.ids, bf16[432,384]{1,0:T(8,128)(2,1)} %copy-done.10, bf16[432,384]{1,0:T(8,128)(2,1)} %copy-done.20, bf16[432,384]{1,0:T(8,128)(2,1)} %copy-done.23, bf16[432,384]{1,0:T(8,128)(2,1)} %collective-permute-done.25.refs_3_, ...), custom_call_target="tpu_custom_call" | custom-call | flops 4400000000 | bytes 4000000 | tf_op jit(solution)/shard_map/unpack_feed/pallas_call | solution.py:83
  354.2 3.5 unpack_attention.1
  (134 shorter events, 20.0 us)
Async XLA Ops:
  15.4 9.1 %collective-permute-start = (bf16[256,1536]{1,0:T(8,128)(2,1)}, bf16[256,1536]{1,0:T(8,128)(2,1)S(1)}, u32[]{:S(2)}, u32[]{:S(2)}) collective-permute-start(bf16[256,1536]{1,0:T(8,128)(2,1)} %get-tuple-element.205), channel_id=1, source_target_pairs={{0,1},{1,0},{2,3},{3,2},{4,5},{5,4},{6,7},{7,6},{8,9},{9,8},{10,11... | collective-permute-start | bytes 2359304 | tf_op jit(solution)/shard_map/ppermute | solution.py:964
  67.4 8.7 %collective-permute-start.1 = (bf16[256,1536]{1,0:T(8,128)(2,1)}, bf16[256,1536]{1,0:T(8,128)(2,1)S(1)}, u32[]{:S(2)}, u32[]{:S(2)}) collective-permute-start(bf16[256,1536]{1,0:T(8,128)(2,1)} %get-tuple-element.212), channel_id=1, source_target_pairs={{0,1},{1,0},{2,3},{3,2},{4,5},{5,4},{6,7},{7,6},{8,9},{9,8},{10,11... | collective-permute-start | bytes 2359304 | tf_op jit(solution)/shard_map/ppermute | solution.py:964
  140.2 11.5 %collective-permute-start.2 = (bf16[8,432,384]{2,1,0:T(8,128)(2,1)}, bf16[8,432,384]{2,1,0:T(8,128)(2,1)}, u32[]{:S(2)}, u32[]{:S(2)}) collective-permute-start(bf16[8,432,384]{2,1,0:T(8,128)(2,1)} %get-tuple-element.222), channel_id=1, source_target_pairs={{0,1},{1,0},{2,3},{3,2},{4,5},{5,4},{6,7},{7,6},{8,9},{9,8},{10,11... | collective-permute-start | bytes 7962632 | tf_op jit(solution)/shard_map/ppermute | solution.py:964
  151.6 23.5 %collective-permute-start.4 = (bf16[2,256,768]{2,1,0:T(8,128)(2,1)}, bf16[2,256,768]{2,1,0:T(8,128)(2,1)}, u32[]{:S(2)}, u32[]{:S(2)}) collective-permute-start(bf16[2,256,768]{2,1,0:T(8,128)(2,1)} %get-tuple-element.240), channel_id=1, source_target_pairs={{0,1},{1,0},{2,3},{3,2},{4,5},{5,4},{6,7},{7,6},{8,9},{9,8},{10,11... | collective-permute-start | bytes 2359304 | tf_op jit(solution)/shard_map/ppermute | solution.py:964
  155.6 33.1 %collective-permute-start.3 = (bf16[4,432,384]{2,1,0:T(8,128)(2,1)}, bf16[4,432,384]{2,1,0:T(8,128)(2,1)}, u32[]{:S(2)}, u32[]{:S(2)}) collective-permute-start(bf16[4,432,384]{2,1,0:T(8,128)(2,1)} %get-tuple-element.228), channel_id=1, source_target_pairs={{0,4},{4,0},{8,12},{12,8},{16,20},{20,16},{24,28},{28,24},{1,5},{5... | collective-permute-start | bytes 3981320 | tf_op jit(solution)/shard_map/ppermute | solution.py:967
  188.7 2.8 collective-permute-start.5
  191.6 33.3 %collective-permute-start.6 = (bf16[2,432,384]{2,1,0:T(8,128)(2,1)}, bf16[2,432,384]{2,1,0:T(8,128)(2,1)}, u32[]{:S(2)}, u32[]{:S(2)}) collective-permute-start(bf16[2,432,384]{2,1,0:T(8,128)(2,1)} %get-tuple-element.253), channel_id=1, source_target_pairs={{0,8},{4,12},{8,0},{12,4},{16,24},{20,28},{24,16},{28,20},{1,9},{5... | collective-permute-start | bytes 1990664 | tf_op jit(solution)/shard_map/ppermute | solution.py:967
  193.3 33.5 %collective-permute-start.7 = (bf16[4,160,384]{2,1,0:T(8,128)(2,1)S(1)}, bf16[4,160,384]{2,1,0:T(8,128)(2,1)}, u32[]{:S(2)}, u32[]{:S(2)}) collective-permute-start(bf16[4,160,384]{2,1,0:T(8,128)(2,1)S(1)} %get-tuple-element.259), channel_id=1, source_target_pairs={{0,4},{4,0},{8,12},{12,8},{16,20},{20,16},{24,28},{28,24},{1,5},{5... | collective-permute-start | bytes 1474568 | tf_op jit(solution)/shard_map/ppermute | solution.py:967
  224.8 14.2 %collective-permute-start.8 = (bf16[8,432,384]{2,1,0:T(8,128)(2,1)}, bf16[8,432,384]{2,1,0:T(8,128)(2,1)}, u32[]{:S(2)}, u32[]{:S(2)}) collective-permute-start(bf16[8,432,384]{2,1,0:T(8,128)(2,1)} %get-tuple-element.273), channel_id=1, source_target_pairs={{0,1},{1,0},{2,3},{3,2},{4,5},{5,4},{6,7},{7,6},{8,9},{9,8},{10,11... | collective-permute-start | bytes 7962632 | tf_op jit(solution)/shard_map/ppermute | solution.py:964
  228.6 7.4 %copy-start.11 = (bf16[1,432,384]{2,1,0:T(8,128)(2,1)S(1)}, bf16[1,432,384]{2,1,0:T(8,128)(2,1)}, u32[]{:S(2)}) copy-start(bf16[1,432,384]{2,1,0:T(8,128)(2,1)} %get-tuple-element.279) | copy-start | bytes 995332
  228.6 10.0 %copy-start.12 = (bf16[2,160,384]{2,1,0:T(8,128)(2,1)S(1)}, bf16[2,160,384]{2,1,0:T(8,128)(2,1)}, u32[]{:S(2)}) copy-start(bf16[2,160,384]{2,1,0:T(8,128)(2,1)} %get-tuple-element.285) | copy-start | bytes 737284
  235.5 21.8 %collective-permute-start.12 = (bf16[2,256,384]{2,1,0:T(8,128)(2,1)}, bf16[2,256,384]{2,1,0:T(8,128)(2,1)S(1)}, u32[]{:S(2)}, u32[]{:S(2)}) collective-permute-start(bf16[2,256,384]{2,1,0:T(8,128)(2,1)} %get-tuple-element.301), channel_id=1, source_target_pairs={{0,1},{1,0},{2,3},{3,2},{4,5},{5,4},{6,7},{7,6},{8,9},{9,8},{10,11... | collective-permute-start | bytes 1179656 | tf_op jit(solution)/shard_map/ppermute | solution.py:964
  236.0 17.7 %collective-permute-start.9 = (bf16[1,432,384]{2,1,0:T(8,128)(2,1)S(1)}, bf16[1,432,384]{2,1,0:T(8,128)(2,1)S(1)}, u32[]{:S(2)}, u32[]{:S(2)}) collective-permute-start(bf16[1,432,384]{2,1,0:T(8,128)(2,1)S(1)} %copy-done.11), channel_id=1, source_target_pairs={{0,16},{4,20},{8,24},{12,28},{16,0},{20,4},{24,8},{28,12},{1,17},{... | collective-permute-start | bytes 995336 | tf_op jit(solution)/shard_map/ppermute | solution.py:967
  238.6 15.8 %collective-permute-start.10 = (bf16[2,160,384]{2,1,0:T(8,128)(2,1)S(1)}, bf16[2,160,384]{2,1,0:T(8,128)(2,1)}, u32[]{:S(2)}, u32[]{:S(2)}) collective-permute-start(bf16[2,160,384]{2,1,0:T(8,128)(2,1)S(1)} %copy-done.12), channel_id=1, source_target_pairs={{0,8},{4,12},{8,0},{12,4},{16,24},{20,28},{24,16},{28,20},{1,9},{5... | collective-permute-start | bytes 737288 | tf_op jit(solution)/shard_map/ppermute | solution.py:967
  256.1 31.4 %collective-permute-start.11 = (bf16[4,432,384]{2,1,0:T(8,128)(2,1)}, bf16[4,432,384]{2,1,0:T(8,128)(2,1)}, u32[]{:S(2)}, u32[]{:S(2)}) collective-permute-start(bf16[4,432,384]{2,1,0:T(8,128)(2,1)} %get-tuple-element.291), channel_id=1, source_target_pairs={{0,4},{4,0},{8,12},{12,8},{16,20},{20,16},{24,28},{28,24},{1,5},{5... | collective-permute-start | bytes 3981320 | tf_op jit(solution)/shard_map/ppermute | solution.py:967
  258.1 12.6 %copy-start = (bf16[768,768]{1,0:T(8,128)(2,1)S(1)}, bf16[768,768]{1,0:T(8,128)(2,1)}, u32[]{:S(2)}) copy-start(bf16[768,768]{1,0:T(8,128)(2,1)} %get-tuple-element.208) | copy-start | bytes 3538948
  270.7 19.1 %collective-permute-start.13 = (bf16[8,160,384]{2,1,0:T(8,128)(2,1)}, bf16[8,160,384]{2,1,0:T(8,128)(2,1)S(1)}, u32[]{:S(2)}, u32[]{:S(2)}) collective-permute-start(bf16[8,160,384]{2,1,0:T(8,128)(2,1)} %get-tuple-element.308), channel_id=1, source_target_pairs={{0,1},{1,0},{2,3},{3,2},{4,5},{5,4},{6,7},{7,6},{8,9},{9,8},{10,11... | collective-permute-start | bytes 2949128 | tf_op jit(solution)/shard_map/ppermute | solution.py:964
  270.7 16.8 %copy-start.1 = (bf16[4,432,384]{2,1,0:T(8,128)(2,1)S(1)}, bf16[4,432,384]{2,1,0:T(8,128)(2,1)}, u32[]{:S(2)}) copy-start(bf16[4,432,384]{2,1,0:T(8,128)(2,1)} %get-tuple-element.293) | copy-start | bytes 3981316
  273.3 18.6 %collective-permute-start.15 = (bf16[768,768]{1,0:T(8,128)(2,1)S(1)}, bf16[768,768]{1,0:T(8,128)(2,1)S(1)}, u32[]{:S(2)}, u32[]{:S(2)}) collective-permute-start(bf16[768,768]{1,0:T(8,128)(2,1)S(1)} %get-tuple-element.417), channel_id=1, source_target_pairs={{0,1},{1,0},{2,3},{3,2},{4,5},{5,4},{6,7},{7,6},{8,9},{9,8},{10,11... | collective-permute-start | bytes 3538952 | tf_op jit(solution)/shard_map/ppermute | solution.py:964
  273.8 16.0 %copy-start.5 = (bf16[8,160,384]{2,1,0:T(8,128)(2,1)S(1)}, bf16[8,160,384]{2,1,0:T(8,128)(2,1)}, u32[]{:S(2)}) copy-start(bf16[8,160,384]{2,1,0:T(8,128)(2,1)} %get-tuple-element.310) | copy-start | bytes 2949124
  273.8 28.4 %collective-permute-start.18 = (bf16[768,768]{1,0:T(8,128)(2,1)}, bf16[768,768]{1,0:T(8,128)(2,1)}, u32[]{:S(2)}, u32[]{:S(2)}) collective-permute-start(bf16[768,768]{1,0:T(8,128)(2,1)} %get-tuple-element.334), channel_id=1, source_target_pairs={{0,2},{1,3},{2,0},{3,1},{4,6},{5,7},{6,4},{7,5},{8,10},{9,11},{10,... | collective-permute-start | bytes 3538952 | tf_op jit(solution)/shard_map/ppermute | solution.py:964
  275.8 28.4 %collective-permute-start.14 = (bf16[1,160,384]{2,1,0:T(8,128)(2,1)}, bf16[1,160,384]{2,1,0:T(8,128)(2,1)S(1)}, u32[]{:S(2)}, u32[]{:S(2)}) collective-permute-start(bf16[1,160,384]{2,1,0:T(8,128)(2,1)} %get-tuple-element.314), channel_id=1, source_target_pairs={{0,16},{4,20},{8,24},{12,28},{16,0},{20,4},{24,8},{28,12},{1,17},{... | collective-permute-start | bytes 368648 | tf_op jit(solution)/shard_map/ppermute | solution.py:967
  290.0 14.9 %collective-permute-start.16 = (bf16[4,160,384]{2,1,0:T(8,128)(2,1)S(1)}, bf16[4,160,384]{2,1,0:T(8,128)(2,1)}, u32[]{:S(2)}, u32[]{:S(2)}) collective-permute-start(bf16[4,160,384]{2,1,0:T(8,128)(2,1)S(1)} %get-tuple-element.323), channel_id=1, source_target_pairs={{0,4},{4,0},{8,12},{12,8},{16,20},{20,16},{24,28},{28,24},{1,5},{5... | collective-permute-start | bytes 1474568 | tf_op jit(solution)/shard_map/ppermute | solution.py:967
  291.2 16.0 %collective-permute-start.17 = (bf16[2,432,384]{2,1,0:T(8,128)(2,1)}, bf16[2,432,384]{2,1,0:T(8,128)(2,1)}, u32[]{:S(2)}, u32[]{:S(2)}) collective-permute-start(bf16[2,432,384]{2,1,0:T(8,128)(2,1)} %get-tuple-element.329), channel_id=1, source_target_pairs={{0,8},{4,12},{8,0},{12,4},{16,24},{20,28},{24,16},{28,20},{1,9},{5... | collective-permute-start | bytes 1990664 | tf_op jit(solution)/shard_map/ppermute | solution.py:967
  298.5 5.7 %copy-start.7 = (bf16[1,160,384]{2,1,0:T(8,128)(2,1)S(1)}, bf16[1,160,384]{2,1,0:T(8,128)(2,1)}, u32[]{:S(2)}) copy-start(bf16[1,160,384]{2,1,0:T(8,128)(2,1)} %get-tuple-element.316) | copy-start | bytes 368644
  310.5 4.8 %collective-permute-start.19 = (bf16[768,768]{1,0:T(8,128)(2,1)S(1)}, bf16[768,768]{1,0:T(8,128)(2,1)}, u32[]{:S(2)}, u32[]{:S(2)}) collective-permute-start(bf16[768,768]{1,0:T(8,128)(2,1)S(1)} %get-tuple-element.415), channel_id=1, source_target_pairs={{0,1},{1,0},{2,3},{3,2},{4,5},{5,4},{6,7},{7,6},{8,9},{9,8},{10,11... | collective-permute-start | bytes 3538952 | tf_op jit(solution)/shard_map/ppermute | solution.py:964
  310.9 20.6 %collective-permute-start.35 = (f32[2,2,2]{2,1,0:T(2,128)S(1)}, f32[2,2,2]{2,1,0:T(2,128)S(1)}, u32[]{:S(2)}, u32[]{:S(2)}) collective-permute-start(f32[2,2,2]{2,1,0:T(2,128)S(1)} %reshape.220), channel_id=1, source_target_pairs={{0,1},{1,0},{2,3},{3,2},{4,5},{5,4},{6,7},{7,6},{8,9},{9,8},{10,11... | collective-permute-start | bytes 104 | tf_op jit(solution)/shard_map/ppermute | solution.py:964
  311.4 20.3 %collective-permute-start.26 = (bf16[432,384]{1,0:T(8,128)(2,1)S(1)}, bf16[432,384]{1,0:T(8,128)(2,1)}, u32[]{:S(2)}, u32[]{:S(2)}) collective-permute-start(bf16[432,384]{1,0:T(8,128)(2,1)S(1)} %copy-done.9), channel_id=1, source_target_pairs={{0,2},{1,3},{2,0},{3,1},{4,6},{5,7},{6,4},{7,5},{8,10},{9,11},{10,... | collective-permute-start | bytes 995336 | tf_op jit(solution)/shard_map/ppermute | solution.py:964
  312.9 11.8 %collective-permute-start.20 = (bf16[2,160,384]{2,1,0:T(8,128)(2,1)S(1)}, bf16[2,160,384]{2,1,0:T(8,128)(2,1)S(1)}, u32[]{:S(2)}, u32[]{:S(2)}) collective-permute-start(bf16[2,160,384]{2,1,0:T(8,128)(2,1)S(1)} %get-tuple-element.342), channel_id=1, source_target_pairs={{0,8},{4,12},{8,0},{12,4},{16,24},{20,28},{24,16},{28,20},{1,9},{5... | collective-permute-start | bytes 737288 | tf_op jit(solution)/shard_map/ppermute | solution.py:967
  313.3 17.5 %collective-permute-start.21 = (bf16[1,432,384]{2,1,0:T(8,128)(2,1)}, bf16[1,432,384]{2,1,0:T(8,128)(2,1)S(1)}, u32[]{:S(2)}, u32[]{:S(2)}) collective-permute-start(bf16[1,432,384]{2,1,0:T(8,128)(2,1)} %get-tuple-element.348), channel_id=1, source_target_pairs={{0,16},{4,20},{8,24},{12,28},{16,0},{20,4},{24,8},{28,12},{1,17},{... | collective-permute-start | bytes 995336 | tf_op jit(solution)/shard_map/ppermute | solution.py:967
  330.8 16.4 %copy-start.10 = (bf16[432,384]{1,0:T(8,128)(2,1)}, bf16[432,384]{1,0:T(8,128)(2,1)S(1)}, u32[]{:S(2)}) copy-start(bf16[432,384]{1,0:T(8,128)(2,1)S(1)} %add_bitcast_fusion.refs_0_) | copy-start | bytes 995332
  330.9 9.7 %collective-permute-start.23 = (bf16[432,384]{1,0:T(8,128)(2,1)S(1)}, bf16[432,384]{1,0:T(8,128)(2,1)S(1)}, u32[]{:S(2)}, u32[]{:S(2)}) collective-permute-start(bf16[432,384]{1,0:T(8,128)(2,1)S(1)} %add_bitcast_fusion.refs_0_), channel_id=1, source_target_pairs={{0,2},{1,3},{2,0},{3,1},{4,6},{5,7},{6,4},{7,5},{8,10},{9,11},{10,... | collective-permute-start | bytes 995336 | tf_op jit(solution)/shard_map/ppermute | solution.py:964
  331.4 6.6 %collective-permute-start.22 = (bf16[1,160,384]{2,1,0:T(8,128)(2,1)S(1)}, bf16[1,160,384]{2,1,0:T(8,128)(2,1)S(1)}, u32[]{:S(2)}, u32[]{:S(2)}) collective-permute-start(bf16[1,160,384]{2,1,0:T(8,128)(2,1)S(1)} %get-tuple-element.354), channel_id=1, source_target_pairs={{0,16},{4,20},{8,24},{12,28},{16,0},{20,4},{24,8},{28,12},{1,17},{... | collective-permute-start | bytes 368648 | tf_op jit(solution)/shard_map/ppermute | solution.py:967
  331.4 9.2 %collective-permute-start.27 = (bf16[432,384]{1,0:T(8,128)(2,1)S(1)}, bf16[432,384]{1,0:T(8,128)(2,1)S(1)}, u32[]{:S(2)}, u32[]{:S(2)}) collective-permute-start(bf16[432,384]{1,0:T(8,128)(2,1)S(1)} %copy-done.9), channel_id=1, source_target_pairs={{0,1},{1,0},{2,3},{3,2},{4,5},{5,4},{6,7},{7,6},{8,9},{9,8},{10,11... | collective-permute-start | bytes 995336 | tf_op jit(solution)/shard_map/ppermute | solution.py:964
  331.7 10.2 %collective-permute-start.28 = (bf16[432,384]{1,0:T(8,128)(2,1)}, bf16[432,384]{1,0:T(8,128)(2,1)S(1)}, u32[]{:S(2)}, u32[]{:S(2)}) collective-permute-start(bf16[432,384]{1,0:T(8,128)(2,1)} %collective-permute-done.26.refs_5_), channel_id=1, source_target_pairs={{0,1},{1,0},{2,3},{3,2},{4,5},{5,4},{6,7},{7,6},{8,9},{9,8},{10,11... | collective-permute-start | bytes 995336 | tf_op jit(solution)/shard_map/ppermute | solution.py:964
  332.3 9.9 %collective-permute-start.32 = (bf16[160,384]{1,0:T(8,128)(2,1)}, bf16[160,384]{1,0:T(8,128)(2,1)S(1)}, u32[]{:S(2)}, u32[]{:S(2)}) collective-permute-start(bf16[160,384]{1,0:T(8,128)(2,1)} %add_bitcast_fusion.3.refs_4_), channel_id=1, source_target_pairs={{0,2},{1,3},{2,0},{3,1},{4,6},{5,7},{6,4},{7,5},{8,10},{9,11},{10,... | collective-permute-start | bytes 368648 | tf_op jit(solution)/shard_map/ppermute | solution.py:964
  338.0 8.4 %collective-permute-start.24 = (bf16[432,384]{1,0:T(8,128)(2,1)S(1)}, bf16[432,384]{1,0:T(8,128)(2,1)S(1)}, u32[]{:S(2)}, u32[]{:S(2)}) collective-permute-start(bf16[432,384]{1,0:T(8,128)(2,1)S(1)} %add_bitcast_fusion.refs_0_), channel_id=1, source_target_pairs={{0,1},{1,0},{2,3},{3,2},{4,5},{5,4},{6,7},{7,6},{8,9},{9,8},{10,11... | collective-permute-start | bytes 995336 | tf_op jit(solution)/shard_map/ppermute | solution.py:964
  340.6 6.6 %copy-start.20 = (bf16[432,384]{1,0:T(8,128)(2,1)}, bf16[432,384]{1,0:T(8,128)(2,1)S(1)}, u32[]{:S(2)}) copy-start(bf16[432,384]{1,0:T(8,128)(2,1)S(1)} %collective-permute-done.23.refs_1_) | copy-start | bytes 995332
  340.6 6.6 %collective-permute-start.25 = (bf16[432,384]{1,0:T(8,128)(2,1)S(1)}, bf16[432,384]{1,0:T(8,128)(2,1)}, u32[]{:S(2)}, u32[]{:S(2)}) collective-permute-start(bf16[432,384]{1,0:T(8,128)(2,1)S(1)} %collective-permute-done.23.refs_1_), channel_id=1, source_target_pairs={{0,1},{1,0},{2,3},{3,2},{4,5},{5,4},{6,7},{7,6},{8,9},{9,8},{10,11... | collective-permute-start | bytes 995336 | tf_op jit(solution)/shard_map/ppermute | solution.py:964
  340.6 12.2 %copy-start.13 = (bf16[160,384]{1,0:T(8,128)(2,1)}, bf16[160,384]{1,0:T(8,128)(2,1)S(1)}, u32[]{:S(2)}) copy-start(bf16[160,384]{1,0:T(8,128)(2,1)S(1)} %add_bitcast_fusion.2.refs_0_) | copy-start | bytes 368644
  340.6 6.6 %copy-start.21 = (bf16[432,384]{1,0:T(8,128)(2,1)}, bf16[432,384]{1,0:T(8,128)(2,1)S(1)}, u32[]{:S(2)}) copy-start(bf16[432,384]{1,0:T(8,128)(2,1)S(1)} %collective-permute-done.27.refs_6_) | copy-start | bytes 995332
  340.6 5.8 %collective-permute-start.29 = (bf16[160,384]{1,0:T(8,128)(2,1)S(1)}, bf16[160,384]{1,0:T(8,128)(2,1)S(1)}, u32[]{:S(2)}, u32[]{:S(2)}) collective-permute-start(bf16[160,384]{1,0:T(8,128)(2,1)S(1)} %add_bitcast_fusion.2.refs_0_), channel_id=1, source_target_pairs={{0,2},{1,3},{2,0},{3,1},{4,6},{5,7},{6,4},{7,5},{8,10},{9,11},{10,... | collective-permute-start | bytes 368648 | tf_op jit(solution)/shard_map/ppermute | solution.py:964
  341.9 10.8 %collective-permute-start.33 = (bf16[160,384]{1,0:T(8,128)(2,1)}, bf16[160,384]{1,0:T(8,128)(2,1)S(1)}, u32[]{:S(2)}, u32[]{:S(2)}) collective-permute-start(bf16[160,384]{1,0:T(8,128)(2,1)} %add_bitcast_fusion.3.refs_4_), channel_id=1, source_target_pairs={{0,1},{1,0},{2,3},{3,2},{4,5},{5,4},{6,7},{7,6},{8,9},{9,8},{10,11... | collective-permute-start | bytes 368648 | tf_op jit(solution)/shard_map/ppermute | solution.py:964
  342.2 10.6 %copy-start.24 = (bf16[160,384]{1,0:T(8,128)(2,1)}, bf16[160,384]{1,0:T(8,128)(2,1)S(1)}, u32[]{:S(2)}) copy-start(bf16[160,384]{1,0:T(8,128)(2,1)S(1)} %collective-permute-done.32.refs_5_) | copy-start | bytes 368644
  342.2 10.6 %collective-permute-start.34 = (bf16[160,384]{1,0:T(8,128)(2,1)S(1)}, bf16[160,384]{1,0:T(8,128)(2,1)S(1)}, u32[]{:S(2)}, u32[]{:S(2)}) collective-permute-start(bf16[160,384]{1,0:T(8,128)(2,1)S(1)} %collective-permute-done.32.refs_5_), channel_id=1, source_target_pairs={{0,1},{1,0},{2,3},{3,2},{4,5},{5,4},{6,7},{7,6},{8,9},{9,8},{10,11... | collective-permute-start | bytes 368648 | tf_op jit(solution)/shard_map/ppermute | solution.py:964
  346.4 6.3 %copy-start.25 = (bf16[160,384]{1,0:T(8,128)(2,1)}, bf16[160,384]{1,0:T(8,128)(2,1)S(1)}, u32[]{:S(2)}) copy-start(bf16[160,384]{1,0:T(8,128)(2,1)S(1)} %collective-permute-done.29.refs_1_) | copy-start | bytes 368644
  346.4 6.4 %collective-permute-start.30 = (bf16[160,384]{1,0:T(8,128)(2,1)S(1)}, bf16[160,384]{1,0:T(8,128)(2,1)S(1)}, u32[]{:S(2)}, u32[]{:S(2)}) collective-permute-start(bf16[160,384]{1,0:T(8,128)(2,1)S(1)} %add_bitcast_fusion.2.refs_0_), channel_id=1, source_target_pairs={{0,1},{1,0},{2,3},{3,2},{4,5},{5,4},{6,7},{7,6},{8,9},{9,8},{10,11... | collective-permute-start | bytes 368648 | tf_op jit(solution)/shard_map/ppermute | solution.py:964
  346.5 6.4 %collective-permute-start.31 = (bf16[160,384]{1,0:T(8,128)(2,1)S(1)}, bf16[160,384]{1,0:T(8,128)(2,1)S(1)}, u32[]{:S(2)}, u32[]{:S(2)}) collective-permute-start(bf16[160,384]{1,0:T(8,128)(2,1)S(1)} %collective-permute-done.29.refs_1_), channel_id=1, source_target_pairs={{0,1},{1,0},{2,3},{3,2},{4,5},{5,4},{6,7},{7,6},{8,9},{9,8},{10,11... | collective-permute-start | bytes 368648 | tf_op jit(solution)/shard_map/ppermute | solution.py:964
  (18 other events, 33.1 us)

commit v6 on v5

--- a/solution.py
+++ b/solution.py
@@ -459,11 +459,13 @@
 def feed_fwd_kernel(
     ids, x0, x1, x2, own_ref, shared_ref, valid_ref, w_out_ref, out_bias_ref, scale_ref, shift_ref,
     in_ref, in_bias_ref, out_ref, ffn_bias_ref,
-    n1_ref, r1_ref, n2_ref, r2_ref, mixed_ref, act_ref, slope_ref, h_ref, squares_ref,
-    feed_ref,
+    n1_out, r1_out, n2_ref, r2_ref, mixed_out, act_ref, slope_ref, h_ref, squares_ref,
+    feed_ref, n1_ref, r1_ref, mixed_ref, sems,
     *, layer, parts,
 ):
     j = pl.program_id(0)
+    pairs = ((n1_ref, n1_out), (r1_ref, r1_out), (mixed_ref, mixed_out))
+    copies = [pltpu.make_async_copy(a, b, sems.at[k]) for k, (a, b) in enumerate(pairs)]
     half = x0.shape[1]
     row = lambda ref, *at: ref[at[:-1] + (slice(at[-1], at[-1] + 1),)].astype(f32)
 
@@ -498,6 +500,8 @@
 
             sums = row_loop(half // rows, chunk, (zero, zero))
             add_squares(sums, 0, t)
+        for copy in copies:
+            copy.start()
 
     cols = in_ref.shape[2] // parts
     at = lambda k: slice(cols * k, cols * k + cols)
@@ -542,6 +546,8 @@
 
             sums = row_loop(half // rows, chunk, (zero, zero))
             add_squares(sums, 4, t)
+        for copy in copies:
+            copy.wait()
 
 
 def feed_fwd(ids, x, gathered, ctx_own, ctx_shared, valid, weights, layer, chunk=768, parts=1):
@@ -555,6 +561,8 @@
             ((8, width), f32)]
     out_specs = [full(*s) for s, _ in outs]
     out_specs[5] = out_specs[6] = spec((tokens, chunk), 0, step)
+    for k in (0, 1, 4):
+        out_specs[k] = pl.BlockSpec(memory_space=pl.ANY)
     return call(
         functools.partial(feed_fwd_kernel, layer=layer, parts=parts), "feed_forward", (ff // chunk,), ids,
         row_tiles(half, width, gathered)
@@ -567,7 +575,11 @@
         ],
         [x, x, x, ctx_own, ctx_shared, valid, w_out, out_bias, ln_scale, ln_shift, ffn_in, ffn_in_bias,
          ffn_out, ffn_out_bias],
-        out_specs, [shape_of(s, d) for s, d in outs], [pltpu.VMEM((tokens, width), f32)],
+        out_specs, [shape_of(s, d) for s, d in outs],
+        [
+            pltpu.VMEM((tokens, width), f32), pltpu.VMEM((tokens, width), bf16), pltpu.VMEM((tokens, 128), f32),
+            pltpu.VMEM((tokens, width), bf16), pltpu.SemaphoreType.DMA((3,)),
+        ],
     )
 
 
@@ -604,10 +616,15 @@
     layer, parts,
 ):
     j = pl.program_id(0)
-    buffers, sems = late[:-1], late[-1]
+    outs, late = (mixed_ref, attn_ref, ctx_ref), late[3:] + late[:3]
+    mixed_ref, attn_ref, ctx_ref = late[-3:]
+    buffers, sems = late[:-4], late[-4]
     sources = (n1_ref, r1_ref, w_out_ref.at[layer], own_ref, shared_ref)
     copies = [pltpu.make_async_copy(a, b, sems.at[k]) for k, (a, b) in enumerate(zip(sources, buffers))]
     n1_ref, r1_ref, w_out_ref, own_ref, shared_ref = buffers
+    results = [
+        pltpu.make_async_copy(a, b, sems.at[5 + k]) for k, (a, b) in enumerate(zip((mixed_ref, attn_ref, ctx_ref), outs))
+    ]
 
     @pl.when(j == 0)
     def _():
@@ -666,12 +683,36 @@
     def _():
         acc_ref[...] += total
 
+    width = mixed_t.shape[0]
+
+    @pl.when(j == pl.num_programs(0) - 1)
+    def _():
+        for copy in copies:
+            copy.wait()
+
+        def chunk(i, sums):
+            to = pl.ds(i * rows, rows)
+            g_mixed = acc_ref[to, :] + res_ref[to, :]
+            mixed_ref[to, :] = g_mixed.astype(bf16)
+            normed = n1_ref[to, :].astype(f32)
+            attn = norm_back(g_mixed, gain(0), normed, r1_ref[to, 0:1]).astype(bf16)
+            attn_ref[to, :] = attn
+            return (sums[0] + fold(g_mixed * normed), sums[1] + fold(g_mixed), sums[2] + fold(attn.astype(f32)))
+
+        zero = jnp.zeros((8, width), f32)
+        sums = row_loop(tokens // rows, chunk, (zero, zero, zero))
+        for k, x in zip((0, 2, 4), sums):
+            sums_ref[k : k + 1, :] = col_sum(x)
+        results[0].start()
+        results[1].start()
+        ctx_ref[...] = dot_nt(attn_ref[...], w_out_ref[...]).astype(bf16)
+        results[2].start()
+
     high = LANES // 2
     slabs = act_ref.shape[1] // LANES
     result = dot(feed_t[...], act_ref[...]).astype(bf16)
     for k in range(slabs):
         store_piece(ids, keep_ref, send_ref, j * slabs + k, high, 0, result[:, LANES * k : LANES * k + LANES])
-    width = mixed_t.shape[0]
     slab_rows = width // SUPER
     half = slab_rows // 2
     steps = 4 // slabs
@@ -689,23 +730,6 @@
 
     @pl.when(j == pl.num_programs(0) - 1)
     def _():
-        for copy in copies:
-            copy.wait()
-
-        def chunk(i, sums):
-            to = pl.ds(i * rows, rows)
-            g_mixed = acc_ref[to, :] + res_ref[to, :]
-            mixed_ref[to, :] = g_mixed.astype(bf16)
-            normed = n1_ref[to, :].astype(f32)
-            attn = norm_back(g_mixed, gain(0), normed, r1_ref[to, 0:1]).astype(bf16)
-            attn_ref[to, :] = attn
-            return (sums[0] + fold(g_mixed * normed), sums[1] + fold(g_mixed), sums[2] + fold(attn.astype(f32)))
-
-        zero = jnp.zeros((8, width), f32)
-        sums = row_loop(tokens // rows, chunk, (zero, zero, zero))
-        for k, x in zip((0, 2, 4), sums):
-            sums_ref[k : k + 1, :] = col_sum(x)
-        ctx_ref[...] = dot_nt(attn_ref[...], w_out_ref[...]).astype(bf16)
         long = own_ref.shape[1]
         for side in range(2):
 
@@ -717,6 +741,8 @@
                 for slab in range(SUPER):
                     store_piece(ids, keep_ref, send_ref, slab, half, high + 4 * half,
                                 result[slab_rows * slab : slab_rows * slab + slab_rows])
+        for copy in results:
+            copy.wait()
 
 
 def feed_bwd(ids, grad, gathered, kept, slope, act, mixed, ctx_own, ctx_shared, weights, layer, chunk=768, parts=3):
@@ -732,6 +758,7 @@
     outs = [dense, dense, dense, ((8, width), f32), ((8, ff), f32), piece, piece]
     out_specs = [full(*s) for s, _ in outs]
     out_specs[4] = spec((8, chunk), 0, step)
+    out_specs[0:3] = [anywhere] * 3
     return call(
         functools.partial(feed_bwd_kernel, layer=layer, parts=parts), "feed_backward", (ff // chunk,), ids,
         row_tiles(half, width, gathered)
@@ -748,9 +775,10 @@
             pltpu.VMEM((tokens, width), f32), pltpu.VMEM((tokens, width), f32),
             pltpu.VMEM((tokens, width), bf16), pltpu.VMEM((tokens, chunk), bf16),
             pltpu.VMEM((LANES, tokens), bf16), pltpu.VMEM((width, tokens), bf16),
+            pltpu.VMEM((tokens, width), bf16), pltpu.VMEM((tokens, width), bf16), pltpu.VMEM((tokens, width), bf16),
             pltpu.VMEM((tokens, width), bf16), pltpu.VMEM((tokens, 128), f32),
             pltpu.VMEM((width, width), bf16), pltpu.VMEM(ctx_own.shape, bf16),
-            pltpu.VMEM(ctx_shared.shape, bf16), pltpu.SemaphoreType.DMA((5,)),
+            pltpu.VMEM(ctx_shared.shape, bf16), pltpu.SemaphoreType.DMA((8,)),
         ],
     )
 

time: 365 us -> 358 us (0.981)
  Pallas kernels: 259 us -> 252 us
    pallas_call x21, Pallas kernels: 259 us -> 252 us  [call(): pl.pallas_call(kernel, grid_spec=pltpu.PrefetchScalarGridSpec(num_scalar_...]
where the time goes in v6:
time: 358 us; the launch traced here: 352 us
  Pallas kernels  252 us (70%)
  waiting for transfers between devices  37 us (10%)
  other arithmetic  30.3 us (8%)
  starting transfers between devices  24.5 us (7%)
  local copies, waits for them, and re-layouts  5.95 us (2%)
    pallas_call x21, Pallas kernels, call(): pl.pallas_call(kernel, grid_spec=pltpu.PrefetchScalarGridSpec(num_scalar_...  252 us
    ppermute x12, waiting for transfers between devices, flip_dp(): return lax.ppermute(x, 'dp', [(i, i ^ bit) for i in range(dp)])  26.3 us
    add x12, other arithmetic, absorb(): return pin((keep[:n] + arrived[:n], keep[n:] + arrived[n:]))  21.8 us
    ppermute x12, starting transfers between devices, flip_dp(): return lax.ppermute(x, 'dp', [(i, i ^ bit) for i in range(dp)])  14 us
    ppermute x24, waiting for transfers between devices, flip(): return lax.ppermute(x, 'section', [(i, i ^ bit) for i in range(sections)])  10.6 us
    ppermute x24, starting transfers between devices, flip(): return lax.ppermute(x, 'section', [(i, i ^ bit) for i in range(sections)])  10.6 us
  transfers between devices with their start and end apart: 36, of which 10 were waited for; matrix products, arithmetic and copies ran while one was open for 8% of the time, Pallas kernels for 38%

profile of v6, /device:TPU:0, one launch (start us, length us, event | category | flops | bytes accessed | tf_op | source)
XLA Modules:
  0.0 351.6 jit_solution(14265562563234037159)
XLA Ops:
  1.3 4.1 %tables.1 = (f32[64,1024]{1,0:T(8,128)}, f32[64,1024]{1,0:T(8,128)}, bf16[1024,128]{1,0:T(8,128)(2,1)}, f32[1024,128]{1,0:T(8,128)}, f32[1024,128]{1,0:T(8,128)}...) custom-call(s32[3]{0:T(128)} %pad_add_fusion.ids, s32[3,4,512]{2,1,0:T(4,128)} %bitcast.67, ...), custom_call_target="tpu_custom_call" | custom-call | flops 4400000000 | bytes 4000000 | tf_op jit(solution)/shard_map/tables/pallas_call | solution.py:83
  5.5 9.9 %projections.2 = (bf16[768,2304]{1,0:T(8,128)(2,1)}, bf16[768,1536]{1,0:T(8,128)(2,1)}, bf16[256,1536]{1,0:T(8,128)(2,1)}) custom-call(s32[3]{0:T(128)} %pad_add_fusion.ids, bf16[6,256,768]{2,1,0:T(8,128)(2,1)} %bitcast.31, bf16[6,256,768]{2,1,0:T(8,128)(2,1)} %bitcast.32, bf16[6,256,768]{2,1,0:T(8,128)(2,1)} %bitcast.33, bf16[2,768,2304]{2,1,0:T(8,128)(2,1)} %w_ref.7, ...), custom_call_target="tpu_custom_call" | custom-call | flops 8800000000 | bytes 8000000 | tf_op jit(solution)/shard_map/projections/pallas_call | solution.py:83
  15.8 8.6 %attention_forward.4 = (bf16[768,512]{1,0:T(8,128)(2,1)}, f32[6,2,512]{2,1,0:T(2,128)}) custom-call(s32[3]{0:T(128)} %pad_add_fusion.ids, f32[1024,128]{1,0:T(8,128)} %get-tuple-element.197.code_ref, f32[8,1024]{1,0:T(8,128)} %get-tuple-element.198.seg_ref, bf16[1024,128]{1,0:T(8,128)(2,1)} %get-tuple-element.199.kf_ref, ...), custom_call_target="tpu_custom_call" | custom-call | flops 7699999744 | bytes 7000000 | tf_op jit(solution)/shard_map/attention_forward/pallas_call | solution.py:83
  25.4 6.3 %attention_forward.5 = (bf16[768,256]{1,0:T(8,128)(2,1)}, f32[6,2,256]{2,1,0:T(2,128)}) custom-call(s32[3]{0:T(128)} %pad_add_fusion.ids, f32[1024,128]{1,0:T(8,128)} %get-tuple-element.197.code_ref, f32[8,1024]{1,0:T(8,128)} %get-tuple-element.198.seg_ref, bf16[1024,128]{1,0:T(8,128)(2,1)} %get-tuple-element.199.kf_ref, ...), custom_call_target="tpu_custom_call" | custom-call | flops 7699999744 | bytes 7000000 | tf_op jit(solution)/shard_map/attention_forward/pallas_call | solution.py:83
  31.7 24.9 %feed_forward.2 = (bf16[768,768]{1,0:T(8,128)(2,1)}, f32[768,128]{1,0:T(8,128)}, bf16[768,768]{1,0:T(8,128)(2,1)}, f32[768,128]{1,0:T(8,128)}, bf16[768,768]{1,0...) custom-call(s32[3]{0:T(128)} %pad_add_fusion.ids, ...), custom_call_target="tpu_custom_call" | custom-call | flops 26400000000 | bytes 24000000 | tf_op jit(solution)/shard_map/feed_forward/pallas_call | solution.py:83
  56.6 9.9 %projections.3 = (bf16[768,2304]{1,0:T(8,128)(2,1)}, bf16[768,1536]{1,0:T(8,128)(2,1)}, bf16[256,1536]{1,0:T(8,128)(2,1)}) custom-call(s32[3]{0:T(128)} %pad_add_fusion.ids, bf16[3,256,768]{2,1,0:T(8,128)(2,1)} %bitcast.40, bf16[3,256,768]{2,1,0:T(8,128)(2,1)} %bitcast.41, bf16[3,256,768]{2,1,0:T(8,128)(2,1)} %bitcast.42, bf16[2,768,2304]{2,1,0:T(8,128)(2,1)} %w_ref.7, ...), custom_call_target="tpu_custom_call" | custom-call | flops 8800000000 | bytes 8000000 | tf_op jit(solution)/shard_map/projections/pallas_call | solution.py:83
  66.6 8.6 %attention_forward.6 = (bf16[768,512]{1,0:T(8,128)(2,1)}, f32[6,2,512]{2,1,0:T(2,128)}) custom-call(s32[3]{0:T(128)} %pad_add_fusion.ids, f32[1024,128]{1,0:T(8,128)} %get-tuple-element.197.code_ref, f32[8,1024]{1,0:T(8,128)} %get-tuple-element.198.seg_ref, bf16[1024,128]{1,0:T(8,128)(2,1)} %get-tuple-element.199.kf_ref, ...), custom_call_target="tpu_custom_call" | custom-call | flops 7699999744 | bytes 7000000 | tf_op jit(solution)/shard_map/attention_forward/pallas_call | solution.py:83
  76.1 6.7 %attention_forward.7 = (bf16[768,256]{1,0:T(8,128)(2,1)}, f32[6,2,256]{2,1,0:T(2,128)}) custom-call(s32[3]{0:T(128)} %pad_add_fusion.ids, f32[1024,128]{1,0:T(8,128)} %get-tuple-element.197.code_ref, f32[8,1024]{1,0:T(8,128)} %get-tuple-element.198.seg_ref, bf16[1024,128]{1,0:T(8,128)(2,1)} %get-tuple-element.199.kf_ref, ...), custom_call_target="tpu_custom_call" | custom-call | flops 7699999744 | bytes 7000000 | tf_op jit(solution)/shard_map/attention_forward/pallas_call | solution.py:83
  82.8 24.6 %feed_forward.3 = (bf16[768,768]{1,0:T(8,128)(2,1)}, f32[768,128]{1,0:T(8,128)}, bf16[768,768]{1,0:T(8,128)(2,1)}, f32[768,128]{1,0:T(8,128)}, bf16[768,768]{1,0...) custom-call(s32[3]{0:T(128)} %pad_add_fusion.ids, ...), custom_call_target="tpu_custom_call" | custom-call | flops 26400000000 | bytes 24000000 | tf_op jit(solution)/shard_map/feed_forward/pallas_call | solution.py:83
  107.4 28.7 %feed_backward.2 = (bf16[768,768]{1,0:T(8,128)(2,1)}, bf16[768,768]{1,0:T(8,128)(2,1)}, bf16[768,768]{1,0:T(8,128)(2,1)}, f32[8,768]{1,0:T(8,128)}, f32[8,3072]{...) custom-call(s32[3]{0:T(128)} %pad_add_fusion.ids, bf16[6,256,768]{2,1,0:T(8,128)(2,1)} %bitcast.57, ...), custom_call_target="tpu_custom_call" | custom-call | flops 32999999488 | bytes 30000000 | tf_op jit(solution)/shard_map/feed_backward/pallas_call | solution.py:83
  136.6 10.9 %attention_backward.5 = (bf16[3,256,768]{2,1,0:T(8,128)(2,1)}, bf16[2,256,768]{2,1,0:T(8,128)(2,1)}, f32[128,768]{1,0:T(8,128)}) custom-call(s32[3]{0:T(128)} %pad_add_fusion.ids, f32[1024,128]{1,0:T(8,128)} %get-tuple-element.197.code_ref, f32[8,1024]{1,0:T(8,128)} %get-tuple-element.198.seg_ref, bf16[1024,128]{1,0:T(8,128)(2,1)} %get-tuple-element.199.kf_ref, ...), custom_call_target="tpu_custom_call" | custom-call | flops 44000002048 | bytes 40000000 | tf_op jit(solution)/shard_map/attention_backward/pallas_call | solution.py:83
  147.6 3.9 %slice_add_fusion.2 = (bf16[4,432,384]{2,1,0:T(8,128)(2,1)}, bf16[4,432,384]{2,1,0:T(8,128)(2,1)S(1)}) fusion(bf16[8,432,384]{2,1,0:T(8,128)(2,1)} %collective-permute-done.2, bf16[8,432,384]{2,1,0:T(8,128)(2,1)} %get-tuple-element.224), kind=kLoop, calls=%fused_computation.2 | loop fusion | flops 1327104 | bytes 7962624 | tf_op jit(solution)/shard_map/add | solution.py:1027
  151.5 2.9 collective-permute-start.3
  154.4 16.6 %attention_backward.4 = (bf16[3,512,768]{2,1,0:T(8,128)(2,1)}, f32[128,768]{1,0:T(8,128)}) custom-call(s32[3]{0:T(128)} %pad_add_fusion.ids, f32[1024,128]{1,0:T(8,128)} %get-tuple-element.197.code_ref, f32[8,1024]{1,0:T(8,128)} %get-tuple-element.198.seg_ref, bf16[1024,128]{1,0:T(8,128)(2,1)} %get-tuple-element.199.kf_ref, ...), custom_call_target="tpu_custom_call" | custom-call | flops 13200000000 | bytes 12000000 | tf_op jit(solution)/shard_map/attention_backward/pallas_call | solution.py:83
  171.0 13.6 %projections_backward.2 = (bf16[768,768]{1,0:T(8,128)(2,1)}, bf16[8,160,384]{2,1,0:T(8,128)(2,1)}, bf16[8,160,384]{2,1,0:T(8,128)(2,1)}) custom-call(s32[3]{0:T(128)} %pad_add_fusion.ids, bf16[3,256,768]{2,1,0:T(8,128)(2,1)} %bitcast.46, bf16[3,256,768]{2,1,0:T(8,128)(2,1)} %bitcast.47, bf16[3,256,768]{2,1,0:T(8,128)(2,1)} %bitcast.48, ...), custom_call_target="tpu_custom_call" | custom-call | flops 3300000000 | bytes 3000000 | tf_op jit(solution)/shard_map/projections_backward/pallas_call | solution.py:83
  184.6 2.4 slice_add_fusion.6
  187.5 1.7 collective-permute-start.6
  190.0 28.4 %feed_backward.3 = (bf16[768,768]{1,0:T(8,128)(2,1)}, bf16[768,768]{1,0:T(8,128)(2,1)}, bf16[768,768]{1,0:T(8,128)(2,1)}, f32[8,768]{1,0:T(8,128)}, f32[8,3072]{...) custom-call(s32[3]{0:T(128)} %pad_add_fusion.ids, bf16[3,256,768]{2,1,0:T(8,128)(2,1)} %bitcast.49, ...), custom_call_target="tpu_custom_call" | custom-call | flops 32999999488 | bytes 30000000 | tf_op jit(solution)/shard_map/feed_backward/pallas_call | solution.py:83
  218.5 1.9 slice_add_fusion.14
  220.3 1.8 slice_add_fusion.18
  222.2 6.9 %attention_backward.7 = (bf16[3,256,384]{2,1,0:T(8,128)(2,1)}, bf16[2,256,384]{2,1,0:T(8,128)(2,1)}, f32[128,384]{1,0:T(8,128)}) custom-call(s32[3]{0:T(128)} %pad_add_fusion.ids, f32[1024,128]{1,0:T(8,128)} %get-tuple-element.197.code_ref, f32[8,1024]{1,0:T(8,128)} %get-tuple-element.198.seg_ref, bf16[1024,128]{1,0:T(8,128)(2,1)} %get-tuple-element.199.kf_ref, ...), custom_call_target="tpu_custom_call" | custom-call | flops 44000002048 | bytes 40000000 | tf_op jit(solution)/shard_map/attention_backward/pallas_call | solution.py:83
  229.5 2.6 collective-permute-start.9
  232.6 4.3 %slice_add_fusion = (bf16[4,432,384]{2,1,0:T(8,128)(2,1)}, bf16[4,432,384]{2,1,0:T(8,128)(2,1)}) fusion(bf16[8,432,384]{2,1,0:T(8,128)(2,1)} %collective-permute-done.8, bf16[8,432,384]{2,1,0:T(8,128)(2,1)} %get-tuple-element.275), kind=kLoop, calls=%fused_computation | loop fusion | flops 1327104 | bytes 7962624 | tf_op jit(solution)/shard_map/add | solution.py:1027
  236.9 9.9 %attention_backward.6 = (bf16[3,512,384]{2,1,0:T(8,128)(2,1)}, f32[128,384]{1,0:T(8,128)}) custom-call(s32[3]{0:T(128)} %pad_add_fusion.ids, f32[1024,128]{1,0:T(8,128)} %get-tuple-element.197.code_ref, f32[8,1024]{1,0:T(8,128)} %get-tuple-element.198.seg_ref, bf16[1024,128]{1,0:T(8,128)(2,1)} %get-tuple-element.199.kf_ref, ...), custom_call_target="tpu_custom_call" | custom-call | flops 13200000000 | bytes 12000000 | tf_op jit(solution)/shard_map/attention_backward/pallas_call | solution.py:83
  248.0 1.7 slice_add_fusion.22
  251.6 12.6 %projections_backward.3 = (bf16[768,768]{1,0:T(8,128)(2,1)}, bf16[8,160,384]{2,1,0:T(8,128)(2,1)}, bf16[8,160,384]{2,1,0:T(8,128)(2,1)}) custom-call(s32[3]{0:T(128)} %pad_add_fusion.ids, bf16[6,256,768]{2,1,0:T(8,128)(2,1)} %bitcast.37, bf16[6,256,768]{2,1,0:T(8,128)(2,1)} %bitcast.38, bf16[6,256,768]{2,1,0:T(8,128)(2,1)} %bitcast.39, ...), custom_call_target="tpu_custom_call" | custom-call | flops 3300000000 | bytes 3000000 | tf_op jit(solution)/shard_map/projections_backward/pallas_call | solution.py:83
  264.2 2.7 broadcast_select_fusion.6
  267.3 1.9 collective-permute-start.18
  269.3 11.7 %collective-permute-done.11 = bf16[4,432,384]{2,1,0:T(8,128)(2,1)} collective-permute-done((bf16[4,432,384]{2,1,0:T(8,128)(2,1)}, bf16[4,432,384]{2,1,0:T(8,128)(2,1)}, u32[]{:S(2)}, u32[]{:S(2)}) %collective-permute-start.11) | collective-permute-done | bytes 1327136 | tf_op jit(solution)/shard_map/ppermute | solution.py:995
  281.0 2.3 slice_add_fusion.4
  283.5 1.3 collective-permute-start.16
  286.5 5.5 %place_rows.2 = bf16[6,256,768]{2,1,0:T(8,128)(2,1)} custom-call(s32[3]{0:T(128)} %pad_add_fusion.ids, bf16[3,256,768]{2,1,0:T(8,128)(2,1)} %bitcast.52, bf16[3,256,768]{2,1,0:T(8,128)(2,1)} %bitcast.60), custom_call_target="tpu_custom_call" | custom-call | flops 4400000000 | bytes 4000000 | tf_op jit(solution)/shard_map/place_rows/pallas_call | solution.py:83
  292.0 3.7 %collective-permute-done.18 = bf16[768,768]{1,0:T(8,128)(2,1)} collective-permute-done((bf16[768,768]{1,0:T(8,128)(2,1)}, bf16[768,768]{1,0:T(8,128)(2,1)}, u32[]{:S(2)}, u32[]{:S(2)}) %collective-permute-start.18) | collective-permute-done | bytes 1179680 | tf_op jit(solution)/shard_map/ppermute | solution.py:992
  295.8 1.9 add.140
  298.4 1.2 slice_add_fusion.16
  300.8 1.9 slice_add_fusion.12
  302.7 1.3 broadcast_select_fusion.4
  304.9 1.6 collective-permute-start.26
  306.8 2.0 collective-permute-start.21
  308.8 6.6 %place_rows.3 = f32[6,256,768]{2,1,0:T(8,128)} custom-call(s32[3]{0:T(128)} %pad_add_fusion.ids, bf16[3,256,768]{2,1,0:T(8,128)(2,1)} %bitcast.53, bf16[3,256,768]{2,1,0:T(8,128)(2,1)} %bitcast.15.other_ref), custom_call_target="tpu_custom_call" | custom-call | flops 4400000000 | bytes 4000000 | tf_op jit(solution)/shard_map/place_rows/pallas_call | solution.py:83
  315.4 2.9 collective-permute-done.20
  318.3 6.0 %collective-permute-done.21 = bf16[1,432,384]{2,1,0:T(8,128)(2,1)S(1)} collective-permute-done((bf16[1,432,384]{2,1,0:T(8,128)(2,1)}, bf16[1,432,384]{2,1,0:T(8,128)(2,1)S(1)}, u32[]{:S(2)}, u32[]{:S(2)}) %collective-permute-start.21) | collective-permute-done | bytes 331808 | tf_op jit(solution)/shard_map/ppermute | solution.py:995
  325.8 1.6 collective-permute-start.32
  327.3 4.2 %collective-permute-done.22 = bf16[1,160,384]{2,1,0:T(8,128)(2,1)S(1)} collective-permute-done((bf16[1,160,384]{2,1,0:T(8,128)(2,1)S(1)}, bf16[1,160,384]{2,1,0:T(8,128)(2,1)S(1)}, u32[]{:S(2)}, u32[]{:S(2)}) %collective-permute-start.22) | collective-permute-done | bytes 122912 | tf_op jit(solution)/shard_map/ppermute | solution.py:995
  331.5 2.6 collective-permute-done.23.refs_1_
  336.0 4.0 %collective-permute-done.29.refs_1_ = bf16[160,384]{1,0:T(8,128)(2,1)S(1)} collective-permute-done((bf16[160,384]{1,0:T(8,128)(2,1)S(1)}, bf16[160,384]{1,0:T(8,128)(2,1)S(1)}, u32[]{:S(2)}, u32[]{:S(2)}) %collective-permute-start.29) | collective-permute-done | bytes 122912 | tf_op jit(solution)/shard_map/ppermute | solution.py:992
  340.8 5.5 %unpack_feed.1 = (f32[2,96,3072]{2,1,0:T(8,128)}, f32[2,384,768]{2,1,0:T(8,128)}, f32[2,96,768]{2,1,0:T(8,128)}) custom-call(s32[3]{0:T(128)} %pad_add_fusion.ids, bf16[432,384]{1,0:T(8,128)(2,1)} %copy-done.10, bf16[432,384]{1,0:T(8,128)(2,1)} %copy-done.20, bf16[432,384]{1,0:T(8,128)(2,1)} %copy-done.23, bf16[432,384]{1,0:T(8,128)(2,1)} %collective-permute-done.25.refs_3_, ...), custom_call_target="tpu_custom_call" | custom-call | flops 4400000000 | bytes 4000000 | tf_op jit(solution)/shard_map/unpack_feed/pallas_call | solution.py:83
  347.7 3.5 unpack_attention.1
  (134 shorter events, 19.9 us)
Async XLA Ops:
  15.4 9.1 %collective-permute-start = (bf16[256,1536]{1,0:T(8,128)(2,1)}, bf16[256,1536]{1,0:T(8,128)(2,1)S(1)}, u32[]{:S(2)}, u32[]{:S(2)}) collective-permute-start(bf16[256,1536]{1,0:T(8,128)(2,1)} %get-tuple-element.205), channel_id=1, source_target_pairs={{0,1},{1,0},{2,3},{3,2},{4,5},{5,4},{6,7},{7,6},{8,9},{9,8},{10,11... | collective-permute-start | bytes 2359304 | tf_op jit(solution)/shard_map/ppermute | solution.py:992
  66.5 8.7 %collective-permute-start.1 = (bf16[256,1536]{1,0:T(8,128)(2,1)}, bf16[256,1536]{1,0:T(8,128)(2,1)S(1)}, u32[]{:S(2)}, u32[]{:S(2)}) collective-permute-start(bf16[256,1536]{1,0:T(8,128)(2,1)} %get-tuple-element.212), channel_id=1, source_target_pairs={{0,1},{1,0},{2,3},{3,2},{4,5},{5,4},{6,7},{7,6},{8,9},{9,8},{10,11... | collective-permute-start | bytes 2359304 | tf_op jit(solution)/shard_map/ppermute | solution.py:992
  136.1 11.5 %collective-permute-start.2 = (bf16[8,432,384]{2,1,0:T(8,128)(2,1)}, bf16[8,432,384]{2,1,0:T(8,128)(2,1)}, u32[]{:S(2)}, u32[]{:S(2)}) collective-permute-start(bf16[8,432,384]{2,1,0:T(8,128)(2,1)} %get-tuple-element.222), channel_id=1, source_target_pairs={{0,1},{1,0},{2,3},{3,2},{4,5},{5,4},{6,7},{7,6},{8,9},{9,8},{10,11... | collective-permute-start | bytes 7962632 | tf_op jit(solution)/shard_map/ppermute | solution.py:992
  147.5 23.5 %collective-permute-start.4 = (bf16[2,256,768]{2,1,0:T(8,128)(2,1)}, bf16[2,256,768]{2,1,0:T(8,128)(2,1)}, u32[]{:S(2)}, u32[]{:S(2)}) collective-permute-start(bf16[2,256,768]{2,1,0:T(8,128)(2,1)} %get-tuple-element.240), channel_id=1, source_target_pairs={{0,1},{1,0},{2,3},{3,2},{4,5},{5,4},{6,7},{7,6},{8,9},{9,8},{10,11... | collective-permute-start | bytes 2359304 | tf_op jit(solution)/shard_map/ppermute | solution.py:992
  151.5 33.1 %collective-permute-start.3 = (bf16[4,432,384]{2,1,0:T(8,128)(2,1)}, bf16[4,432,384]{2,1,0:T(8,128)(2,1)}, u32[]{:S(2)}, u32[]{:S(2)}) collective-permute-start(bf16[4,432,384]{2,1,0:T(8,128)(2,1)} %get-tuple-element.228), channel_id=1, source_target_pairs={{0,4},{4,0},{8,12},{12,8},{16,20},{20,16},{24,28},{28,24},{1,5},{5... | collective-permute-start | bytes 3981320 | tf_op jit(solution)/shard_map/ppermute | solution.py:995
  184.5 2.8 collective-permute-start.5
  187.5 30.9 %collective-permute-start.6 = (bf16[2,432,384]{2,1,0:T(8,128)(2,1)}, bf16[2,432,384]{2,1,0:T(8,128)(2,1)}, u32[]{:S(2)}, u32[]{:S(2)}) collective-permute-start(bf16[2,432,384]{2,1,0:T(8,128)(2,1)} %get-tuple-element.253), channel_id=1, source_target_pairs={{0,8},{4,12},{8,0},{12,4},{16,24},{20,28},{24,16},{28,20},{1,9},{5... | collective-permute-start | bytes 1990664 | tf_op jit(solution)/shard_map/ppermute | solution.py:995
  189.2 31.2 %collective-permute-start.7 = (bf16[4,160,384]{2,1,0:T(8,128)(2,1)S(1)}, bf16[4,160,384]{2,1,0:T(8,128)(2,1)}, u32[]{:S(2)}, u32[]{:S(2)}) collective-permute-start(bf16[4,160,384]{2,1,0:T(8,128)(2,1)S(1)} %get-tuple-element.259), channel_id=1, source_target_pairs={{0,4},{4,0},{8,12},{12,8},{16,20},{20,16},{24,28},{28,24},{1,5},{5... | collective-permute-start | bytes 1474568 | tf_op jit(solution)/shard_map/ppermute | solution.py:995
  218.4 14.2 %collective-permute-start.8 = (bf16[8,432,384]{2,1,0:T(8,128)(2,1)}, bf16[8,432,384]{2,1,0:T(8,128)(2,1)}, u32[]{:S(2)}, u32[]{:S(2)}) collective-permute-start(bf16[8,432,384]{2,1,0:T(8,128)(2,1)} %get-tuple-element.273), channel_id=1, source_target_pairs={{0,1},{1,0},{2,3},{3,2},{4,5},{5,4},{6,7},{7,6},{8,9},{9,8},{10,11... | collective-permute-start | bytes 7962632 | tf_op jit(solution)/shard_map/ppermute | solution.py:992
  222.2 7.4 %copy-start.11 = (bf16[1,432,384]{2,1,0:T(8,128)(2,1)S(1)}, bf16[1,432,384]{2,1,0:T(8,128)(2,1)}, u32[]{:S(2)}) copy-start(bf16[1,432,384]{2,1,0:T(8,128)(2,1)} %get-tuple-element.279) | copy-start | bytes 995332
  222.2 10.0 %copy-start.12 = (bf16[2,160,384]{2,1,0:T(8,128)(2,1)S(1)}, bf16[2,160,384]{2,1,0:T(8,128)(2,1)}, u32[]{:S(2)}) copy-start(bf16[2,160,384]{2,1,0:T(8,128)(2,1)} %get-tuple-element.285) | copy-start | bytes 737284
  229.0 21.8 %collective-permute-start.12 = (bf16[2,256,384]{2,1,0:T(8,128)(2,1)}, bf16[2,256,384]{2,1,0:T(8,128)(2,1)S(1)}, u32[]{:S(2)}, u32[]{:S(2)}) collective-permute-start(bf16[2,256,384]{2,1,0:T(8,128)(2,1)} %get-tuple-element.301), channel_id=1, source_target_pairs={{0,1},{1,0},{2,3},{3,2},{4,5},{5,4},{6,7},{7,6},{8,9},{9,8},{10,11... | collective-permute-start | bytes 1179656 | tf_op jit(solution)/shard_map/ppermute | solution.py:992
  229.5 17.6 %collective-permute-start.9 = (bf16[1,432,384]{2,1,0:T(8,128)(2,1)S(1)}, bf16[1,432,384]{2,1,0:T(8,128)(2,1)S(1)}, u32[]{:S(2)}, u32[]{:S(2)}) collective-permute-start(bf16[1,432,384]{2,1,0:T(8,128)(2,1)S(1)} %copy-done.11), channel_id=1, source_target_pairs={{0,16},{4,20},{8,24},{12,28},{16,0},{20,4},{24,8},{28,12},{1,17},{... | collective-permute-start | bytes 995336 | tf_op jit(solution)/shard_map/ppermute | solution.py:995
  232.1 15.8 %collective-permute-start.10 = (bf16[2,160,384]{2,1,0:T(8,128)(2,1)S(1)}, bf16[2,160,384]{2,1,0:T(8,128)(2,1)}, u32[]{:S(2)}, u32[]{:S(2)}) collective-permute-start(bf16[2,160,384]{2,1,0:T(8,128)(2,1)S(1)} %copy-done.12), channel_id=1, source_target_pairs={{0,8},{4,12},{8,0},{12,4},{16,24},{20,28},{24,16},{28,20},{1,9},{5... | collective-permute-start | bytes 737288 | tf_op jit(solution)/shard_map/ppermute | solution.py:995
  249.7 31.4 %collective-permute-start.11 = (bf16[4,432,384]{2,1,0:T(8,128)(2,1)}, bf16[4,432,384]{2,1,0:T(8,128)(2,1)}, u32[]{:S(2)}, u32[]{:S(2)}) collective-permute-start(bf16[4,432,384]{2,1,0:T(8,128)(2,1)} %get-tuple-element.291), channel_id=1, source_target_pairs={{0,4},{4,0},{8,12},{12,8},{16,20},{20,16},{24,28},{28,24},{1,5},{5... | collective-permute-start | bytes 3981320 | tf_op jit(solution)/shard_map/ppermute | solution.py:995
  251.6 12.6 %copy-start = (bf16[768,768]{1,0:T(8,128)(2,1)S(1)}, bf16[768,768]{1,0:T(8,128)(2,1)}, u32[]{:S(2)}) copy-start(bf16[768,768]{1,0:T(8,128)(2,1)} %get-tuple-element.208) | copy-start | bytes 3538948
  264.2 19.1 %collective-permute-start.13 = (bf16[8,160,384]{2,1,0:T(8,128)(2,1)}, bf16[8,160,384]{2,1,0:T(8,128)(2,1)S(1)}, u32[]{:S(2)}, u32[]{:S(2)}) collective-permute-start(bf16[8,160,384]{2,1,0:T(8,128)(2,1)} %get-tuple-element.308), channel_id=1, source_target_pairs={{0,1},{1,0},{2,3},{3,2},{4,5},{5,4},{6,7},{7,6},{8,9},{9,8},{10,11... | collective-permute-start | bytes 2949128 | tf_op jit(solution)/shard_map/ppermute | solution.py:992
  264.2 16.8 %copy-start.1 = (bf16[4,432,384]{2,1,0:T(8,128)(2,1)S(1)}, bf16[4,432,384]{2,1,0:T(8,128)(2,1)}, u32[]{:S(2)}) copy-start(bf16[4,432,384]{2,1,0:T(8,128)(2,1)} %get-tuple-element.293) | copy-start | bytes 3981316
  266.8 18.6 %collective-permute-start.15 = (bf16[768,768]{1,0:T(8,128)(2,1)S(1)}, bf16[768,768]{1,0:T(8,128)(2,1)S(1)}, u32[]{:S(2)}, u32[]{:S(2)}) collective-permute-start(bf16[768,768]{1,0:T(8,128)(2,1)S(1)} %get-tuple-element.417), channel_id=1, source_target_pairs={{0,1},{1,0},{2,3},{3,2},{4,5},{5,4},{6,7},{7,6},{8,9},{9,8},{10,11... | collective-permute-start | bytes 3538952 | tf_op jit(solution)/shard_map/ppermute | solution.py:992
  267.3 16.0 %copy-start.5 = (bf16[8,160,384]{2,1,0:T(8,128)(2,1)S(1)}, bf16[8,160,384]{2,1,0:T(8,128)(2,1)}, u32[]{:S(2)}) copy-start(bf16[8,160,384]{2,1,0:T(8,128)(2,1)} %get-tuple-element.310) | copy-start | bytes 2949124
  267.3 28.4 %collective-permute-start.18 = (bf16[768,768]{1,0:T(8,128)(2,1)}, bf16[768,768]{1,0:T(8,128)(2,1)}, u32[]{:S(2)}, u32[]{:S(2)}) collective-permute-start(bf16[768,768]{1,0:T(8,128)(2,1)} %get-tuple-element.334), channel_id=1, source_target_pairs={{0,2},{1,3},{2,0},{3,1},{4,6},{5,7},{6,4},{7,5},{8,10},{9,11},{10,... | collective-permute-start | bytes 3538952 | tf_op jit(solution)/shard_map/ppermute | solution.py:992
  269.3 28.4 %collective-permute-start.14 = (bf16[1,160,384]{2,1,0:T(8,128)(2,1)}, bf16[1,160,384]{2,1,0:T(8,128)(2,1)S(1)}, u32[]{:S(2)}, u32[]{:S(2)}) collective-permute-start(bf16[1,160,384]{2,1,0:T(8,128)(2,1)} %get-tuple-element.314), channel_id=1, source_target_pairs={{0,16},{4,20},{8,24},{12,28},{16,0},{20,4},{24,8},{28,12},{1,17},{... | collective-permute-start | bytes 368648 | tf_op jit(solution)/shard_map/ppermute | solution.py:995
  283.5 14.9 %collective-permute-start.16 = (bf16[4,160,384]{2,1,0:T(8,128)(2,1)S(1)}, bf16[4,160,384]{2,1,0:T(8,128)(2,1)}, u32[]{:S(2)}, u32[]{:S(2)}) collective-permute-start(bf16[4,160,384]{2,1,0:T(8,128)(2,1)S(1)} %get-tuple-element.323), channel_id=1, source_target_pairs={{0,4},{4,0},{8,12},{12,8},{16,20},{20,16},{24,28},{28,24},{1,5},{5... | collective-permute-start | bytes 1474568 | tf_op jit(solution)/shard_map/ppermute | solution.py:995
  284.7 16.0 %collective-permute-start.17 = (bf16[2,432,384]{2,1,0:T(8,128)(2,1)}, bf16[2,432,384]{2,1,0:T(8,128)(2,1)}, u32[]{:S(2)}, u32[]{:S(2)}) collective-permute-start(bf16[2,432,384]{2,1,0:T(8,128)(2,1)} %get-tuple-element.329), channel_id=1, source_target_pairs={{0,8},{4,12},{8,0},{12,4},{16,24},{20,28},{24,16},{28,20},{1,9},{5... | collective-permute-start | bytes 1990664 | tf_op jit(solution)/shard_map/ppermute | solution.py:995
  292.0 5.6 %copy-start.7 = (bf16[1,160,384]{2,1,0:T(8,128)(2,1)S(1)}, bf16[1,160,384]{2,1,0:T(8,128)(2,1)}, u32[]{:S(2)}) copy-start(bf16[1,160,384]{2,1,0:T(8,128)(2,1)} %get-tuple-element.316) | copy-start | bytes 368644
  304.0 4.8 %collective-permute-start.19 = (bf16[768,768]{1,0:T(8,128)(2,1)S(1)}, bf16[768,768]{1,0:T(8,128)(2,1)}, u32[]{:S(2)}, u32[]{:S(2)}) collective-permute-start(bf16[768,768]{1,0:T(8,128)(2,1)S(1)} %get-tuple-element.415), channel_id=1, source_target_pairs={{0,1},{1,0},{2,3},{3,2},{4,5},{5,4},{6,7},{7,6},{8,9},{9,8},{10,11... | collective-permute-start | bytes 3538952 | tf_op jit(solution)/shard_map/ppermute | solution.py:992
  304.4 20.6 %collective-permute-start.35 = (f32[2,2,2]{2,1,0:T(2,128)S(1)}, f32[2,2,2]{2,1,0:T(2,128)S(1)}, u32[]{:S(2)}, u32[]{:S(2)}) collective-permute-start(f32[2,2,2]{2,1,0:T(2,128)S(1)} %reshape.220), channel_id=1, source_target_pairs={{0,1},{1,0},{2,3},{3,2},{4,5},{5,4},{6,7},{7,6},{8,9},{9,8},{10,11... | collective-permute-start | bytes 104 | tf_op jit(solution)/shard_map/ppermute | solution.py:992
  304.9 20.3 %collective-permute-start.26 = (bf16[432,384]{1,0:T(8,128)(2,1)S(1)}, bf16[432,384]{1,0:T(8,128)(2,1)}, u32[]{:S(2)}, u32[]{:S(2)}) collective-permute-start(bf16[432,384]{1,0:T(8,128)(2,1)S(1)} %copy-done.9), channel_id=1, source_target_pairs={{0,2},{1,3},{2,0},{3,1},{4,6},{5,7},{6,4},{7,5},{8,10},{9,11},{10,... | collective-permute-start | bytes 995336 | tf_op jit(solution)/shard_map/ppermute | solution.py:992
  306.4 11.8 %collective-permute-start.20 = (bf16[2,160,384]{2,1,0:T(8,128)(2,1)S(1)}, bf16[2,160,384]{2,1,0:T(8,128)(2,1)S(1)}, u32[]{:S(2)}, u32[]{:S(2)}) collective-permute-start(bf16[2,160,384]{2,1,0:T(8,128)(2,1)S(1)} %get-tuple-element.342), channel_id=1, source_target_pairs={{0,8},{4,12},{8,0},{12,4},{16,24},{20,28},{24,16},{28,20},{1,9},{5... | collective-permute-start | bytes 737288 | tf_op jit(solution)/shard_map/ppermute | solution.py:995
  306.8 17.5 %collective-permute-start.21 = (bf16[1,432,384]{2,1,0:T(8,128)(2,1)}, bf16[1,432,384]{2,1,0:T(8,128)(2,1)S(1)}, u32[]{:S(2)}, u32[]{:S(2)}) collective-permute-start(bf16[1,432,384]{2,1,0:T(8,128)(2,1)} %get-tuple-element.348), channel_id=1, source_target_pairs={{0,16},{4,20},{8,24},{12,28},{16,0},{20,4},{24,8},{28,12},{1,17},{... | collective-permute-start | bytes 995336 | tf_op jit(solution)/shard_map/ppermute | solution.py:995
  324.4 16.4 %copy-start.10 = (bf16[432,384]{1,0:T(8,128)(2,1)}, bf16[432,384]{1,0:T(8,128)(2,1)S(1)}, u32[]{:S(2)}) copy-start(bf16[432,384]{1,0:T(8,128)(2,1)S(1)} %add_bitcast_fusion.refs_0_) | copy-start | bytes 995332
  324.4 9.7 %collective-permute-start.23 = (bf16[432,384]{1,0:T(8,128)(2,1)S(1)}, bf16[432,384]{1,0:T(8,128)(2,1)S(1)}, u32[]{:S(2)}, u32[]{:S(2)}) collective-permute-start(bf16[432,384]{1,0:T(8,128)(2,1)S(1)} %add_bitcast_fusion.refs_0_), channel_id=1, source_target_pairs={{0,2},{1,3},{2,0},{3,1},{4,6},{5,7},{6,4},{7,5},{8,10},{9,11},{10,... | collective-permute-start | bytes 995336 | tf_op jit(solution)/shard_map/ppermute | solution.py:992
  324.9 6.6 %collective-permute-start.22 = (bf16[1,160,384]{2,1,0:T(8,128)(2,1)S(1)}, bf16[1,160,384]{2,1,0:T(8,128)(2,1)S(1)}, u32[]{:S(2)}, u32[]{:S(2)}) collective-permute-start(bf16[1,160,384]{2,1,0:T(8,128)(2,1)S(1)} %get-tuple-element.354), channel_id=1, source_target_pairs={{0,16},{4,20},{8,24},{12,28},{16,0},{20,4},{24,8},{28,12},{1,17},{... | collective-permute-start | bytes 368648 | tf_op jit(solution)/shard_map/ppermute | solution.py:995
  324.9 9.2 %collective-permute-start.27 = (bf16[432,384]{1,0:T(8,128)(2,1)S(1)}, bf16[432,384]{1,0:T(8,128)(2,1)S(1)}, u32[]{:S(2)}, u32[]{:S(2)}) collective-permute-start(bf16[432,384]{1,0:T(8,128)(2,1)S(1)} %copy-done.9), channel_id=1, source_target_pairs={{0,1},{1,0},{2,3},{3,2},{4,5},{5,4},{6,7},{7,6},{8,9},{9,8},{10,11... | collective-permute-start | bytes 995336 | tf_op jit(solution)/shard_map/ppermute | solution.py:992
  325.2 10.2 %collective-permute-start.28 = (bf16[432,384]{1,0:T(8,128)(2,1)}, bf16[432,384]{1,0:T(8,128)(2,1)S(1)}, u32[]{:S(2)}, u32[]{:S(2)}) collective-permute-start(bf16[432,384]{1,0:T(8,128)(2,1)} %collective-permute-done.26.refs_5_), channel_id=1, source_target_pairs={{0,1},{1,0},{2,3},{3,2},{4,5},{5,4},{6,7},{7,6},{8,9},{9,8},{10,11... | collective-permute-start | bytes 995336 | tf_op jit(solution)/shard_map/ppermute | solution.py:992
  325.8 9.9 %collective-permute-start.32 = (bf16[160,384]{1,0:T(8,128)(2,1)}, bf16[160,384]{1,0:T(8,128)(2,1)S(1)}, u32[]{:S(2)}, u32[]{:S(2)}) collective-permute-start(bf16[160,384]{1,0:T(8,128)(2,1)} %add_bitcast_fusion.3.refs_4_), channel_id=1, source_target_pairs={{0,2},{1,3},{2,0},{3,1},{4,6},{5,7},{6,4},{7,5},{8,10},{9,11},{10,... | collective-permute-start | bytes 368648 | tf_op jit(solution)/shard_map/ppermute | solution.py:992
  331.5 8.4 %collective-permute-start.24 = (bf16[432,384]{1,0:T(8,128)(2,1)S(1)}, bf16[432,384]{1,0:T(8,128)(2,1)S(1)}, u32[]{:S(2)}, u32[]{:S(2)}) collective-permute-start(bf16[432,384]{1,0:T(8,128)(2,1)S(1)} %add_bitcast_fusion.refs_0_), channel_id=1, source_target_pairs={{0,1},{1,0},{2,3},{3,2},{4,5},{5,4},{6,7},{7,6},{8,9},{9,8},{10,11... | collective-permute-start | bytes 995336 | tf_op jit(solution)/shard_map/ppermute | solution.py:992
  334.1 6.6 %copy-start.20 = (bf16[432,384]{1,0:T(8,128)(2,1)}, bf16[432,384]{1,0:T(8,128)(2,1)S(1)}, u32[]{:S(2)}) copy-start(bf16[432,384]{1,0:T(8,128)(2,1)S(1)} %collective-permute-done.23.refs_1_) | copy-start | bytes 995332
  334.1 6.6 %collective-permute-start.25 = (bf16[432,384]{1,0:T(8,128)(2,1)S(1)}, bf16[432,384]{1,0:T(8,128)(2,1)}, u32[]{:S(2)}, u32[]{:S(2)}) collective-permute-start(bf16[432,384]{1,0:T(8,128)(2,1)S(1)} %collective-permute-done.23.refs_1_), channel_id=1, source_target_pairs={{0,1},{1,0},{2,3},{3,2},{4,5},{5,4},{6,7},{7,6},{8,9},{9,8},{10,11... | collective-permute-start | bytes 995336 | tf_op jit(solution)/shard_map/ppermute | solution.py:992
  334.1 12.2 %copy-start.13 = (bf16[160,384]{1,0:T(8,128)(2,1)}, bf16[160,384]{1,0:T(8,128)(2,1)S(1)}, u32[]{:S(2)}) copy-start(bf16[160,384]{1,0:T(8,128)(2,1)S(1)} %add_bitcast_fusion.2.refs_0_) | copy-start | bytes 368644
  334.2 6.6 %copy-start.21 = (bf16[432,384]{1,0:T(8,128)(2,1)}, bf16[432,384]{1,0:T(8,128)(2,1)S(1)}, u32[]{:S(2)}) copy-start(bf16[432,384]{1,0:T(8,128)(2,1)S(1)} %collective-permute-done.27.refs_6_) | copy-start | bytes 995332
  334.2 5.8 %collective-permute-start.29 = (bf16[160,384]{1,0:T(8,128)(2,1)S(1)}, bf16[160,384]{1,0:T(8,128)(2,1)S(1)}, u32[]{:S(2)}, u32[]{:S(2)}) collective-permute-start(bf16[160,384]{1,0:T(8,128)(2,1)S(1)} %add_bitcast_fusion.2.refs_0_), channel_id=1, source_target_pairs={{0,2},{1,3},{2,0},{3,1},{4,6},{5,7},{6,4},{7,5},{8,10},{9,11},{10,... | collective-permute-start | bytes 368648 | tf_op jit(solution)/shard_map/ppermute | solution.py:992
  335.4 10.9 %collective-permute-start.33 = (bf16[160,384]{1,0:T(8,128)(2,1)}, bf16[160,384]{1,0:T(8,128)(2,1)S(1)}, u32[]{:S(2)}, u32[]{:S(2)}) collective-permute-start(bf16[160,384]{1,0:T(8,128)(2,1)} %add_bitcast_fusion.3.refs_4_), channel_id=1, source_target_pairs={{0,1},{1,0},{2,3},{3,2},{4,5},{5,4},{6,7},{7,6},{8,9},{9,8},{10,11... | collective-permute-start | bytes 368648 | tf_op jit(solution)/shard_map/ppermute | solution.py:992
  335.7 10.6 %copy-start.24 = (bf16[160,384]{1,0:T(8,128)(2,1)}, bf16[160,384]{1,0:T(8,128)(2,1)S(1)}, u32[]{:S(2)}) copy-start(bf16[160,384]{1,0:T(8,128)(2,1)S(1)} %collective-permute-done.32.refs_5_) | copy-start | bytes 368644
  335.7 10.7 %collective-permute-start.34 = (bf16[160,384]{1,0:T(8,128)(2,1)S(1)}, bf16[160,384]{1,0:T(8,128)(2,1)S(1)}, u32[]{:S(2)}, u32[]{:S(2)}) collective-permute-start(bf16[160,384]{1,0:T(8,128)(2,1)S(1)} %collective-permute-done.32.refs_5_), channel_id=1, source_target_pairs={{0,1},{1,0},{2,3},{3,2},{4,5},{5,4},{6,7},{7,6},{8,9},{9,8},{10,11... | collective-permute-start | bytes 368648 | tf_op jit(solution)/shard_map/ppermute | solution.py:992
  340.0 6.3 %copy-start.25 = (bf16[160,384]{1,0:T(8,128)(2,1)}, bf16[160,384]{1,0:T(8,128)(2,1)S(1)}, u32[]{:S(2)}) copy-start(bf16[160,384]{1,0:T(8,128)(2,1)S(1)} %collective-permute-done.29.refs_1_) | copy-start | bytes 368644
  340.0 6.4 %collective-permute-start.30 = (bf16[160,384]{1,0:T(8,128)(2,1)S(1)}, bf16[160,384]{1,0:T(8,128)(2,1)S(1)}, u32[]{:S(2)}, u32[]{:S(2)}) collective-permute-start(bf16[160,384]{1,0:T(8,128)(2,1)S(1)} %add_bitcast_fusion.2.refs_0_), channel_id=1, source_target_pairs={{0,1},{1,0},{2,3},{3,2},{4,5},{5,4},{6,7},{7,6},{8,9},{9,8},{10,11... | collective-permute-start | bytes 368648 | tf_op jit(solution)/shard_map/ppermute | solution.py:992
  340.0 6.4 %collective-permute-start.31 = (bf16[160,384]{1,0:T(8,128)(2,1)S(1)}, bf16[160,384]{1,0:T(8,128)(2,1)S(1)}, u32[]{:S(2)}, u32[]{:S(2)}) collective-permute-start(bf16[160,384]{1,0:T(8,128)(2,1)S(1)} %collective-permute-done.29.refs_1_), channel_id=1, source_target_pairs={{0,1},{1,0},{2,3},{3,2},{4,5},{5,4},{6,7},{7,6},{8,9},{9,8},{10,11... | collective-permute-start | bytes 368648 | tf_op jit(solution)/shard_map/ppermute | solution.py:992
  (18 other events, 33.1 us)

commit v7 on v6

--- a/solution.py
+++ b/solution.py
@@ -185,10 +185,11 @@
 
 
 def qkv_kernel(
-    ids, x0, x1, x2, w_ref, bias_ref, rel_ref, ctab_ref, stab_ref, joint_ref, turned_ref, kv_ref, x_ref,
-    *, layer,
+    ids, x0, x1, x2, w_ref, bias_ref, rel_ref, ctab_ref, stab_ref, joint_ref, turned_out, kv_ref, x_ref,
+    turned_ref, sem, *, layer,
 ):
     j = pl.program_id(0)
+    copy = pltpu.make_async_copy(turned_ref, turned_out, sem)
     half = x0.shape[1]
 
     @pl.when(j == 0)
@@ -214,6 +215,11 @@
                 c = coef[:, 128 * e : 128 * e + 128]
                 at = 256 * p + 128 * e
                 turned_ref[:, at : at + 128] = (c * ctab + pltpu.roll(c, 64, 1) * stab).astype(bf16)
+        copy.start()
+
+    @pl.when(j == pl.num_programs(0) - 1)
+    def _():
+        copy.wait()
 
 
 def project(ids, x, gathered, w_qkv, qv_bias, rel_pairs, ctab, stab, layer):
@@ -230,14 +236,17 @@
         ],
         [x, x, x, w_qkv, qv_bias, rel_pairs, ctab, stab],
         [
-            spec((tokens, width), 0, step), spec((tokens, 2 * width), 0, 0),
+            spec((tokens, width), 0, step), pl.BlockSpec(memory_space=pl.ANY),
             spec((half, width), 0, lambda i, ids: jnp.maximum(i - 1, 0)),
         ],
         [
             shape_of((tokens, 3 * width), bf16), shape_of((tokens, 2 * width), bf16),
             shape_of((half, 2 * width), bf16),
         ],
-        [pltpu.VMEM((tokens, width), bf16)],
+        [
+            pltpu.VMEM((tokens, width), bf16), pltpu.VMEM((tokens, 2 * width), bf16),
+            pltpu.SemaphoreType.DMA(()),
+        ],
     )
 
 
@@ -477,6 +486,19 @@
             at = k + 2 * i + tile // 2
             squares_ref[at : at + 1, :] += col_sum(x)
 
+    def squares_of(bias, result_ref, k):
+        @pl.when(ids[1] == layer)
+        def _():
+            for t in range(3):
+
+                def chunk(i, sums):
+                    to = pl.ds(t * half + i * rows, rows)
+                    valid = valid_ref[to, 0:1]
+                    branch, result = feed_ref[to, :] + bias, result_ref[to, :].astype(f32)
+                    return (sums[0] + fold(branch * branch * valid), sums[1] + fold(result * result * valid))
+
+                add_squares(row_loop(half // rows, chunk, (zero, zero)), k, t)
+
     @pl.when(j == 0)
     def _():
         ctx = jnp.concatenate([own_ref[...].T, shared_ref[...].T], 0)
@@ -488,18 +510,15 @@
             def chunk(i, sums):
                 at = i * rows
                 to = pl.ds(t * half + at, rows)
-                valid = valid_ref[to, 0:1]
                 attention = feed_ref[to, :] + bias
                 normed, inverse = norm_parts(x_ref[0, pl.ds(at, rows), :].astype(f32) + attention)
                 mixed = (normed * gain + shift).astype(bf16)
                 n1_ref[to, :] = normed.astype(bf16)
                 r1_ref[to, :] = jnp.broadcast_to(inverse, (rows, 128))
                 mixed_ref[to, :] = mixed
-                mixed = mixed.astype(f32)
-                return (sums[0] + fold(attention * attention * valid), sums[1] + fold(mixed * mixed * valid))
-
-            sums = row_loop(half // rows, chunk, (zero, zero))
-            add_squares(sums, 0, t)
+
+            row_loop(half // rows, chunk, None)
+        squares_of(bias, mixed_ref, 0)
         for copy in copies:
             copy.start()
 
@@ -535,17 +554,15 @@
 
             def chunk(i, sums):
                 to = pl.ds(t * half + i * rows, rows)
-                valid = valid_ref[to, 0:1]
                 branch = feed_ref[to, :] + bias
                 normed, inverse = norm_parts(mixed_ref[to, :].astype(f32) + branch)
                 out = normed * gain + shift
                 n2_ref[to, :] = normed.astype(bf16)
                 r2_ref[to, :] = jnp.broadcast_to(inverse, (rows, 128))
                 h_ref[to, :] = out.astype(bf16)
-                return (sums[0] + fold(branch * branch * valid), sums[1] + fold(out * out * valid))
-
-            sums = row_loop(half // rows, chunk, (zero, zero))
-            add_squares(sums, 4, t)
+
+            row_loop(half // rows, chunk, None)
+        squares_of(bias, h_ref, 4)
         for copy in copies:
             copy.wait()
 
@@ -785,16 +802,18 @@
 
 def joint_bwd_kernel(
     ids, x0, x1, x2, own_ref, shared_ref, arrived_ref, w_ref, attn_ref, rel0_ref, rel1_ref, vec_ref, pre_sum_ref,
-    h_ref, keep_ref, send_ref, acc_ref, x_t, sums_ref, mine_ref,
+    h_ref, keep_ref, send_ref, acc_ref, x_t, sums_ref, mine_ref, attn, sem,
     *, split,
 ):
     j = pl.program_id(0)
+    copy = pltpu.make_async_copy(attn_ref, attn, sem)
     width = x_t.shape[0]
     rows = width // SUPER
     half = rows // 2
 
     @pl.when(j == 0)
     def _():
+        copy.start()
         x_t[...] = jnp.concatenate([x0[0].T, x1[0].T, x2[0].T], 1)
         sums_ref[...] = jnp.zeros_like(sums_ref)
 
@@ -807,8 +826,7 @@
 
     @pl.when(j == 0)
     def _():
-        flag = (ids[1] == 0).astype(f32) if split else 1.0
-        acc_ref[...] = part + attn_ref[...].astype(f32) * flag
+        acc_ref[...] = part
 
     @pl.when(j > 0)
     def _():
@@ -834,7 +852,9 @@
 
     @pl.when(j == pl.num_programs(0) - 1)
     def _():
-        h_ref[...] = acc_ref[...].astype(bf16)
+        copy.wait()
+        flag = (ids[1] == 0).astype(f32) if split else 1.0
+        h_ref[...] = (acc_ref[...] + attn[...].astype(f32) * flag).astype(bf16)
         rel = (rel0_ref[...] + rel1_ref[...]).astype(bf16)
         count = rel.shape[0] // SUPER
         lines = jnp.concatenate([vec_ref[0:6, :], sums_ref[0, 0:1], sums_ref[2, 0:1]], 0)
@@ -862,7 +882,7 @@
             spec((1, length, cols), step, 0, 0), spec((1, half, cols), step, 0, 0),
             spec((1, half, cols), lambda i, ids: jnp.maximum(i - 1, 0), 0, 0),
             spec((1, width, cols), layer, 0, lambda i, ids: 2 * i + ids[1] if split else i),
-            full(tokens, width), spec((rel0.shape[0], LANES), 0, side), spec((rel0.shape[0], LANES), 0, side),
+            pl.BlockSpec(memory_space=pl.ANY), spec((rel0.shape[0], LANES), 0, side), spec((rel0.shape[0], LANES), 0, side),
             full(*vec.shape), full(*pre_sum.shape),
         ],
         [x, x, x, own, shared, arrived, w_qkv, g_attn, rel0, rel1, vec, pre_sum],
@@ -871,6 +891,7 @@
         [
             pltpu.VMEM((tokens, width), f32), pltpu.VMEM((width, tokens), bf16),
             pltpu.VMEM((3, 8, width), f32), pltpu.VMEM((tokens, LANES), bf16),
+            pltpu.VMEM((tokens, width), bf16), pltpu.SemaphoreType.DMA(()),
         ],
     )
 

time: 358 us -> 356 us (level)
  no operation moved by 1% of the time
where the time goes in v7:
time: 356 us; the launch traced here: 350 us
  Pallas kernels  250 us (70%)
  waiting for transfers between devices  37.8 us (11%)
  other arithmetic  30.3 us (9%)
  starting transfers between devices  24.2 us (7%)
  local copies, waits for them, and re-layouts  5.95 us (2%)
    pallas_call x21, Pallas kernels, call(): pl.pallas_call(kernel, grid_spec=pltpu.PrefetchScalarGridSpec(num_scalar_...  250 us
    ppermute x12, waiting for transfers between devices, flip_dp(): return lax.ppermute(x, 'dp', [(i, i ^ bit) for i in range(dp)])  27 us
    add x12, other arithmetic, absorb(): return pin((keep[:n] + arrived[:n], keep[n:] + arrived[n:]))  21.8 us
    ppermute x12, starting transfers between devices, flip_dp(): return lax.ppermute(x, 'dp', [(i, i ^ bit) for i in range(dp)])  13.4 us
    ppermute x24, waiting for transfers between devices, flip(): return lax.ppermute(x, 'section', [(i, i ^ bit) for i in range(sections)])  10.9 us
    ppermute x24, starting transfers between devices, flip(): return lax.ppermute(x, 'section', [(i, i ^ bit) for i in range(sections)])  10.7 us
  transfers between devices with their start and end apart: 36, of which 10 were waited for; matrix products, arithmetic and copies ran while one was open for 8% of the time, Pallas kernels for 38%

profile of v7, /device:TPU:0, one launch (start us, length us, event | category | flops | bytes accessed | tf_op | source)
XLA Modules:
  0.0 349.8 jit_solution(9683536472804597135)
XLA Ops:
  1.3 4.1 %tables.1 = (f32[64,1024]{1,0:T(8,128)}, f32[64,1024]{1,0:T(8,128)}, bf16[1024,128]{1,0:T(8,128)(2,1)}, f32[1024,128]{1,0:T(8,128)}, f32[1024,128]{1,0:T(8,128)}...) custom-call(s32[3]{0:T(128)} %pad_add_fusion.ids, s32[3,4,512]{2,1,0:T(4,128)} %bitcast.67, ...), custom_call_target="tpu_custom_call" | custom-call | flops 4400000000 | bytes 4000000 | tf_op jit(solution)/shard_map/tables/pallas_call | solution.py:83
  5.5 9.7 %projections.2 = (bf16[768,2304]{1,0:T(8,128)(2,1)}, bf16[768,1536]{1,0:T(8,128)(2,1)}, bf16[256,1536]{1,0:T(8,128)(2,1)}) custom-call(s32[3]{0:T(128)} %pad_add_fusion.ids, bf16[6,256,768]{2,1,0:T(8,128)(2,1)} %bitcast.31, bf16[6,256,768]{2,1,0:T(8,128)(2,1)} %bitcast.32, bf16[6,256,768]{2,1,0:T(8,128)(2,1)} %bitcast.33, bf16[2,768,2304]{2,1,0:T(8,128)(2,1)} %w_ref.7, ...), custom_call_target="tpu_custom_call" | custom-call | flops 8800000000 | bytes 8000000 | tf_op jit(solution)/shard_map/projections/pallas_call | solution.py:83
  15.7 8.6 %attention_forward.4 = (bf16[768,512]{1,0:T(8,128)(2,1)}, f32[6,2,512]{2,1,0:T(2,128)}) custom-call(s32[3]{0:T(128)} %pad_add_fusion.ids, f32[1024,128]{1,0:T(8,128)} %get-tuple-element.197.code_ref, f32[8,1024]{1,0:T(8,128)} %get-tuple-element.198.seg_ref, bf16[1024,128]{1,0:T(8,128)(2,1)} %get-tuple-element.199.kf_ref, ...), custom_call_target="tpu_custom_call" | custom-call | flops 7699999744 | bytes 7000000 | tf_op jit(solution)/shard_map/attention_forward/pallas_call | solution.py:83
  25.2 6.3 %attention_forward.5 = (bf16[768,256]{1,0:T(8,128)(2,1)}, f32[6,2,256]{2,1,0:T(2,128)}) custom-call(s32[3]{0:T(128)} %pad_add_fusion.ids, f32[1024,128]{1,0:T(8,128)} %get-tuple-element.197.code_ref, f32[8,1024]{1,0:T(8,128)} %get-tuple-element.198.seg_ref, bf16[1024,128]{1,0:T(8,128)(2,1)} %get-tuple-element.199.kf_ref, ...), custom_call_target="tpu_custom_call" | custom-call | flops 7699999744 | bytes 7000000 | tf_op jit(solution)/shard_map/attention_forward/pallas_call | solution.py:83
  31.5 24.9 %feed_forward.2 = (bf16[768,768]{1,0:T(8,128)(2,1)}, f32[768,128]{1,0:T(8,128)}, bf16[768,768]{1,0:T(8,128)(2,1)}, f32[768,128]{1,0:T(8,128)}, bf16[768,768]{1,0...) custom-call(s32[3]{0:T(128)} %pad_add_fusion.ids, ...), custom_call_target="tpu_custom_call" | custom-call | flops 26400000000 | bytes 24000000 | tf_op jit(solution)/shard_map/feed_forward/pallas_call | solution.py:83
  56.5 9.7 %projections.3 = (bf16[768,2304]{1,0:T(8,128)(2,1)}, bf16[768,1536]{1,0:T(8,128)(2,1)}, bf16[256,1536]{1,0:T(8,128)(2,1)}) custom-call(s32[3]{0:T(128)} %pad_add_fusion.ids, bf16[3,256,768]{2,1,0:T(8,128)(2,1)} %bitcast.40, bf16[3,256,768]{2,1,0:T(8,128)(2,1)} %bitcast.41, bf16[3,256,768]{2,1,0:T(8,128)(2,1)} %bitcast.42, bf16[2,768,2304]{2,1,0:T(8,128)(2,1)} %w_ref.7, ...), custom_call_target="tpu_custom_call" | custom-call | flops 8800000000 | bytes 8000000 | tf_op jit(solution)/shard_map/projections/pallas_call | solution.py:83
  66.3 8.6 %attention_forward.6 = (bf16[768,512]{1,0:T(8,128)(2,1)}, f32[6,2,512]{2,1,0:T(2,128)}) custom-call(s32[3]{0:T(128)} %pad_add_fusion.ids, f32[1024,128]{1,0:T(8,128)} %get-tuple-element.197.code_ref, f32[8,1024]{1,0:T(8,128)} %get-tuple-element.198.seg_ref, bf16[1024,128]{1,0:T(8,128)(2,1)} %get-tuple-element.199.kf_ref, ...), custom_call_target="tpu_custom_call" | custom-call | flops 7699999744 | bytes 7000000 | tf_op jit(solution)/shard_map/attention_forward/pallas_call | solution.py:83
  75.8 6.7 %attention_forward.7 = (bf16[768,256]{1,0:T(8,128)(2,1)}, f32[6,2,256]{2,1,0:T(2,128)}) custom-call(s32[3]{0:T(128)} %pad_add_fusion.ids, f32[1024,128]{1,0:T(8,128)} %get-tuple-element.197.code_ref, f32[8,1024]{1,0:T(8,128)} %get-tuple-element.198.seg_ref, bf16[1024,128]{1,0:T(8,128)(2,1)} %get-tuple-element.199.kf_ref, ...), custom_call_target="tpu_custom_call" | custom-call | flops 7699999744 | bytes 7000000 | tf_op jit(solution)/shard_map/attention_forward/pallas_call | solution.py:83
  82.5 23.3 %feed_forward.3 = (bf16[768,768]{1,0:T(8,128)(2,1)}, f32[768,128]{1,0:T(8,128)}, bf16[768,768]{1,0:T(8,128)(2,1)}, f32[768,128]{1,0:T(8,128)}, bf16[768,768]{1,0...) custom-call(s32[3]{0:T(128)} %pad_add_fusion.ids, ...), custom_call_target="tpu_custom_call" | custom-call | flops 26400000000 | bytes 24000000 | tf_op jit(solution)/shard_map/feed_forward/pallas_call | solution.py:83
  105.8 28.7 %feed_backward.2 = (bf16[768,768]{1,0:T(8,128)(2,1)}, bf16[768,768]{1,0:T(8,128)(2,1)}, bf16[768,768]{1,0:T(8,128)(2,1)}, f32[8,768]{1,0:T(8,128)}, f32[8,3072]{...) custom-call(s32[3]{0:T(128)} %pad_add_fusion.ids, bf16[6,256,768]{2,1,0:T(8,128)(2,1)} %bitcast.57, ...), custom_call_target="tpu_custom_call" | custom-call | flops 32999999488 | bytes 30000000 | tf_op jit(solution)/shard_map/feed_backward/pallas_call | solution.py:83
  135.0 10.9 %attention_backward.5 = (bf16[3,256,768]{2,1,0:T(8,128)(2,1)}, bf16[2,256,768]{2,1,0:T(8,128)(2,1)}, f32[128,768]{1,0:T(8,128)}) custom-call(s32[3]{0:T(128)} %pad_add_fusion.ids, f32[1024,128]{1,0:T(8,128)} %get-tuple-element.197.code_ref, f32[8,1024]{1,0:T(8,128)} %get-tuple-element.198.seg_ref, bf16[1024,128]{1,0:T(8,128)(2,1)} %get-tuple-element.199.kf_ref, ...), custom_call_target="tpu_custom_call" | custom-call | flops 44000002048 | bytes 40000000 | tf_op jit(solution)/shard_map/attention_backward/pallas_call | solution.py:83
  146.0 3.9 %slice_add_fusion.2 = (bf16[4,432,384]{2,1,0:T(8,128)(2,1)}, bf16[4,432,384]{2,1,0:T(8,128)(2,1)S(1)}) fusion(bf16[8,432,384]{2,1,0:T(8,128)(2,1)} %collective-permute-done.2, bf16[8,432,384]{2,1,0:T(8,128)(2,1)} %get-tuple-element.224), kind=kLoop, calls=%fused_computation.2 | loop fusion | flops 1327104 | bytes 7962624 | tf_op jit(solution)/shard_map/add | solution.py:1048
  149.9 3.0 collective-permute-start.3
  152.8 16.6 %attention_backward.4 = (bf16[3,512,768]{2,1,0:T(8,128)(2,1)}, f32[128,768]{1,0:T(8,128)}) custom-call(s32[3]{0:T(128)} %pad_add_fusion.ids, f32[1024,128]{1,0:T(8,128)} %get-tuple-element.197.code_ref, f32[8,1024]{1,0:T(8,128)} %get-tuple-element.198.seg_ref, bf16[1024,128]{1,0:T(8,128)(2,1)} %get-tuple-element.199.kf_ref, ...), custom_call_target="tpu_custom_call" | custom-call | flops 13200000000 | bytes 12000000 | tf_op jit(solution)/shard_map/attention_backward/pallas_call | solution.py:83
  169.4 13.2 %projections_backward.2 = (bf16[768,768]{1,0:T(8,128)(2,1)}, bf16[8,160,384]{2,1,0:T(8,128)(2,1)}, bf16[8,160,384]{2,1,0:T(8,128)(2,1)}) custom-call(s32[3]{0:T(128)} %pad_add_fusion.ids, bf16[3,256,768]{2,1,0:T(8,128)(2,1)} %bitcast.46, bf16[3,256,768]{2,1,0:T(8,128)(2,1)} %bitcast.47, bf16[3,256,768]{2,1,0:T(8,128)(2,1)} %bitcast.48, ...), custom_call_target="tpu_custom_call" | custom-call | flops 3300000000 | bytes 3000000 | tf_op jit(solution)/shard_map/projections_backward/pallas_call | solution.py:83
  182.8 2.4 slice_add_fusion.6
  185.7 1.6 collective-permute-start.6
  188.4 28.4 %feed_backward.3 = (bf16[768,768]{1,0:T(8,128)(2,1)}, bf16[768,768]{1,0:T(8,128)(2,1)}, bf16[768,768]{1,0:T(8,128)(2,1)}, f32[8,768]{1,0:T(8,128)}, f32[8,3072]{...) custom-call(s32[3]{0:T(128)} %pad_add_fusion.ids, bf16[3,256,768]{2,1,0:T(8,128)(2,1)} %bitcast.49, ...), custom_call_target="tpu_custom_call" | custom-call | flops 32999999488 | bytes 30000000 | tf_op jit(solution)/shard_map/feed_backward/pallas_call | solution.py:83
  216.8 1.9 slice_add_fusion.14
  218.7 1.8 slice_add_fusion.18
  220.5 6.9 %attention_backward.7 = (bf16[3,256,384]{2,1,0:T(8,128)(2,1)}, bf16[2,256,384]{2,1,0:T(8,128)(2,1)}, f32[128,384]{1,0:T(8,128)}) custom-call(s32[3]{0:T(128)} %pad_add_fusion.ids, f32[1024,128]{1,0:T(8,128)} %get-tuple-element.197.code_ref, f32[8,1024]{1,0:T(8,128)} %get-tuple-element.198.seg_ref, bf16[1024,128]{1,0:T(8,128)(2,1)} %get-tuple-element.199.kf_ref, ...), custom_call_target="tpu_custom_call" | custom-call | flops 44000002048 | bytes 40000000 | tf_op jit(solution)/shard_map/attention_backward/pallas_call | solution.py:83
  227.9 2.6 collective-permute-start.9
  231.0 4.3 %slice_add_fusion = (bf16[4,432,384]{2,1,0:T(8,128)(2,1)}, bf16[4,432,384]{2,1,0:T(8,128)(2,1)}) fusion(bf16[8,432,384]{2,1,0:T(8,128)(2,1)} %collective-permute-done.8, bf16[8,432,384]{2,1,0:T(8,128)(2,1)} %get-tuple-element.275), kind=kLoop, calls=%fused_computation | loop fusion | flops 1327104 | bytes 7962624 | tf_op jit(solution)/shard_map/add | solution.py:1048
  235.3 9.9 %attention_backward.6 = (bf16[3,512,384]{2,1,0:T(8,128)(2,1)}, f32[128,384]{1,0:T(8,128)}) custom-call(s32[3]{0:T(128)} %pad_add_fusion.ids, f32[1024,128]{1,0:T(8,128)} %get-tuple-element.197.code_ref, f32[8,1024]{1,0:T(8,128)} %get-tuple-element.198.seg_ref, bf16[1024,128]{1,0:T(8,128)(2,1)} %get-tuple-element.199.kf_ref, ...), custom_call_target="tpu_custom_call" | custom-call | flops 13200000000 | bytes 12000000 | tf_op jit(solution)/shard_map/attention_backward/pallas_call | solution.py:83
  246.4 1.7 slice_add_fusion.22
  249.8 12.2 %projections_backward.3 = (bf16[768,768]{1,0:T(8,128)(2,1)}, bf16[8,160,384]{2,1,0:T(8,128)(2,1)}, bf16[8,160,384]{2,1,0:T(8,128)(2,1)}) custom-call(s32[3]{0:T(128)} %pad_add_fusion.ids, bf16[6,256,768]{2,1,0:T(8,128)(2,1)} %bitcast.37, bf16[6,256,768]{2,1,0:T(8,128)(2,1)} %bitcast.38, bf16[6,256,768]{2,1,0:T(8,128)(2,1)} %bitcast.39, ...), custom_call_target="tpu_custom_call" | custom-call | flops 3300000000 | bytes 3000000 | tf_op jit(solution)/shard_map/projections_backward/pallas_call | solution.py:83
  262.2 2.7 broadcast_select_fusion.6
  265.3 1.9 collective-permute-start.18
  267.2 12.2 %collective-permute-done.11 = bf16[4,432,384]{2,1,0:T(8,128)(2,1)} collective-permute-done((bf16[4,432,384]{2,1,0:T(8,128)(2,1)}, bf16[4,432,384]{2,1,0:T(8,128)(2,1)}, u32[]{:S(2)}, u32[]{:S(2)}) %collective-permute-start.11) | collective-permute-done | bytes 1327136 | tf_op jit(solution)/shard_map/ppermute | solution.py:1016
  279.5 2.3 slice_add_fusion.4
  284.6 5.5 %place_rows.2 = bf16[6,256,768]{2,1,0:T(8,128)(2,1)} custom-call(s32[3]{0:T(128)} %pad_add_fusion.ids, bf16[3,256,768]{2,1,0:T(8,128)(2,1)} %bitcast.52, bf16[3,256,768]{2,1,0:T(8,128)(2,1)} %bitcast.60), custom_call_target="tpu_custom_call" | custom-call | flops 4400000000 | bytes 4000000 | tf_op jit(solution)/shard_map/place_rows/pallas_call | solution.py:83
  290.2 3.5 %collective-permute-done.18 = bf16[768,768]{1,0:T(8,128)(2,1)} collective-permute-done((bf16[768,768]{1,0:T(8,128)(2,1)}, bf16[768,768]{1,0:T(8,128)(2,1)}, u32[]{:S(2)}, u32[]{:S(2)}) %collective-permute-start.18) | collective-permute-done | bytes 1179680 | tf_op jit(solution)/shard_map/ppermute | solution.py:1013
  293.7 1.9 add.140
  296.3 1.2 slice_add_fusion.16
  297.6 1.4 collective-permute-done.17
  299.0 1.9 slice_add_fusion.12
  300.9 1.3 broadcast_select_fusion.4
  303.1 1.6 collective-permute-start.26
  305.0 1.8 collective-permute-start.21
  306.7 6.6 %place_rows.3 = f32[6,256,768]{2,1,0:T(8,128)} custom-call(s32[3]{0:T(128)} %pad_add_fusion.ids, bf16[3,256,768]{2,1,0:T(8,128)(2,1)} %bitcast.53, bf16[3,256,768]{2,1,0:T(8,128)(2,1)} %bitcast.15.other_ref), custom_call_target="tpu_custom_call" | custom-call | flops 4400000000 | bytes 4000000 | tf_op jit(solution)/shard_map/place_rows/pallas_call | solution.py:83
  313.3 2.9 collective-permute-done.20
  316.3 6.2 %collective-permute-done.21 = bf16[1,432,384]{2,1,0:T(8,128)(2,1)S(1)} collective-permute-done((bf16[1,432,384]{2,1,0:T(8,128)(2,1)}, bf16[1,432,384]{2,1,0:T(8,128)(2,1)S(1)}, u32[]{:S(2)}, u32[]{:S(2)}) %collective-permute-start.21) | collective-permute-done | bytes 331808 | tf_op jit(solution)/shard_map/ppermute | solution.py:1016
  323.9 1.6 collective-permute-start.32
  325.5 3.8 %collective-permute-done.22 = bf16[1,160,384]{2,1,0:T(8,128)(2,1)S(1)} collective-permute-done((bf16[1,160,384]{2,1,0:T(8,128)(2,1)S(1)}, bf16[1,160,384]{2,1,0:T(8,128)(2,1)S(1)}, u32[]{:S(2)}, u32[]{:S(2)}) %collective-permute-start.22) | collective-permute-done | bytes 122912 | tf_op jit(solution)/shard_map/ppermute | solution.py:1016
  329.3 2.9 collective-permute-done.23.refs_1_
  334.1 4.0 %collective-permute-done.29.refs_1_ = bf16[160,384]{1,0:T(8,128)(2,1)S(1)} collective-permute-done((bf16[160,384]{1,0:T(8,128)(2,1)S(1)}, bf16[160,384]{1,0:T(8,128)(2,1)S(1)}, u32[]{:S(2)}, u32[]{:S(2)}) %collective-permute-start.29) | collective-permute-done | bytes 122912 | tf_op jit(solution)/shard_map/ppermute | solution.py:1013
  338.9 5.5 %unpack_feed.1 = (f32[2,96,3072]{2,1,0:T(8,128)}, f32[2,384,768]{2,1,0:T(8,128)}, f32[2,96,768]{2,1,0:T(8,128)}) custom-call(s32[3]{0:T(128)} %pad_add_fusion.ids, bf16[432,384]{1,0:T(8,128)(2,1)} %copy-done.10, bf16[432,384]{1,0:T(8,128)(2,1)} %copy-done.20, bf16[432,384]{1,0:T(8,128)(2,1)} %copy-done.23, bf16[432,384]{1,0:T(8,128)(2,1)} %collective-permute-done.25.refs_3_, ...), custom_call_target="tpu_custom_call" | custom-call | flops 4400000000 | bytes 4000000 | tf_op jit(solution)/shard_map/unpack_feed/pallas_call | solution.py:83
  345.8 3.5 unpack_attention.1
  (134 shorter events, 19.9 us)
Async XLA Ops:
  15.1 9.2 %collective-permute-start = (bf16[256,1536]{1,0:T(8,128)(2,1)}, bf16[256,1536]{1,0:T(8,128)(2,1)S(1)}, u32[]{:S(2)}, u32[]{:S(2)}) collective-permute-start(bf16[256,1536]{1,0:T(8,128)(2,1)} %get-tuple-element.205), channel_id=1, source_target_pairs={{0,1},{1,0},{2,3},{3,2},{4,5},{5,4},{6,7},{7,6},{8,9},{9,8},{10,11... | collective-permute-start | bytes 2359304 | tf_op jit(solution)/shard_map/ppermute | solution.py:1013
  66.2 8.7 %collective-permute-start.1 = (bf16[256,1536]{1,0:T(8,128)(2,1)}, bf16[256,1536]{1,0:T(8,128)(2,1)S(1)}, u32[]{:S(2)}, u32[]{:S(2)}) collective-permute-start(bf16[256,1536]{1,0:T(8,128)(2,1)} %get-tuple-element.212), channel_id=1, source_target_pairs={{0,1},{1,0},{2,3},{3,2},{4,5},{5,4},{6,7},{7,6},{8,9},{9,8},{10,11... | collective-permute-start | bytes 2359304 | tf_op jit(solution)/shard_map/ppermute | solution.py:1013
  134.5 11.5 %collective-permute-start.2 = (bf16[8,432,384]{2,1,0:T(8,128)(2,1)}, bf16[8,432,384]{2,1,0:T(8,128)(2,1)}, u32[]{:S(2)}, u32[]{:S(2)}) collective-permute-start(bf16[8,432,384]{2,1,0:T(8,128)(2,1)} %get-tuple-element.222), channel_id=1, source_target_pairs={{0,1},{1,0},{2,3},{3,2},{4,5},{5,4},{6,7},{7,6},{8,9},{9,8},{10,11... | collective-permute-start | bytes 7962632 | tf_op jit(solution)/shard_map/ppermute | solution.py:1013
  145.9 23.5 %collective-permute-start.4 = (bf16[2,256,768]{2,1,0:T(8,128)(2,1)}, bf16[2,256,768]{2,1,0:T(8,128)(2,1)}, u32[]{:S(2)}, u32[]{:S(2)}) collective-permute-start(bf16[2,256,768]{2,1,0:T(8,128)(2,1)} %get-tuple-element.240), channel_id=1, source_target_pairs={{0,1},{1,0},{2,3},{3,2},{4,5},{5,4},{6,7},{7,6},{8,9},{9,8},{10,11... | collective-permute-start | bytes 2359304 | tf_op jit(solution)/shard_map/ppermute | solution.py:1013
  149.9 32.9 %collective-permute-start.3 = (bf16[4,432,384]{2,1,0:T(8,128)(2,1)}, bf16[4,432,384]{2,1,0:T(8,128)(2,1)}, u32[]{:S(2)}, u32[]{:S(2)}) collective-permute-start(bf16[4,432,384]{2,1,0:T(8,128)(2,1)} %get-tuple-element.228), channel_id=1, source_target_pairs={{0,4},{4,0},{8,12},{12,8},{16,20},{20,16},{24,28},{28,24},{1,5},{5... | collective-permute-start | bytes 3981320 | tf_op jit(solution)/shard_map/ppermute | solution.py:1016
  182.7 2.8 collective-permute-start.5
  185.7 31.1 %collective-permute-start.6 = (bf16[2,432,384]{2,1,0:T(8,128)(2,1)}, bf16[2,432,384]{2,1,0:T(8,128)(2,1)}, u32[]{:S(2)}, u32[]{:S(2)}) collective-permute-start(bf16[2,432,384]{2,1,0:T(8,128)(2,1)} %get-tuple-element.253), channel_id=1, source_target_pairs={{0,8},{4,12},{8,0},{12,4},{16,24},{20,28},{24,16},{28,20},{1,9},{5... | collective-permute-start | bytes 1990664 | tf_op jit(solution)/shard_map/ppermute | solution.py:1016
  187.3 31.4 %collective-permute-start.7 = (bf16[4,160,384]{2,1,0:T(8,128)(2,1)S(1)}, bf16[4,160,384]{2,1,0:T(8,128)(2,1)}, u32[]{:S(2)}, u32[]{:S(2)}) collective-permute-start(bf16[4,160,384]{2,1,0:T(8,128)(2,1)S(1)} %get-tuple-element.259), channel_id=1, source_target_pairs={{0,4},{4,0},{8,12},{12,8},{16,20},{20,16},{24,28},{28,24},{1,5},{5... | collective-permute-start | bytes 1474568 | tf_op jit(solution)/shard_map/ppermute | solution.py:1016
  216.7 14.2 %collective-permute-start.8 = (bf16[8,432,384]{2,1,0:T(8,128)(2,1)}, bf16[8,432,384]{2,1,0:T(8,128)(2,1)}, u32[]{:S(2)}, u32[]{:S(2)}) collective-permute-start(bf16[8,432,384]{2,1,0:T(8,128)(2,1)} %get-tuple-element.273), channel_id=1, source_target_pairs={{0,1},{1,0},{2,3},{3,2},{4,5},{5,4},{6,7},{7,6},{8,9},{9,8},{10,11... | collective-permute-start | bytes 7962632 | tf_op jit(solution)/shard_map/ppermute | solution.py:1013
  220.5 7.4 %copy-start.11 = (bf16[1,432,384]{2,1,0:T(8,128)(2,1)S(1)}, bf16[1,432,384]{2,1,0:T(8,128)(2,1)}, u32[]{:S(2)}) copy-start(bf16[1,432,384]{2,1,0:T(8,128)(2,1)} %get-tuple-element.279) | copy-start | bytes 995332
  220.5 10.0 %copy-start.12 = (bf16[2,160,384]{2,1,0:T(8,128)(2,1)S(1)}, bf16[2,160,384]{2,1,0:T(8,128)(2,1)}, u32[]{:S(2)}) copy-start(bf16[2,160,384]{2,1,0:T(8,128)(2,1)} %get-tuple-element.285) | copy-start | bytes 737284
  227.4 21.6 %collective-permute-start.12 = (bf16[2,256,384]{2,1,0:T(8,128)(2,1)}, bf16[2,256,384]{2,1,0:T(8,128)(2,1)S(1)}, u32[]{:S(2)}, u32[]{:S(2)}) collective-permute-start(bf16[2,256,384]{2,1,0:T(8,128)(2,1)} %get-tuple-element.301), channel_id=1, source_target_pairs={{0,1},{1,0},{2,3},{3,2},{4,5},{5,4},{6,7},{7,6},{8,9},{9,8},{10,11... | collective-permute-start | bytes 1179656 | tf_op jit(solution)/shard_map/ppermute | solution.py:1013
  227.9 17.7 %collective-permute-start.9 = (bf16[1,432,384]{2,1,0:T(8,128)(2,1)S(1)}, bf16[1,432,384]{2,1,0:T(8,128)(2,1)S(1)}, u32[]{:S(2)}, u32[]{:S(2)}) collective-permute-start(bf16[1,432,384]{2,1,0:T(8,128)(2,1)S(1)} %copy-done.11), channel_id=1, source_target_pairs={{0,16},{4,20},{8,24},{12,28},{16,0},{20,4},{24,8},{28,12},{1,17},{... | collective-permute-start | bytes 995336 | tf_op jit(solution)/shard_map/ppermute | solution.py:1016
  230.5 15.9 %collective-permute-start.10 = (bf16[2,160,384]{2,1,0:T(8,128)(2,1)S(1)}, bf16[2,160,384]{2,1,0:T(8,128)(2,1)}, u32[]{:S(2)}, u32[]{:S(2)}) collective-permute-start(bf16[2,160,384]{2,1,0:T(8,128)(2,1)S(1)} %copy-done.12), channel_id=1, source_target_pairs={{0,8},{4,12},{8,0},{12,4},{16,24},{20,28},{24,16},{28,20},{1,9},{5... | collective-permute-start | bytes 737288 | tf_op jit(solution)/shard_map/ppermute | solution.py:1016
  248.1 31.4 %collective-permute-start.11 = (bf16[4,432,384]{2,1,0:T(8,128)(2,1)}, bf16[4,432,384]{2,1,0:T(8,128)(2,1)}, u32[]{:S(2)}, u32[]{:S(2)}) collective-permute-start(bf16[4,432,384]{2,1,0:T(8,128)(2,1)} %get-tuple-element.291), channel_id=1, source_target_pairs={{0,4},{4,0},{8,12},{12,8},{16,20},{20,16},{24,28},{28,24},{1,5},{5... | collective-permute-start | bytes 3981320 | tf_op jit(solution)/shard_map/ppermute | solution.py:1016
  249.8 12.3 %copy-start = (bf16[768,768]{1,0:T(8,128)(2,1)S(1)}, bf16[768,768]{1,0:T(8,128)(2,1)}, u32[]{:S(2)}) copy-start(bf16[768,768]{1,0:T(8,128)(2,1)} %get-tuple-element.208) | copy-start | bytes 3538948
  262.1 19.7 %collective-permute-start.13 = (bf16[8,160,384]{2,1,0:T(8,128)(2,1)}, bf16[8,160,384]{2,1,0:T(8,128)(2,1)S(1)}, u32[]{:S(2)}, u32[]{:S(2)}) collective-permute-start(bf16[8,160,384]{2,1,0:T(8,128)(2,1)} %get-tuple-element.308), channel_id=1, source_target_pairs={{0,1},{1,0},{2,3},{3,2},{4,5},{5,4},{6,7},{7,6},{8,9},{9,8},{10,11... | collective-permute-start | bytes 2949128 | tf_op jit(solution)/shard_map/ppermute | solution.py:1013
  262.1 17.3 %copy-start.1 = (bf16[4,432,384]{2,1,0:T(8,128)(2,1)S(1)}, bf16[4,432,384]{2,1,0:T(8,128)(2,1)}, u32[]{:S(2)}) copy-start(bf16[4,432,384]{2,1,0:T(8,128)(2,1)} %get-tuple-element.293) | copy-start | bytes 3981316
  264.8 18.8 %collective-permute-start.15 = (bf16[768,768]{1,0:T(8,128)(2,1)S(1)}, bf16[768,768]{1,0:T(8,128)(2,1)S(1)}, u32[]{:S(2)}, u32[]{:S(2)}) collective-permute-start(bf16[768,768]{1,0:T(8,128)(2,1)S(1)} %get-tuple-element.417), channel_id=1, source_target_pairs={{0,1},{1,0},{2,3},{3,2},{4,5},{5,4},{6,7},{7,6},{8,9},{9,8},{10,11... | collective-permute-start | bytes 3538952 | tf_op jit(solution)/shard_map/ppermute | solution.py:1013
  265.3 16.5 %copy-start.5 = (bf16[8,160,384]{2,1,0:T(8,128)(2,1)S(1)}, bf16[8,160,384]{2,1,0:T(8,128)(2,1)}, u32[]{:S(2)}) copy-start(bf16[8,160,384]{2,1,0:T(8,128)(2,1)} %get-tuple-element.310) | copy-start | bytes 2949124
  265.3 28.4 %collective-permute-start.18 = (bf16[768,768]{1,0:T(8,128)(2,1)}, bf16[768,768]{1,0:T(8,128)(2,1)}, u32[]{:S(2)}, u32[]{:S(2)}) collective-permute-start(bf16[768,768]{1,0:T(8,128)(2,1)} %get-tuple-element.334), channel_id=1, source_target_pairs={{0,2},{1,3},{2,0},{3,1},{4,6},{5,7},{6,4},{7,5},{8,10},{9,11},{10,... | collective-permute-start | bytes 3538952 | tf_op jit(solution)/shard_map/ppermute | solution.py:1013
  267.2 28.4 %collective-permute-start.14 = (bf16[1,160,384]{2,1,0:T(8,128)(2,1)}, bf16[1,160,384]{2,1,0:T(8,128)(2,1)S(1)}, u32[]{:S(2)}, u32[]{:S(2)}) collective-permute-start(bf16[1,160,384]{2,1,0:T(8,128)(2,1)} %get-tuple-element.314), channel_id=1, source_target_pairs={{0,16},{4,20},{8,24},{12,28},{16,0},{20,4},{24,8},{28,12},{1,17},{... | collective-permute-start | bytes 368648 | tf_op jit(solution)/shard_map/ppermute | solution.py:1016
  281.9 14.4 %collective-permute-start.16 = (bf16[4,160,384]{2,1,0:T(8,128)(2,1)S(1)}, bf16[4,160,384]{2,1,0:T(8,128)(2,1)}, u32[]{:S(2)}, u32[]{:S(2)}) collective-permute-start(bf16[4,160,384]{2,1,0:T(8,128)(2,1)S(1)} %get-tuple-element.323), channel_id=1, source_target_pairs={{0,4},{4,0},{8,12},{12,8},{16,20},{20,16},{24,28},{28,24},{1,5},{5... | collective-permute-start | bytes 1474568 | tf_op jit(solution)/shard_map/ppermute | solution.py:1016
  282.9 16.0 %collective-permute-start.17 = (bf16[2,432,384]{2,1,0:T(8,128)(2,1)}, bf16[2,432,384]{2,1,0:T(8,128)(2,1)}, u32[]{:S(2)}, u32[]{:S(2)}) collective-permute-start(bf16[2,432,384]{2,1,0:T(8,128)(2,1)} %get-tuple-element.329), channel_id=1, source_target_pairs={{0,8},{4,12},{8,0},{12,4},{16,24},{20,28},{24,16},{28,20},{1,9},{5... | collective-permute-start | bytes 1990664 | tf_op jit(solution)/shard_map/ppermute | solution.py:1016
  290.2 5.5 %copy-start.7 = (bf16[1,160,384]{2,1,0:T(8,128)(2,1)S(1)}, bf16[1,160,384]{2,1,0:T(8,128)(2,1)}, u32[]{:S(2)}) copy-start(bf16[1,160,384]{2,1,0:T(8,128)(2,1)} %get-tuple-element.316) | copy-start | bytes 368644
  302.2 4.5 %collective-permute-start.19 = (bf16[768,768]{1,0:T(8,128)(2,1)S(1)}, bf16[768,768]{1,0:T(8,128)(2,1)}, u32[]{:S(2)}, u32[]{:S(2)}) collective-permute-start(bf16[768,768]{1,0:T(8,128)(2,1)S(1)} %get-tuple-element.415), channel_id=1, source_target_pairs={{0,1},{1,0},{2,3},{3,2},{4,5},{5,4},{6,7},{7,6},{8,9},{9,8},{10,11... | collective-permute-start | bytes 3538952 | tf_op jit(solution)/shard_map/ppermute | solution.py:1013
  302.6 20.5 %collective-permute-start.35 = (f32[2,2,2]{2,1,0:T(2,128)S(1)}, f32[2,2,2]{2,1,0:T(2,128)S(1)}, u32[]{:S(2)}, u32[]{:S(2)}) collective-permute-start(f32[2,2,2]{2,1,0:T(2,128)S(1)} %reshape.220), channel_id=1, source_target_pairs={{0,1},{1,0},{2,3},{3,2},{4,5},{5,4},{6,7},{7,6},{8,9},{9,8},{10,11... | collective-permute-start | bytes 104 | tf_op jit(solution)/shard_map/ppermute | solution.py:1013
  303.1 20.2 %collective-permute-start.26 = (bf16[432,384]{1,0:T(8,128)(2,1)S(1)}, bf16[432,384]{1,0:T(8,128)(2,1)}, u32[]{:S(2)}, u32[]{:S(2)}) collective-permute-start(bf16[432,384]{1,0:T(8,128)(2,1)S(1)} %copy-done.9), channel_id=1, source_target_pairs={{0,2},{1,3},{2,0},{3,1},{4,6},{5,7},{6,4},{7,5},{8,10},{9,11},{10,... | collective-permute-start | bytes 995336 | tf_op jit(solution)/shard_map/ppermute | solution.py:1013
  304.6 11.6 %collective-permute-start.20 = (bf16[2,160,384]{2,1,0:T(8,128)(2,1)S(1)}, bf16[2,160,384]{2,1,0:T(8,128)(2,1)S(1)}, u32[]{:S(2)}, u32[]{:S(2)}) collective-permute-start(bf16[2,160,384]{2,1,0:T(8,128)(2,1)S(1)} %get-tuple-element.342), channel_id=1, source_target_pairs={{0,8},{4,12},{8,0},{12,4},{16,24},{20,28},{24,16},{28,20},{1,9},{5... | collective-permute-start | bytes 737288 | tf_op jit(solution)/shard_map/ppermute | solution.py:1016
  305.0 17.5 %collective-permute-start.21 = (bf16[1,432,384]{2,1,0:T(8,128)(2,1)}, bf16[1,432,384]{2,1,0:T(8,128)(2,1)S(1)}, u32[]{:S(2)}, u32[]{:S(2)}) collective-permute-start(bf16[1,432,384]{2,1,0:T(8,128)(2,1)} %get-tuple-element.348), channel_id=1, source_target_pairs={{0,16},{4,20},{8,24},{12,28},{16,0},{20,4},{24,8},{28,12},{1,17},{... | collective-permute-start | bytes 995336 | tf_op jit(solution)/shard_map/ppermute | solution.py:1016
  322.5 16.4 %copy-start.10 = (bf16[432,384]{1,0:T(8,128)(2,1)}, bf16[432,384]{1,0:T(8,128)(2,1)S(1)}, u32[]{:S(2)}) copy-start(bf16[432,384]{1,0:T(8,128)(2,1)S(1)} %add_bitcast_fusion.refs_0_) | copy-start | bytes 995332
  322.5 9.7 %collective-permute-start.23 = (bf16[432,384]{1,0:T(8,128)(2,1)S(1)}, bf16[432,384]{1,0:T(8,128)(2,1)S(1)}, u32[]{:S(2)}, u32[]{:S(2)}) collective-permute-start(bf16[432,384]{1,0:T(8,128)(2,1)S(1)} %add_bitcast_fusion.refs_0_), channel_id=1, source_target_pairs={{0,2},{1,3},{2,0},{3,1},{4,6},{5,7},{6,4},{7,5},{8,10},{9,11},{10,... | collective-permute-start | bytes 995336 | tf_op jit(solution)/shard_map/ppermute | solution.py:1013
  323.0 6.3 %collective-permute-start.22 = (bf16[1,160,384]{2,1,0:T(8,128)(2,1)S(1)}, bf16[1,160,384]{2,1,0:T(8,128)(2,1)S(1)}, u32[]{:S(2)}, u32[]{:S(2)}) collective-permute-start(bf16[1,160,384]{2,1,0:T(8,128)(2,1)S(1)} %get-tuple-element.354), channel_id=1, source_target_pairs={{0,16},{4,20},{8,24},{12,28},{16,0},{20,4},{24,8},{28,12},{1,17},{... | collective-permute-start | bytes 368648 | tf_op jit(solution)/shard_map/ppermute | solution.py:1016
  323.0 9.2 %collective-permute-start.27 = (bf16[432,384]{1,0:T(8,128)(2,1)S(1)}, bf16[432,384]{1,0:T(8,128)(2,1)S(1)}, u32[]{:S(2)}, u32[]{:S(2)}) collective-permute-start(bf16[432,384]{1,0:T(8,128)(2,1)S(1)} %copy-done.9), channel_id=1, source_target_pairs={{0,1},{1,0},{2,3},{3,2},{4,5},{5,4},{6,7},{7,6},{8,9},{9,8},{10,11... | collective-permute-start | bytes 995336 | tf_op jit(solution)/shard_map/ppermute | solution.py:1013
  323.3 10.2 %collective-permute-start.28 = (bf16[432,384]{1,0:T(8,128)(2,1)}, bf16[432,384]{1,0:T(8,128)(2,1)S(1)}, u32[]{:S(2)}, u32[]{:S(2)}) collective-permute-start(bf16[432,384]{1,0:T(8,128)(2,1)} %collective-permute-done.26.refs_5_), channel_id=1, source_target_pairs={{0,1},{1,0},{2,3},{3,2},{4,5},{5,4},{6,7},{7,6},{8,9},{9,8},{10,11... | collective-permute-start | bytes 995336 | tf_op jit(solution)/shard_map/ppermute | solution.py:1013
  323.9 9.9 %collective-permute-start.32 = (bf16[160,384]{1,0:T(8,128)(2,1)}, bf16[160,384]{1,0:T(8,128)(2,1)S(1)}, u32[]{:S(2)}, u32[]{:S(2)}) collective-permute-start(bf16[160,384]{1,0:T(8,128)(2,1)} %add_bitcast_fusion.3.refs_4_), channel_id=1, source_target_pairs={{0,2},{1,3},{2,0},{3,1},{4,6},{5,7},{6,4},{7,5},{8,10},{9,11},{10,... | collective-permute-start | bytes 368648 | tf_op jit(solution)/shard_map/ppermute | solution.py:1013
  329.3 8.8 %collective-permute-start.24 = (bf16[432,384]{1,0:T(8,128)(2,1)S(1)}, bf16[432,384]{1,0:T(8,128)(2,1)S(1)}, u32[]{:S(2)}, u32[]{:S(2)}) collective-permute-start(bf16[432,384]{1,0:T(8,128)(2,1)S(1)} %add_bitcast_fusion.refs_0_), channel_id=1, source_target_pairs={{0,1},{1,0},{2,3},{3,2},{4,5},{5,4},{6,7},{7,6},{8,9},{9,8},{10,11... | collective-permute-start | bytes 995336 | tf_op jit(solution)/shard_map/ppermute | solution.py:1013
  332.2 6.6 %copy-start.20 = (bf16[432,384]{1,0:T(8,128)(2,1)}, bf16[432,384]{1,0:T(8,128)(2,1)S(1)}, u32[]{:S(2)}) copy-start(bf16[432,384]{1,0:T(8,128)(2,1)S(1)} %collective-permute-done.23.refs_1_) | copy-start | bytes 995332
  332.2 6.6 %collective-permute-start.25 = (bf16[432,384]{1,0:T(8,128)(2,1)S(1)}, bf16[432,384]{1,0:T(8,128)(2,1)}, u32[]{:S(2)}, u32[]{:S(2)}) collective-permute-start(bf16[432,384]{1,0:T(8,128)(2,1)S(1)} %collective-permute-done.23.refs_1_), channel_id=1, source_target_pairs={{0,1},{1,0},{2,3},{3,2},{4,5},{5,4},{6,7},{7,6},{8,9},{9,8},{10,11... | collective-permute-start | bytes 995336 | tf_op jit(solution)/shard_map/ppermute | solution.py:1013
  332.3 12.2 %copy-start.13 = (bf16[160,384]{1,0:T(8,128)(2,1)}, bf16[160,384]{1,0:T(8,128)(2,1)S(1)}, u32[]{:S(2)}) copy-start(bf16[160,384]{1,0:T(8,128)(2,1)S(1)} %add_bitcast_fusion.2.refs_0_) | copy-start | bytes 368644
  332.3 6.6 %copy-start.21 = (bf16[432,384]{1,0:T(8,128)(2,1)}, bf16[432,384]{1,0:T(8,128)(2,1)S(1)}, u32[]{:S(2)}) copy-start(bf16[432,384]{1,0:T(8,128)(2,1)S(1)} %collective-permute-done.27.refs_6_) | copy-start | bytes 995332
  332.3 5.8 %collective-permute-start.29 = (bf16[160,384]{1,0:T(8,128)(2,1)S(1)}, bf16[160,384]{1,0:T(8,128)(2,1)S(1)}, u32[]{:S(2)}, u32[]{:S(2)}) collective-permute-start(bf16[160,384]{1,0:T(8,128)(2,1)S(1)} %add_bitcast_fusion.2.refs_0_), channel_id=1, source_target_pairs={{0,2},{1,3},{2,0},{3,1},{4,6},{5,7},{6,4},{7,5},{8,10},{9,11},{10,... | collective-permute-start | bytes 368648 | tf_op jit(solution)/shard_map/ppermute | solution.py:1013
  333.5 10.9 %collective-permute-start.33 = (bf16[160,384]{1,0:T(8,128)(2,1)}, bf16[160,384]{1,0:T(8,128)(2,1)S(1)}, u32[]{:S(2)}, u32[]{:S(2)}) collective-permute-start(bf16[160,384]{1,0:T(8,128)(2,1)} %add_bitcast_fusion.3.refs_4_), channel_id=1, source_target_pairs={{0,1},{1,0},{2,3},{3,2},{4,5},{5,4},{6,7},{7,6},{8,9},{9,8},{10,11... | collective-permute-start | bytes 368648 | tf_op jit(solution)/shard_map/ppermute | solution.py:1013
  333.8 10.7 %copy-start.24 = (bf16[160,384]{1,0:T(8,128)(2,1)}, bf16[160,384]{1,0:T(8,128)(2,1)S(1)}, u32[]{:S(2)}) copy-start(bf16[160,384]{1,0:T(8,128)(2,1)S(1)} %collective-permute-done.32.refs_5_) | copy-start | bytes 368644
  333.8 10.7 %collective-permute-start.34 = (bf16[160,384]{1,0:T(8,128)(2,1)S(1)}, bf16[160,384]{1,0:T(8,128)(2,1)S(1)}, u32[]{:S(2)}, u32[]{:S(2)}) collective-permute-start(bf16[160,384]{1,0:T(8,128)(2,1)S(1)} %collective-permute-done.32.refs_5_), channel_id=1, source_target_pairs={{0,1},{1,0},{2,3},{3,2},{4,5},{5,4},{6,7},{7,6},{8,9},{9,8},{10,11... | collective-permute-start | bytes 368648 | tf_op jit(solution)/shard_map/ppermute | solution.py:1013
  338.1 6.3 %copy-start.25 = (bf16[160,384]{1,0:T(8,128)(2,1)}, bf16[160,384]{1,0:T(8,128)(2,1)S(1)}, u32[]{:S(2)}) copy-start(bf16[160,384]{1,0:T(8,128)(2,1)S(1)} %collective-permute-done.29.refs_1_) | copy-start | bytes 368644
  338.1 6.4 %collective-permute-start.30 = (bf16[160,384]{1,0:T(8,128)(2,1)S(1)}, bf16[160,384]{1,0:T(8,128)(2,1)S(1)}, u32[]{:S(2)}, u32[]{:S(2)}) collective-permute-start(bf16[160,384]{1,0:T(8,128)(2,1)S(1)} %add_bitcast_fusion.2.refs_0_), channel_id=1, source_target_pairs={{0,1},{1,0},{2,3},{3,2},{4,5},{5,4},{6,7},{7,6},{8,9},{9,8},{10,11... | collective-permute-start | bytes 368648 | tf_op jit(solution)/shard_map/ppermute | solution.py:1013
  338.1 6.4 %collective-permute-start.31 = (bf16[160,384]{1,0:T(8,128)(2,1)S(1)}, bf16[160,384]{1,0:T(8,128)(2,1)S(1)}, u32[]{:S(2)}, u32[]{:S(2)}) collective-permute-start(bf16[160,384]{1,0:T(8,128)(2,1)S(1)} %collective-permute-done.29.refs_1_), channel_id=1, source_target_pairs={{0,1},{1,0},{2,3},{3,2},{4,5},{5,4},{6,7},{7,6},{8,9},{9,8},{10,11... | collective-permute-start | bytes 368648 | tf_op jit(solution)/shard_map/ppermute | solution.py:1013
  (18 other events, 33.8 us)
